TPU v7x, 32 devices: a whole 2x2x4 slice. The times are simulated.
32 devices in a mesh: shard: 2 (over x), ctx: 4 (over z), tp: 4 (over y, core).
Axes of the slice: x: 2, y: 2, z: 4, core: 2. Of those that a mesh axis runs over, the one named last changes fastest.
Arguments:
- tokens: bfloat16 [16, 1024, 960], P(('shard', 'tp'), 'ctx'), may hold values from -6 to 6
- cotangent: bfloat16 [16, 1024, 960], P(('shard', 'tp'), 'ctx'), may hold values from -6 to 6
- piece_starts: int32 [16, 2], P(('shard', 'tp')), may hold values from 0 to 768, as said below
- doc_lengths: int32 [16, 3], P(('shard', 'tp')), may hold values from 1 to 512, 1024 in all within a row
- attn_gain: bfloat16 [960], P('shard'), may hold values from 0.099609375 to 1.8984375
- w_query: bfloat16 [960, 960], P('shard'), may hold values from -0.1875 to 0.1875
- w_key: bfloat16 [960, 320], P('shard'), may hold values from -0.1875 to 0.1875
- w_value: bfloat16 [960, 320], P('shard'), may hold values from -0.1875 to 0.1875
- w_out: bfloat16 [960, 960], P('shard'), may hold values from -1.5 to 1.5
- ff_gain: bfloat16 [960], P('shard'), may hold values from 0.099609375 to 1.8984375
- w_gate: bfloat16 [960, 2560], P('shard', 'tp'), may hold values from -0.1875 to 0.1875
- w_up: bfloat16 [960, 2560], P('shard', 'tp'), may hold values from -0.1875 to 0.1875
- w_down: bfloat16 [960, 2560], P('shard', 'tp'), may hold values from -0.125 to 0.125
Outputs:
- layer_output: bfloat16 [16, 1024, 960], P(('shard', 'tp'), 'ctx')
- input_grad: float32 [16, 1024, 960], P(('shard', 'tp'), 'ctx')
- attn_gain_grad: float32 [960], P('shard')
- w_query_grad: float32 [960, 960], P('shard')
- w_key_grad: float32 [960, 320], P('shard')
- w_value_grad: float32 [960, 320], P('shard')
- w_out_grad: float32 [960, 960], P('shard')
- ff_gain_grad: float32 [960], P('shard')
- w_gate_grad: float32 [960, 2560], P('shard', 'tp')
- w_up_grad: float32 [960, 2560], P('shard', 'tp')
- w_down_grad: float32 [960, 2560], P('shard', 'tp')
Inputs may be any that keep to these rules, and one draw needn't show every extreme that they name: `piece_starts`: each row holds the first positions of two pieces of 256 tokens of its sequence, multiples of 128, the first below the second, the pieces not intersecting. `doc_lengths`: each row lists the lengths of its sequence's consecutive documents, summing to 1024.
All inputs are finite; a program needn't handle non-finite values.
Results may differ from a plain program's by a relative error of at most 0.013.
Values may be sent and summed in bfloat16 or wider, within the bound.
No kernel may reach another device: no remote copies, remote signals or barrier semaphores. Data moves between devices by JAX's collectives and lax.ppermute only.
A program may use at most 448 MiB of HBM per device.

v0:
```python
import math

import jax
import jax.numpy as jnp
from jax import lax
from jax.sharding import PartitionSpec as P

H = 15
KVH = 5
HD = 64
LEN = 1024
PIECE = 256


EPS = 1e-05
NEG = -1e30


def rotary_tables(offset, length):
    half = HD // 2
    place = (offset + jnp.arange(length, dtype=jnp.int32)).astype(jnp.float32)
    freq = jnp.exp(jnp.arange(half).astype(jnp.float32) * (-2.0 * math.log(10000.0) / HD))
    angle = place[:, None] * freq[None, :]
    return (jnp.cos(angle), jnp.sin(angle))


def rotate(value, cosine, sine):
    half = HD // 2
    first = value[..., :half]
    second = value[..., half:]
    cosine = cosine[:, None, :]
    sine = sine[:, None, :]
    return jnp.concatenate(
        [first * cosine - second * sine, second * cosine + first * sine], axis=-1
    )


def labels(starts, lengths):
    where = jnp.arange(LEN, dtype=jnp.int32)
    ends = jnp.cumsum(lengths, axis=1)
    segment = jnp.sum((where[None, :, None] >= ends[:, None, :-1]).astype(jnp.int32), axis=2)
    inside = (where[None, :, None] >= starts[:, None, :]) & (
        where[None, :, None] < starts[:, None, :] + PIECE
    )
    number = jnp.sum(
        inside.astype(jnp.int32) * jnp.arange(1, 3, dtype=jnp.int32)[None, None, :], axis=2
    )
    return (segment, number)


def allowed(query_pos, key_pos, query_seg, key_seg, query_num, key_num):
    same_doc = query_seg[:, None] == key_seg[None, :]
    causal = key_pos[None, :] <= query_pos[:, None]
    picture = (query_num[:, None] == key_num[None, :]) & (query_num[:, None] > 0)
    return same_doc & (causal | picture)


def outer(left, right):
    return lax.dot_general(
        left, right, (((0,), (0,)), ((), ())), preferred_element_type=jnp.float32
    )


def contract_last(left, right):
    return lax.dot_general(
        left, right, (((1,), (1,)), ((), ())), preferred_element_type=jnp.float32
    )


def norm_back(source, scale_rows, gain, grad):
    weighted = grad * gain
    grad_source = scale_rows * weighted - source * scale_rows**3 * jnp.mean(
        source * weighted, axis=-1, keepdims=True
    )
    grad_gain = jnp.sum(grad * source * scale_rows, axis=0)
    return (grad_source, grad_gain)


def per_device(
    tokens,
    cotangent,
    piece_starts,
    doc_lengths,
    attn_gain,
    w_query,
    w_key,
    w_value,
    w_out,
    ff_gain,
    w_gate,
    w_up,
    w_down,
):
    (
        gain_one,
        query_weight,
        key_weight,
        value_weight,
        out_weight,
        gain_two,
        gate_weight,
        up_weight,
        down_weight,
    ) = (
        lax.all_gather(attn_gain, "shard", axis=0, tiled=True),
        lax.all_gather(w_query, "shard", axis=0, tiled=True),
        lax.all_gather(w_key, "shard", axis=0, tiled=True),
        lax.all_gather(w_value, "shard", axis=0, tiled=True),
        lax.all_gather(w_out, "shard", axis=0, tiled=True),
        lax.all_gather(ff_gain, "shard", axis=0, tiled=True),
        lax.all_gather(w_gate, "shard", axis=0, tiled=True),
        lax.all_gather(w_up, "shard", axis=0, tiled=True),
        lax.all_gather(w_down, "shard", axis=0, tiled=True),
    )
    seqs_here, local_len, width = tokens.shape
    rows = seqs_here * local_len
    group = H // KVH
    scale = HD ** (-0.5)
    offset = lax.axis_index("ctx") * local_len
    cosine, sine = rotary_tables(offset, local_len)
    gain_one = gain_one.astype(jnp.float32)
    gain_two = gain_two.astype(jnp.float32)
    source_one = tokens.reshape(rows, width).astype(jnp.float32)
    scale_one = lax.rsqrt(jnp.mean(source_one * source_one, axis=-1, keepdims=True) + EPS)
    normed_one = (source_one * scale_one * gain_one).astype(jnp.bfloat16)
    query_raw = jnp.dot(normed_one, query_weight, preferred_element_type=jnp.float32)
    key_raw = jnp.dot(normed_one, key_weight, preferred_element_type=jnp.float32)
    value_raw = jnp.dot(normed_one, value_weight, preferred_element_type=jnp.float32)
    query_rot = rotate(query_raw.reshape(seqs_here, local_len, H, HD), cosine, sine).astype(
        jnp.bfloat16
    )
    key_rot = rotate(key_raw.reshape(seqs_here, local_len, KVH, HD), cosine, sine).astype(
        jnp.bfloat16
    )
    key_rot = key_rot.reshape(seqs_here, local_len, KVH * HD)
    value_low = value_raw.astype(jnp.bfloat16).reshape(seqs_here, local_len, KVH * HD)
    keys_all, values_all = (
        lax.all_gather(key_rot, "ctx", axis=1, tiled=True),
        lax.all_gather(value_low, "ctx", axis=1, tiled=True),
    )
    segment, number = labels(piece_starts, doc_lengths)
    key_pos = jnp.arange(LEN, dtype=jnp.int32)
    query_pos = offset + jnp.arange(local_len, dtype=jnp.int32)

    def scores_of(index):
        query_seg = lax.dynamic_slice_in_dim(segment[index], offset, local_len)
        query_num = lax.dynamic_slice_in_dim(number[index], offset, local_len)
        permit = allowed(query_pos, key_pos, query_seg, segment[index], query_num, number[index])
        query_seq = query_rot[index].reshape(local_len, KVH, group, HD)
        keys_seq = keys_all[index].reshape(LEN, KVH, HD)
        scores = (
            jnp.einsum("qhgd,khd->hgqk", query_seq, keys_seq, preferred_element_type=jnp.float32)
            * scale
        )
        return jnp.where(permit[None, None], scores, NEG)

    mixed_parts = []
    logsum_parts = []
    for index in range(seqs_here):
        scores = scores_of(index)
        top = jnp.max(scores, axis=-1, keepdims=True)
        raised = jnp.exp(scores - top)
        total = jnp.sum(raised, axis=-1, keepdims=True)
        probs = (raised / total).astype(jnp.bfloat16)
        values_seq = values_all[index].reshape(LEN, KVH, HD)
        mixed_seq = jnp.einsum(
            "hgqk,khd->qhgd", probs, values_seq, preferred_element_type=jnp.float32
        )
        mixed_parts.append(mixed_seq.reshape(local_len, H * HD))
        logsum_parts.append(top + jnp.log(total))
    mixed = jnp.concatenate(mixed_parts, axis=0).astype(jnp.bfloat16)
    hidden_state = source_one + jnp.dot(mixed, out_weight, preferred_element_type=jnp.float32)
    scale_two = lax.rsqrt(jnp.mean(hidden_state * hidden_state, axis=-1, keepdims=True) + EPS)
    normed_two = (hidden_state * scale_two * gain_two).astype(jnp.bfloat16)
    gate_use, up_use, down_use = (gate_weight, up_weight, down_weight)
    ff_rows = lax.all_gather(normed_two, "tp", axis=0, tiled=True)
    gate = jnp.dot(ff_rows, gate_use, preferred_element_type=jnp.float32)
    up = jnp.dot(ff_rows, up_use, preferred_element_type=jnp.float32)
    sigma = jax.nn.sigmoid(gate)
    inner = (gate * sigma * up).astype(jnp.bfloat16)
    cot_rows = cotangent.reshape(rows, width)
    ff_out = lax.psum_scatter(
        contract_last(inner, down_use).astype(jnp.bfloat16), "tp", scatter_dimension=0, tiled=True
    ).astype(jnp.float32)
    grad_rows = lax.all_gather(cot_rows, "tp", axis=0, tiled=True)
    layer_output = (hidden_state + ff_out).astype(jnp.bfloat16).reshape(seqs_here, local_len, width)
    grad_inner = jnp.dot(grad_rows, down_use, preferred_element_type=jnp.float32)
    grad_down = outer(grad_rows, inner)
    grad_gate = (grad_inner * up * sigma * (1.0 + gate * (1.0 - sigma))).astype(jnp.bfloat16)
    grad_up = (grad_inner * gate * sigma).astype(jnp.bfloat16)
    grad_gate_w = outer(ff_rows, grad_gate)
    grad_up_w = outer(ff_rows, grad_up)
    grad_normed_two = lax.psum_scatter(
        contract_last(grad_gate, gate_use) + contract_last(grad_up, up_use),
        "tp",
        scatter_dimension=0,
        tiled=True,
    )
    grad_source_two, grad_gain_two = norm_back(hidden_state, scale_two, gain_two, grad_normed_two)
    grad_hidden = cot_rows.astype(jnp.float32) + grad_source_two
    grad_branch = grad_hidden.astype(jnp.bfloat16)
    grad_out_w = outer(mixed, grad_branch)
    grad_mixed = contract_last(grad_branch, out_weight).astype(jnp.bfloat16)
    key_grads = []
    value_grads = []
    query_grads = []
    for index in range(seqs_here):
        scores = scores_of(index)
        probs = jnp.exp(scores - logsum_parts[index])
        probs_low = probs.astype(jnp.bfloat16)
        grad_out = grad_mixed[index * local_len : (index + 1) * local_len].reshape(
            local_len, KVH, group, HD
        )
        query_seq = query_rot[index].reshape(local_len, KVH, group, HD)
        keys_seq = keys_all[index].reshape(LEN, KVH, HD)
        values_seq = values_all[index].reshape(LEN, KVH, HD)
        grad_probs = jnp.einsum(
            "qhgd,khd->hgqk", grad_out, values_seq, preferred_element_type=jnp.float32
        )
        value_grads.append(
            jnp.einsum(
                "hgqk,qhgd->khd", probs_low, grad_out, preferred_element_type=jnp.float32
            ).reshape(LEN, KVH * HD)
        )
        delta = jnp.sum(probs * grad_probs, axis=-1, keepdims=True)
        grad_scores = (probs * (grad_probs - delta) * scale).astype(jnp.bfloat16)
        query_grads.append(
            jnp.einsum(
                "hgqk,khd->qhgd", grad_scores, keys_seq, preferred_element_type=jnp.float32
            ).reshape(local_len, H, HD)
        )
        key_grads.append(
            jnp.einsum(
                "hgqk,qhgd->khd", grad_scores, query_seq, preferred_element_type=jnp.float32
            ).reshape(LEN, KVH * HD)
        )
    key_grad, value_grad = (
        lax.psum_scatter(jnp.stack(key_grads), "ctx", scatter_dimension=1, tiled=True),
        lax.psum_scatter(jnp.stack(value_grads), "ctx", scatter_dimension=1, tiled=True),
    )
    grad_query = (
        rotate(jnp.stack(query_grads), cosine, -sine).astype(jnp.bfloat16).reshape(rows, H * HD)
    )
    grad_key = (
        rotate(key_grad.reshape(seqs_here, local_len, KVH, HD), cosine, -sine)
        .astype(jnp.bfloat16)
        .reshape(rows, KVH * HD)
    )
    grad_value = value_grad.astype(jnp.bfloat16).reshape(rows, KVH * HD)
    grad_query_w = outer(normed_one, grad_query)
    grad_key_w = outer(normed_one, grad_key)
    grad_value_w = outer(normed_one, grad_value)
    grad_normed_one = (
        contract_last(grad_query, query_weight)
        + contract_last(grad_key, key_weight)
        + contract_last(grad_value, value_weight)
    )
    grad_source_one, grad_gain_one = norm_back(source_one, scale_one, gain_one, grad_normed_one)
    input_grad = (grad_hidden + grad_source_one).reshape(seqs_here, local_len, width)
    (
        sum_gain_one,
        sum_query,
        sum_key,
        sum_value,
        sum_out,
        sum_gain_two,
        sum_gate,
        sum_up,
        sum_down,
    ) = (
        lax.psum_scatter(grad_gain_one, "shard", scatter_dimension=0, tiled=True),
        lax.psum_scatter(grad_query_w, "shard", scatter_dimension=0, tiled=True),
        lax.psum_scatter(grad_key_w, "shard", scatter_dimension=0, tiled=True),
        lax.psum_scatter(grad_value_w, "shard", scatter_dimension=0, tiled=True),
        lax.psum_scatter(grad_out_w, "shard", scatter_dimension=0, tiled=True),
        lax.psum_scatter(grad_gain_two, "shard", scatter_dimension=0, tiled=True),
        lax.psum_scatter(grad_gate_w, "shard", scatter_dimension=0, tiled=True),
        lax.psum_scatter(grad_up_w, "shard", scatter_dimension=0, tiled=True),
        lax.psum_scatter(grad_down, "shard", scatter_dimension=0, tiled=True),
    )
    sum_gain_one, sum_query, sum_key, sum_value, sum_out, sum_gain_two = lax.psum(
        (sum_gain_one, sum_query, sum_key, sum_value, sum_out, sum_gain_two), ("ctx", "tp")
    )
    sum_gate, sum_up, sum_down = lax.psum((sum_gate, sum_up, sum_down), "ctx")
    return (
        layer_output,
        input_grad,
        sum_gain_one,
        sum_query,
        sum_key,
        sum_value,
        sum_out,
        sum_gain_two,
        sum_gate,
        sum_up,
        sum_down,
    )


def solution(mesh):
    placed = (
        P(("shard", "tp"), "ctx", None),
        P(("shard", "tp"), "ctx", None),
        P(("shard", "tp"), None),
        P(("shard", "tp"), None),
        P("shard"),
        P("shard", None),
        P("shard", None),
        P("shard", None),
        P("shard", None),
        P("shard"),
        P("shard", "tp"),
        P("shard", "tp"),
        P("shard", "tp"),
    )
    return jax.shard_map(
        per_device,
        mesh=mesh,
        in_specs=placed,
        out_specs=(
            P(("shard", "tp"), "ctx", None),
            P(("shard", "tp"), "ctx", None),
            P("shard"),
            P("shard", None),
            P("shard", None),
            P("shard", None),
            P("shard", None),
            P("shard"),
            P("shard", "tp"),
            P("shard", "tp"),
            P("shard", "tp"),
        ),
        check_vma=False,
    )
```

profile of v0, /device:TPU:1, one launch (start us, length us, event | category | flops | bytes accessed | tf_op | source)
XLA Modules:
  0.0 1335.0 jit_solution(17249326635128893481)
XLA Ops:
  11.8 4.3 all-reduce.8
  16.1 13.3 all-gather.1
  33.4 16.7 %all-gather = bf16[2,480,320]{1,2,0:T(8,128)(2,1)S(1)} all-gather(bf16[1,480,320]{1,2,0:T(8,128)(2,1)S(1)} %bitcast.287), channel_id=1, replica_groups=mesh['shard'=2,'ctx'=4,'tp'=4] {'shard'}, dimensions={0}, use_global_device_ids=true | all-gather | bytes 921600 | tf_op jit(solution)/shard_map/all_gather | solution.py:108
  58.8 3.8 copy.85
  62.6 2.8 fusion.36
  66.6 24.0 %all-gather.14.cloned.1.call-done = bf16[2,1024,320]{1,2,0:T(8,128)(2,1)} async-done(((bf16[2,256,320]{1,2,0:T(8,128)(2,1)}), bf16[2,1024,320]{1,2,0:T(8,128)(2,1)}) %all-gather.14.cloned.1.call-update) | async-done | bytes 1310736 | tf_op jit(solution)/shard_map/all_gather | solution.py:138
  92.0 6.7 fusion.72
  98.8 7.8 fusion.9
  106.6 18.2 %all-gather.12.cloned.1.call-done = bf16[2,1024,320]{1,2,0:T(8,128)(2,1)} async-done(((bf16[2,256,320]{1,2,0:T(8,128)(2,1)}), bf16[2,1024,320]{1,2,0:T(8,128)(2,1)}) %all-gather.12.cloned.1.call-update) | async-done | bytes 1310736 | tf_op jit(solution)/shard_map/all_gather | solution.py:139
  126.2 8.3 fusion.29
  134.5 6.8 fusion.73
  141.3 7.6 fusion.8
  148.9 7.5 fusion.30
  157.6 2.8 multiply_reduce_fusion.4
  165.6 16.8 %all-gather.24.cloned.1.call-done = bf16[960,640]{1,0:T(8,128)(2,1)} async-done(((bf16[480,640]{1,0:T(8,128)(2,1)}), bf16[960,640]{1,0:T(8,128)(2,1)}) %all-gather.24.cloned.1.call-update) | async-done | bytes 1228816 | tf_op jit(solution)/shard_map/all_gather | solution.py:112
  182.4 35.4 %all-gather.20.cloned.1.call-done = bf16[2048,960]{0,1:T(8,128)(2,1)} async-done(((bf16[512,960]{0,1:T(8,128)(2,1)}), bf16[2048,960]{0,1:T(8,128)(2,1)}) %all-gather.20.cloned.1.call-update) | async-done | bytes 3932176 | tf_op jit(solution)/shard_map/all_gather | solution.py:176
  217.8 8.4 fusion.75
  226.2 16.1 %all-gather.22.cloned.1.call-done = bf16[960,640]{1,0:T(8,128)(2,1)} async-done(((bf16[480,640]{1,0:T(8,128)(2,1)}), bf16[960,640]{1,0:T(8,128)(2,1)}) %all-gather.22.cloned.1.call-update) | async-done | bytes 1228816 | tf_op jit(solution)/shard_map/all_gather | solution.py:111
  242.3 8.3 fusion.74
  250.6 16.6 %all-gather.26.cloned.1.call-done = bf16[960,640]{1,0:T(8,128)(2,1)} async-done(((bf16[480,640]{1,0:T(8,128)(2,1)}), bf16[960,640]{1,0:T(8,128)(2,1)}) %all-gather.26.cloned.1.call-update) | async-done | bytes 1228816 | tf_op jit(solution)/shard_map/all_gather | solution.py:113
  267.2 35.6 %all-gather.28.cloned.1.call-done = bf16[2048,960]{0,1:T(8,128)(2,1)} async-done(((bf16[512,960]{0,1:T(8,128)(2,1)}), bf16[2048,960]{0,1:T(8,128)(2,1)}) %all-gather.28.cloned.1.call-update) | async-done | bytes 3932176 | tf_op jit(solution)/shard_map/all_gather | solution.py:185
  302.8 10.9 multiply_convert_fusion
  313.7 3.3 fusion.76
  317.0 5.5 convolution_add_fusion
  323.8 6.5 convolution_convert_fusion
  330.7 60.6 %reduce-scatter.20.cloned.1.call-done = f32[512,960]{0,1:T(8,128)} async-done(((f32[2048,960]{0,1:T(8,128)}), f32[512,960]{0,1:T(8,128)}) %reduce-scatter.20.cloned.1.call-update) | async-done | bytes 1966096 | tf_op jit(solution)/shard_map/reduce_scatter | solution.py:193
  391.3 2.7 multiply_reduce_fusion
  394.0 42.9 %reduce-scatter.18.cloned.1.call-done = bf16[512,960]{0,1:T(8,128)(2,1)} async-done(((bf16[2048,960]{0,1:T(8,128)(2,1)}), bf16[512,960]{0,1:T(8,128)(2,1)}) %reduce-scatter.18.cloned.1.call-update) | async-done | bytes 983056 | tf_op jit(solution)/shard_map/reduce_scatter | solution.py:182
  436.9 3.5 subtract_add_fusion.1
  442.0 7.8 fusion.77
  449.8 7.8 fusion.78
  457.6 21.5 %fusion.22 = f32[5,64,1024,1]{2,1,3,0:T(8,128)S(1)} fusion(bf16[256,5,3,64]{0,3,2,1:T(8,128)(2,1)S(1)} %bitcast.267, f32[5,1024,256,3]{2,1,3,0:T(8,128)} %fusion.77, f32[5,3,256,1024]{2,3,1,0:T(8,128)} %get-tuple-element.111, f32[5,3,256]{2,1,0:T(4,128)S(1)} %log_add_fusion.1), kind=kOutput, calls=%fused_computation.32 | convolution fusion | flops 530846464 | bytes 33274880 | tf_op jit(solution)/shard_map/hgqk,qhgd->khd/dot_general | solution.py:233
  479.2 22.5 %fusion.18 = f32[5,64,1024,1]{2,1,3,0:T(8,128)} fusion(bf16[256,5,3,64]{0,3,2,1:T(8,128)(2,1)S(1)} %bitcast.265, f32[5,1024,256,3]{2,1,3,0:T(8,128)} %fusion.78, f32[5,3,256,1024]{2,3,1,0:T(8,128)} %get-tuple-element.109, f32[5,3,256]{2,1,0:T(4,128)S(1)} %log_add_fusion), kind=kOutput, calls=%fused_computation.28 | convolution fusion | flops 530846464 | bytes 33274880 | tf_op jit(solution)/shard_map/hgqk,qhgd->khd/dot_general | solution.py:233
  501.7 3.0 pad_maximum_fusion
  505.2 8.0 fusion.12
  514.6 8.0 fusion.14
  524.0 2.4 pad_maximum_fusion.1
  526.3 76.9 %copy.120 = f32[2,1024,320]{0,2,1:T(8,128)} copy(f32[2,1024,320]{1,0,2:T(2,128)S(1)} %pad_maximum_fusion.1) | data formatting | bytes 5242880
  603.2 113.8 %reshape.550 = f32[1024,640]{1,0:T(8,128)} reshape(f32[1024,320,2]{2,1,0:T(8,128)} %bitcast.77) | data formatting | bytes 5242880
  718.8 6.7 convolution_bitcast_fusion
  725.6 7.7 fusion.82
  733.4 6.8 fusion.83
  745.6 23.5 %reduce-scatter.34.cloned.1.call-done = f32[256,640]{1,0:T(8,128)} async-done(((f32[1024,640]{1,0:T(8,128)}), f32[256,640]{1,0:T(8,128)}) %reduce-scatter.34.cloned.1.call-update) | async-done | bytes 655376
  769.2 47.3 %reshape.551 = bf16[256,320,2]{2,1,0:T(8,128)(2,1)} reshape(f32[256,640]{1,0:T(8,128)} %reduce-scatter.34.cloned.1.call-done) | data formatting | bytes 983040
  816.5 19.3 %copy.121 = bf16[2,256,320]{1,0,2:T(2,128)(2,1)} copy(bf16[2,256,320]{0,2,1:T(8,128)(2,1)} %bitcast.235) | data formatting | bytes 655360
  835.8 3.0 convolution_bitcast_fusion.1
  838.8 4.3 fusion.42
  844.2 22.3 %fusion.23 = f32[5,64,3,256]{3,1,2,0:T(8,128)S(1)} fusion(bf16[1024,5,64,1]{0,2,3,1:T(8,128)(2,1)S(1)} %bitcast.256, f32[5,1024,256,3]{2,1,3,0:T(8,128)} %fusion.77, f32[5,3,256,1024]{2,3,1,0:T(8,128)} %get-tuple-element.111, f32[5,3,256]{2,1,0:T(4,128)S(1)} %log_add_fusion.1), kind=kOutput, calls=%fused_computation.33 | convolution fusion | flops 530846464 | bytes 33111040 | tf_op jit(solution)/shard_map/hgqk,khd->qhgd/dot_general | solution.py:228
  866.5 22.6 %fusion.19 = f32[5,64,3,256]{3,1,2,0:T(8,128)} fusion(bf16[1024,5,64,1]{0,2,3,1:T(8,128)(2,1)S(1)} %bitcast.254, f32[5,1024,256,3]{2,1,3,0:T(8,128)} %fusion.78, f32[5,3,256,1024]{2,3,1,0:T(8,128)} %get-tuple-element.109, f32[5,3,256]{2,1,0:T(4,128)S(1)} %copy-done.44), kind=kOutput, calls=%fused_computation.29 | convolution fusion | flops 530846464 | bytes 33111040 | tf_op jit(solution)/shard_map/hgqk,khd->qhgd/dot_general | solution.py:228
  892.2 3.2 fusion.80
  896.4 14.2 %reduce-scatter.36.cloned.1.call-done = f32[480,320]{1,0:T(8,128)} async-done(((f32[960,320]{1,0:T(8,128)}), f32[480,320]{1,0:T(8,128)}) %reduce-scatter.36.cloned.1.call-update) | async-done | bytes 614416
  910.6 2.2 copy.123
  912.8 24.9 %reduce-scatter.38.cloned.1.call-done = f32[480,320]{1,0:T(8,128)} async-done(((f32[960,320]{1,0:T(8,128)}), f32[480,320]{1,0:T(8,128)}) %reduce-scatter.38.cloned.1.call-update) | async-done | bytes 614416
  937.7 2.2 copy.125
  939.9 52.1 %reduce-scatter.26.cloned.1.call-done = f32[480,960]{1,0:T(8,128)} async-done(((f32[960,960]{1,0:T(8,128)}), f32[480,960]{1,0:T(8,128)}) %reduce-scatter.26.cloned.1.call-update) | async-done | bytes 1843216 | tf_op jit(solution)/shard_map/reduce_scatter | solution.py:275
  992.0 54.2 %reduce-scatter.24.cloned.1.call-done = f32[480,960]{1,0:T(8,128)} async-done(((f32[960,960]{1,0:T(8,128)}), f32[480,960]{1,0:T(8,128)}) %reduce-scatter.24.cloned.1.call-update) | async-done | bytes 1843216 | tf_op jit(solution)/shard_map/reduce_scatter | solution.py:272
  1048.4 2.8 fusion.84
  1052.9 2.3 multiply_reduce_fusion.1
  1055.3 4.2 all-reduce.7
  1059.6 2.6 subtract_add_fusion
  1063.7 32.6 %all-reduce.4 = (f32[480]{0:T(512)}, f32[480]{0:T(512)}) all-reduce(f32[480]{0:T(512)S(1)} %dynamic-slice.7, f32[480]{0:T(512)S(1)} %dynamic-slice.9), channel_id=1, replica_groups=mesh['shard'=2,'ctx'=4,'tp'=4] {'ctx','tp'}, use_global_device_ids=true, to_apply=%region_19.20 | all-reduce | flops 960 | bytes 7680 | tf_op jit(solution)/shard_map/psum | solution.py:281
  1096.3 92.3 %all-reduce.14.cloned.1.call-done = (f32[480,640]{1,0:T(8,128)}, f32[480,640]{1,0:T(8,128)}, f32[480,640]{1,0:T(8,128)}) async-done(((f32[480,640]{1,0:T(8,128)}, f32[480,640]{1,0:T(8,128)}, f32[480,640]{1,0:T(8,128)}), (f32[480,640]{1,0:T(8,128)}, f32[480,640]{1,0:T(8,128)}, f32[480,640]{1,0:T(8,128)})) %all-reduce.14.cloned.1.call-update) | async-done | bytes 3686416 | tf_op jit(solution)/shard_map/psum | solution.py:284
  1188.6 130.1 %all-reduce.12.cloned.1.call-done = (f32[480,960]{1,0:T(8,128)}, f32[480,320]{0,1:T(8,128)}, f32[480,320]{0,1:T(8,128)}, f32[480,960]{1,0:T(8,128)}) async-done(((f32[480,960]{1,0:T(8,128)}, f32[480,320]{0,1:T(8,128)}, f32[480,320]{0,1:T(8,128)}, f32[480,960]{1,0:T(8,128)}), (f32[480,960]{1,0:T(8,128)}, f32[480,320]{0,1:T(8,128)}, f32[480,320]{0,1:T(8,128)}, ...) | async-done | bytes 4915216 | tf_op jit(solution)/shard_map/psum | solution.py:281
  1318.7 3.2 copy.153
  (247 shorter events, 55.8 us)
Async XLA Ops:
  7.2 23.6 %copy-start.4 = (bf16[2,256,960]{1,2,0:T(8,128)(2,1)S(1)}, bf16[2,256,960]{1,2,0:T(8,128)(2,1)}, u32[]{:S(2)}) copy-start(bf16[2,256,960]{1,2,0:T(8,128)(2,1)} %param.13) | copy-start | bytes 2949124
  7.2 51.6 %all-gather.16.cloned.1.call-start = ((), (), s32[]{:S(2)}) async-start(), calls=%async_computation.13 | async-start | bytes 2949120 | tf_op jit(solution)/shard_map/all_gather | solution.py:106
  7.9 82.7 %all-gather.14.cloned.1.call-start = ((), (), s32[]{:S(2)}) async-start(), calls=%async_computation.12 | async-start | bytes 1638400 | tf_op jit(solution)/shard_map/all_gather | solution.py:138
  16.1 46.5 %copy-start.45 = (f32[960]{0:T(1024)}, f32[960]{0:T(1024)S(1)}, u32[]{:S(2)}) copy-start(f32[960]{0:T(1024)S(1)} %convert_element_type.142) | copy-start | bytes 11524
  30.7 2.6 copy-start.24
  31.0 2.4 copy-start.41
  31.0 31.6 %copy-start.50 = (f32[2,256]{1,0:T(2,128)}, f32[2,256]{1,0:T(2,128)S(1)}, u32[]{:S(2)}) copy-start(f32[2,256]{1,0:T(2,128)S(1)} %get-tuple-element.99) | copy-start | bytes 6148
  31.8 33.6 %copy-start.37 = (f32[256,32]{0,1:T(8,128)}, f32[256,32]{0,1:T(8,128)S(1)}, u32[]{:S(2)}) copy-start(f32[256,32]{0,1:T(8,128)S(1)} %get-tuple-element.103) | copy-start | bytes 98308
  33.3 91.5 %all-gather.12.cloned.1.call-start = ((), (), s32[]{:S(2)}) async-start(), calls=%async_computation.11 | async-start | bytes 1638400 | tf_op jit(solution)/shard_map/all_gather | solution.py:139
  33.4 19.2 %copy-start.47 = (f32[1,2,2,128]{3,1,2,0:T(2,128)}, f32[1,2,2,128]{3,1,2,0:T(2,128)S(1)}, u32[]{:S(2)}) copy-start(f32[1,2,2,128]{3,1,2,0:T(2,128)S(1)} %copy.132) | copy-start | bytes 6148
  52.6 105.0 %copy-start = (f32[2,120,8,256]{3,2,0,1:T(8,128)}, f32[2,120,8,256]{3,2,0,1:T(8,128)S(1)}, u32[]{:S(2)}) copy-start(f32[2,120,8,256]{3,2,0,1:T(8,128)S(1)} %copy.129) | copy-start | bytes 5898244
  53.4 2.9 copy-start.53
  53.4 3.1 copy-start.52
  54.8 102.8 %all-gather.18.cloned.1.call-start = ((), (), s32[]{:S(2)}) async-start(), calls=%async_computation.14 | async-start | bytes 2949120 | tf_op jit(solution)/shard_map/all_gather | solution.py:109
  55.4 127.0 %all-gather.24.cloned.1.call-start = ((), (), s32[]{:S(2)}) async-start(), calls=%async_computation.17 | async-start | bytes 1843200 | tf_op jit(solution)/shard_map/all_gather | solution.py:112
  56.0 161.8 %all-gather.20.cloned.1.call-start = ((), (), s32[]{:S(2)}) async-start(), calls=%async_computation.15 | async-start | bytes 4915200 | tf_op jit(solution)/shard_map/all_gather | solution.py:176
  66.6 32.2 %copy-start.26 = (bf16[1,256,15,64]{1,3,2,0:T(8,128)(2,1)}, bf16[1,256,15,64]{1,3,2,0:T(8,128)(2,1)S(1)}, u32[]{:S(2)}) copy-start(bf16[1,256,15,64]{1,3,2,0:T(8,128)(2,1)S(1)} %get-tuple-element.88) | copy-start | bytes 1474564
  92.0 6.8 copy-start.16
  92.0 42.4 %copy-start.18 = (bf16[1,1024,320]{1,2,0:T(8,128)(2,1)}, bf16[1,1024,320]{1,2,0:T(8,128)(2,1)S(1)}, u32[]{:S(2)}) copy-start(bf16[1,1024,320]{1,2,0:T(8,128)(2,1)S(1)} %get-tuple-element.81) | copy-start | bytes 1966084
  126.1 8.3 copy-start.20
  126.2 22.7 %copy-start.22 = (bf16[1,1024,320]{1,2,0:T(8,128)(2,1)}, bf16[1,1024,320]{1,2,0:T(8,128)(2,1)S(1)}, u32[]{:S(2)}) copy-start(bf16[1,1024,320]{1,2,0:T(8,128)(2,1)S(1)} %get-tuple-element.83) | copy-start | bytes 1966084
  126.2 8.3 copy-start.28
  126.2 8.3 copy-start.29
  148.9 8.7 copy-start.57
  156.4 4.0 copy-start.58
  160.4 4.0 copy-start.36
  162.9 79.4 %all-gather.22.cloned.1.call-start = ((), (), s32[]{:S(2)}) async-start(), calls=%async_computation.16 | async-start | bytes 1843200 | tf_op jit(solution)/shard_map/all_gather | solution.py:111
  163.7 103.5 %all-gather.26.cloned.1.call-start = ((), (), s32[]{:S(2)}) async-start(), calls=%async_computation.18 | async-start | bytes 1843200 | tf_op jit(solution)/shard_map/all_gather | solution.py:113
  164.4 138.4 %all-gather.28.cloned.1.call-start = ((), (), s32[]{:S(2)}) async-start(), calls=%async_computation.20 | async-start | bytes 4915200 | tf_op jit(solution)/shard_map/all_gather | solution.py:185
  165.5 225.8 %reduce-scatter.20.cloned.1.call-start = ((), (), s32[]{:S(2)}) async-start(), calls=%async_computation.21 | async-start | bytes 9830400 | tf_op jit(solution)/shard_map/reduce_scatter | solution.py:193
  250.6 63.1 %copy-start.56 = (bf16[960,640]{1,0:T(8,128)(2,1)S(1)}, bf16[960,640]{1,0:T(8,128)(2,1)}, u32[]{:S(2)}) copy-start(bf16[960,640]{1,0:T(8,128)(2,1)} %all-gather.22.cloned.1.call-done) | copy-start | bytes 3686404
  313.7 3.3 copy-start.59
  313.7 3.3 copy-start.11
  313.7 3.3 copy-start.32
  322.5 114.4 %reduce-scatter.18.cloned.1.call-start = ((), (), s32[]{:S(2)}) async-start(), calls=%async_computation.19 | async-start | bytes 4915200 | tf_op jit(solution)/shard_map/reduce_scatter | solution.py:182
  330.4 60.9 %copy-start.3 = (f32[512,960]{0,1:T(8,128)S(1)}, f32[512,960]{0,1:T(8,128)}, u32[]{:S(2)}) copy-start(f32[512,960]{0,1:T(8,128)} %copy-done.2) | copy-start | bytes 5898244
  330.4 106.5 %copy-start.6 = (bf16[2,120,8,256]{3,2,0,1:T(8,128)(2,1)S(1)}, bf16[2,120,8,256]{3,2,0,1:T(8,128)(2,1)}, u32[]{:S(2)}) copy-start(bf16[2,120,8,256]{3,2,0,1:T(8,128)(2,1)} %copy.130) | copy-start | bytes 2949124
  330.4 411.4 %reduce-scatter.22.cloned.1.call-start = ((), (), s32[]{:S(2)}) async-start(), calls=%async_computation.22 | async-start | bytes 3276800 | tf_op jit(solution)/shard_map/reduce_scatter | solution.py:238
  330.7 174.5 %copy-start.43 = (f32[5,3,256]{2,1,0:T(4,128)}, f32[5,3,256]{2,1,0:T(4,128)S(1)}, u32[]{:S(2)}) copy-start(f32[5,3,256]{2,1,0:T(4,128)S(1)} %log_add_fusion) | copy-start | bytes 46084
  436.9 3.5 copy-start.54
  442.0 7.8 copy-start.21
  457.6 21.5 %copy-start.27 = (bf16[1,256,15,64]{1,3,2,0:T(8,128)(2,1)S(1)}, bf16[1,256,15,64]{1,3,2,0:T(8,128)(2,1)}, u32[]{:S(2)}) copy-start(bf16[1,256,15,64]{1,3,2,0:T(8,128)(2,1)} %copy-done.26) | copy-start | bytes 1474564
  504.7 264.4 %reduce-scatter.34.cloned.1.call-start = ((), (), s32[]{:S(2)}) async-start(), calls=%async_computation.28 | async-start | bytes 3276800
  717.1 178.4 %reduce-scatter.32.cloned.1.call-start = ((), (), s32[]{:S(2)}) async-start(), calls=%async_computation.27 | async-start | bytes 3686400 | tf_op jit(solution)/shard_map/reduce_scatter | solution.py:279
  725.5 7.9 copy-start.12
  725.6 169.9 %reduce-scatter.28.cloned.1.call-start = ((), (), s32[]{:S(2)}) async-start(), calls=%async_computation.25 | async-start | bytes 3686400 | tf_op jit(solution)/shard_map/reduce_scatter | solution.py:277
  733.3 7.0 copy-start.46
  733.3 7.0 copy-start.51
  733.4 162.1 %reduce-scatter.30.cloned.1.call-start = ((), (), s32[]{:S(2)}) async-start(), calls=%async_computation.26 | async-start | bytes 3686400 | tf_op jit(solution)/shard_map/reduce_scatter | solution.py:278
  740.2 170.3 %reduce-scatter.36.cloned.1.call-start = ((), (), s32[]{:S(2)}) async-start(), calls=%async_computation.29 | async-start | bytes 2211840
  741.8 3.8 copy-start.13
  745.6 192.2 %reduce-scatter.38.cloned.1.call-start = ((), (), s32[]{:S(2)}) async-start(), calls=%async_computation.30 | async-start | bytes 2211840
  835.8 3.0 copy-start.8
  838.8 153.2 %reduce-scatter.26.cloned.1.call-start = ((), (), s32[]{:S(2)}) async-start(), calls=%async_computation.24 | async-start | bytes 5898240 | tf_op jit(solution)/shard_map/reduce_scatter | solution.py:275
  843.1 23.4 %copy-start.17 = (bf16[1,1024,320]{1,2,0:T(8,128)(2,1)S(1)}, bf16[1,1024,320]{1,2,0:T(8,128)(2,1)}, u32[]{:S(2)}) copy-start(bf16[1,1024,320]{1,2,0:T(8,128)(2,1)} %copy-done.16) | copy-start | bytes 1966084
  843.2 23.4 %copy-start.44 = (f32[5,3,256]{2,1,0:T(4,128)S(1)}, f32[5,3,256]{2,1,0:T(4,128)}, u32[]{:S(2)}) copy-start(f32[5,3,256]{2,1,0:T(4,128)} %copy-done.43) | copy-start | bytes 46084
  843.2 203.0 %reduce-scatter.24.cloned.1.call-start = ((), (), s32[]{:S(2)}) async-start(), calls=%async_computation.23 | async-start | bytes 5898240 | tf_op jit(solution)/shard_map/reduce_scatter | solution.py:272
  895.4 293.3 %all-reduce.14.cloned.1.call-start = ((), (), s32[]{:S(2)}) async-start(), calls=%async_computation.32 | async-start | bytes 7372800 | tf_op jit(solution)/shard_map/psum | solution.py:284
  896.1 422.6 %all-reduce.12.cloned.1.call-start = ((), (), s32[]{:S(2)}) async-start(), calls=%async_computation.31 | async-start | bytes 10485760 | tf_op jit(solution)/shard_map/psum | solution.py:281
  1048.4 2.8 copy-start.31
  1048.4 2.9 copy-start.25
  1318.7 3.2 copy-start.40
  1318.7 4.0 copy-start.39
  1318.7 4.9 copy-start.30
  (19 other events, 29.1 us)
Sparse Core Ops, SparseCore 0:
  9.6 45.4 all-gather.15
  57.2 33.3 all-gather.13
  92.8 31.9 all-gather.11
  126.2 31.3 all-gather.17
  159.0 23.3 all-gather.23
  184.4 33.4 all-gather.19
  219.3 22.9 all-gather.21
  243.8 23.3 all-gather.25
  269.4 33.4 all-gather.27
  322.7 68.5 reduce-scatter.19
  394.0 42.8 reduce-scatter.17
  504.9 51.9 reduce-scatter.21
  717.2 51.9 reduce-scatter.33
  771.3 35.6 reduce-scatter.31
  809.1 35.8 reduce-scatter.27
  847.0 35.7 reduce-scatter.29
  885.5 25.0 reduce-scatter.35
  912.7 24.9 reduce-scatter.37
  940.0 51.9 reduce-scatter.25
  994.2 51.9 reduce-scatter.23
  1048.8 139.7 all-reduce.13
  1193.8 124.7 all-reduce.11
where the time goes:
time: 1340 us
  waiting for transfers between devices  663 us (49%)
  local copies, waits for them, and re-layouts  302 us (23%)
  matrix products  240 us (18%)
  blocking collectives  71.2 us (5%)
  other arithmetic  40 us (3%)
  between operations  17 us (1%)
    unnamed x148, local copies, waits for them, and re-layouts  285 us
    psum x1, waiting for transfers between devices, per_device(): lax.psum((sum_gain_one, sum_query, sum_key, sum_value, sum_out, sum_gain_...  130 us
    psum x1, waiting for transfers between devices, per_device(): sum_gate, sum_up, sum_down = lax.psum((sum_gate, sum_up, sum_down), 'ctx')  92.3 us
    unnamed x25, waiting for transfers between devices  66.7 us
    reduce_scatter x1, waiting for transfers between devices, per_device(): lax.psum_scatter(contract_last(grad_gate, gate_use) + contract_last(grad_...  60.6 us
    reduce_scatter x1, waiting for transfers between devices, per_device(): lax.psum_scatter(grad_query_w, 'shard', scatter_dimension=0, tiled=True)  54.2 us
    reduce_scatter x1, waiting for transfers between devices, per_device(): lax.psum_scatter(grad_out_w, 'shard', scatter_dimension=0, tiled=True)  52.1 us
    dot_general x2, matrix products, per_device(): jnp.einsum('hgqk,khd->qhgd', grad_scores, keys_seq, preferred_element_typ...  44.9 us
  transfers between devices with their start and end apart: 22, of which 17 were waited for; matrix products, arithmetic and copies ran while one was open for 36% of the time, Pallas kernels for 0%

commit v1 on v0

v1 whole, which is shorter than its diff:
```python
import functools
import math

import jax
import jax.numpy as jnp
from jax import lax
from jax.experimental import pallas as pl
from jax.experimental.pallas import tpu as pltpu
from jax.sharding import PartitionSpec as P

H = 15
KVH = 5
HD = 64
LEN = 1024
PIECE = 256
GRAIN = 128
MAXDOC = 512
GROUP = H // KVH
KW = KVH * HD
QW = H * HD
SPAN = MAXDOC + 2 * GRAIN

EPS = 1e-05
NEG = -1e30
F32 = jnp.float32
BF16 = jnp.bfloat16
VMEM_LIMIT = 56 * 1024 * 1024


def dot(left, right, dims):
    return lax.dot_general(left, right, (dims, ((), ())), preferred_element_type=F32)


def nn(left, right):
    return dot(left, right, ((1,), (0,)))


def nt(left, right):
    return dot(left, right, ((1,), (1,)))


def tn(left, right):
    return dot(left, right, ((0,), (0,)))


def call(kernel, outs, args, *, grid, in_specs, out_specs, scratch=(), flops=0, transcendentals=0):
    moved = sum(math.prod(a.shape) * a.dtype.itemsize for a in (*args, *outs))
    return pl.pallas_call(
        kernel,
        out_shape=outs,
        grid=grid,
        in_specs=in_specs,
        out_specs=out_specs,
        scratch_shapes=list(scratch),
        compiler_params=pltpu.CompilerParams(vmem_limit_bytes=VMEM_LIMIT),
        cost_estimate=pl.CostEstimate(
            flops=int(flops), bytes_accessed=int(moved), transcendentals=int(transcendentals)
        ),
    )(*args)


def seq_block(*shape):
    return pl.BlockSpec((1, *shape), lambda s, *_: (s,) + (0,) * len(shape))


def whole(*shape):
    return pl.BlockSpec(shape, lambda *_: (0,) * len(shape))


def smem():
    return pl.BlockSpec(memory_space=pltpu.SMEM)


def struct(shape, dtype):
    return jax.ShapeDtypeStruct(shape, dtype)


def rotary_tables(offset, length):
    half = HD // 2
    place = (offset + jnp.arange(length, dtype=jnp.int32)).astype(F32)
    freq = jnp.exp(jnp.arange(half).astype(F32) * (-2.0 * math.log(10000.0) / HD))
    angle = place[:, None] * freq[None, :]
    cosine, sine = jnp.cos(angle), jnp.sin(angle)
    return (
        jnp.concatenate([cosine] * 4, axis=1),
        jnp.concatenate([-sine, sine, -sine, sine], axis=1),
    )


def rotate(tile, cosine, sine):
    lane = lax.broadcasted_iota(jnp.int32, tile.shape, 1)
    partner = jnp.where(lane % HD < HD // 2, pltpu.roll(tile, 96, 1), pltpu.roll(tile, 32, 1))
    return tile * cosine + partner * sine


def rotate_into(out_ref, value_ref, width, cosine, sine, factor):
    for start in range(0, width, 128):
        stop = min(start + 128, width)
        turned = rotate(value_ref[:, start : start + 128], cosine, sine) * factor
        out_ref[0, :, start:stop] = turned[:, : stop - start].astype(out_ref.dtype)


def inverse_mean(value):
    return lax.rsqrt(jnp.mean(value * value, axis=-1, keepdims=True) + EPS)


def project_kernel(
    tok_ref, gain_ref, wq_ref, wkv_ref, cos_ref, sin_ref, normed_ref, q_ref, kv_ref, qs, ks
):
    source = tok_ref[0].astype(F32)
    normed = (source * inverse_mean(source) * gain_ref[...]).astype(BF16)
    normed_ref[0] = normed
    cosine, sine = cos_ref[...], sin_ref[...]
    raw = nn(normed, wkv_ref[...])
    ks[:, :KW] = raw[:, :KW]
    kv_ref[0, :, KW:] = raw[:, KW:].astype(BF16)
    rotate_into(kv_ref, ks, KW, cosine, sine, 1.0)
    qs[:, :QW] = nn(normed, wq_ref[...])
    rotate_into(q_ref, qs, QW, cosine, sine, HD**-0.5)


def project(tokens, gain, wq, wkv, cosine, sine):
    n, rows, width = tokens.shape
    up = lambda w: -(-w // 128) * 128
    return call(
        project_kernel,
        [
            struct((n, rows, width), BF16),
            struct((n, rows, QW), BF16),
            struct((n, rows, 2 * KW), BF16),
        ],
        (tokens, gain, wq, wkv, cosine, sine),
        grid=(n,),
        in_specs=[
            seq_block(rows, width),
            whole(1, width),
            whole(width, QW),
            whole(width, 2 * KW),
            whole(rows, 128),
            whole(rows, 128),
        ],
        out_specs=[seq_block(rows, width), seq_block(rows, QW), seq_block(rows, 2 * KW)],
        scratch=[pltpu.VMEM((rows, up(QW)), F32), pltpu.VMEM((rows, up(KW)), F32)],
        flops=2 * n * rows * width * (QW + 2 * KW),
    )


def marks(scal_ref, seq, pos, valid):
    segment = jnp.zeros(pos.shape, jnp.int32)
    for d in range(2):
        segment += (pos >= scal_ref[seq, d]).astype(jnp.int32)
    number = jnp.zeros(pos.shape, jnp.int32)
    for j in range(2):
        start = scal_ref[seq, 2 + j]
        number += jnp.where((pos >= start) & (pos < start + PIECE), j + 1, 0)
    return jnp.where(valid, segment, -1), number


def bias_of(scal_ref, seq, start, across):
    q_shape, k_shape, q_dim, k_dim = (
        ((GRAIN, 1), (1, SPAN), 0, 1) if across else ((1, GRAIN), (SPAN, 1), 1, 0)
    )
    q_pos = start + lax.broadcasted_iota(jnp.int32, q_shape, q_dim)
    k_pos = start - MAXDOC + lax.broadcasted_iota(jnp.int32, k_shape, k_dim)
    q_seg, q_num = marks(scal_ref, seq, q_pos, q_pos >= 0)
    k_seg, k_num = marks(scal_ref, seq, k_pos, (k_pos >= 0) & (k_pos < LEN))
    q_num = jnp.where(q_num > 0, q_num, -1)
    permit = (q_seg == k_seg) & ((k_pos <= q_pos) | (q_num == k_num))
    return jnp.where(permit, 0.0, NEG).astype(F32)


def load_window(window, parts):
    row = 0
    for part in parts:
        window[row : row + part.shape[1], :] = part[0]
        row += part.shape[1]


def attend_kernel(scal_ref, q_ref, far_ref, near_ref, own_ref, next_ref, mixed_ref, lse_ref, window):
    seq, sub = pl.program_id(0), pl.program_id(1)

    @pl.when(sub == 0)
    def _():
        load_window(window, (far_ref, near_ref, own_ref, next_ref))

    bias = bias_of(scal_ref, seq, scal_ref[seq, 4] + sub * GRAIN, True)
    rows = pl.ds(pl.multiple_of(sub * GRAIN, GRAIN), SPAN)
    lse = jnp.zeros((GRAIN, 128), F32)
    lane = lax.broadcasted_iota(jnp.int32, (GRAIN, 128), 1)
    for j in range(KVH):
        key = window[rows, j * HD : (j + 1) * HD]
        value = window[rows, KW + j * HD : KW + (j + 1) * HD]
        for g in range(GROUP):
            h = j * GROUP + g
            scores = nt(q_ref[0, :, h * HD : (h + 1) * HD], key) + bias
            top = jnp.max(scores, axis=-1, keepdims=True)
            raised = jnp.exp(scores - top)
            total = jnp.sum(raised, axis=-1, keepdims=True)
            out = nn(raised.astype(BF16), value) / total
            mixed_ref[0, :, h * HD : (h + 1) * HD] = out.astype(BF16)
            lse = jnp.where(lane == h, top + jnp.log(total), lse)
    lse_ref[0] = lse


def window_specs(local):
    return [
        seq_block(local, 2 * KW),
        seq_block(local, 2 * KW),
        seq_block(local, 2 * KW),
        seq_block(GRAIN, 2 * KW),
    ]


def sub_block(width):
    return pl.BlockSpec((1, GRAIN, width), lambda s, i: (s, i, 0))


def attend(scal, q, parts):
    n, local, _ = q.shape
    return call(
        attend_kernel,
        [struct((n, local, QW), BF16), struct((n, local, 128), F32)],
        (scal, q, *parts),
        grid=(n, local // GRAIN),
        in_specs=[smem(), sub_block(QW), *window_specs(local)],
        out_specs=[sub_block(QW), sub_block(128)],
        scratch=[pltpu.VMEM((MAXDOC + local + GRAIN, 2 * KW), BF16)],
        flops=16 * n * local * SPAN * QW,
        transcendentals=n * local * SPAN * H,
    )


def attend_back_kernel(
    scal_ref,
    q_ref,
    far_ref,
    near_ref,
    own_ref,
    next_ref,
    mixed_ref,
    lse_ref,
    grad_ref,
    dq_ref,
    dfar_ref,
    dnear_ref,
    down_ref,
    dnext_ref,
    window,
    sums,
):
    seq, sub = pl.program_id(0), pl.program_id(1)

    @pl.when(sub == 0)
    def _():
        load_window(window, (far_ref, near_ref, own_ref, next_ref))
        sums[...] = jnp.zeros_like(sums)

    bias = bias_of(scal_ref, seq, scal_ref[seq, 4] + sub * GRAIN, False)
    bias = jnp.concatenate([bias] * GROUP, axis=1)
    rows = pl.ds(pl.multiple_of(sub * GRAIN, GRAIN), SPAN)
    lane = lax.broadcasted_iota(jnp.int32, (GRAIN, 128), 1)
    product = mixed_ref[0].astype(F32) * grad_ref[0].astype(F32)
    delta = jnp.zeros((GRAIN, 128), F32)
    for h in range(H):
        part = jnp.sum(product[:, h * HD : (h + 1) * HD], axis=-1, keepdims=True)
        delta = jnp.where(lane == h, part, delta)
    delta = delta.T
    lse = lse_ref[0].T

    def heads(array, j):
        return [array[h : h + 1, :] for h in range(j * GROUP, (j + 1) * GROUP)]

    for j in range(KVH):
        k_cols = slice(j * HD, (j + 1) * HD)
        v_cols = slice(KW + j * HD, KW + (j + 1) * HD)
        key, value = window[rows, k_cols], window[rows, v_cols]
        cols = [slice(h * HD, (h + 1) * HD) for h in range(j * GROUP, (j + 1) * GROUP)]
        query = jnp.concatenate([q_ref[0, :, c] for c in cols], axis=0)
        grad = jnp.concatenate([grad_ref[0, :, c] for c in cols], axis=0)
        lse_row = jnp.concatenate(heads(lse, j), axis=1)
        delta_row = jnp.concatenate(heads(delta, j), axis=1)
        probs = jnp.exp(nt(key, query) + bias - lse_row)
        grad_scores = (probs * (nt(value, grad) - delta_row)).astype(BF16)
        sums[rows, v_cols] += nn(probs.astype(BF16), grad)
        sums[rows, k_cols] += nn(grad_scores, query)
        dq = tn(grad_scores, key)
        for g, c in enumerate(cols):
            dq_ref[0, :, c] = dq[g * GRAIN : (g + 1) * GRAIN, :]

    @pl.when(sub == pl.num_programs(1) - 1)
    def _():
        row = 0
        for part in (dfar_ref, dnear_ref, down_ref, dnext_ref):
            part[0] = sums[row : row + part.shape[1], :].astype(part.dtype)
            row += part.shape[1]


def attend_back(scal, q, parts, mixed, lse, grad):
    n, local, _ = q.shape
    window = MAXDOC + local + GRAIN
    return call(
        attend_back_kernel,
        [
            struct((n, local, QW), F32),
            struct((n, local, 2 * KW), BF16),
            struct((n, local, 2 * KW), BF16),
            struct((n, local, 2 * KW), F32),
            struct((n, GRAIN, 2 * KW), BF16),
        ],
        (scal, q, *parts, mixed, lse, grad),
        grid=(n, local // GRAIN),
        in_specs=[
            smem(),
            sub_block(QW),
            *window_specs(local),
            sub_block(QW),
            sub_block(128),
            sub_block(QW),
        ],
        out_specs=[sub_block(QW), *window_specs(local)],
        scratch=[pltpu.VMEM((window, 2 * KW), BF16), pltpu.VMEM((window, 2 * KW), F32)],
        flops=40 * n * local * SPAN * QW,
        transcendentals=n * local * SPAN * H,
    )


def residual_kernel(tok_ref, mixed_ref, wo_ref, gain_ref, hidden_ref, normed_ref):
    hidden = tok_ref[0].astype(F32) + nn(mixed_ref[0], wo_ref[...])
    hidden_ref[0] = hidden
    normed_ref[0] = (hidden * inverse_mean(hidden) * gain_ref[...]).astype(BF16)


def residual(tokens, mixed, wo, gain):
    n, rows, width = tokens.shape
    return call(
        residual_kernel,
        [struct((n, rows, width), F32), struct((n, rows, width), BF16)],
        (tokens, mixed, wo, gain),
        grid=(n,),
        in_specs=[seq_block(rows, width), seq_block(rows, QW), whole(QW, width), whole(1, width)],
        out_specs=[seq_block(rows, width), seq_block(rows, width)],
        flops=2 * n * rows * width * QW,
    )


def ff_kernel(
    nrm_a, nrm_b, cot_a, cot_b, wg_ref, wu_ref, wd_ref, inner_ref, gg_ref, gu_ref, ff_ref, gn_ref
):
    rows = nrm_a.shape[0]
    step = min(rows, 256)
    for half, (nrm_ref, cot_ref) in enumerate(((nrm_a, cot_a), (nrm_b, cot_b))):
        for start in range(0, rows, step):
            at = slice(half * rows + start, half * rows + start + step)
            normed = nrm_ref[start : start + step, :]
            gate = nn(normed, wg_ref[...])
            up = nn(normed, wu_ref[...])
            grad = nn(cot_ref[start : start + step, :], wd_ref[...])
            sigma = jax.nn.sigmoid(gate)
            raised = gate * sigma
            inner = (raised * up).astype(BF16)
            grad_gate = (grad * up * (sigma + raised * (1.0 - sigma))).astype(BF16)
            grad_up = (grad * raised).astype(BF16)
            inner_ref[at, :] = inner
            gg_ref[at, :] = grad_gate
            gu_ref[at, :] = grad_up
            gn_ref[at, :] = (nt(grad_gate, wg_ref[...]) + nt(grad_up, wu_ref[...])).astype(BF16)
            ff_ref[at, :] = nt(inner, wd_ref[...]).astype(BF16)


def ff(normed_pair, cot_pair, wg, wu, wd):
    rows, width = normed_pair[0].shape
    units = wg.shape[1]
    args = (*normed_pair, *cot_pair, wg, wu, wd)
    outs = [struct((2 * rows, units), BF16)] * 3 + [struct((2 * rows, width), BF16)] * 2
    return call(
        ff_kernel,
        outs,
        args,
        grid=(1,),
        in_specs=[whole(*a.shape) for a in args],
        out_specs=[whole(*o.shape) for o in outs],
        flops=24 * rows * width * units,
        transcendentals=2 * rows * units,
    )


def ff_back_kernel(hidden_ref, cot_ref, a_ref, b_ref, gain_ref, wo_ref, gh_ref, gb_ref, gm_ref, gg_ref):
    hidden, gain = hidden_ref[0], gain_ref[...]
    factor = inverse_mean(hidden)
    grad = a_ref[0].astype(F32) + b_ref[0].astype(F32)
    weighted = grad * gain
    back = factor * weighted - hidden * factor**3 * jnp.mean(
        hidden * weighted, axis=-1, keepdims=True
    )
    grad_hidden = cot_ref[0].astype(F32) + back
    branch = grad_hidden.astype(BF16)
    gh_ref[0] = grad_hidden
    gb_ref[0] = branch
    gm_ref[0] = nt(branch, wo_ref[...]).astype(BF16)
    gg_ref[0] = jnp.sum(grad * hidden * factor, axis=0, keepdims=True)


def ff_back(hidden, cotangent, part_a, part_b, gain, wo):
    n, rows, width = hidden.shape
    block = seq_block(rows, width)
    return call(
        ff_back_kernel,
        [
            struct((n, rows, width), F32),
            struct((n, rows, width), BF16),
            struct((n, rows, QW), BF16),
            struct((n, 1, width), F32),
        ],
        (hidden, cotangent, part_a, part_b, gain, wo),
        grid=(n,),
        in_specs=[block, block, block, block, whole(1, width), whole(QW, width)],
        out_specs=[block, block, seq_block(rows, QW), seq_block(1, width)],
        flops=2 * n * rows * width * QW,
    )


def query_back_kernel(dq_ref, cos_ref, sin_ref, out_ref, qs):
    qs[:, :QW] = dq_ref[0]
    rotate_into(out_ref, qs, QW, cos_ref[...], -sin_ref[...], HD**-0.5)


def query_back(dq, cosine, sine):
    n, rows, _ = dq.shape
    return call(
        query_back_kernel,
        [struct((n, rows, QW), BF16)],
        (dq, cosine, sine),
        grid=(n,),
        in_specs=[seq_block(rows, QW), whole(rows, 128), whole(rows, 128)],
        out_specs=[seq_block(rows, QW)],
        scratch=[pltpu.VMEM((rows, -(-QW // 128) * 128), F32)],
    )[0]


def input_kernel(
    tok_ref,
    gh_ref,
    gq_ref,
    own_ref,
    left_ref,
    right_ref,
    gain_ref,
    wq_ref,
    wkv_ref,
    cos_ref,
    sin_ref,
    ig_ref,
    gkv_ref,
    gg_ref,
    ks,
):
    total = own_ref[0] + right_ref[0].astype(F32)
    ks[...] = total
    ks[:GRAIN, :] += left_ref[0].astype(F32)
    gkv_ref[0, :, KW:] = ks[:, KW:].astype(BF16)
    rotate_into(gkv_ref, ks, KW, cos_ref[...], -sin_ref[...], 1.0)
    grad = nt(gq_ref[0], wq_ref[...]) + nt(gkv_ref[0], wkv_ref[...])
    source, gain = tok_ref[0].astype(F32), gain_ref[...]
    factor = inverse_mean(source)
    weighted = grad * gain
    back = factor * weighted - source * factor**3 * jnp.mean(
        source * weighted, axis=-1, keepdims=True
    )
    ig_ref[0] = gh_ref[0] + back
    gg_ref[0] = jnp.sum(grad * source * factor, axis=0, keepdims=True)


def input_back(tokens, grad_hidden, gq, own, left, right, gain, wq, wkv, cosine, sine):
    n, rows, width = tokens.shape
    block, kv_block = seq_block(rows, width), seq_block(rows, 2 * KW)
    return call(
        input_kernel,
        [
            struct((n, rows, width), F32),
            struct((n, rows, 2 * KW), BF16),
            struct((n, 1, width), F32),
        ],
        (tokens, grad_hidden, gq, own, left, right, gain, wq, wkv, cosine, sine),
        grid=(n,),
        in_specs=[
            block,
            block,
            seq_block(rows, QW),
            kv_block,
            seq_block(GRAIN, 2 * KW),
            kv_block,
            whole(1, width),
            whole(width, QW),
            whole(width, 2 * KW),
            whole(rows, 128),
            whole(rows, 128),
        ],
        out_specs=[block, kv_block, seq_block(1, width)],
        scratch=[pltpu.VMEM((rows, 2 * KW), F32)],
        flops=2 * n * rows * width * (QW + 2 * KW),
    )


def program(mesh):
    shards, ctxs, tps = (mesh.shape[axis] for axis in ("shard", "ctx", "tp"))

    def swap(value, axis, bit):
        count = mesh.shape[axis]
        return lax.ppermute(value, axis, [(i, i ^ bit) for i in range(count)])

    def shift(value, by):
        pairs = [(i, i + by) for i in range(ctxs) if 0 <= i + by < ctxs]
        return lax.ppermute(value, "ctx", pairs)

    def in_order(index, own, other):
        first = jnp.concatenate([own, other], axis=0)
        return jnp.where(index == 0, first, jnp.concatenate([other, own], axis=0))

    def pick(value, index):
        return lax.dynamic_index_in_dim(value, index, 0, keepdims=False)

    def gather_rows(value, split):
        if shards != 2:
            return lax.all_gather(value, "shard", axis=0, tiled=True)
        mine = lax.axis_index("shard")
        if not split:
            return in_order(mine, value, swap(value, "shard", 1))
        core = lax.axis_index("tp") % 2
        half = value.shape[0] // 2
        part = swap(lax.dynamic_slice_in_dim(value, core * half, half), "shard", 1)
        return in_order(mine, value, in_order(core, part, swap(part, "tp", 1)))

    def over_shard(grad):
        if shards != 2:
            return lax.psum_scatter(grad, "shard", scatter_dimension=0, tiled=True)
        mine = lax.axis_index("shard")
        halves = grad.reshape(2, grad.shape[0] // 2, *grad.shape[1:])
        got = swap(pick(halves, 1 - mine).astype(BF16), "shard", 1)
        return pick(halves, mine) + got.astype(F32)

    def all_over_ctx(value):
        bit = 1
        while bit < ctxs:
            low = value.astype(BF16)
            value = low.astype(F32) + swap(low, "ctx", bit).astype(F32)
            bit *= 2
        return value

    def reduce_attention(grad):
        if shards != 2:
            return lax.psum(over_shard(grad), ("ctx", "tp"))
        mine, tp = lax.axis_index("shard"), lax.axis_index("tp")
        core, row = tp % 2, tp // 2
        quarter = grad.shape[0] // 4
        parts = grad.reshape(2, 2, quarter, -1)
        take = lambda c: lax.dynamic_index_in_dim(parts, c, 1, keepdims=False)
        held = take(core) + swap(take(1 - core).astype(BF16), "tp", 1).astype(F32)
        held = pick(held, mine) + swap(pick(held, 1 - mine).astype(BF16), "shard", 1).astype(F32)
        held = held.reshape(2, quarter // 2, -1)
        held = pick(held, row) + swap(pick(held, 1 - row).astype(BF16), "tp", 2).astype(F32)
        held = all_over_ctx(held).astype(BF16)
        held = in_order(row, held, swap(held, "tp", 2))
        return in_order(core, held, swap(held, "tp", 1)).astype(F32)

    def per_device(
        tokens,
        cotangent,
        piece_starts,
        doc_lengths,
        attn_gain,
        w_query,
        w_key,
        w_value,
        w_out,
        ff_gain,
        w_gate,
        w_up,
        w_down,
    ):
        seqs, local, width = tokens.shape
        offset = lax.axis_index("ctx") * local
        wq = gather_rows(w_query, True)
        wkv = gather_rows(jnp.concatenate([w_key, w_value], axis=1), True)
        gains = gather_rows(jnp.stack([attn_gain, ff_gain], axis=1), False).astype(F32).T
        gain_one, gain_two = gains[:1], gains[1:]
        wo = gather_rows(w_out, True)
        wg, wu, wd = (gather_rows(w, False) for w in (w_gate, w_up, w_down))
        cosine, sine = rotary_tables(offset, local)
        ends = jnp.cumsum(doc_lengths, axis=1)[:, :-1]
        scal = jnp.concatenate(
            [ends, piece_starts, jnp.broadcast_to(offset, (seqs, 1)).astype(jnp.int32)], axis=1
        )

        chunks = [slice(s, s + 1) for s in range(seqs)]
        rows = local
        state = []
        for c in chunks:
            tok, cot = tokens[c], cotangent[c]
            cot_own = cot.reshape(rows, width)
            cot_y = swap(cot_own, "tp", 2)
            cot_core = swap(cot_own, "tp", 1)
            cot_diag = swap(cot_y, "tp", 1)
            normed_one, q, kv = project(tok, gain_one, wq, wkv, cosine, sine)
            near = shift(kv, 1)
            far = shift(near, 1)
            ahead = shift(kv[:, :GRAIN], -1)
            parts = (far, near, kv, ahead)
            state.append((c, tok, cot, (cot_own, cot_core, cot_y, cot_diag), normed_one, q, parts))
        after = []
        for c, tok, cot, cots, normed_one, q, parts in state:
            mixed, lse = attend(scal[c], q, parts)
            hidden, normed_two = residual(tok, mixed, wo, gain_two)
            own = normed_two.reshape(rows, width)
            n_y = swap(own, "tp", 2)
            n_core = swap(own, "tp", 1)
            n_diag = swap(n_y, "tp", 1)
            after.append((mixed, lse, hidden, (own, n_core, n_y, n_diag)))
        middle = []
        outputs = []
        for (c, tok, cot, cots, *_), (mixed, lse, hidden, nrm) in zip(state, after):
            near_ff = ff(nrm[:2], cots[:2], wg, wu, wd)
            far_ff = ff(nrm[2:], cots[2:], wg, wu, wd)

            def scatter(a, b):
                own, core = a[:rows], a[rows:]
                facing, diag = b[:rows], b[rows:]
                from_core = swap(jnp.concatenate([core, diag], axis=0), "tp", 1)
                mine = own.astype(F32) + from_core[:rows].astype(F32)
                theirs = (facing.astype(F32) + from_core[rows:].astype(F32)).astype(BF16)
                return mine[None], swap(theirs, "tp", 2)[None]

            grads = scatter(near_ff[4], far_ff[4])
            outs = scatter(near_ff[3], far_ff[3])
            output = (hidden + outs[0] + outs[1].astype(F32)).astype(BF16)
            outputs.append(output)
            grad_hidden, branch, grad_mixed, gain_grad = ff_back(hidden, cot, *grads, gain_two, wo)
            middle.append((near_ff, far_ff, grad_hidden, branch, grad_mixed, gain_grad))

        def joined(pick_array):
            return jnp.concatenate([pick_array(i) for i in range(len(chunks))], axis=0)

        ff_rows = joined(lambda i: jnp.concatenate(after[i][3], axis=0))
        cot_rows = joined(lambda i: jnp.concatenate(state[i][3], axis=0))
        ff_units = [
            joined(lambda i: jnp.concatenate([middle[i][0][k], middle[i][1][k]], axis=0))
            for k in range(3)
        ]
        sums = [over_shard(tn(cot_rows, ff_units[0]))]
        sums += [over_shard(tn(ff_rows, ff_units[k])) for k in (1, 2)]
        sum_down, sum_gate, sum_up = [
            lax.psum(total.astype(BF16), "ctx").astype(F32) for total in sums
        ]
        mixed_rows = joined(lambda i: after[i][0].reshape(rows, QW))
        branch_rows = joined(lambda i: middle[i][3].reshape(rows, width))
        sum_out = reduce_attention(tn(mixed_rows, branch_rows))

        last = []
        for i, (c, tok, cot, cots, normed_one, q, parts) in enumerate(state):
            mixed, lse, hidden, _ = after[i]
            dq, dfar, dnear, down, dnext = attend_back(scal[c], q, parts, mixed, lse, middle[i][4])
            passed = shift(dfar, -1)
            right = shift((dnear.astype(F32) + passed.astype(F32)).astype(BF16), -1)
            left = shift(dnext, 1)
            gq = query_back(dq, cosine, sine)
            input_grad, gkv, gain_grad = input_back(
                tok, middle[i][2], gq, down, left, right, gain_one, wq, wkv, cosine, sine
            )
            last.append((input_grad, gq, gkv, gain_grad, normed_one))
        normed_rows = joined(lambda i: last[i][4].reshape(rows, width))
        gq_rows = joined(lambda i: last[i][1].reshape(rows, QW))
        gkv_rows = joined(lambda i: last[i][2].reshape(rows, 2 * KW))
        sum_query = reduce_attention(tn(normed_rows, gq_rows))
        sum_kv = reduce_attention(tn(normed_rows, gkv_rows))
        gain_grads = jnp.stack(
            [sum(m[3][0, 0] for m in last), sum(m[5][0, 0] for m in middle)], axis=1
        )
        sum_gain = reduce_attention(gain_grads)
        return (
            jnp.concatenate(outputs, axis=0),
            jnp.concatenate([m[0] for m in last], axis=0),
            sum_gain[:, 0],
            sum_query,
            sum_kv[:, :KW],
            sum_kv[:, KW:],
            sum_out,
            sum_gain[:, 1],
            sum_gate,
            sum_up,
            sum_down,
        )

    return per_device


def solution(mesh):
    rows = P(("shard", "tp"), "ctx", None)
    seq = P(("shard", "tp"), None)
    gain, weight, ff_weight = P("shard"), P("shard", None), P("shard", "tp")
    weights = (gain, weight, weight, weight, weight, gain, ff_weight, ff_weight, ff_weight)
    return jax.shard_map(
        program(mesh),
        mesh=mesh,
        in_specs=(rows, rows, seq, seq, *weights),
        out_specs=(rows, rows, *weights),
        check_vma=False,
    )
```

time: 1340 us -> 528 us (0.39)
  waiting for transfers between devices: 663 us -> 126 us
  local copies, waits for them, and re-layouts: 302 us -> 74.7 us
  matrix products: 240 us -> 23.6 us
  Pallas kernels: 0 us -> 131 us
  starting transfers between devices: 2.05 us -> 95.9 us
  blocking collectives: 71.2 us -> 0 us
    unnamed x148 -> x188, local copies, waits for them, and re-layouts: 285 us -> 35.8 us
    psum x2 -> x1, waiting for transfers between devices: 222 us -> 0.01 us  [per_device(): lax.psum(total.astype(BF16), 'ctx').astype(F32)]
    dot_general x32 -> x6, matrix products: 238 us -> 23.6 us  [dot(): lax.dot_general(left, right, (dims, ((), ())), preferred_element_type=F32)]
    reduce_scatter x8 -> x0, waiting for transfers between devices: 210 us -> none  [the longest x1 60.6 us: per_device(): lax.psum_scatter(contract_last(grad_gate, gate_use) + contract_last(grad_...]
    all_gather x9 -> x0, waiting for transfers between devices: 164 us -> none  [the longest x1 35.6 us: per_device(): grad_rows = lax.all_gather(cot_rows, 'tp', axis=0, tiled=True)]
    pallas_call x0 -> x18, Pallas kernels: none -> 131 us  [call(): pl.pallas_call(kernel, out_shape=outs, grid=grid, in_specs=in_specs, out_...]
    ppermute x0 -> x73, waiting for transfers between devices: none -> 126 us  [the longest x61 109 us: swap(): return lax.ppermute(value, axis, [(i, i ^ bit) for i in range(count)])]
    ppermute x0 -> x73, starting transfers between devices: none -> 95.9 us  [the longest x61 65 us: swap(): return lax.ppermute(value, axis, [(i, i ^ bit) for i in range(count)])]
  transfers between devices with their start and end apart: 22 -> 74, of which waited for: 17 -> 22; matrix products, arithmetic and copies ran while one was open for 36% -> 27% of each run, Pallas kernels for 0% -> 25%
where the time goes in v1:
time: 528 us; the launch traced here: 518 us
  Pallas kernels  131 us (25%)
  waiting for transfers between devices  126 us (24%)
  starting transfers between devices  95.9 us (18%)
  local copies, waits for them, and re-layouts  74.7 us (14%)
  other arithmetic  52.1 us (10%)
  matrix products  23.6 us (4%)
  between operations  15.6 us (3%)
    pallas_call x18, Pallas kernels, call(): pl.pallas_call(kernel, out_shape=outs, grid=grid, in_specs=in_specs, out_...  131 us
    ppermute x61, waiting for transfers between devices, swap(): return lax.ppermute(value, axis, [(i, i ^ bit) for i in range(count)])  109 us
    ppermute x61, starting transfers between devices, swap(): return lax.ppermute(value, axis, [(i, i ^ bit) for i in range(count)])  65 us
    unnamed x188, local copies, waits for them, and re-layouts  35.8 us
    ppermute x12, starting transfers between devices, shift(): return lax.ppermute(value, 'ctx', pairs)  30.9 us
    dot_general x6, matrix products, dot(): lax.dot_general(left, right, (dims, ((), ())), preferred_element_type=F32)  23.6 us
    ppermute x12, waiting for transfers between devices, shift(): return lax.ppermute(value, 'ctx', pairs)  17.1 us
    select_n x13, other arithmetic, in_order(): return jnp.where(index == 0, first, jnp.concatenate([other, own], axis=0))  15.9 us
  transfers between devices with their start and end apart: 74, of which 22 were waited for; matrix products, arithmetic and copies ran while one was open for 27% of the time, Pallas kernels for 25%

profile of v1, /device:TPU:1, one launch (start us, length us, event | category | flops | bytes accessed | tf_op | source)
XLA Modules:
  0.0 518.4 jit_solution(12696488801776508851)
XLA Ops:
  22.1 2.2 fusion.86
  41.0 5.0 collective-permute-done.12
  46.0 3.3 collective-permute-start.4
  51.2 3.1 maximum_select_fusion.3.wg_ref
  54.3 4.8 collective-permute-done.13
  59.1 3.3 collective-permute-start.2
  63.9 5.7 %collective-permute-done.8 = bf16[240,960]{1,0:T(8,128)(2,1)S(1)} collective-permute-done((bf16[240,960]{1,0:T(8,128)(2,1)}, bf16[240,960]{1,0:T(8,128)(2,1)S(1)}, u32[]{:S(2)}, u32[]{:S(2)}) %collective-permute-start.8) | collective-permute-done | bytes 460832 | tf_op jit(solution)/shard_map/ppermute | solution.py:509
  69.6 3.3 collective-permute-start.25
  74.8 8.0 %collective-permute-done.14 = bf16[480,640]{1,0:T(8,128)(2,1)S(1)} collective-permute-done((bf16[480,640]{1,0:T(8,128)(2,1)}, bf16[480,640]{1,0:T(8,128)(2,1)S(1)}, u32[]{:S(2)}, u32[]{:S(2)}) %collective-permute-start.14) | collective-permute-done | bytes 614432 | tf_op jit(solution)/shard_map/ppermute | solution.py:509
  89.5 2.2 maximum_select_fusion.wq_ref
  91.7 4.6 shard_map.217
  97.2 3.4 collective-permute-start.21
  100.6 4.5 shard_map.212
  106.0 3.4 collective-permute-start.5
  109.8 2.2 maximum_select_fusion.1.wo_ref
  116.4 4.6 collective-permute-start.22
  123.6 3.4 collective-permute-start.6
  127.8 12.2 %shard_map.218 = (bf16[1,256,960]{2,1,0:T(8,128)(2,1)}, f32[1,256,128]{2,1,0:T(8,128)}) custom-call(s32[1,5]{1,0:T(1,128)} %get-tuple-element.198.scal_ref, bf16[1,256,960]{2,1,0:T(8,128)(2,1)} %get-tuple-element.76.q_ref, bf16[1,256,640]{2,1,0:T(8,128)(2,1)} %copy-done.63, bf16[1,256,640]{2,1,0:T(8,128)(2,1)} %copy-done.61, ...), custom_call_target="tpu_custom_call" | custom-call | flops 3019898880 | bytes 2261012 | tf_op jit(solution)/shard_map/pallas_call | solution.py:48
  140.0 3.7 shard_map.219
  143.8 2.7 collective-permute-start.24
  147.3 12.5 %shard_map.213 = (bf16[1,256,960]{2,1,0:T(8,128)(2,1)}, f32[1,256,128]{2,1,0:T(8,128)}) custom-call(s32[1,5]{1,0:T(1,128)} %get-tuple-element.197.scal_ref, bf16[1,256,960]{2,1,0:T(8,128)(2,1)} %get-tuple-element.69.q_ref, bf16[1,256,640]{2,1,0:T(8,128)(2,1)} %copy-done.62, bf16[1,256,640]{2,1,0:T(8,128)(2,1)} %copy-done.60, ...), custom_call_target="tpu_custom_call" | custom-call | flops 3019898880 | bytes 2261012 | tf_op jit(solution)/shard_map/pallas_call | solution.py:48
  159.8 3.8 shard_map.214
  168.1 9.3 %shard_map.220 = (bf16[512,640]{1,0:T(8,128)(2,1)}, bf16[512,640]{1,0:T(8,128)(2,1)}, bf16[512,640]{1,0:T(8,128)(2,1)}, bf16[512,960]{1,0:T(8,128)(2,1)}, bf16[512,960]{1,0:T(8,128)(2,1)}) custom-call(bf16[256,960]{1,0:T(8,128)(2,1)} %bitcast.173, bf16[256,960]{1,0:T(8,128)(2,1)} %copy-done.33, bf16[256,960]{1,0:T(8,128)(2,1)} %bitcast.151, ...), custom_call_target="tpu_custom_call" | custom-call | flops 3774873600 | bytes 9584640 | tf_op jit(solution)/shard_map/pallas_call | solution.py:48
  179.5 9.1 %collective-permute-done.26.nrm_a = bf16[256,960]{1,0:T(8,128)(2,1)S(1)} collective-permute-done((bf16[256,960]{1,0:T(8,128)(2,1)S(1)}, bf16[256,960]{1,0:T(8,128)(2,1)S(1)}, u32[]{:S(2)}, u32[]{:S(2)}) %collective-permute-start.26) | collective-permute-done | bytes 491552 | tf_op jit(solution)/shard_map/ppermute | solution.py:509
  190.2 9.3 %shard_map.215 = (bf16[512,640]{1,0:T(8,128)(2,1)}, bf16[512,640]{1,0:T(8,128)(2,1)}, bf16[512,640]{1,0:T(8,128)(2,1)}, bf16[512,960]{1,0:T(8,128)(2,1)}, bf16[512,960]{1,0:T(8,128)(2,1)}) custom-call(bf16[256,960]{1,0:T(8,128)(2,1)} %bitcast.177, bf16[256,960]{1,0:T(8,128)(2,1)} %copy-done.40, bf16[256,960]{1,0:T(8,128)(2,1)} %bitcast.148, ...), custom_call_target="tpu_custom_call" | custom-call | flops 3774873600 | bytes 9584640 | tf_op jit(solution)/shard_map/pallas_call | solution.py:48
  204.4 9.5 %shard_map.221 = (bf16[512,640]{1,0:T(8,128)(2,1)}, bf16[512,640]{1,0:T(8,128)(2,1)}, bf16[512,640]{1,0:T(8,128)(2,1)}, bf16[512,960]{1,0:T(8,128)(2,1)}, bf16[512,960]{1,0:T(8,128)(2,1)}) custom-call(bf16[256,960]{1,0:T(8,128)(2,1)} %copy-done.35, bf16[256,960]{1,0:T(8,128)(2,1)} %copy-done.38, bf16[256,960]{1,0:T(8,128)(2,1)} %copy-done.27, ...), custom_call_target="tpu_custom_call" | custom-call | flops 3774873600 | bytes 9584640 | tf_op jit(solution)/shard_map/pallas_call | solution.py:48
  219.4 9.6 %shard_map.216 = (bf16[512,640]{1,0:T(8,128)(2,1)}, bf16[512,640]{1,0:T(8,128)(2,1)}, bf16[512,640]{1,0:T(8,128)(2,1)}, bf16[512,960]{1,0:T(8,128)(2,1)}, bf16[512,960]{1,0:T(8,128)(2,1)}) custom-call(bf16[256,960]{1,0:T(8,128)(2,1)} %copy-done.37, bf16[256,960]{1,0:T(8,128)(2,1)} %collective-permute-done.16.nrm_b, ...), custom_call_target="tpu_custom_call" | custom-call | flops 3774873600 | bytes 9584640 | tf_op jit(solution)/shard_map/pallas_call | solution.py:48
  229.0 4.7 fusion.16
  237.3 3.3 fusion
  242.1 5.0 fusion.8
  248.6 2.2 fusion.49
  254.3 2.5 fusion.24
  256.9 6.3 %collective-permute-done.70 = bf16[480,640]{1,0:T(8,128)(2,1)} collective-permute-done((bf16[480,640]{1,0:T(8,128)(2,1)}, bf16[480,640]{1,0:T(8,128)(2,1)}, u32[]{:S(2)}, u32[]{:S(2)}) %collective-permute-start.70) | collective-permute-done | bytes 614432 | tf_op jit(solution)/shard_map/ppermute | solution.py:509
  263.2 2.2 collective-permute-start.19
  267.3 9.0 %collective-permute-done.71 = bf16[480,640]{1,0:T(8,128)(2,1)} collective-permute-done((bf16[480,640]{1,0:T(8,128)(2,1)}, bf16[480,640]{1,0:T(8,128)(2,1)}, u32[]{:S(2)}, u32[]{:S(2)}) %collective-permute-start.71) | collective-permute-done | bytes 614432 | tf_op jit(solution)/shard_map/ppermute | solution.py:509
  294.7 2.2 add_bitcast_fusion.a_ref
  298.1 4.5 shard_map.226
  302.6 13.1 %shard_map.227 = (f32[1,256,960]{2,1,0:T(8,128)}, bf16[1,256,640]{2,1,0:T(8,128)(2,1)}, bf16[1,256,640]{2,1,0:T(8,128)(2,1)}, f32[1,256,640]{2,1,0:T(8,128)}, bf16[1,128,640]{2,1,0:T(8,128)(2,1)}) custom-call(s32[1,5]{1,0:T(1,128)} %get-tuple-element.198.scal_ref, bf16[1,256,960]{2,1,0:T(8,128)(2,1)} %get-tuple-element.76.q_ref, ...), custom_call_target="tpu_custom_call" | custom-call | flops 7549747200 | bytes 5210132 | tf_op jit(solution)/shard_map/pallas_call | solution.py:48
  315.7 3.9 collective-permute-start.39
  321.0 4.6 shard_map.222
  325.6 12.9 %shard_map.223 = (f32[1,256,960]{2,1,0:T(8,128)}, bf16[1,256,640]{2,1,0:T(8,128)(2,1)}, bf16[1,256,640]{2,1,0:T(8,128)(2,1)}, f32[1,256,640]{2,1,0:T(8,128)}, bf16[1,128,640]{2,1,0:T(8,128)(2,1)}) custom-call(s32[1,5]{1,0:T(1,128)} %get-tuple-element.197.scal_ref, bf16[1,256,960]{2,1,0:T(8,128)(2,1)} %get-tuple-element.69.q_ref, ...), custom_call_target="tpu_custom_call" | custom-call | flops 7549747200 | bytes 5210132 | tf_op jit(solution)/shard_map/pallas_call | solution.py:48
  338.5 4.3 collective-permute-start.34
  346.1 2.9 shard_map.228.gq_ref
  349.0 2.8 shard_map.224.gq_ref
  353.3 14.8 %collective-permute-done.35 = bf16[1,256,640]{2,1,0:T(8,128)(2,1)S(1)} collective-permute-done((bf16[1,256,640]{2,1,0:T(8,128)(2,1)}, bf16[1,256,640]{2,1,0:T(8,128)(2,1)S(1)}, u32[]{:S(2)}, u32[]{:S(2)}) %collective-permute-start.35) | collective-permute-done | bytes 327712 | tf_op jit(solution)/shard_map/ppermute | solution.py:513
  369.5 4.1 fusion.27
  375.8 5.5 %shard_map.229 = (f32[1,256,960]{2,1,0:T(8,128)}, bf16[1,256,640]{2,1,0:T(8,128)(2,1)}, f32[1,1,960]{2,1,0:T(1,128)}) custom-call(bf16[1,256,960]{2,1,0:T(8,128)(2,1)} %copy.114.tok_ref, f32[1,256,960]{2,1,0:T(8,128)} %get-tuple-element.96.gh_ref, bf16[1,256,960]{2,1,0:T(8,128)(2,1)} %shard_map.228.gq_ref, f32[1,256,640]{2,1,0:T(8,128)} %get-tuple-element.100.own_ref, ...), custom_call_target="tpu_custom_call" | custom-call | flops 786432000 | bytes 7765504 | tf_op jit(solution)/shard_map/pallas_call | solution.py:48
  382.8 5.5 %shard_map.225 = (f32[1,256,960]{2,1,0:T(8,128)}, bf16[1,256,640]{2,1,0:T(8,128)(2,1)}, f32[1,1,960]{2,1,0:T(1,128)}) custom-call(bf16[1,256,960]{2,1,0:T(8,128)(2,1)} %copy.110.tok_ref, f32[1,256,960]{2,1,0:T(8,128)} %get-tuple-element.85.gh_ref, bf16[1,256,960]{2,1,0:T(8,128)(2,1)} %shard_map.224.gq_ref, f32[1,256,640]{2,1,0:T(8,128)} %get-tuple-element.89.own_ref, ...), custom_call_target="tpu_custom_call" | custom-call | flops 786432000 | bytes 7765504 | tf_op jit(solution)/shard_map/pallas_call | solution.py:48
  390.3 4.4 fusion.31
  398.6 2.6 fusion.40
  404.2 2.1 collective-permute-start.45
  406.3 2.6 fusion.41
  410.9 2.2 fusion.44
  415.6 2.2 collective-permute-start.48
  426.9 8.2 %collective-permute-done.50 = bf16[240,960]{1,0:T(8,128)(2,1)S(1)} collective-permute-done((bf16[240,960]{1,0:T(8,128)(2,1)S(1)}, bf16[240,960]{1,0:T(8,128)(2,1)S(1)}, u32[]{:S(2)}, u32[]{:S(2)}) %collective-permute-start.50) | collective-permute-done | bytes 460832 | tf_op jit(solution)/shard_map/ppermute | solution.py:509
  435.5 10.1 %collective-permute-done.64 = bf16[240,960]{1,0:T(8,128)(2,1)S(1)} collective-permute-done((bf16[240,960]{1,0:T(8,128)(2,1)S(1)}, bf16[240,960]{1,0:T(8,128)(2,1)S(1)}, u32[]{:S(2)}, u32[]{:S(2)}) %collective-permute-start.64) | collective-permute-done | bytes 460832 | tf_op jit(solution)/shard_map/ppermute | solution.py:509
  446.1 6.1 %collective-permute-done.57 = bf16[240,640]{1,0:T(8,128)(2,1)S(1)} collective-permute-done((bf16[240,640]{1,0:T(8,128)(2,1)S(1)}, bf16[240,640]{1,0:T(8,128)(2,1)S(1)}, u32[]{:S(2)}, u32[]{:S(2)}) %collective-permute-start.57) | collective-permute-done | bytes 307232 | tf_op jit(solution)/shard_map/ppermute | solution.py:509
  454.3 2.1 collective-permute-done.58
  460.6 9.2 %collective-permute-done.59 = bf16[120,640]{1,0:T(8,128)(2,1)S(1)} collective-permute-done((bf16[120,640]{1,0:T(8,128)(2,1)S(1)}, bf16[120,640]{1,0:T(8,128)(2,1)S(1)}, u32[]{:S(2)}, u32[]{:S(2)}) %collective-permute-start.59) | collective-permute-done | bytes 153632 | tf_op jit(solution)/shard_map/ppermute | solution.py:509
  472.3 15.8 %collective-permute-done.60 = bf16[120,640]{1,0:T(8,128)(2,1)S(1)} collective-permute-done((bf16[120,640]{1,0:T(8,128)(2,1)S(1)}, bf16[120,640]{1,0:T(8,128)(2,1)S(1)}, u32[]{:S(2)}, u32[]{:S(2)}) %collective-permute-start.60) | collective-permute-done | bytes 153632 | tf_op jit(solution)/shard_map/ppermute | solution.py:509
  489.8 3.6 collective-permute-done.67
  494.9 2.8 collective-permute-start.62
  498.3 2.2 convert_element_type.466
  500.5 2.2 convert_element_type.471
  (417 shorter events, 159.2 us)
Async XLA Ops:
  7.2 491.1 %all-reduce.3.cloned.1.call-start = ((), (), s32[]{:S(2)}) async-start(), calls=%async_computation | async-start | bytes 3686400 | tf_op jit(solution)/shard_map/psum | solution.py:651
  8.8 16.9 %collective-permute-start = (bf16[480,2]{0,1:T(2,128)(2,1)S(1)}, bf16[480,2]{0,1:T(2,128)(2,1)S(1)}, u32[]{:S(2)}, u32[]{:S(2)}) collective-permute-start(bf16[480,2]{0,1:T(2,128)(2,1)S(1)} %pad_maximum_fusion.11), channel_id=1, source_target_pairs={{0,16},{16,0},{1,17},{17,1},{2,18},{18,2},{3,19},{19,3},{4,20},{20... | collective-permute-start | bytes 5768 | tf_op jit(solution)/shard_map/ppermute | solution.py:509
  14.2 19.7 %collective-permute-start.3 = (bf16[240,640]{1,0:T(8,128)(2,1)}, bf16[240,640]{1,0:T(8,128)(2,1)}, u32[]{:S(2)}, u32[]{:S(2)}) collective-permute-start(bf16[240,640]{1,0:T(8,128)(2,1)} %fusion.58), channel_id=1, source_target_pairs={{0,16},{16,0},{1,17},{17,1},{2,18},{18,2},{3,19},{19,3},{4,20},{20... | collective-permute-start | bytes 921608 | tf_op jit(solution)/shard_map/ppermute | solution.py:509
  15.0 20.7 %collective-permute-start.1 = (bf16[240,960]{1,0:T(8,128)(2,1)}, bf16[240,960]{1,0:T(8,128)(2,1)}, u32[]{:S(2)}, u32[]{:S(2)}) collective-permute-start(bf16[240,960]{1,0:T(8,128)(2,1)} %constant_dynamic-slice_fusion.9), channel_id=1, source_target_pairs={{0,16},{16,0},{1,17},{17,1},{2,18},{18,2},{3,19},{19,3},{4,20},{20... | collective-permute-start | bytes 1382408 | tf_op jit(solution)/shard_map/ppermute | solution.py:509
  16.4 29.6 %collective-permute-start.12 = (bf16[480,640]{1,0:T(8,128)(2,1)}, bf16[480,640]{1,0:T(8,128)(2,1)}, u32[]{:S(2)}, u32[]{:S(2)}) collective-permute-start(bf16[480,640]{1,0:T(8,128)(2,1)} %param.23), channel_id=1, source_target_pairs={{0,16},{16,0},{1,17},{17,1},{2,18},{18,2},{3,19},{19,3},{4,20},{20... | collective-permute-start | bytes 1843208 | tf_op jit(solution)/shard_map/ppermute | solution.py:509
  18.8 17.2 %collective-permute-start.11 = (bf16[256,960]{1,0:T(8,128)(2,1)S(1)}, bf16[256,960]{1,0:T(8,128)(2,1)}, u32[]{:S(2)}, u32[]{:S(2)}) collective-permute-start(bf16[256,960]{1,0:T(8,128)(2,1)S(1)} %bitcast.146), channel_id=1, source_target_pairs={{0,1},{1,0},{2,3},{3,2},{4,5},{5,4},{6,7},{7,6},{8,9},{9,8},{10,11... | collective-permute-start | bytes 1474568 | tf_op jit(solution)/shard_map/ppermute | solution.py:509
  25.7 14.0 %collective-permute-start.17 = (bf16[256,960]{1,0:T(8,128)(2,1)S(1)}, bf16[256,960]{1,0:T(8,128)(2,1)}, u32[]{:S(2)}, u32[]{:S(2)}) collective-permute-start(bf16[256,960]{1,0:T(8,128)(2,1)S(1)} %bitcast.147), channel_id=1, source_target_pairs={{0,2},{1,3},{2,0},{3,1},{4,6},{5,7},{6,4},{7,5},{8,10},{9,11},{10,... | collective-permute-start | bytes 1474568 | tf_op jit(solution)/shard_map/ppermute | solution.py:509
  33.9 25.2 %collective-permute-start.13 = (bf16[480,640]{1,0:T(8,128)(2,1)S(1)}, bf16[480,640]{1,0:T(8,128)(2,1)S(1)}, u32[]{:S(2)}, u32[]{:S(2)}) collective-permute-start(bf16[480,640]{1,0:T(8,128)(2,1)S(1)} %copy-done.25), channel_id=1, source_target_pairs={{0,16},{16,0},{1,17},{17,1},{2,18},{18,2},{3,19},{19,3},{4,20},{20... | collective-permute-start | bytes 1843208 | tf_op jit(solution)/shard_map/ppermute | solution.py:509
  35.7 33.8 %collective-permute-start.8 = (bf16[240,960]{1,0:T(8,128)(2,1)}, bf16[240,960]{1,0:T(8,128)(2,1)S(1)}, u32[]{:S(2)}, u32[]{:S(2)}) collective-permute-start(bf16[240,960]{1,0:T(8,128)(2,1)} %constant_dynamic-slice_fusion.7), channel_id=1, source_target_pairs={{0,16},{16,0},{1,17},{17,1},{2,18},{18,2},{3,19},{19,3},{4,20},{20... | collective-permute-start | bytes 1382408 | tf_op jit(solution)/shard_map/ppermute | solution.py:509
  36.0 46.8 %collective-permute-start.14 = (bf16[480,640]{1,0:T(8,128)(2,1)}, bf16[480,640]{1,0:T(8,128)(2,1)S(1)}, u32[]{:S(2)}, u32[]{:S(2)}) collective-permute-start(bf16[480,640]{1,0:T(8,128)(2,1)} %param.25), channel_id=1, source_target_pairs={{0,16},{16,0},{1,17},{17,1},{2,18},{18,2},{3,19},{19,3},{4,20},{20... | collective-permute-start | bytes 1843208 | tf_op jit(solution)/shard_map/ppermute | solution.py:509
  39.7 34.5 %collective-permute-start.28 = (bf16[256,960]{1,0:T(8,128)(2,1)S(1)}, bf16[256,960]{1,0:T(8,128)(2,1)S(1)}, u32[]{:S(2)}, u32[]{:S(2)}) collective-permute-start(bf16[256,960]{1,0:T(8,128)(2,1)S(1)} %bitcast.149), channel_id=1, source_target_pairs={{0,2},{1,3},{2,0},{3,1},{4,6},{5,7},{6,4},{7,5},{8,10},{9,11},{10,... | collective-permute-start | bytes 1474568 | tf_op jit(solution)/shard_map/ppermute | solution.py:509
  46.0 26.9 %collective-permute-start.4 = (bf16[240,640]{1,0:T(8,128)(2,1)}, bf16[240,640]{1,0:T(8,128)(2,1)S(1)}, u32[]{:S(2)}, u32[]{:S(2)}) collective-permute-start(bf16[240,640]{1,0:T(8,128)(2,1)} %collective-permute-done.3), channel_id=1, source_target_pairs={{0,1},{1,0},{2,3},{3,2},{4,5},{5,4},{6,7},{7,6},{8,9},{9,8},{10,11... | collective-permute-start | bytes 921608 | tf_op jit(solution)/shard_map/ppermute | solution.py:509
  59.1 28.8 %collective-permute-start.2 = (bf16[240,960]{1,0:T(8,128)(2,1)}, bf16[240,960]{1,0:T(8,128)(2,1)S(1)}, u32[]{:S(2)}, u32[]{:S(2)}) collective-permute-start(bf16[240,960]{1,0:T(8,128)(2,1)} %collective-permute-done.1), channel_id=1, source_target_pairs={{0,1},{1,0},{2,3},{3,2},{4,5},{5,4},{6,7},{7,6},{8,9},{9,8},{10,11... | collective-permute-start | bytes 1382408 | tf_op jit(solution)/shard_map/ppermute | solution.py:509
  69.6 45.5 %collective-permute-start.25 = (bf16[256,960]{1,0:T(8,128)(2,1)S(1)}, bf16[256,960]{1,0:T(8,128)(2,1)S(1)}, u32[]{:S(2)}, u32[]{:S(2)}) collective-permute-start(bf16[256,960]{1,0:T(8,128)(2,1)S(1)} %bitcast.150), channel_id=1, source_target_pairs={{0,1},{1,0},{2,3},{3,2},{4,5},{5,4},{6,7},{7,6},{8,9},{9,8},{10,11... | collective-permute-start | bytes 1474568 | tf_op jit(solution)/shard_map/ppermute | solution.py:509
  72.9 33.1 %collective-permute-start.9 = (bf16[240,960]{1,0:T(8,128)(2,1)S(1)}, bf16[240,960]{1,0:T(8,128)(2,1)S(1)}, u32[]{:S(2)}, u32[]{:S(2)}) collective-permute-start(bf16[240,960]{1,0:T(8,128)(2,1)S(1)} %collective-permute-done.8), channel_id=1, source_target_pairs={{0,1},{1,0},{2,3},{3,2},{4,5},{5,4},{6,7},{7,6},{8,9},{9,8},{10,11... | collective-permute-start | bytes 1382408 | tf_op jit(solution)/shard_map/ppermute | solution.py:509
  74.2 37.9 %collective-permute-start.18 = (bf16[256,960]{1,0:T(8,128)(2,1)}, bf16[256,960]{1,0:T(8,128)(2,1)S(1)}, u32[]{:S(2)}, u32[]{:S(2)}) collective-permute-start(bf16[256,960]{1,0:T(8,128)(2,1)} %collective-permute-done.17.cot_a), channel_id=1, source_target_pairs={{0,1},{1,0},{2,3},{3,2},{4,5},{5,4},{6,7},{7,6},{8,9},{9,8},{10,11... | collective-permute-start | bytes 1474568 | tf_op jit(solution)/shard_map/ppermute | solution.py:509
  82.8 39.9 %collective-permute-start.29 = (bf16[256,960]{1,0:T(8,128)(2,1)S(1)}, bf16[256,960]{1,0:T(8,128)(2,1)S(1)}, u32[]{:S(2)}, u32[]{:S(2)}) collective-permute-start(bf16[256,960]{1,0:T(8,128)(2,1)S(1)} %collective-permute-done.28.cot_a), channel_id=1, source_target_pairs={{0,1},{1,0},{2,3},{3,2},{4,5},{5,4},{6,7},{7,6},{8,9},{9,8},{10,11... | collective-permute-start | bytes 1474568 | tf_op jit(solution)/shard_map/ppermute | solution.py:509
  97.2 19.1 %collective-permute-start.21 = (bf16[1,256,640]{2,1,0:T(8,128)(2,1)}, bf16[1,256,640]{2,1,0:T(8,128)(2,1)S(1)}, u32[]{:S(2)}, u32[]{:S(2)}) collective-permute-start(bf16[1,256,640]{2,1,0:T(8,128)(2,1)} %get-tuple-element.77.own_ref), channel_id=1, source_target_pairs={{0,4},{4,8},{8,12},{1,5},{5,9},{9,13},{2,6},{6,10},{10,14},{3,7},{... | collective-permute-start | bytes 983048 | tf_op jit(solution)/shard_map/ppermute | solution.py:513
  106.0 17.6 %collective-permute-start.5 = (bf16[1,256,640]{2,1,0:T(8,128)(2,1)}, bf16[1,256,640]{2,1,0:T(8,128)(2,1)S(1)}, u32[]{:S(2)}, u32[]{:S(2)}) collective-permute-start(bf16[1,256,640]{2,1,0:T(8,128)(2,1)} %get-tuple-element.70.own_ref), channel_id=1, source_target_pairs={{0,4},{4,8},{8,12},{1,5},{5,9},{9,13},{2,6},{6,10},{10,14},{3,7},{... | collective-permute-start | bytes 983048 | tf_op jit(solution)/shard_map/ppermute | solution.py:513
  112.1 14.9 %collective-permute-start.23 = (bf16[1,128,640]{2,1,0:T(8,128)(2,1)S(1)}, bf16[1,128,640]{2,1,0:T(8,128)(2,1)S(1)}, u32[]{:S(2)}, u32[]{:S(2)}) collective-permute-start(bf16[1,128,640]{2,1,0:T(8,128)(2,1)S(1)} %slice.134), channel_id=1, source_target_pairs={{4,0},{8,4},{12,8},{5,1},{9,5},{13,9},{6,2},{10,6},{14,10},{7,3},{... | collective-permute-start | bytes 491528 | tf_op jit(solution)/shard_map/ppermute | solution.py:513
  115.0 31.4 %collective-permute-start.7 = (bf16[1,128,640]{2,1,0:T(8,128)(2,1)S(1)}, bf16[1,128,640]{2,1,0:T(8,128)(2,1)S(1)}, u32[]{:S(2)}, u32[]{:S(2)}) collective-permute-start(bf16[1,128,640]{2,1,0:T(8,128)(2,1)S(1)} %slice.123), channel_id=1, source_target_pairs={{4,0},{8,4},{12,8},{5,1},{9,5},{13,9},{6,2},{10,6},{14,10},{7,3},{... | collective-permute-start | bytes 491528 | tf_op jit(solution)/shard_map/ppermute | solution.py:513
  116.4 10.8 %collective-permute-start.22 = (bf16[1,256,640]{2,1,0:T(8,128)(2,1)S(1)}, bf16[1,256,640]{2,1,0:T(8,128)(2,1)S(1)}, u32[]{:S(2)}, u32[]{:S(2)}) collective-permute-start(bf16[1,256,640]{2,1,0:T(8,128)(2,1)S(1)} %collective-permute-done.21.near_ref), channel_id=1, source_target_pairs={{0,4},{4,8},{8,12},{1,5},{5,9},{9,13},{2,6},{6,10},{10,14},{3,7},{... | collective-permute-start | bytes 983048 | tf_op jit(solution)/shard_map/ppermute | solution.py:513
  123.6 22.9 %collective-permute-start.6 = (bf16[1,256,640]{2,1,0:T(8,128)(2,1)S(1)}, bf16[1,256,640]{2,1,0:T(8,128)(2,1)S(1)}, u32[]{:S(2)}, u32[]{:S(2)}) collective-permute-start(bf16[1,256,640]{2,1,0:T(8,128)(2,1)S(1)} %collective-permute-done.5.near_ref), channel_id=1, source_target_pairs={{0,4},{4,8},{8,12},{1,5},{5,9},{9,13},{2,6},{6,10},{10,14},{3,7},{... | collective-permute-start | bytes 983048 | tf_op jit(solution)/shard_map/ppermute | solution.py:513
  143.8 23.5 %collective-permute-start.24 = (bf16[256,960]{1,0:T(8,128)(2,1)}, bf16[256,960]{1,0:T(8,128)(2,1)S(1)}, u32[]{:S(2)}, u32[]{:S(2)}) collective-permute-start(bf16[256,960]{1,0:T(8,128)(2,1)} %bitcast.172), channel_id=1, source_target_pairs={{0,1},{1,0},{2,3},{3,2},{4,5},{5,4},{6,7},{7,6},{8,9},{9,8},{10,11... | collective-permute-start | bytes 1474568 | tf_op jit(solution)/shard_map/ppermute | solution.py:509
  163.6 38.1 %collective-permute-start.15 = (bf16[256,960]{1,0:T(8,128)(2,1)}, bf16[256,960]{1,0:T(8,128)(2,1)S(1)}, u32[]{:S(2)}, u32[]{:S(2)}) collective-permute-start(bf16[256,960]{1,0:T(8,128)(2,1)} %bitcast.175), channel_id=1, source_target_pairs={{0,2},{1,3},{2,0},{3,1},{4,6},{5,7},{6,4},{7,5},{8,10},{9,11},{10,... | collective-permute-start | bytes 1474568 | tf_op jit(solution)/shard_map/ppermute | solution.py:509
  164.9 24.5 %collective-permute-start.10 = (bf16[256,960]{1,0:T(8,128)(2,1)}, bf16[256,960]{1,0:T(8,128)(2,1)S(1)}, u32[]{:S(2)}, u32[]{:S(2)}) collective-permute-start(bf16[256,960]{1,0:T(8,128)(2,1)} %bitcast.176), channel_id=1, source_target_pairs={{0,1},{1,0},{2,3},{3,2},{4,5},{5,4},{6,7},{7,6},{8,9},{9,8},{10,11... | collective-permute-start | bytes 1474568 | tf_op jit(solution)/shard_map/ppermute | solution.py:509
  165.2 23.5 %collective-permute-start.26 = (bf16[256,960]{1,0:T(8,128)(2,1)S(1)}, bf16[256,960]{1,0:T(8,128)(2,1)S(1)}, u32[]{:S(2)}, u32[]{:S(2)}) collective-permute-start(bf16[256,960]{1,0:T(8,128)(2,1)S(1)} %bitcast.174), channel_id=1, source_target_pairs={{0,2},{1,3},{2,0},{3,1},{4,6},{5,7},{6,4},{7,5},{8,10},{9,11},{10,... | collective-permute-start | bytes 1474568 | tf_op jit(solution)/shard_map/ppermute | solution.py:509
  188.6 14.9 %collective-permute-start.27 = (bf16[256,960]{1,0:T(8,128)(2,1)S(1)}, bf16[256,960]{1,0:T(8,128)(2,1)S(1)}, u32[]{:S(2)}, u32[]{:S(2)}) collective-permute-start(bf16[256,960]{1,0:T(8,128)(2,1)S(1)} %collective-permute-done.26.nrm_a), channel_id=1, source_target_pairs={{0,1},{1,0},{2,3},{3,2},{4,5},{5,4},{6,7},{7,6},{8,9},{9,8},{10,11... | collective-permute-start | bytes 1474568 | tf_op jit(solution)/shard_map/ppermute | solution.py:509
  201.7 17.6 %collective-permute-start.16 = (bf16[256,960]{1,0:T(8,128)(2,1)S(1)}, bf16[256,960]{1,0:T(8,128)(2,1)}, u32[]{:S(2)}, u32[]{:S(2)}) collective-permute-start(bf16[256,960]{1,0:T(8,128)(2,1)S(1)} %collective-permute-done.15.nrm_a), channel_id=1, source_target_pairs={{0,1},{1,0},{2,3},{3,2},{4,5},{5,4},{6,7},{7,6},{8,9},{9,8},{10,11... | collective-permute-start | bytes 1474568 | tf_op jit(solution)/shard_map/ppermute | solution.py:509
  218.8 59.6 %collective-permute-start.37 = (bf16[512,960]{0,1:T(8,128)(2,1)}, bf16[512,960]{0,1:T(8,128)(2,1)}, u32[]{:S(2)}, u32[]{:S(2)}) collective-permute-start(bf16[512,960]{0,1:T(8,128)(2,1)} %copy.97), channel_id=1, source_target_pairs={{0,1},{1,0},{2,3},{3,2},{4,5},{5,4},{6,7},{7,6},{8,9},{9,8},{10,11... | collective-permute-start | bytes 2949128 | tf_op jit(solution)/shard_map/ppermute | solution.py:509
  219.3 64.2 %collective-permute-start.30 = (bf16[512,960]{0,1:T(8,128)(2,1)}, bf16[512,960]{0,1:T(8,128)(2,1)}, u32[]{:S(2)}, u32[]{:S(2)}) collective-permute-start(bf16[512,960]{0,1:T(8,128)(2,1)} %copy.91), channel_id=1, source_target_pairs={{0,1},{1,0},{2,3},{3,2},{4,5},{5,4},{6,7},{7,6},{8,9},{9,8},{10,11... | collective-permute-start | bytes 2949128 | tf_op jit(solution)/shard_map/ppermute | solution.py:509
  234.6 18.5 %collective-permute-start.72 = (bf16[480,640]{1,0:T(8,128)(2,1)}, bf16[480,640]{1,0:T(8,128)(2,1)S(1)}, u32[]{:S(2)}, u32[]{:S(2)}) collective-permute-start(bf16[480,640]{1,0:T(8,128)(2,1)} %fusion.50), channel_id=1, source_target_pairs={{0,16},{16,0},{1,17},{17,1},{2,18},{18,2},{3,19},{19,3},{4,20},{20... | collective-permute-start | bytes 1843208 | tf_op jit(solution)/shard_map/ppermute | solution.py:509
  241.6 21.6 %collective-permute-start.70 = (bf16[480,640]{1,0:T(8,128)(2,1)}, bf16[480,640]{1,0:T(8,128)(2,1)}, u32[]{:S(2)}, u32[]{:S(2)}) collective-permute-start(bf16[480,640]{1,0:T(8,128)(2,1)} %fusion.48), channel_id=1, source_target_pairs={{0,16},{16,0},{1,17},{17,1},{2,18},{18,2},{3,19},{19,3},{4,20},{20... | collective-permute-start | bytes 1843208 | tf_op jit(solution)/shard_map/ppermute | solution.py:509
  250.8 25.6 %collective-permute-start.71 = (bf16[480,640]{1,0:T(8,128)(2,1)}, bf16[480,640]{1,0:T(8,128)(2,1)}, u32[]{:S(2)}, u32[]{:S(2)}) collective-permute-start(bf16[480,640]{1,0:T(8,128)(2,1)} %fusion.49), channel_id=1, source_target_pairs={{0,16},{16,0},{1,17},{17,1},{2,18},{18,2},{3,19},{19,3},{4,20},{20... | collective-permute-start | bytes 1843208 | tf_op jit(solution)/shard_map/ppermute | solution.py:509
  253.1 33.2 %collective-permute-start.32 = (bf16[512,960]{0,1:T(8,128)(2,1)}, bf16[512,960]{0,1:T(8,128)(2,1)}, u32[]{:S(2)}, u32[]{:S(2)}) collective-permute-start(bf16[512,960]{0,1:T(8,128)(2,1)} %copy.94), channel_id=1, source_target_pairs={{0,1},{1,0},{2,3},{3,2},{4,5},{5,4},{6,7},{7,6},{8,9},{9,8},{10,11... | collective-permute-start | bytes 2949128 | tf_op jit(solution)/shard_map/ppermute | solution.py:509
  263.2 28.3 %collective-permute-start.19 = (bf16[512,960]{0,1:T(8,128)(2,1)}, bf16[512,960]{0,1:T(8,128)(2,1)}, u32[]{:S(2)}, u32[]{:S(2)}) collective-permute-start(bf16[512,960]{0,1:T(8,128)(2,1)} %copy.86), channel_id=1, source_target_pairs={{0,1},{1,0},{2,3},{3,2},{4,5},{5,4},{6,7},{7,6},{8,9},{9,8},{10,11... | collective-permute-start | bytes 2949128 | tf_op jit(solution)/shard_map/ppermute | solution.py:509
  282.2 15.9 %collective-permute-start.38 = (bf16[256,960]{1,0:T(8,128)(2,1)}, bf16[256,960]{1,0:T(8,128)(2,1)}, u32[]{:S(2)}, u32[]{:S(2)}) collective-permute-start(bf16[256,960]{1,0:T(8,128)(2,1)} %add_convert_fusion), channel_id=1, source_target_pairs={{0,2},{1,3},{2,0},{3,1},{4,6},{5,7},{6,4},{7,5},{8,10},{9,11},{10,... | collective-permute-start | bytes 1474568 | tf_op jit(solution)/shard_map/ppermute | solution.py:509
  286.1 56.7 %collective-permute-start.31 = (bf16[256,960]{1,0:T(8,128)(2,1)}, bf16[256,960]{1,0:T(8,128)(2,1)}, u32[]{:S(2)}, u32[]{:S(2)}) collective-permute-start(bf16[256,960]{1,0:T(8,128)(2,1)} %add_convert_fusion.2), channel_id=1, source_target_pairs={{0,2},{1,3},{2,0},{3,1},{4,6},{5,7},{6,4},{7,5},{8,10},{9,11},{10,... | collective-permute-start | bytes 1474568 | tf_op jit(solution)/shard_map/ppermute | solution.py:509
  290.2 30.7 %collective-permute-start.33 = (bf16[256,960]{1,0:T(8,128)(2,1)}, bf16[256,960]{1,0:T(8,128)(2,1)}, u32[]{:S(2)}, u32[]{:S(2)}) collective-permute-start(bf16[256,960]{1,0:T(8,128)(2,1)} %add_convert_fusion.1), channel_id=1, source_target_pairs={{0,2},{1,3},{2,0},{3,1},{4,6},{5,7},{6,4},{7,5},{8,10},{9,11},{10,... | collective-permute-start | bytes 1474568 | tf_op jit(solution)/shard_map/ppermute | solution.py:509
  294.4 51.3 %collective-permute-start.20 = (bf16[256,960]{1,0:T(8,128)(2,1)S(1)}, bf16[256,960]{1,0:T(8,128)(2,1)S(1)}, u32[]{:S(2)}, u32[]{:S(2)}) collective-permute-start(bf16[256,960]{1,0:T(8,128)(2,1)S(1)} %add_convert_fusion.3), channel_id=1, source_target_pairs={{0,2},{1,3},{2,0},{3,1},{4,6},{5,7},{6,4},{7,5},{8,10},{9,11},{10,... | collective-permute-start | bytes 1474568 | tf_op jit(solution)/shard_map/ppermute | solution.py:509
  315.7 58.0 %collective-permute-start.39 = (bf16[1,128,640]{2,1,0:T(8,128)(2,1)}, bf16[1,128,640]{2,1,0:T(8,128)(2,1)S(1)}, u32[]{:S(2)}, u32[]{:S(2)}) collective-permute-start(bf16[1,128,640]{2,1,0:T(8,128)(2,1)} %get-tuple-element.101), channel_id=1, source_target_pairs={{0,4},{4,8},{8,12},{1,5},{5,9},{9,13},{2,6},{6,10},{10,14},{3,7},{... | collective-permute-start | bytes 491528 | tf_op jit(solution)/shard_map/ppermute | solution.py:513
  319.7 32.2 %collective-permute-start.40 = (bf16[1,256,640]{2,1,0:T(8,128)(2,1)}, bf16[1,256,640]{2,1,0:T(8,128)(2,1)S(1)}, u32[]{:S(2)}, u32[]{:S(2)}) collective-permute-start(bf16[1,256,640]{2,1,0:T(8,128)(2,1)} %get-tuple-element.103), channel_id=1, source_target_pairs={{4,0},{8,4},{12,8},{5,1},{9,5},{13,9},{6,2},{10,6},{14,10},{7,3},{... | collective-permute-start | bytes 983048 | tf_op jit(solution)/shard_map/ppermute | solution.py:513
  338.5 42.7 %collective-permute-start.34 = (bf16[1,128,640]{2,1,0:T(8,128)(2,1)}, bf16[1,128,640]{2,1,0:T(8,128)(2,1)S(1)}, u32[]{:S(2)}, u32[]{:S(2)}) collective-permute-start(bf16[1,128,640]{2,1,0:T(8,128)(2,1)} %get-tuple-element.90), channel_id=1, source_target_pairs={{0,4},{4,8},{8,12},{1,5},{5,9},{9,13},{2,6},{6,10},{10,14},{3,7},{... | collective-permute-start | bytes 491528 | tf_op jit(solution)/shard_map/ppermute | solution.py:513
  342.9 25.2 %collective-permute-start.35 = (bf16[1,256,640]{2,1,0:T(8,128)(2,1)}, bf16[1,256,640]{2,1,0:T(8,128)(2,1)S(1)}, u32[]{:S(2)}, u32[]{:S(2)}) collective-permute-start(bf16[1,256,640]{2,1,0:T(8,128)(2,1)} %get-tuple-element.92), channel_id=1, source_target_pairs={{4,0},{8,4},{12,8},{5,1},{9,5},{13,9},{6,2},{10,6},{14,10},{7,3},{... | collective-permute-start | bytes 983048 | tf_op jit(solution)/shard_map/ppermute | solution.py:513
  352.0 23.1 %collective-permute-start.41 = (bf16[1,256,640]{2,1,0:T(8,128)(2,1)S(1)}, bf16[1,256,640]{2,1,0:T(8,128)(2,1)S(1)}, u32[]{:S(2)}, u32[]{:S(2)}) collective-permute-start(bf16[1,256,640]{2,1,0:T(8,128)(2,1)S(1)} %add_convert_fusion.4), channel_id=1, source_target_pairs={{4,0},{8,4},{12,8},{5,1},{9,5},{13,9},{6,2},{10,6},{14,10},{7,3},{... | collective-permute-start | bytes 983048 | tf_op jit(solution)/shard_map/ppermute | solution.py:513
  368.1 14.0 %collective-permute-start.36 = (bf16[1,256,640]{2,1,0:T(8,128)(2,1)S(1)}, bf16[1,256,640]{2,1,0:T(8,128)(2,1)S(1)}, u32[]{:S(2)}, u32[]{:S(2)}) collective-permute-start(bf16[1,256,640]{2,1,0:T(8,128)(2,1)S(1)} %add_convert_fusion.5), channel_id=1, source_target_pairs={{4,0},{8,4},{12,8},{5,1},{9,5},{13,9},{6,2},{10,6},{14,10},{7,3},{... | collective-permute-start | bytes 983048 | tf_op jit(solution)/shard_map/ppermute | solution.py:513
  397.3 6.9 %collective-permute-start.44 = (bf16[120,2]{0,1:T(2,128)(2,1)S(1)}, bf16[120,2]{0,1:T(2,128)(2,1)S(1)}, u32[]{:S(2)}, u32[]{:S(2)}) collective-permute-start(bf16[120,2]{0,1:T(2,128)(2,1)S(1)} %convert_bitcast_fusion.1), channel_id=1, source_target_pairs={{0,2},{1,3},{2,0},{3,1},{4,6},{5,7},{6,4},{7,5},{8,10},{9,11},{10,... | collective-permute-start | bytes 1448 | tf_op jit(solution)/shard_map/ppermute | solution.py:509
  402.7 17.9 %collective-permute-start.49 = (bf16[2,240,960]{2,1,0:T(8,128)(2,1)}, bf16[2,240,960]{2,1,0:T(8,128)(2,1)S(1)}, u32[]{:S(2)}, u32[]{:S(2)}) collective-permute-start(bf16[2,240,960]{2,1,0:T(8,128)(2,1)} %fusion.40), channel_id=1, source_target_pairs={{0,1},{1,0},{2,3},{3,2},{4,5},{5,4},{6,7},{7,6},{8,9},{9,8},{10,11... | collective-permute-start | bytes 2764808 | tf_op jit(solution)/shard_map/ppermute | solution.py:509
  408.9 14.0 %collective-permute-start.63 = (bf16[2,240,960]{2,1,0:T(8,128)(2,1)}, bf16[2,240,960]{2,1,0:T(8,128)(2,1)}, u32[]{:S(2)}, u32[]{:S(2)}) collective-permute-start(bf16[2,240,960]{2,1,0:T(8,128)(2,1)} %fusion.41), channel_id=1, source_target_pairs={{0,1},{1,0},{2,3},{3,2},{4,5},{5,4},{6,7},{7,6},{8,9},{9,8},{10,11... | collective-permute-start | bytes 2764808 | tf_op jit(solution)/shard_map/ppermute | solution.py:509
  422.7 12.4 %collective-permute-start.50 = (bf16[240,960]{1,0:T(8,128)(2,1)S(1)}, bf16[240,960]{1,0:T(8,128)(2,1)S(1)}, u32[]{:S(2)}, u32[]{:S(2)}) collective-permute-start(bf16[240,960]{1,0:T(8,128)(2,1)S(1)} %fusion.53), channel_id=1, source_target_pairs={{0,16},{16,0},{1,17},{17,1},{2,18},{18,2},{3,19},{19,3},{4,20},{20... | collective-permute-start | bytes 1382408 | tf_op jit(solution)/shard_map/ppermute | solution.py:509
  425.1 20.5 %collective-permute-start.64 = (bf16[240,960]{1,0:T(8,128)(2,1)S(1)}, bf16[240,960]{1,0:T(8,128)(2,1)S(1)}, u32[]{:S(2)}, u32[]{:S(2)}) collective-permute-start(bf16[240,960]{1,0:T(8,128)(2,1)S(1)} %fusion.54), channel_id=1, source_target_pairs={{0,16},{16,0},{1,17},{17,1},{2,18},{18,2},{3,19},{19,3},{4,20},{20... | collective-permute-start | bytes 1382408 | tf_op jit(solution)/shard_map/ppermute | solution.py:509
  426.2 26.0 %collective-permute-start.57 = (bf16[240,640]{1,0:T(8,128)(2,1)S(1)}, bf16[240,640]{1,0:T(8,128)(2,1)S(1)}, u32[]{:S(2)}, u32[]{:S(2)}) collective-permute-start(bf16[240,640]{1,0:T(8,128)(2,1)S(1)} %fusion.57), channel_id=1, source_target_pairs={{0,16},{16,0},{1,17},{17,1},{2,18},{18,2},{3,19},{19,3},{4,20},{20... | collective-permute-start | bytes 921608 | tf_op jit(solution)/shard_map/ppermute | solution.py:509
  435.3 17.3 %collective-permute-start.51 = (bf16[120,960]{1,0:T(8,128)(2,1)S(1)}, bf16[120,960]{1,0:T(8,128)(2,1)S(1)}, u32[]{:S(2)}, u32[]{:S(2)}) collective-permute-start(bf16[120,960]{1,0:T(8,128)(2,1)S(1)} %fusion.60), channel_id=1, source_target_pairs={{0,2},{1,3},{2,0},{3,1},{4,6},{5,7},{6,4},{7,5},{8,10},{9,11},{10,... | collective-permute-start | bytes 691208 | tf_op jit(solution)/shard_map/ppermute | solution.py:509
  445.8 8.0 %collective-permute-start.65 = (bf16[120,960]{1,0:T(8,128)(2,1)S(1)}, bf16[120,960]{1,0:T(8,128)(2,1)S(1)}, u32[]{:S(2)}, u32[]{:S(2)}) collective-permute-start(bf16[120,960]{1,0:T(8,128)(2,1)S(1)} %fusion.61), channel_id=1, source_target_pairs={{0,2},{1,3},{2,0},{3,1},{4,6},{5,7},{6,4},{7,5},{8,10},{9,11},{10,... | collective-permute-start | bytes 691208 | tf_op jit(solution)/shard_map/ppermute | solution.py:509
  452.6 5.9 %collective-permute-start.52 = (bf16[120,960]{1,0:T(8,128)(2,1)S(1)}, bf16[120,960]{1,0:T(8,128)(2,1)S(1)}, u32[]{:S(2)}, u32[]{:S(2)}) collective-permute-start(bf16[120,960]{1,0:T(8,128)(2,1)S(1)} %fusion.56), channel_id=1, source_target_pairs={{0,4},{4,0},{8,12},{12,8},{1,5},{5,1},{9,13},{13,9},{2,6},{6,2},{1... | collective-permute-start | bytes 691208 | tf_op jit(solution)/shard_map/ppermute | solution.py:509
  453.8 16.8 %collective-permute-start.66 = (bf16[120,960]{1,0:T(8,128)(2,1)S(1)}, bf16[120,960]{1,0:T(8,128)(2,1)S(1)}, u32[]{:S(2)}, u32[]{:S(2)}) collective-permute-start(bf16[120,960]{1,0:T(8,128)(2,1)S(1)} %fusion.55), channel_id=1, source_target_pairs={{0,4},{4,0},{8,12},{12,8},{1,5},{5,1},{9,13},{13,9},{2,6},{6,2},{1... | collective-permute-start | bytes 691208 | tf_op jit(solution)/shard_map/ppermute | solution.py:509
  456.5 13.3 %collective-permute-start.59 = (bf16[120,640]{1,0:T(8,128)(2,1)S(1)}, bf16[120,640]{1,0:T(8,128)(2,1)S(1)}, u32[]{:S(2)}, u32[]{:S(2)}) collective-permute-start(bf16[120,640]{1,0:T(8,128)(2,1)S(1)} %fusion.59), channel_id=1, source_target_pairs={{0,4},{4,0},{8,12},{12,8},{1,5},{5,1},{9,13},{13,9},{2,6},{6,2},{1... | collective-permute-start | bytes 460808 | tf_op jit(solution)/shard_map/ppermute | solution.py:509
  458.6 30.9 %collective-permute-start.53 = (bf16[120,960]{1,0:T(8,128)(2,1)S(1)}, bf16[120,960]{1,0:T(8,128)(2,1)S(1)}, u32[]{:S(2)}, u32[]{:S(2)}) collective-permute-start(bf16[120,960]{1,0:T(8,128)(2,1)S(1)} %add_convert_fusion.9), channel_id=1, source_target_pairs={{0,8},{4,12},{8,0},{12,4},{1,9},{5,13},{9,1},{13,5},{2,10},{6,14},... | collective-permute-start | bytes 691208 | tf_op jit(solution)/shard_map/ppermute | solution.py:509
  469.8 18.3 %collective-permute-start.60 = (bf16[120,640]{1,0:T(8,128)(2,1)S(1)}, bf16[120,640]{1,0:T(8,128)(2,1)S(1)}, u32[]{:S(2)}, u32[]{:S(2)}) collective-permute-start(bf16[120,640]{1,0:T(8,128)(2,1)S(1)} %add_convert_fusion.11), channel_id=1, source_target_pairs={{0,8},{4,12},{8,0},{12,4},{1,9},{5,13},{9,1},{13,5},{2,10},{6,14},... | collective-permute-start | bytes 460808 | tf_op jit(solution)/shard_map/ppermute | solution.py:509
  470.7 22.7 %collective-permute-start.67 = (bf16[120,960]{1,0:T(8,128)(2,1)S(1)}, bf16[120,960]{1,0:T(8,128)(2,1)S(1)}, u32[]{:S(2)}, u32[]{:S(2)}) collective-permute-start(bf16[120,960]{1,0:T(8,128)(2,1)S(1)} %add_convert_fusion.7), channel_id=1, source_target_pairs={{0,8},{4,12},{8,0},{12,4},{1,9},{5,13},{9,1},{13,5},{2,10},{6,14},... | collective-permute-start | bytes 691208 | tf_op jit(solution)/shard_map/ppermute | solution.py:509
  488.2 6.6 %collective-permute-start.61 = (bf16[120,640]{1,0:T(8,128)(2,1)S(1)}, bf16[120,640]{1,0:T(8,128)(2,1)S(1)}, u32[]{:S(2)}, u32[]{:S(2)}) collective-permute-start(bf16[120,640]{1,0:T(8,128)(2,1)S(1)} %add_convert_fusion.10), channel_id=1, source_target_pairs={{0,2},{1,3},{2,0},{3,1},{4,6},{5,7},{6,4},{7,5},{8,10},{9,11},{10,... | collective-permute-start | bytes 460808 | tf_op jit(solution)/shard_map/ppermute | solution.py:509
  489.6 14.2 %collective-permute-start.54 = (bf16[120,960]{1,0:T(8,128)(2,1)S(1)}, bf16[120,960]{1,0:T(8,128)(2,1)S(1)}, u32[]{:S(2)}, u32[]{:S(2)}) collective-permute-start(bf16[120,960]{1,0:T(8,128)(2,1)S(1)} %add_convert_fusion.8), channel_id=1, source_target_pairs={{0,2},{1,3},{2,0},{3,1},{4,6},{5,7},{6,4},{7,5},{8,10},{9,11},{10,... | collective-permute-start | bytes 691208 | tf_op jit(solution)/shard_map/ppermute | solution.py:509
  493.4 10.6 %collective-permute-start.68 = (bf16[120,960]{1,0:T(8,128)(2,1)S(1)}, bf16[120,960]{1,0:T(8,128)(2,1)S(1)}, u32[]{:S(2)}, u32[]{:S(2)}) collective-permute-start(bf16[120,960]{1,0:T(8,128)(2,1)S(1)} %add_convert_fusion.6), channel_id=1, source_target_pairs={{0,2},{1,3},{2,0},{3,1},{4,6},{5,7},{6,4},{7,5},{8,10},{9,11},{10,... | collective-permute-start | bytes 691208 | tf_op jit(solution)/shard_map/ppermute | solution.py:509
  494.9 10.5 %collective-permute-start.62 = (bf16[240,640]{1,0:T(8,128)(2,1)S(1)}, bf16[240,640]{1,0:T(8,128)(2,1)S(1)}, u32[]{:S(2)}, u32[]{:S(2)}) collective-permute-start(bf16[240,640]{1,0:T(8,128)(2,1)S(1)} %maximum_select_fusion.14), channel_id=1, source_target_pairs={{0,1},{1,0},{2,3},{3,2},{4,5},{5,4},{6,7},{7,6},{8,9},{9,8},{10,11... | collective-permute-start | bytes 921608 | tf_op jit(solution)/shard_map/ppermute | solution.py:509
  (88 other events, 758.1 us)
Sparse Core Ops, SparseCore 0:
  278.5 89.0 all-reduce.2

commit v2 on v1

v2 whole, which is shorter than its diff:
```python
import functools
import math

import jax
import jax.numpy as jnp
from jax import lax
from jax.experimental import pallas as pl
from jax.experimental.pallas import tpu as pltpu
from jax.sharding import PartitionSpec as P

H = 15
KVH = 5
HD = 64
LEN = 1024
PIECE = 256
GRAIN = 128
MAXDOC = 512
GROUP = H // KVH
KW = KVH * HD
QW = H * HD
SPAN = MAXDOC + 2 * GRAIN

EPS = 1e-05
NEG = -1e30
F32 = jnp.float32
BF16 = jnp.bfloat16
VMEM_LIMIT = 56 * 1024 * 1024
COST = 0.1


def dot(left, right, dims):
    return lax.dot_general(left, right, (dims, ((), ())), preferred_element_type=F32)


def nn(left, right):
    return dot(left, right, ((1,), (0,)))


def nt(left, right):
    return dot(left, right, ((1,), (1,)))


def tn(left, right):
    return dot(left, right, ((0,), (0,)))


def call(kernel, outs, args, in_specs, out_specs, *, grid=(1,), scratch=(), flops=0, aliases=None):
    return pl.pallas_call(
        kernel,
        out_shape=outs,
        grid=grid,
        in_specs=in_specs,
        out_specs=out_specs,
        scratch_shapes=list(scratch),
        input_output_aliases=aliases or {},
        compiler_params=pltpu.CompilerParams(vmem_limit_bytes=VMEM_LIMIT),
        cost_estimate=pl.CostEstimate(
            flops=int(flops * COST), bytes_accessed=int(flops * COST / 300), transcendentals=0
        ),
    )(*args)


def part(array, seq):
    index = seq if array.shape[0] > 1 else 0
    return pl.BlockSpec((1, *array.shape[1:]), lambda *_: (index,) + (0,) * (len(array.shape) - 1))


def sub_part(array):
    return pl.BlockSpec((1, GRAIN, array.shape[2]), lambda i: (0, i, 0))


def whole(array):
    return pl.BlockSpec(array.shape, lambda *_: (0,) * len(array.shape))


def untouched():
    return pl.BlockSpec(memory_space=pl.ANY)


def smem():
    return pl.BlockSpec(memory_space=pltpu.SMEM)


def struct(shape, dtype):
    return jax.ShapeDtypeStruct(shape, dtype)


def after(value, *deps):
    return lax.optimization_barrier((value, deps))[0]


def rotary_tables(offset, length):
    half = HD // 2
    place = (offset + jnp.arange(length, dtype=jnp.int32)).astype(F32)
    freq = jnp.exp(jnp.arange(half).astype(F32) * (-2.0 * math.log(10000.0) / HD))
    angle = place[:, None] * freq[None, :]
    cosine, sine = jnp.cos(angle), jnp.sin(angle)
    return (
        jnp.concatenate([cosine] * 4, axis=1),
        jnp.concatenate([-sine, sine, -sine, sine], axis=1),
    )


def rotate(tile, cosine, sine):
    lane = lax.broadcasted_iota(jnp.int32, tile.shape, 1)
    partner = jnp.where(lane % HD < HD // 2, pltpu.roll(tile, 96, 1), pltpu.roll(tile, 32, 1))
    return tile * cosine + partner * sine


def rotate_into(out_ref, value_ref, width, cosine, sine, factor):
    for start in range(0, width, 128):
        stop = min(start + 128, width)
        turned = rotate(value_ref[:, start : start + 128], cosine, sine) * factor
        out_ref[0, :, start:stop] = turned[:, : stop - start].astype(out_ref.dtype)


def inverse_mean(value):
    return lax.rsqrt(jnp.mean(value * value, axis=-1, keepdims=True) + EPS)


def wide(width):
    return -(-width // 128) * 128


def project_rows(tok_ref, gain_ref, wq_ref, wkv_ref, cos_ref, sin_ref, normed_ref, q_ref, kv_ref, qs, ks):
    source = tok_ref[0].astype(F32)
    normed = (source * inverse_mean(source) * gain_ref[...]).astype(BF16)
    normed_ref[0] = normed
    cosine, sine = cos_ref[...], sin_ref[...]
    raw = nn(normed, wkv_ref[...])
    ks[:, :KW] = raw[:, :KW]
    kv_ref[0, :, KW:] = raw[:, KW:].astype(BF16)
    rotate_into(kv_ref, ks, KW, cosine, sine, 1.0)
    qs[:, :QW] = nn(normed, wq_ref[...])
    rotate_into(q_ref, qs, QW, cosine, sine, HD**-0.5)


def project_first_kernel(pieces, place_ref, tok_ref, gain_ref, cos_ref, sin_ref, *refs):
    q_pieces, kv_pieces = refs[:pieces], refs[pieces : 2 * pieces]
    normed_ref, q_ref, kv_ref, wq_ref, wkv_ref, qs, ks = refs[2 * pieces :]
    for out_ref, parts in ((wq_ref, q_pieces), (wkv_ref, kv_pieces)):
        for i, piece in enumerate(parts):
            count = piece.shape[0]
            out_ref[pl.ds(pl.multiple_of(place_ref[i], 16), count), :] = piece[...]
    project_rows(
        tok_ref, gain_ref, wq_ref, wkv_ref, cos_ref, sin_ref, normed_ref, q_ref, kv_ref, qs, ks
    )


def project_outs(tokens):
    rows, width = tokens.shape[1:]
    return (
        [
            struct((1, rows, width), BF16),
            struct((1, rows, QW), BF16),
            struct((1, rows, 2 * KW), BF16),
        ],
        [pltpu.VMEM((rows, wide(QW)), F32), pltpu.VMEM((rows, wide(KW)), F32)],
        2 * rows * width * (QW + 2 * KW),
    )


def project_first(tokens, seq, gain, q_pieces, kv_pieces, places, cosine, sine):
    width = tokens.shape[2]
    outs, scratch, flops = project_outs(tokens)
    outs = outs + [struct((width, QW), BF16), struct((width, 2 * KW), BF16)]
    rest = (gain, cosine, sine, *q_pieces, *kv_pieces)
    return call(
        functools.partial(project_first_kernel, len(q_pieces)),
        outs,
        (places, tokens, *rest),
        [smem(), part(tokens, seq), *map(whole, rest)],
        [whole(o) for o in outs],
        scratch=scratch,
        flops=flops,
    )


def project(tokens, seq, gain, wq, wkv, cosine, sine):
    outs, scratch, flops = project_outs(tokens)
    rest = (gain, wq, wkv, cosine, sine)
    return call(
        project_rows,
        outs,
        (tokens, *rest),
        [part(tokens, seq), *map(whole, rest)],
        [whole(o) for o in outs],
        scratch=scratch,
        flops=flops,
    )


def marks(scal_ref, pos, valid):
    segment = jnp.zeros(pos.shape, jnp.int32)
    for d in range(2):
        segment += (pos >= scal_ref[0, d]).astype(jnp.int32)
    number = jnp.zeros(pos.shape, jnp.int32)
    for j in range(2):
        start = scal_ref[0, 2 + j]
        number += jnp.where((pos >= start) & (pos < start + PIECE), j + 1, 0)
    return jnp.where(valid, segment, -1), number


def bias_of(scal_ref, start, across):
    q_shape, k_shape, q_dim, k_dim = (
        ((GRAIN, 1), (1, SPAN), 0, 1) if across else ((1, GRAIN), (SPAN, 1), 1, 0)
    )
    q_pos = start + lax.broadcasted_iota(jnp.int32, q_shape, q_dim)
    k_pos = start - MAXDOC + lax.broadcasted_iota(jnp.int32, k_shape, k_dim)
    q_seg, q_num = marks(scal_ref, q_pos, q_pos >= 0)
    k_seg, k_num = marks(scal_ref, k_pos, (k_pos >= 0) & (k_pos < LEN))
    q_num = jnp.where(q_num > 0, q_num, -1)
    permit = (q_seg == k_seg) & ((k_pos <= q_pos) | (q_num == k_num))
    return jnp.where(permit, 0.0, NEG).astype(F32)


def load_window(window, parts):
    row = 0
    for part in parts:
        window[row : row + part.shape[1], :] = part[0]
        row += part.shape[1]


def attend_kernel(scal_ref, q_ref, far_ref, near_ref, own_ref, next_ref, mixed_ref, lse_ref, window):
    sub = pl.program_id(0)

    @pl.when(sub == 0)
    def _():
        load_window(window, (far_ref, near_ref, own_ref, next_ref))

    bias = bias_of(scal_ref, scal_ref[0, 4] + sub * GRAIN, True)
    rows = pl.ds(pl.multiple_of(sub * GRAIN, GRAIN), SPAN)
    lse = jnp.zeros((GRAIN, 128), F32)
    lane = lax.broadcasted_iota(jnp.int32, (GRAIN, 128), 1)
    for j in range(KVH):
        key = window[rows, j * HD : (j + 1) * HD]
        value = window[rows, KW + j * HD : KW + (j + 1) * HD]
        for g in range(GROUP):
            h = j * GROUP + g
            scores = nt(q_ref[0, :, h * HD : (h + 1) * HD], key) + bias
            top = jnp.max(scores, axis=-1, keepdims=True)
            raised = jnp.exp(scores - top)
            total = jnp.sum(raised, axis=-1, keepdims=True)
            out = nn(raised.astype(BF16), value) / total
            mixed_ref[0, :, h * HD : (h + 1) * HD] = out.astype(BF16)
            lse = jnp.where(lane == h, top + jnp.log(total), lse)
    lse_ref[0] = lse


def attend(scal, q, parts):
    local = q.shape[1]
    outs = [struct((1, local, QW), BF16), struct((1, local, 128), F32)]
    return call(
        attend_kernel,
        outs,
        (scal, q, *parts),
        [smem(), sub_part(q), *map(whole, parts)],
        [sub_part(o) for o in outs],
        grid=(local // GRAIN,),
        scratch=[pltpu.VMEM((MAXDOC + local + GRAIN, 2 * KW), BF16)],
        flops=16 * local * SPAN * QW,
    )


def attend_back_kernel(
    scal_ref,
    q_ref,
    far_ref,
    near_ref,
    own_ref,
    next_ref,
    mixed_ref,
    lse_ref,
    grad_ref,
    dq_ref,
    dfar_ref,
    dnear_ref,
    down_ref,
    dnext_ref,
    window,
    sums,
):
    sub = pl.program_id(0)

    @pl.when(sub == 0)
    def _():
        load_window(window, (far_ref, near_ref, own_ref, next_ref))
        sums[...] = jnp.zeros_like(sums)

    bias = bias_of(scal_ref, scal_ref[0, 4] + sub * GRAIN, False)
    bias = jnp.concatenate([bias] * GROUP, axis=1)
    rows = pl.ds(pl.multiple_of(sub * GRAIN, GRAIN), SPAN)
    lane = lax.broadcasted_iota(jnp.int32, (GRAIN, 128), 1)
    product = mixed_ref[0].astype(F32) * grad_ref[0].astype(F32)
    delta = jnp.zeros((GRAIN, 128), F32)
    for h in range(H):
        part = jnp.sum(product[:, h * HD : (h + 1) * HD], axis=-1, keepdims=True)
        delta = jnp.where(lane == h, part, delta)
    delta = delta.T
    lse = lse_ref[0].T

    def heads(array, j):
        return [array[h : h + 1, :] for h in range(j * GROUP, (j + 1) * GROUP)]

    for j in range(KVH):
        k_cols = slice(j * HD, (j + 1) * HD)
        v_cols = slice(KW + j * HD, KW + (j + 1) * HD)
        key, value = window[rows, k_cols], window[rows, v_cols]
        cols = [slice(h * HD, (h + 1) * HD) for h in range(j * GROUP, (j + 1) * GROUP)]
        query = jnp.concatenate([q_ref[0, :, c] for c in cols], axis=0)
        grad = jnp.concatenate([grad_ref[0, :, c] for c in cols], axis=0)
        lse_row = jnp.concatenate(heads(lse, j), axis=1)
        delta_row = jnp.concatenate(heads(delta, j), axis=1)
        probs = jnp.exp(nt(key, query) + bias - lse_row)
        grad_scores = (probs * (nt(value, grad) - delta_row)).astype(BF16)
        sums[rows, v_cols] += nn(probs.astype(BF16), grad)
        sums[rows, k_cols] += nn(grad_scores, query)
        dq = tn(grad_scores, key)
        for g, c in enumerate(cols):
            dq_ref[0, :, c] = dq[g * GRAIN : (g + 1) * GRAIN, :]

    @pl.when(sub == pl.num_programs(0) - 1)
    def _():
        row = 0
        for part in (dfar_ref, dnear_ref, down_ref, dnext_ref):
            part[0] = sums[row : row + part.shape[1], :].astype(part.dtype)
            row += part.shape[1]


def attend_back(scal, q, parts, mixed, lse, grad):
    local = q.shape[1]
    window = MAXDOC + local + GRAIN
    outs = [
        struct((1, local, QW), F32),
        struct((1, local, 2 * KW), BF16),
        struct((1, local, 2 * KW), BF16),
        struct((1, local, 2 * KW), F32),
        struct((1, GRAIN, 2 * KW), BF16),
    ]
    return call(
        attend_back_kernel,
        outs,
        (scal, q, *parts, mixed, lse, grad),
        [smem(), sub_part(q), *map(whole, parts), sub_part(mixed), sub_part(lse), sub_part(grad)],
        [sub_part(outs[0]), *map(whole, outs[1:])],
        grid=(local // GRAIN,),
        scratch=[pltpu.VMEM((window, 2 * KW), BF16), pltpu.VMEM((window, 2 * KW), F32)],
        flops=40 * local * SPAN * QW,
    )


def residual_kernel(tok_ref, mixed_ref, wo_ref, gain_ref, hidden_ref, normed_ref):
    hidden = tok_ref[0].astype(F32) + nn(mixed_ref[0], wo_ref[...])
    hidden_ref[0] = hidden
    normed_ref[0] = (hidden * inverse_mean(hidden) * gain_ref[...]).astype(BF16)


def residual(tokens, seq, mixed, wo, gain):
    rows, width = tokens.shape[1:]
    outs = [struct((1, rows, width), F32), struct((1, rows, width), BF16)]
    return call(
        residual_kernel,
        outs,
        (tokens, mixed, wo, gain),
        [part(tokens, seq), whole(mixed), whole(wo), whole(gain)],
        [whole(o) for o in outs],
        flops=2 * rows * width * QW,
    )


def ff_kernel(
    nrm_a,
    nrm_b,
    cot_a,
    cot_b,
    wg_ref,
    wu_ref,
    wd_ref,
    *refs,
):
    inner_ref, gg_ref, gu_ref, rows_ref, ff_a, ff_b, gn_a, gn_b = refs[-8:]
    first = pl.program_id(0) == 0
    normed = jnp.where(first, nrm_a[0], nrm_b[0])
    rows_ref[...] = normed
    gate = nn(normed, wg_ref[...])
    up = nn(normed, wu_ref[...])
    grad = nn(jnp.where(first, cot_a[0], cot_b[0]), wd_ref[...])
    sigma = jax.nn.sigmoid(gate)
    raised = gate * sigma
    inner = (raised * up).astype(BF16)
    grad_gate = (grad * up * (sigma + raised * (1.0 - sigma))).astype(BF16)
    grad_up = (grad * raised).astype(BF16)
    inner_ref[...] = inner
    gg_ref[...] = grad_gate
    gu_ref[...] = grad_up
    grad_normed = (nt(grad_gate, wg_ref[...]) + nt(grad_up, wu_ref[...])).astype(BF16)
    out = nt(inner, wd_ref[...]).astype(BF16)

    @pl.when(first)
    def _():
        ff_a[0] = out
        gn_a[0] = grad_normed

    @pl.when(jnp.logical_not(first))
    def _():
        ff_b[0] = out
        gn_b[0] = grad_normed


def ff(normed_pair, cot_pair, weights, seq, base, seqs, kept):
    _, rows, width = normed_pair[0].shape
    units = weights[0].shape[1]

    def block(columns):
        return pl.BlockSpec((rows, columns), lambda i: (base + i * seqs + seq, 0))

    args = (*normed_pair, *cot_pair, *weights, *kept)
    count = 4 * seqs * rows
    outs = [struct((count, units), BF16)] * 3 + [struct((count, width), BF16)]
    outs += [struct((1, rows, width), BF16)] * 4
    result = call(
        ff_kernel,
        outs,
        args,
        [
            *map(whole, normed_pair),
            *(part(c, seq) for c in cot_pair),
            *map(whole, weights),
            *(untouched() for _ in kept),
        ],
        [block(units)] * 3 + [block(width)] + [whole(o) for o in outs[4:]],
        grid=(2,),
        aliases={7 + i: i for i in range(len(kept))},
        flops=24 * rows * width * units,
    )
    return result[:4], result[4:6], result[6:]


def ff_back_kernel(
    hidden_ref, cot_ref, a_ref, b_ref, c_ref, gain_ref, wo_ref, gh_ref, gb_ref, gm_ref, gg_ref
):
    hidden, gain = hidden_ref[0], gain_ref[...]
    factor = inverse_mean(hidden)
    grad = a_ref[0].astype(F32) + b_ref[0].astype(F32) + c_ref[0].astype(F32)
    weighted = grad * gain
    back = factor * weighted - hidden * factor**3 * jnp.mean(
        hidden * weighted, axis=-1, keepdims=True
    )
    grad_hidden = cot_ref[0].astype(F32) + back
    branch = grad_hidden.astype(BF16)
    gh_ref[0] = grad_hidden
    gb_ref[0] = branch
    gm_ref[0] = nt(branch, wo_ref[...]).astype(BF16)
    gg_ref[0] = jnp.sum(grad * hidden * factor, axis=0, keepdims=True)


def ff_back(hidden, cotangent, seq, terms, gain, wo):
    _, rows, width = hidden.shape
    outs = [
        struct((1, rows, width), F32),
        struct((1, rows, width), BF16),
        struct((1, rows, QW), BF16),
        struct((1, 1, width), F32),
    ]
    return call(
        ff_back_kernel,
        outs,
        (hidden, cotangent, *terms, gain, wo),
        [whole(hidden), part(cotangent, seq), *map(whole, terms), whole(gain), whole(wo)],
        [whole(o) for o in outs],
        flops=2 * rows * width * QW,
    )


def query_back_kernel(dq_ref, cos_ref, sin_ref, out_ref, qs):
    qs[:, :QW] = dq_ref[0]
    rotate_into(out_ref, qs, QW, cos_ref[...], -sin_ref[...], HD**-0.5)


def query_back(dq, cosine, sine):
    rows = dq.shape[1]
    return call(
        query_back_kernel,
        [struct((1, rows, QW), BF16)],
        (dq, cosine, sine),
        [whole(dq), whole(cosine), whole(sine)],
        [whole(dq)],
        scratch=[pltpu.VMEM((rows, wide(QW)), F32)],
        flops=rows * QW * 100,
    )[0]


def input_kernel(
    tok_ref,
    gh_ref,
    gq_ref,
    own_ref,
    left_ref,
    right_ref,
    gain_ref,
    wq_ref,
    wkv_ref,
    cos_ref,
    sin_ref,
    *refs,
):
    ig_ref, gkv_ref, gg_ref, ks = refs[-4:]
    ks[...] = own_ref[0] + right_ref[0].astype(F32)
    ks[:GRAIN, :] += left_ref[0].astype(F32)
    gkv_ref[0, :, KW:] = ks[:, KW:].astype(BF16)
    rotate_into(gkv_ref, ks, KW, cos_ref[...], -sin_ref[...], 1.0)
    grad = nt(gq_ref[0], wq_ref[...]) + nt(gkv_ref[0], wkv_ref[...])
    source, gain = tok_ref[0].astype(F32), gain_ref[...]
    factor = inverse_mean(source)
    weighted = grad * gain
    back = factor * weighted - source * factor**3 * jnp.mean(
        source * weighted, axis=-1, keepdims=True
    )
    ig_ref[0] = gh_ref[0] + back
    gg_ref[0] = jnp.sum(grad * source * factor, axis=0, keepdims=True)


def input_back(tokens, seq, args, kept):
    _, rows, width = tokens.shape
    outs = [
        struct(tokens.shape, F32),
        struct((1, rows, 2 * KW), BF16),
        struct((1, 1, width), F32),
    ]
    return call(
        input_kernel,
        outs,
        (tokens, *args, *kept),
        [part(tokens, seq), *map(whole, args), *(untouched() for _ in kept)],
        [part(outs[0], seq), whole(outs[1]), whole(outs[2])],
        aliases={1 + len(args): 0} if kept else None,
        scratch=[pltpu.VMEM((rows, 2 * KW), F32)],
        flops=2 * rows * width * (QW + 2 * KW),
    )


def program(mesh):
    shards, ctxs = mesh.shape["shard"], mesh.shape["ctx"]

    def swap(value, axis, bit):
        count = mesh.shape[axis]
        return lax.ppermute(value, axis, [(i, i ^ bit) for i in range(count)])

    def shift(value, by):
        pairs = [(i, i + by) for i in range(ctxs) if 0 <= i + by < ctxs]
        return lax.ppermute(value, "ctx", pairs)

    def in_order(index, own, other):
        first = jnp.concatenate([own, other], axis=0)
        return jnp.where(index == 0, first, jnp.concatenate([other, own], axis=0))

    def pick(value, index):
        return lax.dynamic_index_in_dim(value, index, 0, keepdims=False)

    def fetch(value):
        half = value.shape[0] // 2
        core = lax.axis_index("tp") % 2
        return swap(lax.dynamic_slice_in_dim(value, core * half, half), "shard", 1)

    def over_shard(grad):
        if shards != 2:
            return lax.psum_scatter(grad, "shard", scatter_dimension=0, tiled=True)
        mine = lax.axis_index("shard")
        halves = grad.reshape(2, grad.shape[0] // 2, *grad.shape[1:])
        got = swap(pick(halves, 1 - mine).astype(BF16), "shard", 1)
        return pick(halves, mine) + got.astype(F32)

    def all_over_ctx(value):
        bit = 1
        while bit < ctxs:
            low = value.astype(BF16)
            value = low.astype(F32) + swap(low, "ctx", bit).astype(F32)
            bit *= 2
        return value

    def reduce_attention(grad):
        if shards != 2:
            return lax.psum(over_shard(grad), ("ctx", "tp"))
        mine, tp = lax.axis_index("shard"), lax.axis_index("tp")
        core, row = tp % 2, tp // 2
        quarter = grad.shape[0] // 4
        parts = grad.reshape(2, 2, quarter, -1)
        take = lambda c: lax.dynamic_index_in_dim(parts, c, 1, keepdims=False)
        held = take(core) + swap(take(1 - core).astype(BF16), "tp", 1).astype(F32)
        held = pick(held, mine) + swap(pick(held, 1 - mine).astype(BF16), "shard", 1).astype(F32)
        held = held.reshape(2, quarter // 2, -1)
        held = pick(held, row) + swap(pick(held, 1 - row).astype(BF16), "tp", 2).astype(F32)
        held = all_over_ctx(held).astype(BF16)
        held = in_order(row, held, swap(held, "tp", 2))
        return in_order(core, held, swap(held, "tp", 1)).astype(F32)

    def reduce_gains(grad):
        if shards != 2:
            return lax.psum(over_shard(grad), ("ctx", "tp"))
        for axis in ("tp", "shard", "ctx"):
            bit = 1
            while bit < mesh.shape[axis]:
                grad = grad + swap(grad, axis, bit)
                bit *= 2
        half = grad.shape[1] // 2
        return lax.dynamic_slice_in_dim(grad, lax.axis_index("shard") * half, half, axis=1)

    def per_device(
        tokens,
        cotangent,
        piece_starts,
        doc_lengths,
        attn_gain,
        w_query,
        w_key,
        w_value,
        w_out,
        ff_gain,
        w_gate,
        w_up,
        w_down,
    ):
        seqs, rows, width = tokens.shape
        offset = (lax.axis_index("ctx") * rows).astype(jnp.int32)
        mine, core = lax.axis_index("shard"), lax.axis_index("tp") % 2
        every = range(seqs)

        w_kv = jnp.concatenate([w_key, w_value], axis=1)
        gains = jnp.stack([attn_gain, ff_gain])
        ff_weights = (w_gate, w_up, w_down)
        if shards == 2:
            half = w_query.shape[0] // 2
            q_part, kv_part = fetch(w_query), fetch(w_kv)
            q_pieces = (w_query, q_part, swap(q_part, "tp", 1))
            kv_pieces = (w_kv, kv_part, swap(kv_part, "tp", 1))
            other = (1 - mine) * 2 * half
            places = jnp.stack([mine * 2 * half, other + core * half, other + (1 - core) * half])
            got = swap(gains, "shard", 1)
            gains = jnp.where(
                mine == 0,
                jnp.concatenate([gains, got], axis=1),
                jnp.concatenate([got, gains], axis=1),
            )
            out_part = fetch(after(w_out, q_part, kv_part))
            wo = in_order(mine, w_out, in_order(core, out_part, swap(out_part, "tp", 1)))
            ff_weights = [
                in_order(mine, w, swap(after(w, out_part), "shard", 1)) for w in ff_weights
            ]
        else:
            gather = lambda w, axis: lax.all_gather(w, "shard", axis=axis, tiled=True)
            q_pieces, kv_pieces = (gather(w_query, 0),), (gather(w_kv, 0),)
            places = jnp.zeros((1,), jnp.int32)
            gains, wo = gather(gains, 1), gather(w_out, 0)
            ff_weights = [gather(w, 0) for w in ff_weights]
        gain_one, gain_two = gains[:1].astype(F32), gains[1:].astype(F32)

        cot_y = swap(cotangent, "tp", 2)
        cots = (cotangent, swap(cotangent, "tp", 1), cot_y, swap(cot_y, "tp", 1))
        cosine, sine = rotary_tables(offset, rows)
        ends = jnp.cumsum(doc_lengths, axis=1)[:, :-1]
        scal = jnp.concatenate(
            [ends, piece_starts, jnp.broadcast_to(offset, (seqs, 1))], axis=1
        ).astype(jnp.int32)
        scals = [scal[s : s + 1] for s in every]

        normed_one, query, windows = [], [], []
        previous = ()
        for s in every:
            if s == 0:
                *made, wq, wkv = project_first(
                    tokens, s, gain_one, q_pieces, kv_pieces, places.astype(jnp.int32), cosine, sine
                )
            else:
                made = project(tokens, s, gain_one, wq, wkv, cosine, sine)
            normed_one.append(made[0])
            query.append(made[1])
            kv = made[2]
            near = shift(after(kv, *previous), 1)
            ahead = shift(after(kv[:, :GRAIN], *previous), -1)
            previous = (near, ahead)
            windows.append((shift(near, 1), near, kv, ahead))

        mixed, lse, hidden, normed_rows = [], [], [], []
        for s in every:
            m, l = attend(scals[s], query[s] if s == 0 else after(query[s], hidden[-1]), windows[s])
            h, own = residual(tokens, s, m, wo, gain_two)
            facing = swap(own, "tp", 2)
            normed_rows.append((own, swap(own, "tp", 1), facing, swap(facing, "tp", 1)))
            mixed.append(m)
            lse.append(l)
            hidden.append(h)

        kept = ()
        last = hidden[-1]
        grad_terms, out_pairs = [], []
        for s in every:
            own, beside, facing, diagonal = normed_rows[s]
            kept, near_out, near_grad = ff(
                (after(own, last), beside), cots[:2], ff_weights, s, 0, seqs, kept
            )
            kept, far_out, far_grad = ff(
                (after(facing, near_out[0]), diagonal), cots[2:], ff_weights, s, 2 * seqs, seqs, kept
            )
            last = far_out[0]

            def scatter(near, far):
                here, there = swap(near[1], "tp", 1), swap(far[1], "tp", 1)
                facing = (far[0].astype(F32) + there.astype(F32)).astype(BF16)
                return near[0], here, swap(facing, "tp", 2)

            grad_terms.append(scatter(near_grad, far_grad))
            out_pairs.append((near_out, far_out))
        inner_all, gate_all, up_all, rows_all = kept
        cot_all = jnp.concatenate([c.reshape(seqs * rows, width) for c in cots], axis=0)

        down_w = over_shard(tn(cot_all, after(inner_all, last)))
        gate_w = over_shard(tn(rows_all, after(gate_all, last)))
        up_w = over_shard(tn(rows_all, after(up_all, last)))
        sum_down = lax.psum(down_w.astype(BF16), "ctx")
        sum_gate = lax.psum(after(gate_w.astype(BF16), sum_down), "ctx")
        sum_up = lax.psum(after(up_w.astype(BF16), sum_gate), "ctx")

        branch, gain_two_grad, grad_hidden = [], 0.0, []
        backs = []
        order = up_w
        for s in every:
            gh, gb, gm, gg = ff_back(
                after(hidden[s], order), cotangent, s, grad_terms[s], gain_two, wo
            )
            grad_hidden.append(gh)
            branch.append(gb[0])
            gain_two_grad = gain_two_grad + gg[0]
            dq, dfar, dnear, down, dnext = attend_back(
                scals[s], query[s], windows[s], mixed[s], lse[s], gm
            )
            order = dq
            passed = shift(dfar, -1)
            left = shift(dnext, 1)
            right = shift((dnear.astype(F32) + passed.astype(F32)).astype(BF16), -1)
            backs.append((dq, down, left, right))
        stack = lambda blocks: jnp.concatenate(blocks, axis=0)
        out_grad = tn(stack([m[0] for m in mixed]), after(stack(branch), order))
        sum_out = reduce_attention(out_grad)
        gq = [query_back(after(backs[s][0], out_grad), cosine, sine) for s in every]
        one_all = stack([n[0] for n in normed_one])
        query_grad = tn(one_all, stack([g[0] for g in gq]))
        sum_query = reduce_attention(query_grad)

        outputs = []
        for s in every:
            near_out, far_out = out_pairs[s]
            terms = scatter(near_out, (far_out[0], after(far_out[1], *(t[2] for t in grad_terms))))
            outputs.append((hidden[s] + sum(t.astype(F32) for t in terms)).astype(BF16))

        kept, gain_one_grad, gkv = (), 0.0, []
        order = query_grad
        for s in every:
            _, down, left, right = backs[s]
            args = (grad_hidden[s], gq[s], down, left, right)
            args += (gain_one, wq, wkv, cosine, sine)
            input_grad, g, gg = input_back(tokens, s, (after(args[0], order), *args[1:]), kept)
            kept = (input_grad,)
            order = g
            gkv.append(g[0])
            gain_one_grad = gain_one_grad + gg[0]
        sum_kv = reduce_attention(tn(one_all, stack(gkv)))
        gain_grads = jnp.concatenate([gain_one_grad, gain_two_grad], axis=0)
        sum_gain = reduce_gains(gain_grads if shards == 2 else gain_grads.T)
        if shards != 2:
            sum_gain = sum_gain.T
        return (
            stack(outputs),
            input_grad,
            sum_gain[0],
            sum_query,
            sum_kv[:, :KW],
            sum_kv[:, KW:],
            sum_out,
            sum_gain[1],
            sum_gate.astype(F32),
            sum_up.astype(F32),
            sum_down.astype(F32),
        )

    return per_device


def solution(mesh):
    rows = P(("shard", "tp"), "ctx", None)
    seq = P(("shard", "tp"), None)
    gain, weight, ff_weight = P("shard"), P("shard", None), P("shard", "tp")
    weights = (gain, weight, weight, weight, weight, gain, ff_weight, ff_weight, ff_weight)
    return jax.shard_map(
        program(mesh),
        mesh=mesh,
        in_specs=(rows, rows, seq, seq, *weights),
        out_specs=(rows, rows, *weights),
        check_vma=False,
    )
```

time: 528 us -> 465 us (0.88)
  local copies, waits for them, and re-layouts: 74.7 us -> 33.1 us
  waiting for transfers between devices: 126 us -> 118 us
  starting transfers between devices: 95.9 us -> 88.5 us
  matrix products: 23.6 us -> 16.8 us
    unnamed x188 -> x118, local copies, waits for them, and re-layouts: 35.8 us -> 14.3 us
    psum x1 -> x3, waiting for transfers between devices: 0.01 us -> 19.4 us  [the longest x1 19.4 us: per_device(): sum_gate = lax.psum(after(gate_w.astype(BF16), sum_down), 'ctx')]
    ppermute x12, waiting for transfers between devices: 17.1 us -> 0.03 us  [shift(): return lax.ppermute(value, 'ctx', pairs)]
    slice x19 -> x4, local copies, waits for them, and re-layouts: 18.5 us -> 4.34 us  [the longest x2 3.22 us: per_device(): ahead = shift(after(kv[:, :GRAIN], *previous), -1)]
    ppermute x61 -> x60, waiting for transfers between devices: 109 us -> 98.6 us  [swap(): return lax.ppermute(value, axis, [(i, i ^ bit) for i in range(count)])]
    ppermute x61 -> x60, starting transfers between devices: 65 us -> 55.7 us  [swap(): return lax.ppermute(value, axis, [(i, i ^ bit) for i in range(count)])]
    dot_general x6, matrix products: 23.6 us -> 16.8 us  [dot(): lax.dot_general(left, right, (dims, ((), ())), preferred_element_type=F32)]
    concatenate x7 -> x1, local copies, waits for them, and re-layouts: 6.24 us -> 0.07 us  [per_device(): jnp.concatenate([ends, piece_starts, jnp.broadcast_to(offset, (seqs, 1))]...]
  transfers between devices with their start and end apart: 74 -> 75, of which waited for: 22 -> 18; matrix products, arithmetic and copies ran while one was open for 27% -> 21% of each run, Pallas kernels for 25% -> 29%
where the time goes in v2:
time: 465 us; the launch traced here: 457 us
  Pallas kernels  135 us (29%)
  waiting for transfers between devices  118 us (25%)
  starting transfers between devices  88.5 us (19%)
  other arithmetic  50.9 us (11%)
  local copies, waits for them, and re-layouts  33.1 us (7%)
  matrix products  16.8 us (4%)
  between operations  15 us (3%)
    pallas_call x18, Pallas kernels, call(): pl.pallas_call(kernel, out_shape=outs, grid=grid, in_specs=in_specs, out_...  135 us
    ppermute x60, waiting for transfers between devices, swap(): return lax.ppermute(value, axis, [(i, i ^ bit) for i in range(count)])  98.6 us
    ppermute x60, starting transfers between devices, swap(): return lax.ppermute(value, axis, [(i, i ^ bit) for i in range(count)])  55.7 us
    ppermute x12, starting transfers between devices, shift(): return lax.ppermute(value, 'ctx', pairs)  32.5 us
    psum x1, waiting for transfers between devices, per_device(): sum_gate = lax.psum(after(gate_w.astype(BF16), sum_down), 'ctx')  19.4 us
    dot_general x6, matrix products, dot(): lax.dot_general(left, right, (dims, ((), ())), preferred_element_type=F32)  16.8 us
    unnamed x118, local copies, waits for them, and re-layouts  14.3 us
    select_n x8, other arithmetic, in_order(): return jnp.where(index == 0, first, jnp.concatenate([other, own], axis=0))  14 us
  transfers between devices with their start and end apart: 75, of which 18 were waited for; matrix products, arithmetic and copies ran while one was open for 21% of the time, Pallas kernels for 29%

profile of v2, /device:TPU:1, one launch (start us, length us, event | category | flops | bytes accessed | tf_op | source)
XLA Modules:
  0.0 457.2 jit_solution(15295853796958076536)
XLA Ops:
  7.4 2.7 collective-permute-start.21
  20.5 2.3 copy.113.tok_ref
  22.7 10.0 %collective-permute-done.1.refs_1_ = bf16[240,960]{1,0:T(8,128)(2,1)} collective-permute-done((bf16[240,960]{1,0:T(8,128)(2,1)S(1)}, bf16[240,960]{1,0:T(8,128)(2,1)}, u32[]{:S(2)}, u32[]{:S(2)}) %collective-permute-start.1) | collective-permute-done | bytes 460832 | tf_op jit(solution)/shard_map/ppermute | solution.py:547
  36.9 4.7 %shard_map.212 = (bf16[1,256,960]{2,1,0:T(8,128)(2,1)}, bf16[1,256,960]{2,1,0:T(8,128)(2,1)}, bf16[1,256,640]{2,1,0:T(8,128)(2,1)}, bf16[960,960]{1,0:T(8,128)(2,1)}, bf16[960,640]{1,0:T(8,128)(2,1)}) custom-call(s32[3]{0:T(128)} %pad_add_fusion.place_ref, bf16[2,256,960]{2,1,0:T(8,128)(2,1)} %copy.113.tok_ref, f32[1,960]{1,0:T(1,128)} %get-tuple-element.254.gain_ref, ...), custom_call_target="tpu_custom_call" | custom-call | flops 78643200 | bytes 262144 | tf_op jit(solution)/shard_map/pallas_call | solution.py:48
  41.7 3.2 collective-permute-start.5
  49.1 4.6 %shard_map.215 = (bf16[1,256,960]{2,1,0:T(8,128)(2,1)}, bf16[1,256,960]{2,1,0:T(8,128)(2,1)}, bf16[1,256,640]{2,1,0:T(8,128)(2,1)}) custom-call(bf16[2,256,960]{2,1,0:T(8,128)(2,1)} %copy.113.tok_ref, f32[1,960]{1,0:T(1,128)} %get-tuple-element.254.gain_ref, bf16[960,960]{1,0:T(8,128)(2,1)} %get-tuple-element.114.wq_ref, ...), custom_call_target="tpu_custom_call" | custom-call | flops 78643200 | bytes 262144 | tf_op jit(solution)/shard_map/pallas_call | solution.py:48
  54.5 4.3 collective-permute-start.10
  63.1 4.0 collective-permute-start.6
  67.1 3.1 collective-permute-start.11
  73.7 2.2 maximum_select_fusion.wo_ref
  76.0 2.8 collective-permute-start.22
  78.8 12.7 %shard_map.213 = (bf16[1,256,960]{2,1,0:T(8,128)(2,1)}, f32[1,256,128]{2,1,0:T(8,128)}) custom-call(s32[1,5]{1,0:T(1,128)} %get-tuple-element.258.scal_ref, bf16[1,256,960]{2,1,0:T(8,128)(2,1)} %get-tuple-element.108.q_ref, bf16[1,256,640]{2,1,0:T(8,128)(2,1)} %copy-done.19, bf16[1,256,640]{2,1,0:T(8,128)(2,1)} %copy-done.17, ...), custom_call_target="tpu_custom_call" | custom-call | flops 301989888 | bytes 1006632 | tf_op jit(solution)/shard_map/pallas_call | solution.py:48
  91.5 3.7 shard_map.214
  96.0 12.1 %shard_map.216 = (bf16[1,256,960]{2,1,0:T(8,128)(2,1)}, f32[1,256,128]{2,1,0:T(8,128)}) custom-call(s32[1,5]{1,0:T(1,128)} %get-tuple-element.259.scal_ref, bf16[1,256,960]{2,1,0:T(8,128)(2,1)} %get-tuple-element.117.q_ref, bf16[1,256,640]{2,1,0:T(8,128)(2,1)} %copy-done.18, bf16[1,256,640]{2,1,0:T(8,128)(2,1)} %copy-done.16, ...), custom_call_target="tpu_custom_call" | custom-call | flops 301989888 | bytes 1006632 | tf_op jit(solution)/shard_map/pallas_call | solution.py:48
  108.1 3.8 shard_map.217
  120.8 4.2 collective-permute-done.25.nrm_a
  126.5 3.1 maximum_select_fusion.1.wg_ref
  129.6 2.7 maximum_select_fusion.2.wu_ref
  132.3 2.7 maximum_select_fusion.3.wd_ref
  136.3 2.3 copy.119.cot_b
  138.5 10.3 %shard_map.218 = (bf16[2048,640]{1,0:T(8,128)(2,1)}, bf16[2048,640]{1,0:T(8,128)(2,1)}, bf16[2048,640]{1,0:T(8,128)(2,1)}, bf16[2048,960]{1,0:T(8,128)(2,1)}, bf...) custom-call(bf16[1,256,960]{2,1,0:T(8,128)(2,1)} %get-tuple-element., ...), custom_call_target="tpu_custom_call" | custom-call | flops 377487360 | bytes 1258291 | tf_op jit(solution)/shard_map/pallas_call | solution.py:48
  148.9 10.2 %shard_map.219 = (bf16[2048,640]{1,0:T(8,128)(2,1)}, bf16[2048,640]{1,0:T(8,128)(2,1)}, bf16[2048,640]{1,0:T(8,128)(2,1)}, bf16[2048,960]{1,0:T(8,128)(2,1)}, bf...) custom-call(bf16[1,256,960]{2,1,0:T(8,128)(2,1)} %collective-permute, ...), custom_call_target="tpu_custom_call", output_to_operand_aliasing={{0}: (7, {}), {1}: (8, {}), {2}: (9, {}), {3}: (10, {})} | custom-call | flops 377487360 | bytes 1258291 | tf_op jit(solution)/shard_map/pallas_call | solution.py:48
  159.2 10.3 %shard_map.220 = (bf16[2048,640]{1,0:T(8,128)(2,1)}, bf16[2048,640]{1,0:T(8,128)(2,1)}, bf16[2048,640]{1,0:T(8,128)(2,1)}, bf16[2048,960]{1,0:T(8,128)(2,1)}, bf...) custom-call(bf16[1,256,960]{2,1,0:T(8,128)(2,1)} %get-tuple-element., ...), custom_call_target="tpu_custom_call", output_to_operand_aliasing={{0}: (7, {}), {1}: (8, {}), {2}: (9, {}), {3}: (10, {})} | custom-call | flops 377487360 | bytes 1258291 | tf_op jit(solution)/shard_map/pallas_call | solution.py:48
  170.1 10.6 %shard_map.221 = (bf16[2048,640]{1,0:T(8,128)(2,1)}, bf16[2048,640]{1,0:T(8,128)(2,1)}, bf16[2048,640]{1,0:T(8,128)(2,1)}, bf16[2048,960]{1,0:T(8,128)(2,1)}, bf...) custom-call(bf16[1,256,960]{2,1,0:T(8,128)(2,1)} %copy-done.29, ...), custom_call_target="tpu_custom_call", output_to_operand_aliasing={{0}: (7, {}), {1}: (8, {}), {2}: (9, {}), {3}: (10, {})} | custom-call | flops 377487360 | bytes 1258291 | tf_op jit(solution)/shard_map/pallas_call | solution.py:48
  180.7 5.1 %fusion = f32[960,640]{1,0:T(8,128)S(1)} fusion(bf16[2048,640]{1,0:T(8,128)(2,1)} %get-tuple-element.202, bf16[512,960]{0,1:T(8,128)(2,1)S(1)} %bitcast.142, bf16[512,960]{0,1:T(8,128)(2,1)S(1)} %bitcast.140, bf16[512,960]{0,1:T(8,128)(2,1)S(1)} %bitcast.141, bf16[512,960]{0,1:T(8,128)(2,1)S(1)} %bitcast.139), kind=kOutput, calls=%fused_computation | convolution fusion | flops 2532311040 | bytes 9011200 | tf_op jit(solution)/shard_map/dot_general | solution.py:32
  186.3 3.4 fusion.52
  189.7 3.4 fusion.51
  198.4 2.6 collective-permute-done.71
  202.8 11.4 %collective-permute-done.35 = bf16[480,640]{1,0:T(8,128)(2,1)} collective-permute-done((bf16[480,640]{1,0:T(8,128)(2,1)}, bf16[480,640]{1,0:T(8,128)(2,1)}, u32[]{:S(2)}, u32[]{:S(2)}) %collective-permute-start.35) | collective-permute-done | bytes 614432 | tf_op jit(solution)/shard_map/ppermute | solution.py:547
  215.0 2.4 bitcast_add_fusion.5
  217.5 10.0 %collective-permute-done.70 = bf16[480,640]{1,0:T(8,128)(2,1)} collective-permute-done((bf16[480,640]{1,0:T(8,128)(2,1)S(1)}, bf16[480,640]{1,0:T(8,128)(2,1)}, u32[]{:S(2)}, u32[]{:S(2)}) %collective-permute-start.70) | collective-permute-done | bytes 614432 | tf_op jit(solution)/shard_map/ppermute | solution.py:547
  228.7 2.0 fusion.9
  230.7 4.7 %shard_map.222 = (f32[1,256,960]{2,1,0:T(8,128)}, bf16[1,256,960]{2,1,0:T(8,128)(2,1)}, bf16[1,256,960]{2,1,0:T(8,128)(2,1)}, f32[1,1,960]{2,1,0:T(1,128)}) custom-call(f32[1,256,960]{2,1,0:T(8,128)} %get-tuple-element.161.hidden_ref, bf16[2,256,960]{2,1,0:T(8,128)(2,1)} %copy.116.cot_a.cot_ref, bf16[1,256,960]{2,1,0:T(8,128)(2,1)} %get-tuple-element.162.a_ref, ...), custom_call_target="tpu_custom_call" | custom-call | flops 47185920 | bytes 157286 | tf_op jit(solution)/shard_map/pallas_call | solution.py:48
  235.4 13.1 %shard_map.223 = (f32[1,256,960]{2,1,0:T(8,128)}, bf16[1,256,640]{2,1,0:T(8,128)(2,1)}, bf16[1,256,640]{2,1,0:T(8,128)(2,1)}, f32[1,256,640]{2,1,0:T(8,128)}, bf16[1,128,640]{2,1,0:T(8,128)(2,1)}) custom-call(s32[1,5]{1,0:T(1,128)} %get-tuple-element.258.scal_ref, bf16[1,256,960]{2,1,0:T(8,128)(2,1)} %get-tuple-element.108.q_ref, ...), custom_call_target="tpu_custom_call" | custom-call | flops 754974720 | bytes 2516582 | tf_op jit(solution)/shard_map/pallas_call | solution.py:48
  249.8 4.7 %collective-permute-start.38 = (bf16[1,128,640]{2,1,0:T(8,128)(2,1)}, bf16[1,128,640]{2,1,0:T(8,128)(2,1)}, u32[]{:S(2)}, u32[]{:S(2)}) collective-permute-start(bf16[1,128,640]{2,1,0:T(8,128)(2,1)} %get-tuple-element.183), channel_id=1, source_target_pairs={{0,4},{4,8},{8,12},{1,5},{5,9},{9,13},{2,6},{6,10},{10,14},{3,7},{... | collective-permute-start | bytes 491528 | tf_op jit(solution)/shard_map/ppermute | solution.py:551
  254.4 4.7 %shard_map.224 = (f32[1,256,960]{2,1,0:T(8,128)}, bf16[1,256,960]{2,1,0:T(8,128)(2,1)}, bf16[1,256,960]{2,1,0:T(8,128)(2,1)}, f32[1,1,960]{2,1,0:T(1,128)}) custom-call(f32[1,256,960]{2,1,0:T(8,128)} %get-tuple-element.166.hidden_ref, bf16[2,256,960]{2,1,0:T(8,128)(2,1)} %copy.116.cot_a.cot_ref, bf16[1,256,960]{2,1,0:T(8,128)(2,1)} %get-tuple-element.167.a_ref, ...), custom_call_target="tpu_custom_call" | custom-call | flops 47185920 | bytes 157286 | tf_op jit(solution)/shard_map/pallas_call | solution.py:48
  260.4 12.7 %shard_map.225 = (f32[1,256,960]{2,1,0:T(8,128)}, bf16[1,256,640]{2,1,0:T(8,128)(2,1)}, bf16[1,256,640]{2,1,0:T(8,128)(2,1)}, f32[1,256,640]{2,1,0:T(8,128)}, bf16[1,128,640]{2,1,0:T(8,128)(2,1)}) custom-call(s32[1,5]{1,0:T(1,128)} %get-tuple-element.259.scal_ref, bf16[1,256,960]{2,1,0:T(8,128)(2,1)} %get-tuple-element.117.q_ref, ...), custom_call_target="tpu_custom_call" | custom-call | flops 754974720 | bytes 2516582 | tf_op jit(solution)/shard_map/pallas_call | solution.py:48
  277.9 5.3 %collective-permute-start.41 = (bf16[1,128,640]{2,1,0:T(8,128)(2,1)}, bf16[1,128,640]{2,1,0:T(8,128)(2,1)}, u32[]{:S(2)}, u32[]{:S(2)}) collective-permute-start(bf16[1,128,640]{2,1,0:T(8,128)(2,1)} %get-tuple-element.189), channel_id=1, source_target_pairs={{0,4},{4,8},{8,12},{1,5},{5,9},{9,13},{2,6},{6,10},{10,14},{3,7},{... | collective-permute-start | bytes 491528 | tf_op jit(solution)/shard_map/ppermute | solution.py:551
  283.2 2.8 shard_map.226.gq_ref
  286.0 2.8 shard_map.227.gq_ref
  290.9 2.7 fusion.14
  296.1 5.5 %shard_map.228 = (f32[2,256,960]{2,1,0:T(8,128)}, bf16[1,256,640]{2,1,0:T(8,128)(2,1)}, f32[1,1,960]{2,1,0:T(1,128)}) custom-call(bf16[2,256,960]{2,1,0:T(8,128)(2,1)} %copy.113.tok_ref, f32[1,256,960]{2,1,0:T(8,128)} %get-tuple-element.181.gh_ref, bf16[1,256,960]{2,1,0:T(8,128)(2,1)} %shard_map.226.gq_ref, f32[1,256,640]{2,1,0:T(8,128)} %get-tuple-element.182.own_ref, ...), custom_call_target="tpu_custom_call" | custom-call | flops 78643200 | bytes 262144 | tf_op jit(solution)/shard_map/pallas_call | solution.py:48
  302.9 5.5 %shard_map.229 = (f32[2,256,960]{2,1,0:T(8,128)}, bf16[1,256,640]{2,1,0:T(8,128)(2,1)}, f32[1,1,960]{2,1,0:T(1,128)}) custom-call(bf16[2,256,960]{2,1,0:T(8,128)(2,1)} %copy.113.tok_ref, f32[1,256,960]{2,1,0:T(8,128)} %get-tuple-element.187.gh_ref, bf16[1,256,960]{2,1,0:T(8,128)(2,1)} %shard_map.227.gq_ref, ...), custom_call_target="tpu_custom_call", output_to_operand_aliasing={{0}: (11, {})} | custom-call | flops 78643200 | bytes 262144 | tf_op jit(solution)/shard_map/pallas_call | solution.py:48
  310.7 2.3 convert_element_type.391
  314.4 2.0 add_convert_fusion.3
  320.3 2.4 collective-permute-start.47
  324.2 2.4 collective-permute-start.48
  330.8 19.4 %all-reduce.6.cloned.1.call-done = bf16[480,640]{1,0:T(8,128)(2,1)} async-done(((bf16[480,640]{1,0:T(8,128)(2,1)}), bf16[480,640]{1,0:T(8,128)(2,1)}) %all-reduce.6.cloned.1.call-update) | async-done | bytes 614416 | tf_op jit(solution)/shard_map/psum | solution.py:720
  350.2 2.2 convert_element_type.388
  353.7 2.2 bitcast_add_fusion
  360.7 4.4 collective-permute-done.34
  368.0 2.8 collective-permute-done.64
  371.5 9.8 %collective-permute-done.50 = bf16[240,960]{1,0:T(8,128)(2,1)S(1)} collective-permute-done((bf16[240,960]{1,0:T(8,128)(2,1)S(1)}, bf16[240,960]{1,0:T(8,128)(2,1)S(1)}, u32[]{:S(2)}, u32[]{:S(2)}) %collective-permute-start.50) | collective-permute-done | bytes 460832 | tf_op jit(solution)/shard_map/ppermute | solution.py:547
  381.9 5.8 %collective-permute-done.57 = bf16[240,640]{1,0:T(8,128)(2,1)S(1)} collective-permute-done((bf16[240,640]{1,0:T(8,128)(2,1)S(1)}, bf16[240,640]{1,0:T(8,128)(2,1)S(1)}, u32[]{:S(2)}, u32[]{:S(2)}) %collective-permute-start.57) | collective-permute-done | bytes 307232 | tf_op jit(solution)/shard_map/ppermute | solution.py:547
  390.3 2.4 collective-permute-done.58
  394.2 2.1 collective-permute-done.66
  397.4 12.8 %collective-permute-done.59 = bf16[120,640]{1,0:T(8,128)(2,1)S(1)} collective-permute-done((bf16[120,640]{1,0:T(8,128)(2,1)S(1)}, bf16[120,640]{1,0:T(8,128)(2,1)S(1)}, u32[]{:S(2)}, u32[]{:S(2)}) %collective-permute-start.59) | collective-permute-done | bytes 153632 | tf_op jit(solution)/shard_map/ppermute | solution.py:547
  410.3 2.4 collective-permute-start.53
  412.7 11.8 %collective-permute-done.60 = bf16[120,640]{1,0:T(8,128)(2,1)S(1)} collective-permute-done((bf16[120,640]{1,0:T(8,128)(2,1)S(1)}, bf16[120,640]{1,0:T(8,128)(2,1)S(1)}, u32[]{:S(2)}, u32[]{:S(2)}) %collective-permute-start.60) | collective-permute-done | bytes 153632 | tf_op jit(solution)/shard_map/ppermute | solution.py:547
  424.5 1.9 collective-permute-start.61
  426.6 3.2 collective-permute-done.53
  434.0 2.2 convert_element_type.390
  437.6 3.2 collective-permute-done.54
  447.6 2.8 fusion.20
  (322 shorter events, 104.4 us)
Async XLA Ops:
  7.2 303.2 %all-reduce.4.cloned.1.call-start = ((), (), s32[]{:S(2)}) async-start(), calls=%async_computation | async-start | bytes 1228800 | tf_op jit(solution)/shard_map/psum | solution.py:719
  7.2 54.1 %collective-permute-start.14 = (bf16[2,256,960]{1,2,0:T(8,128)(2,1)}, bf16[2,256,960]{1,2,0:T(8,128)(2,1)S(1)}, u32[]{:S(2)}, u32[]{:S(2)}) collective-permute-start(bf16[2,256,960]{1,2,0:T(8,128)(2,1)} %param.14), channel_id=1, source_target_pairs={{0,1},{1,0},{2,3},{3,2},{4,5},{5,4},{6,7},{7,6},{8,9},{9,8},{10,11... | collective-permute-start | bytes 2949128 | tf_op jit(solution)/shard_map/ppermute | solution.py:547
  7.4 64.8 %collective-permute-start.21 = (bf16[2,256,960]{1,2,0:T(8,128)(2,1)}, bf16[2,256,960]{1,2,0:T(8,128)(2,1)S(1)}, u32[]{:S(2)}, u32[]{:S(2)}) collective-permute-start(bf16[2,256,960]{1,2,0:T(8,128)(2,1)} %param.14), channel_id=1, source_target_pairs={{0,2},{1,3},{2,0},{3,1},{4,6},{5,7},{6,4},{7,5},{8,10},{9,11},{10,... | collective-permute-start | bytes 2949128 | tf_op jit(solution)/shard_map/ppermute | solution.py:547
  13.4 20.7 %collective-permute-start.3 = (bf16[240,640]{1,0:T(8,128)(2,1)}, bf16[240,640]{1,0:T(8,128)(2,1)}, u32[]{:S(2)}, u32[]{:S(2)}) collective-permute-start(bf16[240,640]{1,0:T(8,128)(2,1)} %fusion.36), channel_id=1, source_target_pairs={{0,16},{16,0},{1,17},{17,1},{2,18},{18,2},{3,19},{19,3},{4,20},{20... | collective-permute-start | bytes 921608 | tf_op jit(solution)/shard_map/ppermute | solution.py:547
  15.6 17.1 %collective-permute-start.1 = (bf16[240,960]{1,0:T(8,128)(2,1)S(1)}, bf16[240,960]{1,0:T(8,128)(2,1)}, u32[]{:S(2)}, u32[]{:S(2)}) collective-permute-start(bf16[240,960]{1,0:T(8,128)(2,1)S(1)} %constant_dynamic-slice_fusion.3), channel_id=1, source_target_pairs={{0,16},{16,0},{1,17},{17,1},{2,18},{18,2},{3,19},{19,3},{4,20},{20... | collective-permute-start | bytes 1382408 | tf_op jit(solution)/shard_map/ppermute | solution.py:547
  16.0 17.9 %collective-permute-start = (bf16[2,480]{1,0:T(2,128)(2,1)S(1)}, bf16[2,480]{1,0:T(2,128)(2,1)S(1)}, u32[]{:S(2)}, u32[]{:S(2)}) collective-permute-start(bf16[2,480]{1,0:T(2,128)(2,1)S(1)} %pad_maximum_fusion.9), channel_id=1, source_target_pairs={{0,16},{16,0},{1,17},{17,1},{2,18},{18,2},{3,19},{19,3},{4,20},{20... | collective-permute-start | bytes 5768 | tf_op jit(solution)/shard_map/ppermute | solution.py:547
  34.2 13.6 %collective-permute-start.8 = (bf16[240,960]{1,0:T(8,128)(2,1)S(1)}, bf16[240,960]{1,0:T(8,128)(2,1)}, u32[]{:S(2)}, u32[]{:S(2)}) collective-permute-start(bf16[240,960]{1,0:T(8,128)(2,1)S(1)} %constant_dynamic-slice_fusion.1), channel_id=1, source_target_pairs={{0,16},{16,0},{1,17},{17,1},{2,18},{18,2},{3,19},{19,3},{4,20},{20... | collective-permute-start | bytes 1382408 | tf_op jit(solution)/shard_map/ppermute | solution.py:547
  41.7 12.1 %collective-permute-start.5 = (bf16[1,256,640]{2,1,0:T(8,128)(2,1)}, bf16[1,256,640]{2,1,0:T(8,128)(2,1)S(1)}, u32[]{:S(2)}, u32[]{:S(2)}) collective-permute-start(bf16[1,256,640]{2,1,0:T(8,128)(2,1)} %get-tuple-element.109.own_ref), channel_id=1, source_target_pairs={{0,4},{4,8},{8,12},{1,5},{5,9},{9,13},{2,6},{6,10},{10,14},{3,7},{... | collective-permute-start | bytes 983048 | tf_op jit(solution)/shard_map/ppermute | solution.py:551
  46.5 7.2 %collective-permute-start.7 = (bf16[1,128,640]{2,1,0:T(8,128)(2,1)}, bf16[1,128,640]{2,1,0:T(8,128)(2,1)S(1)}, u32[]{:S(2)}, u32[]{:S(2)}) collective-permute-start(bf16[1,128,640]{2,1,0:T(8,128)(2,1)} %slice.36), channel_id=1, source_target_pairs={{4,0},{8,4},{12,8},{5,1},{9,5},{13,9},{6,2},{10,6},{14,10},{7,3},{... | collective-permute-start | bytes 491528 | tf_op jit(solution)/shard_map/ppermute | solution.py:551
  47.8 15.3 %collective-permute-start.9 = (bf16[240,960]{1,0:T(8,128)(2,1)}, bf16[240,960]{1,0:T(8,128)(2,1)}, u32[]{:S(2)}, u32[]{:S(2)}) collective-permute-start(bf16[240,960]{1,0:T(8,128)(2,1)} %collective-permute-done.8), channel_id=1, source_target_pairs={{0,1},{1,0},{2,3},{3,2},{4,5},{5,4},{6,7},{7,6},{8,9},{9,8},{10,11... | collective-permute-start | bytes 1382408 | tf_op jit(solution)/shard_map/ppermute | solution.py:547
  54.5 12.6 %collective-permute-start.10 = (bf16[1,256,640]{2,1,0:T(8,128)(2,1)}, bf16[1,256,640]{2,1,0:T(8,128)(2,1)S(1)}, u32[]{:S(2)}, u32[]{:S(2)}) collective-permute-start(bf16[1,256,640]{2,1,0:T(8,128)(2,1)} %get-tuple-element.119.own_ref), channel_id=1, source_target_pairs={{0,4},{4,8},{8,12},{1,5},{5,9},{9,13},{2,6},{6,10},{10,14},{3,7},{... | collective-permute-start | bytes 983048 | tf_op jit(solution)/shard_map/ppermute | solution.py:551
  60.5 51.5 %collective-permute-start.15 = (bf16[480,640]{1,0:T(8,128)(2,1)}, bf16[480,640]{1,0:T(8,128)(2,1)}, u32[]{:S(2)}, u32[]{:S(2)}) collective-permute-start(bf16[480,640]{1,0:T(8,128)(2,1)} %param.23), channel_id=1, source_target_pairs={{0,16},{16,0},{1,17},{17,1},{2,18},{18,2},{3,19},{19,3},{4,20},{20... | collective-permute-start | bytes 1843208 | tf_op jit(solution)/shard_map/ppermute | solution.py:547
  61.3 11.6 %collective-permute-start.12 = (bf16[1,128,640]{2,1,0:T(8,128)(2,1)}, bf16[1,128,640]{2,1,0:T(8,128)(2,1)S(1)}, u32[]{:S(2)}, u32[]{:S(2)}) collective-permute-start(bf16[1,128,640]{2,1,0:T(8,128)(2,1)} %slice.39), channel_id=1, source_target_pairs={{4,0},{8,4},{12,8},{5,1},{9,5},{13,9},{6,2},{10,6},{14,10},{7,3},{... | collective-permute-start | bytes 491528 | tf_op jit(solution)/shard_map/ppermute | solution.py:551
  63.1 12.8 %collective-permute-start.6 = (bf16[1,256,640]{2,1,0:T(8,128)(2,1)}, bf16[1,256,640]{2,1,0:T(8,128)(2,1)S(1)}, u32[]{:S(2)}, u32[]{:S(2)}) collective-permute-start(bf16[1,256,640]{2,1,0:T(8,128)(2,1)} %copy-done.17), channel_id=1, source_target_pairs={{0,4},{4,8},{8,12},{1,5},{5,9},{9,13},{2,6},{6,10},{10,14},{3,7},{... | collective-permute-start | bytes 983048 | tf_op jit(solution)/shard_map/ppermute | solution.py:551
  67.1 28.1 %collective-permute-start.11 = (bf16[1,256,640]{2,1,0:T(8,128)(2,1)S(1)}, bf16[1,256,640]{2,1,0:T(8,128)(2,1)S(1)}, u32[]{:S(2)}, u32[]{:S(2)}) collective-permute-start(bf16[1,256,640]{2,1,0:T(8,128)(2,1)S(1)} %collective-permute-done.10.near_ref), channel_id=1, source_target_pairs={{0,4},{4,8},{8,12},{1,5},{5,9},{9,13},{2,6},{6,10},{10,14},{3,7},{... | collective-permute-start | bytes 983048 | tf_op jit(solution)/shard_map/ppermute | solution.py:551
  72.2 40.5 %collective-permute-start.16 = (bf16[480,640]{1,0:T(8,128)(2,1)}, bf16[480,640]{1,0:T(8,128)(2,1)}, u32[]{:S(2)}, u32[]{:S(2)}) collective-permute-start(bf16[480,640]{1,0:T(8,128)(2,1)} %param.24), channel_id=1, source_target_pairs={{0,16},{16,0},{1,17},{17,1},{2,18},{18,2},{3,19},{19,3},{4,20},{20... | collective-permute-start | bytes 1843208 | tf_op jit(solution)/shard_map/ppermute | solution.py:547
  72.9 47.4 %collective-permute-start.17 = (bf16[480,640]{1,0:T(8,128)(2,1)}, bf16[480,640]{1,0:T(8,128)(2,1)}, u32[]{:S(2)}, u32[]{:S(2)}) collective-permute-start(bf16[480,640]{1,0:T(8,128)(2,1)} %param.25), channel_id=1, source_target_pairs={{0,16},{16,0},{1,17},{17,1},{2,18},{18,2},{3,19},{19,3},{4,20},{20... | collective-permute-start | bytes 1843208 | tf_op jit(solution)/shard_map/ppermute | solution.py:547
  76.0 59.0 %collective-permute-start.22 = (bf16[2,256,960]{1,2,0:T(8,128)(2,1)S(1)}, bf16[2,256,960]{1,2,0:T(8,128)(2,1)}, u32[]{:S(2)}, u32[]{:S(2)}) collective-permute-start(bf16[2,256,960]{1,2,0:T(8,128)(2,1)S(1)} %collective-permute-done.21), channel_id=1, source_target_pairs={{0,1},{1,0},{2,3},{3,2},{4,5},{5,4},{6,7},{7,6},{8,9},{9,8},{10,11... | collective-permute-start | bytes 2949128 | tf_op jit(solution)/shard_map/ppermute | solution.py:547
  95.2 18.7 %collective-permute-start.19 = (bf16[1,256,960]{2,1,0:T(8,128)(2,1)}, bf16[1,256,960]{2,1,0:T(8,128)(2,1)}, u32[]{:S(2)}, u32[]{:S(2)}) collective-permute-start(bf16[1,256,960]{2,1,0:T(8,128)(2,1)} %get-tuple-element.123.nrm_a), channel_id=1, source_target_pairs={{0,2},{1,3},{2,0},{3,1},{4,6},{5,7},{6,4},{7,5},{8,10},{9,11},{10,... | collective-permute-start | bytes 1474568 | tf_op jit(solution)/shard_map/ppermute | solution.py:547
  111.9 13.0 %collective-permute-start.25 = (bf16[1,256,960]{2,1,0:T(8,128)(2,1)}, bf16[1,256,960]{2,1,0:T(8,128)(2,1)S(1)}, u32[]{:S(2)}, u32[]{:S(2)}) collective-permute-start(bf16[1,256,960]{2,1,0:T(8,128)(2,1)} %get-tuple-element.139.nrm_a), channel_id=1, source_target_pairs={{0,2},{1,3},{2,0},{3,1},{4,6},{5,7},{6,4},{7,5},{8,10},{9,11},{10,... | collective-permute-start | bytes 1474568 | tf_op jit(solution)/shard_map/ppermute | solution.py:547
  112.7 25.8 %collective-permute-start.13 = (bf16[1,256,960]{2,1,0:T(8,128)(2,1)}, bf16[1,256,960]{2,1,0:T(8,128)(2,1)}, u32[]{:S(2)}, u32[]{:S(2)}) collective-permute-start(bf16[1,256,960]{2,1,0:T(8,128)(2,1)} %get-tuple-element.123.nrm_a), channel_id=1, source_target_pairs={{0,1},{1,0},{2,3},{3,2},{4,5},{5,4},{6,7},{7,6},{8,9},{9,8},{10,11... | collective-permute-start | bytes 1474568 | tf_op jit(solution)/shard_map/ppermute | solution.py:547
  113.9 35.0 %collective-permute-start.20 = (bf16[1,256,960]{2,1,0:T(8,128)(2,1)}, bf16[1,256,960]{2,1,0:T(8,128)(2,1)}, u32[]{:S(2)}, u32[]{:S(2)}) collective-permute-start(bf16[1,256,960]{2,1,0:T(8,128)(2,1)} %collective-permute-done.19.nrm_a), channel_id=1, source_target_pairs={{0,1},{1,0},{2,3},{3,2},{4,5},{5,4},{6,7},{7,6},{8,9},{9,8},{10,11... | collective-permute-start | bytes 1474568 | tf_op jit(solution)/shard_map/ppermute | solution.py:547
  120.3 38.9 %collective-permute-start.26 = (bf16[1,256,960]{2,1,0:T(8,128)(2,1)}, bf16[1,256,960]{2,1,0:T(8,128)(2,1)}, u32[]{:S(2)}, u32[]{:S(2)}) collective-permute-start(bf16[1,256,960]{2,1,0:T(8,128)(2,1)} %get-tuple-element.139.nrm_a), channel_id=1, source_target_pairs={{0,1},{1,0},{2,3},{3,2},{4,5},{5,4},{6,7},{7,6},{8,9},{9,8},{10,11... | collective-permute-start | bytes 1474568 | tf_op jit(solution)/shard_map/ppermute | solution.py:547
  125.0 45.2 %collective-permute-start.27 = (bf16[1,256,960]{2,1,0:T(8,128)(2,1)S(1)}, bf16[1,256,960]{2,1,0:T(8,128)(2,1)}, u32[]{:S(2)}, u32[]{:S(2)}) collective-permute-start(bf16[1,256,960]{2,1,0:T(8,128)(2,1)S(1)} %collective-permute-done.25.nrm_a), channel_id=1, source_target_pairs={{0,1},{1,0},{2,3},{3,2},{4,5},{5,4},{6,7},{7,6},{8,9},{9,8},{10,11... | collective-permute-start | bytes 1474568 | tf_op jit(solution)/shard_map/ppermute | solution.py:547
  148.8 81.9 %collective-permute-start.36 = (bf16[1,256,960]{2,1,0:T(8,128)(2,1)}, bf16[1,256,960]{2,1,0:T(8,128)(2,1)}, u32[]{:S(2)}, u32[]{:S(2)}) collective-permute-start(bf16[1,256,960]{2,1,0:T(8,128)(2,1)} %get-tuple-element.163), channel_id=1, source_target_pairs={{0,1},{1,0},{2,3},{3,2},{4,5},{5,4},{6,7},{7,6},{8,9},{9,8},{10,11... | collective-permute-start | bytes 1474568 | tf_op jit(solution)/shard_map/ppermute | solution.py:547
  169.5 25.4 %collective-permute-start.23 = (bf16[1,256,960]{2,1,0:T(8,128)(2,1)S(1)}, bf16[1,256,960]{2,1,0:T(8,128)(2,1)S(1)}, u32[]{:S(2)}, u32[]{:S(2)}) collective-permute-start(bf16[1,256,960]{2,1,0:T(8,128)(2,1)S(1)} %copy-done.51), channel_id=1, source_target_pairs={{0,1},{1,0},{2,3},{3,2},{4,5},{5,4},{6,7},{7,6},{8,9},{9,8},{10,11... | collective-permute-start | bytes 1474568 | tf_op jit(solution)/shard_map/ppermute | solution.py:547
  170.0 84.4 %collective-permute-start.37 = (bf16[1,256,960]{2,1,0:T(8,128)(2,1)}, bf16[1,256,960]{2,1,0:T(8,128)(2,1)}, u32[]{:S(2)}, u32[]{:S(2)}) collective-permute-start(bf16[1,256,960]{2,1,0:T(8,128)(2,1)} %get-tuple-element.168), channel_id=1, source_target_pairs={{0,1},{1,0},{2,3},{3,2},{4,5},{5,4},{6,7},{7,6},{8,9},{9,8},{10,11... | collective-permute-start | bytes 1474568 | tf_op jit(solution)/shard_map/ppermute | solution.py:547
  185.9 15.1 %collective-permute-start.71 = (bf16[480,640]{1,0:T(8,128)(2,1)S(1)}, bf16[480,640]{1,0:T(8,128)(2,1)S(1)}, u32[]{:S(2)}, u32[]{:S(2)}) collective-permute-start(bf16[480,640]{1,0:T(8,128)(2,1)S(1)} %fusion.28), channel_id=1, source_target_pairs={{0,16},{16,0},{1,17},{17,1},{2,18},{18,2},{3,19},{19,3},{4,20},{20... | collective-permute-start | bytes 1843208 | tf_op jit(solution)/shard_map/ppermute | solution.py:547
  194.9 19.3 %collective-permute-start.35 = (bf16[480,640]{1,0:T(8,128)(2,1)}, bf16[480,640]{1,0:T(8,128)(2,1)}, u32[]{:S(2)}, u32[]{:S(2)}) collective-permute-start(bf16[480,640]{1,0:T(8,128)(2,1)} %fusion.26), channel_id=1, source_target_pairs={{0,16},{16,0},{1,17},{17,1},{2,18},{18,2},{3,19},{19,3},{4,20},{20... | collective-permute-start | bytes 1843208 | tf_op jit(solution)/shard_map/ppermute | solution.py:547
  197.1 30.3 %collective-permute-start.70 = (bf16[480,640]{1,0:T(8,128)(2,1)S(1)}, bf16[480,640]{1,0:T(8,128)(2,1)}, u32[]{:S(2)}, u32[]{:S(2)}) collective-permute-start(bf16[480,640]{1,0:T(8,128)(2,1)S(1)} %fusion.27), channel_id=1, source_target_pairs={{0,16},{16,0},{1,17},{17,1},{2,18},{18,2},{3,19},{19,3},{4,20},{20... | collective-permute-start | bytes 1843208 | tf_op jit(solution)/shard_map/ppermute | solution.py:547
  201.0 29.7 %collective-permute-start.24 = (bf16[1,256,960]{2,1,0:T(8,128)(2,1)}, bf16[1,256,960]{2,1,0:T(8,128)(2,1)}, u32[]{:S(2)}, u32[]{:S(2)}) collective-permute-start(bf16[1,256,960]{2,1,0:T(8,128)(2,1)} %add_convert_fusion.5), channel_id=1, source_target_pairs={{0,2},{1,3},{2,0},{3,1},{4,6},{5,7},{6,4},{7,5},{8,10},{9,11},{10,... | collective-permute-start | bytes 1474568 | tf_op jit(solution)/shard_map/ppermute | solution.py:547
  202.8 147.4 %all-reduce.6.cloned.1.call-start = ((), (), s32[]{:S(2)}) async-start(), calls=%async_computation.1 | async-start | bytes 1228800 | tf_op jit(solution)/shard_map/psum | solution.py:720
  214.2 40.2 %collective-permute-start.29 = (bf16[1,256,960]{2,1,0:T(8,128)(2,1)}, bf16[1,256,960]{2,1,0:T(8,128)(2,1)}, u32[]{:S(2)}, u32[]{:S(2)}) collective-permute-start(bf16[1,256,960]{2,1,0:T(8,128)(2,1)} %add_convert_fusion.4), channel_id=1, source_target_pairs={{0,2},{1,3},{2,0},{3,1},{4,6},{5,7},{6,4},{7,5},{8,10},{9,11},{10,... | collective-permute-start | bytes 1474568 | tf_op jit(solution)/shard_map/ppermute | solution.py:547
  227.4 130.3 %collective-permute-start.18 = (bf16[1,256,960]{2,1,0:T(8,128)(2,1)}, bf16[1,256,960]{2,1,0:T(8,128)(2,1)}, u32[]{:S(2)}, u32[]{:S(2)}) collective-permute-start(bf16[1,256,960]{2,1,0:T(8,128)(2,1)} %get-tuple-element.128), channel_id=1, source_target_pairs={{0,1},{1,0},{2,3},{3,2},{4,5},{5,4},{6,7},{7,6},{8,9},{9,8},{10,11... | collective-permute-start | bytes 1474568 | tf_op jit(solution)/shard_map/ppermute | solution.py:547
  248.5 27.3 %collective-permute-start.39 = (bf16[1,256,640]{2,1,0:T(8,128)(2,1)}, bf16[1,256,640]{2,1,0:T(8,128)(2,1)S(1)}, u32[]{:S(2)}, u32[]{:S(2)}) collective-permute-start(bf16[1,256,640]{2,1,0:T(8,128)(2,1)} %get-tuple-element.185), channel_id=1, source_target_pairs={{4,0},{8,4},{12,8},{5,1},{9,5},{13,9},{6,2},{10,6},{14,10},{7,3},{... | collective-permute-start | bytes 983048 | tf_op jit(solution)/shard_map/ppermute | solution.py:551
  249.8 45.2 %collective-permute-start.38 = (bf16[1,128,640]{2,1,0:T(8,128)(2,1)}, bf16[1,128,640]{2,1,0:T(8,128)(2,1)}, u32[]{:S(2)}, u32[]{:S(2)}) collective-permute-start(bf16[1,128,640]{2,1,0:T(8,128)(2,1)} %get-tuple-element.183), channel_id=1, source_target_pairs={{0,4},{4,8},{8,12},{1,5},{5,9},{9,13},{2,6},{6,10},{10,14},{3,7},{... | collective-permute-start | bytes 491528 | tf_op jit(solution)/shard_map/ppermute | solution.py:551
  273.0 15.8 %collective-permute-start.42 = (bf16[1,256,640]{2,1,0:T(8,128)(2,1)}, bf16[1,256,640]{2,1,0:T(8,128)(2,1)S(1)}, u32[]{:S(2)}, u32[]{:S(2)}) collective-permute-start(bf16[1,256,640]{2,1,0:T(8,128)(2,1)} %get-tuple-element.191), channel_id=1, source_target_pairs={{4,0},{8,4},{12,8},{5,1},{9,5},{13,9},{6,2},{10,6},{14,10},{7,3},{... | collective-permute-start | bytes 983048 | tf_op jit(solution)/shard_map/ppermute | solution.py:551
  276.6 19.4 %collective-permute-start.40 = (bf16[1,256,640]{2,1,0:T(8,128)(2,1)}, bf16[1,256,640]{2,1,0:T(8,128)(2,1)}, u32[]{:S(2)}, u32[]{:S(2)}) collective-permute-start(bf16[1,256,640]{2,1,0:T(8,128)(2,1)} %add_convert_fusion.7), channel_id=1, source_target_pairs={{4,0},{8,4},{12,8},{5,1},{9,5},{13,9},{6,2},{10,6},{14,10},{7,3},{... | collective-permute-start | bytes 983048 | tf_op jit(solution)/shard_map/ppermute | solution.py:551
  277.9 23.8 %collective-permute-start.41 = (bf16[1,128,640]{2,1,0:T(8,128)(2,1)}, bf16[1,128,640]{2,1,0:T(8,128)(2,1)}, u32[]{:S(2)}, u32[]{:S(2)}) collective-permute-start(bf16[1,128,640]{2,1,0:T(8,128)(2,1)} %get-tuple-element.189), channel_id=1, source_target_pairs={{0,4},{4,8},{8,12},{1,5},{5,9},{9,13},{2,6},{6,10},{10,14},{3,7},{... | collective-permute-start | bytes 491528 | tf_op jit(solution)/shard_map/ppermute | solution.py:551
  289.6 12.5 %collective-permute-start.43 = (bf16[1,256,640]{2,1,0:T(8,128)(2,1)}, bf16[1,256,640]{2,1,0:T(8,128)(2,1)S(1)}, u32[]{:S(2)}, u32[]{:S(2)}) collective-permute-start(bf16[1,256,640]{2,1,0:T(8,128)(2,1)} %add_convert_fusion.6), channel_id=1, source_target_pairs={{4,0},{8,4},{12,8},{5,1},{9,5},{13,9},{6,2},{10,6},{14,10},{7,3},{... | collective-permute-start | bytes 983048 | tf_op jit(solution)/shard_map/ppermute | solution.py:551
  294.9 65.7 %collective-permute-start.32 = (bf16[1,256,960]{2,1,0:T(8,128)(2,1)}, bf16[1,256,960]{2,1,0:T(8,128)(2,1)}, u32[]{:S(2)}, u32[]{:S(2)}) collective-permute-start(bf16[1,256,960]{2,1,0:T(8,128)(2,1)} %get-tuple-element.153), channel_id=1, source_target_pairs={{0,1},{1,0},{2,3},{3,2},{4,5},{5,4},{6,7},{7,6},{8,9},{9,8},{10,11... | collective-permute-start | bytes 1474568 | tf_op jit(solution)/shard_map/ppermute | solution.py:547
  296.1 56.3 %collective-permute-start.63 = (bf16[2,240,960]{2,1,0:T(8,128)(2,1)}, bf16[2,240,960]{2,1,0:T(8,128)(2,1)}, u32[]{:S(2)}, u32[]{:S(2)}) collective-permute-start(bf16[2,240,960]{2,1,0:T(8,128)(2,1)} %fusion.19), channel_id=1, source_target_pairs={{0,1},{1,0},{2,3},{3,2},{4,5},{5,4},{6,7},{7,6},{8,9},{9,8},{10,11... | collective-permute-start | bytes 2764808 | tf_op jit(solution)/shard_map/ppermute | solution.py:547
  301.7 11.8 %collective-permute-start.30 = (bf16[1,256,960]{2,1,0:T(8,128)(2,1)}, bf16[1,256,960]{2,1,0:T(8,128)(2,1)}, u32[]{:S(2)}, u32[]{:S(2)}) collective-permute-start(bf16[1,256,960]{2,1,0:T(8,128)(2,1)} %get-tuple-element.152), channel_id=1, source_target_pairs={{0,1},{1,0},{2,3},{3,2},{4,5},{5,4},{6,7},{7,6},{8,9},{9,8},{10,11... | collective-permute-start | bytes 1474568 | tf_op jit(solution)/shard_map/ppermute | solution.py:547
  310.4 123.7 %all-reduce.8.cloned.1.call-start = ((), (), s32[]{:S(2)}) async-start(), calls=%async_computation.2 | async-start | bytes 1228800 | tf_op jit(solution)/shard_map/psum | solution.py:721
  316.4 39.4 %collective-permute-start.49 = (bf16[2,240,960]{2,1,0:T(8,128)(2,1)}, bf16[2,240,960]{2,1,0:T(8,128)(2,1)S(1)}, u32[]{:S(2)}, u32[]{:S(2)}) collective-permute-start(bf16[2,240,960]{2,1,0:T(8,128)(2,1)} %fusion.18), channel_id=1, source_target_pairs={{0,1},{1,0},{2,3},{3,2},{4,5},{5,4},{6,7},{7,6},{8,9},{9,8},{10,11... | collective-permute-start | bytes 2764808 | tf_op jit(solution)/shard_map/ppermute | solution.py:547
  329.3 29.7 %collective-permute-start.31 = (bf16[1,256,960]{2,1,0:T(8,128)(2,1)}, bf16[1,256,960]{2,1,0:T(8,128)(2,1)S(1)}, u32[]{:S(2)}, u32[]{:S(2)}) collective-permute-start(bf16[1,256,960]{2,1,0:T(8,128)(2,1)} %add_convert_fusion.3), channel_id=1, source_target_pairs={{0,2},{1,3},{2,0},{3,1},{4,6},{5,7},{6,4},{7,5},{8,10},{9,11},{10,... | collective-permute-start | bytes 1474568 | tf_op jit(solution)/shard_map/ppermute | solution.py:547
  352.4 12.7 %collective-permute-start.34 = (bf16[1,256,960]{2,1,0:T(8,128)(2,1)S(1)}, bf16[1,256,960]{2,1,0:T(8,128)(2,1)S(1)}, u32[]{:S(2)}, u32[]{:S(2)}) collective-permute-start(bf16[1,256,960]{2,1,0:T(8,128)(2,1)S(1)} %copy-done.30), channel_id=1, source_target_pairs={{0,2},{1,3},{2,0},{3,1},{4,6},{5,7},{6,4},{7,5},{8,10},{9,11},{10,... | collective-permute-start | bytes 1474568 | tf_op jit(solution)/shard_map/ppermute | solution.py:547
  355.9 10.6 %collective-permute-start.56 = (bf16[2,240,640]{2,1,0:T(8,128)(2,1)S(1)}, bf16[2,240,640]{2,1,0:T(8,128)(2,1)S(1)}, u32[]{:S(2)}, u32[]{:S(2)}) collective-permute-start(bf16[2,240,640]{2,1,0:T(8,128)(2,1)S(1)} %copy-done.26), channel_id=1, source_target_pairs={{0,1},{1,0},{2,3},{3,2},{4,5},{5,4},{6,7},{7,6},{8,9},{9,8},{10,11... | collective-permute-start | bytes 1843208 | tf_op jit(solution)/shard_map/ppermute | solution.py:547
  357.7 13.0 %collective-permute-start.64 = (bf16[240,960]{1,0:T(8,128)(2,1)S(1)}, bf16[240,960]{1,0:T(8,128)(2,1)S(1)}, u32[]{:S(2)}, u32[]{:S(2)}) collective-permute-start(bf16[240,960]{1,0:T(8,128)(2,1)S(1)} %fusion.32), channel_id=1, source_target_pairs={{0,16},{16,0},{1,17},{17,1},{2,18},{18,2},{3,19},{19,3},{4,20},{20... | collective-permute-start | bytes 1382408 | tf_op jit(solution)/shard_map/ppermute | solution.py:547
  359.0 22.3 %collective-permute-start.50 = (bf16[240,960]{1,0:T(8,128)(2,1)S(1)}, bf16[240,960]{1,0:T(8,128)(2,1)S(1)}, u32[]{:S(2)}, u32[]{:S(2)}) collective-permute-start(bf16[240,960]{1,0:T(8,128)(2,1)S(1)} %fusion.31), channel_id=1, source_target_pairs={{0,16},{16,0},{1,17},{17,1},{2,18},{18,2},{3,19},{19,3},{4,20},{20... | collective-permute-start | bytes 1382408 | tf_op jit(solution)/shard_map/ppermute | solution.py:547
  366.7 21.0 %collective-permute-start.57 = (bf16[240,640]{1,0:T(8,128)(2,1)S(1)}, bf16[240,640]{1,0:T(8,128)(2,1)S(1)}, u32[]{:S(2)}, u32[]{:S(2)}) collective-permute-start(bf16[240,640]{1,0:T(8,128)(2,1)S(1)} %fusion.35), channel_id=1, source_target_pairs={{0,16},{16,0},{1,17},{17,1},{2,18},{18,2},{3,19},{19,3},{4,20},{20... | collective-permute-start | bytes 921608 | tf_op jit(solution)/shard_map/ppermute | solution.py:547
  370.9 17.6 %collective-permute-start.65 = (bf16[120,960]{1,0:T(8,128)(2,1)S(1)}, bf16[120,960]{1,0:T(8,128)(2,1)S(1)}, u32[]{:S(2)}, u32[]{:S(2)}) collective-permute-start(bf16[120,960]{1,0:T(8,128)(2,1)S(1)} %fusion.39), channel_id=1, source_target_pairs={{0,2},{1,3},{2,0},{3,1},{4,6},{5,7},{6,4},{7,5},{8,10},{9,11},{10,... | collective-permute-start | bytes 691208 | tf_op jit(solution)/shard_map/ppermute | solution.py:547
  381.4 8.3 %collective-permute-start.51 = (bf16[120,960]{1,0:T(8,128)(2,1)S(1)}, bf16[120,960]{1,0:T(8,128)(2,1)S(1)}, u32[]{:S(2)}, u32[]{:S(2)}) collective-permute-start(bf16[120,960]{1,0:T(8,128)(2,1)S(1)} %fusion.38), channel_id=1, source_target_pairs={{0,2},{1,3},{2,0},{3,1},{4,6},{5,7},{6,4},{7,5},{8,10},{9,11},{10,... | collective-permute-start | bytes 691208 | tf_op jit(solution)/shard_map/ppermute | solution.py:547
  388.6 7.7 %collective-permute-start.66 = (bf16[120,960]{1,0:T(8,128)(2,1)S(1)}, bf16[120,960]{1,0:T(8,128)(2,1)S(1)}, u32[]{:S(2)}, u32[]{:S(2)}) collective-permute-start(bf16[120,960]{1,0:T(8,128)(2,1)S(1)} %fusion.33), channel_id=1, source_target_pairs={{0,4},{4,0},{8,12},{12,8},{1,5},{5,1},{9,13},{13,9},{2,6},{6,2},{1... | collective-permute-start | bytes 691208 | tf_op jit(solution)/shard_map/ppermute | solution.py:547
  389.8 20.5 %collective-permute-start.52 = (bf16[120,960]{1,0:T(8,128)(2,1)S(1)}, bf16[120,960]{1,0:T(8,128)(2,1)S(1)}, u32[]{:S(2)}, u32[]{:S(2)}) collective-permute-start(bf16[120,960]{1,0:T(8,128)(2,1)S(1)} %fusion.34), channel_id=1, source_target_pairs={{0,4},{4,0},{8,12},{12,8},{1,5},{5,1},{9,13},{13,9},{2,6},{6,2},{1... | collective-permute-start | bytes 691208 | tf_op jit(solution)/shard_map/ppermute | solution.py:547
  392.7 17.4 %collective-permute-start.59 = (bf16[120,640]{1,0:T(8,128)(2,1)S(1)}, bf16[120,640]{1,0:T(8,128)(2,1)S(1)}, u32[]{:S(2)}, u32[]{:S(2)}) collective-permute-start(bf16[120,640]{1,0:T(8,128)(2,1)S(1)} %fusion.37), channel_id=1, source_target_pairs={{0,4},{4,0},{8,12},{12,8},{1,5},{5,1},{9,13},{13,9},{2,6},{6,2},{1... | collective-permute-start | bytes 460808 | tf_op jit(solution)/shard_map/ppermute | solution.py:547
  396.3 30.1 %collective-permute-start.67 = (bf16[120,960]{1,0:T(8,128)(2,1)S(1)}, bf16[120,960]{1,0:T(8,128)(2,1)S(1)}, u32[]{:S(2)}, u32[]{:S(2)}) collective-permute-start(bf16[120,960]{1,0:T(8,128)(2,1)S(1)} %add_convert_fusion.9), channel_id=1, source_target_pairs={{0,8},{4,12},{8,0},{12,4},{1,9},{5,13},{9,1},{13,5},{2,10},{6,14},... | collective-permute-start | bytes 691208 | tf_op jit(solution)/shard_map/ppermute | solution.py:547
  410.2 14.3 %collective-permute-start.60 = (bf16[120,640]{1,0:T(8,128)(2,1)S(1)}, bf16[120,640]{1,0:T(8,128)(2,1)S(1)}, u32[]{:S(2)}, u32[]{:S(2)}) collective-permute-start(bf16[120,640]{1,0:T(8,128)(2,1)S(1)} %add_convert_fusion.13), channel_id=1, source_target_pairs={{0,8},{4,12},{8,0},{12,4},{1,9},{5,13},{9,1},{13,5},{2,10},{6,14},... | collective-permute-start | bytes 460808 | tf_op jit(solution)/shard_map/ppermute | solution.py:547
  410.3 19.4 %collective-permute-start.53 = (bf16[120,960]{1,0:T(8,128)(2,1)S(1)}, bf16[120,960]{1,0:T(8,128)(2,1)S(1)}, u32[]{:S(2)}, u32[]{:S(2)}) collective-permute-start(bf16[120,960]{1,0:T(8,128)(2,1)S(1)} %add_convert_fusion.11), channel_id=1, source_target_pairs={{0,8},{4,12},{8,0},{12,4},{1,9},{5,13},{9,1},{13,5},{2,10},{6,14},... | collective-permute-start | bytes 691208 | tf_op jit(solution)/shard_map/ppermute | solution.py:547
  424.5 7.2 %collective-permute-start.61 = (bf16[120,640]{1,0:T(8,128)(2,1)S(1)}, bf16[120,640]{1,0:T(8,128)(2,1)S(1)}, u32[]{:S(2)}, u32[]{:S(2)}) collective-permute-start(bf16[120,640]{1,0:T(8,128)(2,1)S(1)} %add_convert_fusion.12), channel_id=1, source_target_pairs={{0,2},{1,3},{2,0},{3,1},{4,6},{5,7},{6,4},{7,5},{8,10},{9,11},{10,... | collective-permute-start | bytes 460808 | tf_op jit(solution)/shard_map/ppermute | solution.py:547
  426.5 9.7 %collective-permute-start.68 = (bf16[120,960]{1,0:T(8,128)(2,1)S(1)}, bf16[120,960]{1,0:T(8,128)(2,1)S(1)}, u32[]{:S(2)}, u32[]{:S(2)}) collective-permute-start(bf16[120,960]{1,0:T(8,128)(2,1)S(1)} %add_convert_fusion.8), channel_id=1, source_target_pairs={{0,2},{1,3},{2,0},{3,1},{4,6},{5,7},{6,4},{7,5},{8,10},{9,11},{10,... | collective-permute-start | bytes 691208 | tf_op jit(solution)/shard_map/ppermute | solution.py:547
  429.8 11.0 %collective-permute-start.54 = (bf16[120,960]{1,0:T(8,128)(2,1)S(1)}, bf16[120,960]{1,0:T(8,128)(2,1)}, u32[]{:S(2)}, u32[]{:S(2)}) collective-permute-start(bf16[120,960]{1,0:T(8,128)(2,1)S(1)} %add_convert_fusion.10), channel_id=1, source_target_pairs={{0,2},{1,3},{2,0},{3,1},{4,6},{5,7},{6,4},{7,5},{8,10},{9,11},{10,... | collective-permute-start | bytes 691208 | tf_op jit(solution)/shard_map/ppermute | solution.py:547
  431.8 11.5 %collective-permute-start.62 = (bf16[240,640]{1,0:T(8,128)(2,1)S(1)}, bf16[240,640]{1,0:T(8,128)(2,1)S(1)}, u32[]{:S(2)}, u32[]{:S(2)}) collective-permute-start(bf16[240,640]{1,0:T(8,128)(2,1)S(1)} %maximum_select_fusion.10), channel_id=1, source_target_pairs={{0,1},{1,0},{2,3},{3,2},{4,5},{5,4},{6,7},{7,6},{8,9},{9,8},{10,11... | collective-permute-start | bytes 921608 | tf_op jit(solution)/shard_map/ppermute | solution.py:547
  436.3 9.6 %collective-permute-start.69 = (bf16[240,960]{1,0:T(8,128)(2,1)S(1)}, bf16[240,960]{1,0:T(8,128)(2,1)S(1)}, u32[]{:S(2)}, u32[]{:S(2)}) collective-permute-start(bf16[240,960]{1,0:T(8,128)(2,1)S(1)} %maximum_select_fusion.9), channel_id=1, source_target_pairs={{0,1},{1,0},{2,3},{3,2},{4,5},{5,4},{6,7},{7,6},{8,9},{9,8},{10,11... | collective-permute-start | bytes 1382408 | tf_op jit(solution)/shard_map/ppermute | solution.py:547
  (66 other events, 477.7 us)
Sparse Core Ops, SparseCore 0:
  202.9 39.9 all-reduce.3
  310.5 39.6 all-reduce.5
  352.5 39.2 all-reduce.7

commit v3 on v2

v3 whole, which is shorter than its diff:
```python
import functools
import math

import jax
import jax.numpy as jnp
from jax import lax
from jax.experimental import pallas as pl
from jax.experimental.pallas import tpu as pltpu
from jax.sharding import PartitionSpec as P

H = 15
KVH = 5
HD = 64
LEN = 1024
PIECE = 256
GRAIN = 128
MAXDOC = 512
GROUP = H // KVH
KW = KVH * HD
QW = H * HD
SPAN = MAXDOC + 2 * GRAIN

EPS = 1e-05
NEG = -1e30
F32 = jnp.float32
BF16 = jnp.bfloat16
VMEM_LIMIT = 20 * 1024 * 1024
COST = 0.1


def dot(left, right, dims):
    return lax.dot_general(left, right, (dims, ((), ())), preferred_element_type=F32)


def nn(left, right):
    return dot(left, right, ((1,), (0,)))


def nt(left, right):
    return dot(left, right, ((1,), (1,)))


def tn(left, right):
    return dot(left, right, ((0,), (0,)))


def call(kernel, outs, args, in_specs, out_specs, *, grid=(1,), scratch=(), flops=0):
    return pl.pallas_call(
        kernel,
        out_shape=outs,
        grid=grid,
        in_specs=in_specs,
        out_specs=out_specs,
        scratch_shapes=list(scratch),
        compiler_params=pltpu.CompilerParams(vmem_limit_bytes=VMEM_LIMIT),
        cost_estimate=pl.CostEstimate(
            flops=int(flops * COST), bytes_accessed=int(flops * COST / 300), transcendentals=0
        ),
    )(*args)


def part(array, seq):
    index = seq if array.shape[0] > 1 else 0
    return pl.BlockSpec((1, *array.shape[1:]), lambda *_: (index,) + (0,) * (len(array.shape) - 1))


def sub_part(array):
    return pl.BlockSpec((1, GRAIN, array.shape[2]), lambda i: (0, i, 0))


def whole(array):
    return pl.BlockSpec(array.shape, lambda *_: (0,) * len(array.shape))


def smem():
    return pl.BlockSpec(memory_space=pltpu.SMEM)


def struct(shape, dtype):
    return jax.ShapeDtypeStruct(shape, dtype)


def after(value, *deps):
    return lax.optimization_barrier((value, deps))[0] if deps else value


class Chain:
    def __init__(self, steps):
        self.steps, self.result = steps, None
        self.step(None)

    def step(self, deps=()):
        if self.result is None:
            try:
                self.got = self.steps.send(deps)
            except StopIteration as stop:
                self.got = self.result = stop.value

    def finish(self):
        while self.result is None:
            self.step()
        return self.result


def rotary_tables(offset, length):
    half = HD // 2
    place = (offset + jnp.arange(length, dtype=jnp.int32)).astype(F32)
    freq = jnp.exp(jnp.arange(half).astype(F32) * (-2.0 * math.log(10000.0) / HD))
    angle = place[:, None] * freq[None, :]
    cosine, sine = jnp.cos(angle), jnp.sin(angle)
    return (
        jnp.concatenate([cosine] * 4, axis=1),
        jnp.concatenate([-sine, sine, -sine, sine], axis=1),
    )


def rotate(tile, cosine, sine):
    lane = lax.broadcasted_iota(jnp.int32, tile.shape, 1)
    partner = jnp.where(lane % HD < HD // 2, pltpu.roll(tile, 96, 1), pltpu.roll(tile, 32, 1))
    return tile * cosine + partner * sine


def rotate_into(out_ref, value_ref, width, cosine, sine, factor):
    for start in range(0, width, 128):
        stop = min(start + 128, width)
        turned = rotate(value_ref[:, start : start + 128], cosine, sine) * factor
        out_ref[0, :, start:stop] = turned[:, : stop - start].astype(out_ref.dtype)


def inverse_mean(value):
    return lax.rsqrt(jnp.mean(value * value, axis=-1, keepdims=True) + EPS)


def wide(width):
    return -(-width // 128) * 128


def prepare_kernel(*refs):
    count = len(refs) // 2
    for source, out in zip(refs[:count], refs[count:]):
        out[0] = source[0].T


def prepare(*arrays):
    seqs, width, rows = arrays[0].shape
    block = lambda *shape: pl.BlockSpec((1, *shape), lambda s: (s, 0, 0))
    return call(
        prepare_kernel,
        [struct((seqs, rows, width), a.dtype) for a in arrays],
        arrays,
        [block(width, rows)] * len(arrays),
        [block(rows, width)] * len(arrays),
        grid=(seqs,),
        flops=seqs * width * rows * 100,
    )


def put_rows(out_ref, place_ref, pieces):
    for i, piece in enumerate(pieces):
        rows = pl.ds(pl.multiple_of(place_ref[i], 16), piece.shape[0])
        out_ref[rows, :] = piece[...]


def kv_kernel(tok_ref, gain_ref, cos_ref, sin_ref, w_ref, normed_ref, kv_ref, ks):
    source = tok_ref[0].astype(F32)
    normed = (source * inverse_mean(source) * gain_ref[...]).astype(BF16)
    normed_ref[0] = normed
    raw = nn(normed, w_ref[...])
    ks[:, :KW] = raw[:, :KW]
    kv_ref[0, :, KW:] = raw[:, KW:].astype(BF16)
    rotate_into(kv_ref, ks, KW, cos_ref[...], sin_ref[...], 1.0)


def q_kernel(normed_ref, cos_ref, sin_ref, w_ref, q_ref, qs):
    qs[:, :QW] = nn(normed_ref[0], w_ref[...])
    rotate_into(q_ref, qs, QW, cos_ref[...], sin_ref[...], HD**-0.5)


def residual_kernel(tok_ref, mixed_ref, gain_ref, w_ref, hidden_ref, normed_ref):
    hidden = tok_ref[0].astype(F32) + nn(mixed_ref[0], w_ref[...])
    hidden_ref[0] = hidden
    normed_ref[0] = (hidden * inverse_mean(hidden) * gain_ref[...]).astype(BF16)


def with_weight(kernel, outs, args, specs, pieces, places, scratch, flops):
    if len(pieces) == 1:
        return (
            *call(
                kernel,
                outs,
                (*args, pieces[0]),
                [*specs, whole(pieces[0])],
                [whole(o) for o in outs],
                scratch=scratch,
                flops=flops,
            ),
            pieces[0],
        )
    count = len(outs)
    outs = [*outs, struct((2 * pieces[0].shape[0], pieces[0].shape[1]), pieces[0].dtype)]
    return call(
        functools.partial(place_first, kernel, len(args), len(pieces), count),
        outs,
        (places, *args, *pieces),
        [smem(), *specs, *map(whole, pieces)],
        [whole(o) for o in outs],
        scratch=scratch,
        flops=flops,
    )


def place_first(kernel, ins, count, outs, place_ref, *refs):
    args, parts, rest = refs[:ins], refs[ins : ins + count], refs[ins + count :]
    w_ref = rest[outs]
    put_rows(w_ref, place_ref, parts)
    kernel(*args, w_ref, *rest[:outs], *rest[outs + 1 :])


def project_kv(tokens, seq, gain, cosine, sine, pieces, places):
    rows, width = tokens.shape[1:]
    args = (tokens, gain, cosine, sine)
    return with_weight(
        kv_kernel,
        [struct((1, rows, width), BF16), struct((1, rows, 2 * KW), BF16)],
        args,
        [part(tokens, seq), *map(whole, args[1:])],
        pieces,
        places,
        [pltpu.VMEM((rows, wide(KW)), F32)],
        4 * rows * width * KW,
    )


def project_q(normed, cosine, sine, pieces, places):
    _, rows, width = normed.shape
    args = (normed, cosine, sine)
    return with_weight(
        q_kernel,
        [struct((1, rows, QW), BF16)],
        args,
        [*map(whole, args)],
        pieces,
        places,
        [pltpu.VMEM((rows, wide(QW)), F32)],
        2 * rows * width * QW,
    )


def residual(tokens, seq, mixed, gain, pieces, places):
    rows, width = tokens.shape[1:]
    args = (tokens, mixed, gain)
    return with_weight(
        residual_kernel,
        [struct((1, rows, width), F32), struct((1, rows, width), BF16)],
        args,
        [part(tokens, seq), whole(mixed), whole(gain)],
        pieces,
        places,
        [],
        2 * rows * width * QW,
    )


def marks(scal_ref, pos, valid):
    segment = jnp.zeros(pos.shape, jnp.int32)
    for d in range(2):
        segment += (pos >= scal_ref[0, d]).astype(jnp.int32)
    number = jnp.zeros(pos.shape, jnp.int32)
    for j in range(2):
        start = scal_ref[0, 2 + j]
        number += jnp.where((pos >= start) & (pos < start + PIECE), j + 1, 0)
    return jnp.where(valid, segment, -1), number


def bias_of(scal_ref, start, across):
    q_shape, k_shape, q_dim, k_dim = (
        ((GRAIN, 1), (1, SPAN), 0, 1) if across else ((1, GRAIN), (SPAN, 1), 1, 0)
    )
    q_pos = start + lax.broadcasted_iota(jnp.int32, q_shape, q_dim)
    k_pos = start - MAXDOC + lax.broadcasted_iota(jnp.int32, k_shape, k_dim)
    q_seg, q_num = marks(scal_ref, q_pos, q_pos >= 0)
    k_seg, k_num = marks(scal_ref, k_pos, (k_pos >= 0) & (k_pos < LEN))
    q_num = jnp.where(q_num > 0, q_num, -1)
    permit = (q_seg == k_seg) & ((k_pos <= q_pos) | (q_num == k_num))
    return jnp.where(permit, 0.0, NEG).astype(F32)


def load_window(window, parts):
    row = 0
    for part in parts:
        window[row : row + part.shape[1], :] = part[0]
        row += part.shape[1]


def attend_kernel(scal_ref, q_ref, far_ref, near_ref, own_ref, next_ref, mixed_ref, lse_ref, window):
    sub = pl.program_id(0)

    @pl.when(sub == 0)
    def _():
        load_window(window, (far_ref, near_ref, own_ref, next_ref))

    bias = bias_of(scal_ref, scal_ref[0, 4] + sub * GRAIN, True)
    bias = jnp.concatenate([bias] * GROUP, axis=0)
    rows = pl.ds(pl.multiple_of(sub * GRAIN, GRAIN), SPAN)
    lse = jnp.zeros((GRAIN, 128), F32)
    lane = lax.broadcasted_iota(jnp.int32, (GRAIN, 128), 1)
    for j in range(KVH):
        key = window[rows, j * HD : (j + 1) * HD]
        value = window[rows, KW + j * HD : KW + (j + 1) * HD]
        cols = [slice(h * HD, (h + 1) * HD) for h in range(j * GROUP, (j + 1) * GROUP)]
        query = jnp.concatenate([q_ref[0, :, c] for c in cols], axis=0)
        scores = nt(query, key) + bias
        top = jnp.max(scores, axis=-1, keepdims=True)
        raised = jnp.exp(scores - top)
        total = jnp.sum(raised, axis=-1, keepdims=True)
        out = nn(raised.astype(BF16), value) / total
        logsum = top + jnp.log(total)
        for g, c in enumerate(cols):
            at = slice(g * GRAIN, (g + 1) * GRAIN)
            mixed_ref[0, :, c] = out[at].astype(BF16)
            lse = jnp.where(lane == j * GROUP + g, logsum[at], lse)
    lse_ref[0] = lse


def attend(scal, q, parts):
    local = q.shape[1]
    outs = [struct((1, local, QW), BF16), struct((1, local, 128), F32)]
    return call(
        attend_kernel,
        outs,
        (scal, q, *parts),
        [smem(), sub_part(q), *map(whole, parts)],
        [sub_part(o) for o in outs],
        grid=(local // GRAIN,),
        scratch=[pltpu.VMEM((MAXDOC + local + GRAIN, 2 * KW), BF16)],
        flops=16 * local * SPAN * QW,
    )


def attend_back_kernel(
    scal_ref,
    q_ref,
    far_ref,
    near_ref,
    own_ref,
    next_ref,
    mixed_ref,
    lse_ref,
    grad_ref,
    dq_ref,
    dfar_ref,
    dnear_ref,
    down_ref,
    dnext_ref,
    window,
    sums,
):
    sub = pl.program_id(0)

    @pl.when(sub == 0)
    def _():
        load_window(window, (far_ref, near_ref, own_ref, next_ref))
        sums[...] = jnp.zeros_like(sums)

    bias = bias_of(scal_ref, scal_ref[0, 4] + sub * GRAIN, False)
    bias = jnp.concatenate([bias] * GROUP, axis=1)
    rows = pl.ds(pl.multiple_of(sub * GRAIN, GRAIN), SPAN)
    lane = lax.broadcasted_iota(jnp.int32, (GRAIN, 128), 1)
    product = mixed_ref[0].astype(F32) * grad_ref[0].astype(F32)
    delta = jnp.zeros((GRAIN, 128), F32)
    for h in range(H):
        part = jnp.sum(product[:, h * HD : (h + 1) * HD], axis=-1, keepdims=True)
        delta = jnp.where(lane == h, part, delta)
    delta = delta.T
    lse = lse_ref[0].T

    def heads(array, j):
        return [array[h : h + 1, :] for h in range(j * GROUP, (j + 1) * GROUP)]

    for j in range(KVH):
        k_cols = slice(j * HD, (j + 1) * HD)
        v_cols = slice(KW + j * HD, KW + (j + 1) * HD)
        key, value = window[rows, k_cols], window[rows, v_cols]
        cols = [slice(h * HD, (h + 1) * HD) for h in range(j * GROUP, (j + 1) * GROUP)]
        query = jnp.concatenate([q_ref[0, :, c] for c in cols], axis=0)
        grad = jnp.concatenate([grad_ref[0, :, c] for c in cols], axis=0)
        lse_row = jnp.concatenate(heads(lse, j), axis=1)
        delta_row = jnp.concatenate(heads(delta, j), axis=1)
        probs = jnp.exp(nt(key, query) + bias - lse_row)
        grad_scores = (probs * (nt(value, grad) - delta_row)).astype(BF16)
        sums[rows, v_cols] += nn(probs.astype(BF16), grad)
        sums[rows, k_cols] += nn(grad_scores, query)
        dq = tn(key, grad_scores).T
        for g, c in enumerate(cols):
            dq_ref[0, :, c] = dq[g * GRAIN : (g + 1) * GRAIN, :]

    @pl.when(sub == pl.num_programs(0) - 1)
    def _():
        row = 0
        for part in (dfar_ref, dnear_ref, down_ref, dnext_ref):
            part[0] = sums[row : row + part.shape[1], :].astype(part.dtype)
            row += part.shape[1]


def attend_back(scal, q, parts, mixed, lse, grad):
    local = q.shape[1]
    window = MAXDOC + local + GRAIN
    outs = [
        struct((1, local, QW), F32),
        struct((1, local, 2 * KW), BF16),
        struct((1, local, 2 * KW), BF16),
        struct((1, local, 2 * KW), F32),
        struct((1, GRAIN, 2 * KW), BF16),
    ]
    return call(
        attend_back_kernel,
        outs,
        (scal, q, *parts, mixed, lse, grad),
        [smem(), sub_part(q), *map(whole, parts), sub_part(mixed), sub_part(lse), sub_part(grad)],
        [sub_part(outs[0]), *map(whole, outs[1:])],
        grid=(local // GRAIN,),
        scratch=[pltpu.VMEM((window, 2 * KW), BF16), pltpu.VMEM((window, 2 * KW), F32)],
        flops=40 * local * SPAN * QW,
    )


def ff_kernel(nrm_a, nrm_b, cot_a, cot_b, w_ref, inner_ref, gg_ref, gu_ref, ff_a, ff_b, gn_a, gn_b):
    first = pl.program_id(0) == 0
    units = inner_ref.shape[1]
    wg, wu, wd = (w_ref[:, k * units : (k + 1) * units] for k in range(3))
    normed = jnp.where(first, nrm_a[0], nrm_b[0])
    gate = nn(normed, wg)
    up = nn(normed, wu)
    grad = nn(jnp.where(first, cot_a[0], cot_b[0]), wd)
    sigma = jax.nn.sigmoid(gate)
    raised = gate * sigma
    inner = (raised * up).astype(BF16)
    grad_gate = (grad * up * (sigma + raised * (1.0 - sigma))).astype(BF16)
    grad_up = (grad * raised).astype(BF16)
    inner_ref[...] = inner
    gg_ref[...] = grad_gate
    gu_ref[...] = grad_up
    grad_normed = (nt(grad_gate, wg) + nt(grad_up, wu)).astype(BF16)
    out = nt(inner, wd).astype(BF16)

    @pl.when(first)
    def _():
        ff_a[0] = out
        gn_a[0] = grad_normed

    @pl.when(jnp.logical_not(first))
    def _():
        ff_b[0] = out
        gn_b[0] = grad_normed


def ff(normed_pair, cot_pair, weights, seq):
    _, rows, width = normed_pair[0].shape
    units = weights.shape[1] // 3
    args = (*normed_pair, *cot_pair, weights)
    outs = [struct((2 * rows, units), BF16)] * 3 + [struct((1, rows, width), BF16)] * 4
    result = call(
        ff_kernel,
        outs,
        args,
        [*map(whole, normed_pair), *(part(c, seq) for c in cot_pair), whole(weights)],
        [pl.BlockSpec((rows, units), lambda i: (i, 0))] * 3 + [whole(o) for o in outs[3:]],
        grid=(2,),
        flops=24 * rows * width * units,
    )
    return result[:3], result[3:5], result[5:]


def outer_kernel(lefts, rights, gains, split, place_ref, *refs):
    outs = refs[lefts + rights + gains : -1]
    acc = refs[-1]
    gain_refs = refs[lefts + rights : lefts + rights + gains]
    rows = lambda ref: ref[...].reshape(-1, ref.shape[-1])
    width = refs[lefts].shape[-1]
    per = lefts // rights
    for i, right in enumerate(refs[lefts : lefts + rights]):
        left = jnp.concatenate([rows(r) for r in refs[i * per : (i + 1) * per]], axis=0)
        product = tn(left, rows(right))
        if i == 0:
            acc[:, :width] = product
        else:
            acc[:, :width] += product
    if gains:
        total = functools.reduce(jnp.add, [g[0] for g in gain_refs])
        across = jnp.broadcast_to(total, (128, total.shape[1])).T
        acc[:, width:] = across[:, : acc.shape[1] - width]
    if split is None:
        outs[0][...] = acc[...]
        return
    keep_ref, send_ref = outs
    half = keep_ref.shape[-2]
    for s in range(acc.shape[0] // (2 * half)):
        kept = acc[pl.ds(pl.multiple_of(2 * s * half + place_ref[0], 16), half), :]
        sent = acc[pl.ds(pl.multiple_of((2 * s + 1) * half - place_ref[0], 16), half), :]
        if split == "shard":
            keep_ref[...], send_ref[...] = kept, sent.astype(BF16)
        else:
            keep_ref[s], send_ref[s] = kept, sent.astype(BF16)


def outer(lefts, rights, place, split, gains=()):
    width = lefts[0][0].shape[-1]
    columns = rights[0].shape[-1]
    full = wide(columns) if gains else columns
    if split is None:
        outs = [struct((width, full), F32)]
    else:
        shape = (width // 2, full) if split == "shard" else (2, width // 4, full)
        outs = [struct(shape, F32), struct(shape, BF16)]
    count = sum(math.prod(r.shape[:-1]) for r in rights)
    return call(
        functools.partial(outer_kernel, len(lefts), len(rights), len(gains), split),
        outs,
        (place, *(a for a, _ in lefts), *rights, *gains),
        [smem(), *(part(a, s) for a, s in lefts), *map(whole, rights), *map(whole, gains)],
        [whole(o) for o in outs],
        scratch=[pltpu.VMEM((width, full), F32)],
        flops=2 * count * width * columns,
    )


def output_kernel(hidden_ref, *refs):
    total = hidden_ref[0]
    for term in refs[:-1]:
        total += term[0].astype(F32)
    refs[-1][0] = total.T.astype(BF16)


def output_of(hidden, terms):
    _, rows, width = hidden.shape
    out = struct((1, width, rows), BF16)
    return call(
        output_kernel,
        [out],
        (hidden, *terms),
        [whole(hidden), *map(whole, terms)],
        [whole(out)],
        flops=rows * width * 100,
    )[0]


def ff_back_kernel(
    hidden_ref, cot_ref, a_ref, b_ref, c_ref, gain_ref, wo_ref, gh_ref, gb_ref, gm_ref, gg_ref
):
    hidden, gain = hidden_ref[0], gain_ref[...]
    factor = inverse_mean(hidden)
    grad = a_ref[0].astype(F32) + b_ref[0].astype(F32) + c_ref[0].astype(F32)
    weighted = grad * gain
    back = factor * weighted - hidden * factor**3 * jnp.mean(
        hidden * weighted, axis=-1, keepdims=True
    )
    grad_hidden = cot_ref[0].astype(F32) + back
    branch = grad_hidden.astype(BF16)
    gh_ref[0] = grad_hidden
    gb_ref[0] = branch
    gm_ref[0] = nt(branch, wo_ref[...]).astype(BF16)
    gg_ref[0] = jnp.sum(grad * hidden * factor, axis=0, keepdims=True)


def ff_back(hidden, cotangent, seq, terms, gain, wo):
    _, rows, width = hidden.shape
    outs = [
        struct((1, rows, width), F32),
        struct((1, rows, width), BF16),
        struct((1, rows, QW), BF16),
        struct((1, 1, width), F32),
    ]
    return call(
        ff_back_kernel,
        outs,
        (hidden, cotangent, *terms, gain, wo),
        [whole(hidden), part(cotangent, seq), *map(whole, terms), whole(gain), whole(wo)],
        [whole(o) for o in outs],
        flops=2 * rows * width * QW,
    )


def query_back_kernel(dq_ref, cos_ref, sin_ref, out_ref, qs):
    qs[:, :QW] = dq_ref[0]
    rotate_into(out_ref, qs, QW, cos_ref[...], -sin_ref[...], HD**-0.5)


def query_back(dq, cosine, sine):
    rows = dq.shape[1]
    return call(
        query_back_kernel,
        [struct((1, rows, QW), BF16)],
        (dq, cosine, sine),
        [whole(dq), whole(cosine), whole(sine)],
        [whole(dq)],
        scratch=[pltpu.VMEM((rows, wide(QW)), F32)],
        flops=rows * QW * 100,
    )[0]


def input_kernel(
    tok_ref,
    gh_ref,
    gq_ref,
    own_ref,
    left_ref,
    right_ref,
    gain_ref,
    wq_ref,
    wkv_ref,
    cos_ref,
    sin_ref,
    ig_ref,
    gkv_ref,
    ks,
):
    ks[...] = own_ref[0] + right_ref[0].astype(F32)
    ks[:GRAIN, :] += left_ref[0].astype(F32)
    gkv_ref[0, :, KW:] = ks[:, KW:].astype(BF16)
    rotate_into(gkv_ref, ks, KW, cos_ref[...], -sin_ref[...], 1.0)
    grad = nt(gq_ref[0], wq_ref[...]) + nt(gkv_ref[0], wkv_ref[...])
    source, gain = tok_ref[0].astype(F32), gain_ref[...]
    factor = inverse_mean(source)
    weighted = grad * gain
    back = factor * weighted - source * factor**3 * jnp.mean(
        source * weighted, axis=-1, keepdims=True
    )
    ig_ref[0] = (gh_ref[0] + back).T


def input_back(tokens, seq, args):
    _, rows, width = tokens.shape
    outs = [struct((1, width, rows), F32), struct((1, rows, 2 * KW), BF16)]
    return call(
        input_kernel,
        outs,
        (tokens, *args),
        [part(tokens, seq), *map(whole, args)],
        [whole(o) for o in outs],
        scratch=[pltpu.VMEM((rows, 2 * KW), F32)],
        flops=2 * rows * width * (QW + 2 * KW),
    )


def program(mesh):
    shards, ctxs = mesh.shape["shard"], mesh.shape["ctx"]

    def swap(value, axis, bit):
        count = mesh.shape[axis]
        return lax.ppermute(value, axis, [(i, i ^ bit) for i in range(count)])

    def shift(value, by):
        pairs = [(i, i + by) for i in range(ctxs) if 0 <= i + by < ctxs]
        return lax.ppermute(value, "ctx", pairs)

    def in_order(index, own, other):
        first = jnp.concatenate([own, other], axis=0)
        return jnp.where(index == 0, first, jnp.concatenate([other, own], axis=0))

    def pick(value, index):
        return lax.dynamic_index_in_dim(value, index, 0, keepdims=False)

    def add(terms):
        return functools.reduce(jnp.add, [t.astype(F32) for t in terms])

    def over_shard(terms):
        if shards != 2:
            return (lax.psum_scatter(terms[0], "shard", scatter_dimension=0, tiled=True),)
        return terms[0], swap(terms[1], "shard", 1)

    def reduce_attention(terms):
        if shards != 2:
            return lax.psum(add(over_shard(terms)), ("ctx", "tp"))
        mine, tp = lax.axis_index("shard"), lax.axis_index("tp")
        core, row = tp % 2, tp // 2
        keep, send = terms
        got = swap(send, "tp", 1)
        deps = yield got
        held = keep + after(got, *deps).astype(F32)
        got = swap(pick(held, 1 - mine).astype(BF16), "shard", 1)
        deps = yield got
        held = pick(held, mine) + after(got, *deps).astype(F32)
        held = held.reshape(2, held.shape[0] // 2, -1)
        got = swap(pick(held, 1 - row).astype(BF16), "tp", 2)
        deps = yield got
        held = pick(held, row) + after(got, *deps).astype(F32)
        bit = 1
        while bit < ctxs:
            low = held.astype(BF16)
            got = swap(low, "ctx", bit)
            deps = yield got
            held = low.astype(F32) + after(got, *deps).astype(F32)
            bit *= 2
        held = held.astype(BF16)
        got = swap(held, "tp", 2)
        deps = yield got
        held = in_order(row, held, after(got, *deps))
        got = swap(held, "tp", 1)
        deps = yield got
        return in_order(core, held, after(got, *deps)).astype(F32)

    def per_device(
        tokens,
        cotangent,
        piece_starts,
        doc_lengths,
        attn_gain,
        w_query,
        w_key,
        w_value,
        w_out,
        ff_gain,
        w_gate,
        w_up,
        w_down,
    ):
        seqs, rows, width = tokens.shape
        offset = (lax.axis_index("ctx") * rows).astype(jnp.int32)
        mine, tp = lax.axis_index("shard"), lax.axis_index("tp")
        core, row = tp % 2, tp // 2
        every = range(seqs)
        last = seqs - 1

        w_kv = jnp.concatenate([w_key, w_value], axis=1)
        gains = jnp.stack([attn_gain, ff_gain])
        w_ff = jnp.concatenate([w_gate, w_up, w_down], axis=1)
        if shards == 2:
            full = w_query.shape[0]
            half = full // 2
            span = -(-half // 32) * 16
            other = (1 - mine) * full
            here, there = other + core * half, other + (1 - core) * half
            step, back = row * (half - span), (1 - row) * (half - span)
            kv_places = jnp.stack([mine * full, here, there])
            places = jnp.stack([mine * full, here + step, here + back, there + step, there + back])
            kv_places, places = kv_places.astype(jnp.int32), places.astype(jnp.int32)

            got = swap(gains, "shard", 1)
            gains = jnp.where(
                mine == 0,
                jnp.concatenate([gains, got], axis=1),
                jnp.concatenate([got, gains], axis=1),
            )
            kv_part = swap(lax.dynamic_slice_in_dim(w_kv, core * half, half), "shard", 1)
            kv_pieces = (w_kv, kv_part, swap(kv_part, "tp", 1))
            quarter = lambda w: lax.dynamic_slice_in_dim(w, core * half + step, span)
            q_part = swap(after(quarter(w_query), kv_part), "shard", 1)
            q_facing = swap(q_part, "tp", 2)
            q_pieces = (w_query, q_part, q_facing, swap(q_part, "tp", 1), swap(q_facing, "tp", 1))
            out_part = swap(after(quarter(w_out), q_part), "shard", 1)
            out_facing = swap(after(out_part, q_facing), "tp", 2)
            out_pieces = (w_out, out_part, out_facing)
            out_pieces += (swap(out_part, "tp", 1), swap(out_facing, "tp", 1))
            w_ff = after(w_ff, out_part)
        else:
            gather = lambda w: lax.all_gather(w, "shard", axis=0, tiled=True)
            kv_places = places = jnp.zeros((1,), jnp.int32)
            gains = lax.all_gather(gains, "shard", axis=1, tiled=True)
            kv_pieces, q_pieces, out_pieces = (gather(w_kv),), (gather(w_query),), (gather(w_out),)
            q_facing = q_pieces[-1]
        ff_weights = lax.all_gather(w_ff, "shard", axis=0, tiled=True)
        gain_one, gain_two = gains[:1].astype(F32), gains[1:].astype(F32)

        tokens, cotangent = prepare(tokens.transpose(0, 2, 1), cotangent.transpose(0, 2, 1))
        cosine, sine = rotary_tables(offset, rows)
        ends = jnp.cumsum(doc_lengths, axis=1)[:, :-1]
        scal = jnp.concatenate(
            [ends, piece_starts, jnp.broadcast_to(offset, (seqs, 1))], axis=1
        ).astype(jnp.int32)
        scals = [scal[s : s + 1] for s in every]

        normed_one, query, windows = [], [], []
        previous, order = (), ()
        for s in every:
            normed, kv, wkv = project_kv(
                after(tokens, *order), s, gain_one, cosine, sine, kv_pieces, kv_places
            )
            kv_pieces = (wkv,)
            normed_one.append(normed)
            order = (kv,)
            near = shift(after(kv, *previous), 1)
            ahead = shift(after(kv[:, :GRAIN], *previous), -1)
            previous = (near, ahead)
            windows.append((shift(near, 1), near, kv, ahead))
        cot_y = swap(after(cotangent, q_facing), "tp", 2)
        cot_core = swap(cotangent, "tp", 1)
        for s in every:
            normed = after(normed_one[s], *order)
            q, wq = project_q(normed, cosine, sine, q_pieces, places)
            q_pieces = (wq,)
            query.append(q)
            order = (q,)

        mixed, lse, hidden, normed_rows = [], [], [], []
        order = (query[last], *out_pieces)
        for s in every:
            m, l = attend(scals[s], after(query[s], *order), windows[s])
            deps = (*windows[min(s + 1, last)], cot_y) if s == 0 else (normed_rows[-1][2],)
            h, own, wo = residual(tokens, s, after(m, *deps), gain_two, out_pieces, places)
            out_pieces = (wo,)
            normed_rows.append((own, swap(own, "tp", 1), swap(own, "tp", 2)))
            mixed.append(m)
            lse.append(l)
            hidden.append(h)
            order = (h,)
        cots = (cotangent, cot_core, cot_y, swap(after(cot_y, hidden[0]), "tp", 1))

        def to_facing(near, far):
            here, there = swap(near[1], "tp", 1), swap(far[1], "tp", 1)
            return (near[0], here), (far[0].astype(F32) + there.astype(F32)).astype(BF16)

        row_blocks, units, out_pairs = [], [], []
        grad_terms, crossed = [], []
        order = (hidden[last],)
        for s in every:
            own, beside, facing = normed_rows[s]
            unit, near_out, near_grad = ff((after(own, *order), beside), cots[:2], ff_weights, s)
            units.append(unit)
            diagonal = swap(after(facing, hidden[last], *(u[0] for u in units[: 2 * s])), "tp", 1)
            order = (unit[0], *(t[1] for t in crossed), *(n[2] for n in normed_rows[s + 1 :]))
            unit, far_out, far_grad = ff(
                (after(facing, *order), diagonal), cots[2:], ff_weights, s
            )
            units.append(unit)
            order = (unit[0],)
            terms, partial = to_facing(near_grad, far_grad)
            crossed.append((terms, partial, swap(partial, "tp", 2)))
            grad_terms.append((*terms, crossed[-1][2]))
            out_pairs.append((near_out, far_out))
            row_blocks += [own, beside, facing, diagonal]

        by_shard, by_core = ("shard", "core") if shards == 2 else (None, None)
        shard_place = (mine * (width // 2)).astype(jnp.int32)[None]
        core_place = (core * (width // 4)).astype(jnp.int32)[None]

        def unit_outer(lefts, k, *deps):
            rights = [u[k] for u in units]
            return outer(lefts, [after(rights[0], *deps), *rights[1:]], shard_place, by_shard)

        cot_lefts = [(c, s) for s in every for c in cots]
        row_lefts = [(b, 0) for b in row_blocks]
        down_grad = unit_outer(cot_lefts, 0, *order, *(t[2] for t in crossed[:-1]))
        down_terms = over_shard(down_grad)
        gate_grad = unit_outer(row_lefts, 1, down_grad[0], crossed[-1][1])
        gate_terms = over_shard(gate_grad)
        branch, gain_two_grad, grad_hidden = [], [], []
        backs = []
        order = gate_grad[0]
        for s in every:
            deps = ()
            if s == last:
                facing_outs = []
                for near_out, far_out in out_pairs:
                    held = after((near_out, far_out), down_grad[0])
                    facing_outs.append(to_facing(*held))
                deps = tuple(f[1] for f in facing_outs)
            gh, gb, gm, gg = ff_back(
                after(hidden[s], order, *deps), cotangent, s, grad_terms[s], gain_two, wo
            )
            grad_hidden.append(gh)
            branch.append(gb)
            gain_two_grad.append(gg)
            deps = ()
            if s == last:
                out_grad = outer([(m, 0) for m in mixed], branch, core_place, by_core, gain_two_grad)
                out_chain = Chain(reduce_attention(out_grad))
                deps = (out_grad[0], *(b[2] for b in backs))
            dq, dfar, dnear, down, dnext = attend_back(
                scals[s], query[s], windows[s], mixed[s], lse[s], after(gm, *deps)
            )
            order = dq
            passed = shift(dfar, -1)
            left = shift(dnext, 1)
            if s == 0:
                up_grad = unit_outer(row_lefts, 2, dq)
                up_terms = over_shard(up_grad)
                order = up_grad[0]
                sum_down = lax.psum(add(after(down_terms, dq)).astype(BF16), "ctx")
            nearer = (dnear.astype(F32) + passed.astype(F32)).astype(BF16)
            backs.append((dq, down, nearer, left, shift(nearer, -1)))
        out_chain.step((order,))
        outs_got = [swap(after(f[1], *(t[2] for t in crossed)), "tp", 2) for f in facing_outs]
        arrived = [a for b in backs[:-1] for a in b[3:]]
        gq = [query_back(after(b[0], order, *arrived), cosine, sine) for b in backs]
        ones = [(n, 0) for n in normed_one]
        query_grad = outer(ones, gq, core_place, by_core)
        query_chain = Chain(reduce_attention(query_grad))
        order = (query_grad[0], outs_got[0], backs[last][2], out_chain.got, query_chain.got)
        out_chain.step((query_grad[0],))
        query_chain.step()

        input_grads, gkv = [], []
        for s in every:
            _, down, _, left, right = backs[s]
            args = (grad_hidden[s], gq[s], down, left, right)
            args += (gain_one, wq, wkv, cosine, sine)
            input_grad, g = input_back(tokens, s, (after(args[0], *order), *args[1:]))
            input_grads.append(input_grad)
            gkv.append(g)
            order = (g, outs_got[last], out_chain.got, query_chain.got)
        out_chain.step((g,))
        query_chain.step((g,))
        kv_grad = outer(ones, gkv, core_place, by_core)
        kv_chain = Chain(reduce_attention(kv_grad))
        sums = [add(t).astype(BF16) for t in after((gate_terms, up_terms), query_grad[0])]
        sum_gate, sum_up = lax.psum(after(sums, sum_down, kv_grad[0]), "ctx")
        outputs = [
            output_of(after(hidden[s], kv_grad[0]), (*facing_outs[s][0], outs_got[s]))
            for s in every
        ]
        sum_out, sum_query, sum_kv = (c.finish() for c in (out_chain, query_chain, kv_chain))
        sum_key, sum_value = sum_kv[:, :KW], sum_kv[:, KW:]
        sum_gain = functools.reduce(
            jnp.add,
            [
                jnp.sum(w.astype(F32) * g, axis=1)
                for w, g in ((w_query, sum_query), (w_key, sum_key), (w_value, sum_value))
            ],
        ) / attn_gain.astype(F32)
        join = lambda blocks: jnp.concatenate(blocks, axis=0).transpose(0, 2, 1)
        return (
            join(outputs),
            join(input_grads),
            sum_gain,
            sum_query,
            sum_key,
            sum_value,
            sum_out[:, :width],
            sum_out[:, width],
            sum_gate.astype(F32),
            sum_up.astype(F32),
            sum_down.astype(F32),
        )

    return per_device


def solution(mesh):
    rows = P(("shard", "tp"), "ctx", None)
    seq = P(("shard", "tp"), None)
    gain, weight, ff_weight = P("shard"), P("shard", None), P("shard", "tp")
    weights = (gain, weight, weight, weight, weight, gain, ff_weight, ff_weight, ff_weight)
    return jax.shard_map(
        program(mesh),
        mesh=mesh,
        in_specs=(rows, rows, seq, seq, *weights),
        out_specs=(rows, rows, *weights),
        check_vma=False,
    )
```

time: 465 us -> 423 us (0.910)
  local copies, waits for them, and re-layouts: 33.1 us -> 62.2 us
  Pallas kernels: 135 us -> 111 us
  matrix products: 16.8 us -> 0 us
  other arithmetic: 50.9 us -> 37 us
  waiting for transfers between devices: 118 us -> 108 us
  starting transfers between devices: 88.5 us -> 80.8 us
    unnamed x118 -> x245, local copies, waits for them, and re-layouts: 14.3 us -> 45.5 us
    ppermute x60 -> x56, waiting for transfers between devices: 98.6 us -> 73.3 us  [swap(): return lax.ppermute(value, axis, [(i, i ^ bit) for i in range(count)])]
    pallas_call x18 -> x29, Pallas kernels: 135 us -> 111 us  [call(): pl.pallas_call(kernel, out_shape=outs, grid=grid, in_specs=in_specs, out_...]
    dot_general x6 -> x0, matrix products: 16.8 us -> none  [dot(): lax.dot_general(left, right, (dims, ((), ())), preferred_element_type=F32)]
    select_n x8 -> x3, other arithmetic: 14 us -> 0.52 us  [in_order(): return jnp.where(index == 0, first, jnp.concatenate([other, own], axis=0))]
    psum x3 -> x2, waiting for transfers between devices: 19.4 us -> 31.1 us  [the longest x1 23.2 us: per_device(): sum_gate, sum_up = lax.psum(after(sums, sum_down, kv_grad[0]), 'ctx')]
    ppermute x60 -> x56, starting transfers between devices: 55.7 us -> 49.2 us  [swap(): return lax.ppermute(value, axis, [(i, i ^ bit) for i in range(count)])]
    convert_element_type x22 -> x20, other arithmetic: 17.5 us -> 15.6 us  [the longest x2 4.09 us: per_device(): add(t).astype(BF16)]
  transfers between devices with their start and end apart: 75 -> 71, of which waited for: 18 -> 19; matrix products, arithmetic and copies ran while one was open for 21% -> 12% of each run, Pallas kernels for 29% -> 25%
where the time goes in v3:
time: 423 us; the launch traced here: 415 us
  Pallas kernels  111 us (26%)
  waiting for transfers between devices  108 us (26%)
  starting transfers between devices  80.8 us (19%)
  local copies, waits for them, and re-layouts  62.2 us (15%)
  other arithmetic  37 us (9%)
  between operations  15.6 us (4%)
    pallas_call x29, Pallas kernels, call(): pl.pallas_call(kernel, out_shape=outs, grid=grid, in_specs=in_specs, out_...  111 us
    ppermute x56, waiting for transfers between devices, swap(): return lax.ppermute(value, axis, [(i, i ^ bit) for i in range(count)])  73.3 us
    ppermute x56, starting transfers between devices, swap(): return lax.ppermute(value, axis, [(i, i ^ bit) for i in range(count)])  49.2 us
    unnamed x245, local copies, waits for them, and re-layouts  45.5 us
    ppermute x12, starting transfers between devices, shift(): return lax.ppermute(value, 'ctx', pairs)  31.5 us
    psum x1, waiting for transfers between devices, per_device(): sum_gate, sum_up = lax.psum(after(sums, sum_down, kv_grad[0]), 'ctx')  23.2 us
  transfers between devices with their start and end apart: 71, of which 19 were waited for; matrix products, arithmetic and copies ran while one was open for 12% of the time, Pallas kernels for 25%

profile of v3, /device:TPU:1, one launch (start us, length us, event | category | flops | bytes accessed | tf_op | source)
XLA Modules:
  0.0 415.3 jit_solution(4628932068945929819)
XLA Ops:
  10.0 2.1 collective-permute-start.1
  13.1 6.0 %collective-permute-done.1.refs_5_ = bf16[240,640]{1,0:T(8,128)(2,1)S(1)} collective-permute-done((bf16[240,640]{1,0:T(8,128)(2,1)S(1)}, bf16[240,640]{1,0:T(8,128)(2,1)S(1)}, u32[]{:S(2)}, u32[]{:S(2)}) %collective-permute-start.1) | collective-permute-done | bytes 307232 | tf_op jit(solution)/shard_map/ppermute | solution.py:650
  20.2 1.7 constant_dynamic-slice_fusion.2
  21.9 3.9 collective-permute-done.3.refs_4_
  28.0 3.8 collective-permute-done.7.refs_4_
  36.9 4.0 collective-permute-start.2
  43.3 2.1 shard_map.213
  46.2 3.9 collective-permute-start.11
  55.6 1.5 shard_map.214
  57.9 2.2 collective-permute-done.13.next_ref
  60.9 3.1 collective-permute-start.14
  63.9 2.2 collective-permute-start.5
  69.5 3.3 collective-permute-start.12
  72.8 7.3 %collective-permute-done.8.refs_5_ = bf16[128,960]{1,0:T(8,128)(2,1)S(1)} collective-permute-done((bf16[128,960]{1,0:T(8,128)(2,1)}, bf16[128,960]{1,0:T(8,128)(2,1)S(1)}, u32[]{:S(2)}, u32[]{:S(2)}) %collective-permute-start.8) | collective-permute-done | bytes 245792 | tf_op jit(solution)/shard_map/ppermute | solution.py:650
  81.5 3.3 collective-permute-start.15
  93.5 2.2 shard_map.215
  97.9 7.1 %shard_map.217 = (bf16[1,256,960]{2,1,0:T(8,128)(2,1)S(1)}, f32[1,256,128]{2,1,0:T(8,128)S(1)}) custom-call(s32[1,5]{1,0:T(1,128)S(1)} %get-tuple-element.296.scal_ref, bf16[1,256,960]{2,1,0:T(8,128)(2,1)S(1)} %get-tuple-element.160.q_ref, bf16[1,256,640]{2,1,0:T(8,128)(2,1)} %collective-permute-done.12.far_ref, ...), custom_call_target="tpu_custom_call" | custom-call | flops 301989888 | bytes 1006632 | tf_op jit(solution)/shard_map/pallas_call | solution.py:48
  105.8 3.0 shard_map.218
  111.6 6.9 %shard_map.219 = (bf16[1,256,960]{2,1,0:T(8,128)(2,1)S(1)}, f32[1,256,128]{2,1,0:T(8,128)S(1)}) custom-call(s32[1,5]{1,0:T(1,128)S(1)} %get-tuple-element.297.scal_ref, bf16[1,256,960]{2,1,0:T(8,128)(2,1)S(1)} %shard_map.216.q_ref, bf16[1,256,640]{2,1,0:T(8,128)(2,1)} %collective-permute-done.15.far_ref, ...), custom_call_target="tpu_custom_call" | custom-call | flops 301989888 | bytes 1006632 | tf_op jit(solution)/shard_map/pallas_call | solution.py:48
  118.5 5.0 %collective-permute-done.19.nrm_a.refs_2_ = bf16[1,256,960]{2,1,0:T(8,128)(2,1)} collective-permute-done((bf16[1,256,960]{2,1,0:T(8,128)(2,1)}, bf16[1,256,960]{2,1,0:T(8,128)(2,1)}, u32[]{:S(2)}, u32[]{:S(2)}) %collective-permute-start.19) | collective-permute-done | bytes 491552 | tf_op jit(solution)/shard_map/ppermute | solution.py:650
  123.5 1.6 shard_map.220
  128.6 1.5 copy.55.cot_b.refs_1_.refs_5_
  130.1 2.3 copy.56.cot_a.refs_2_.refs_6_
  132.4 2.3 copy.57.cot_b.refs_3_.refs_7_
  134.6 2.0 copy-done
  136.7 7.8 %shard_map.221 = (bf16[512,640]{1,0:T(8,128)(2,1)S(1)}, bf16[512,640]{1,0:T(8,128)(2,1)S(1)}, bf16[512,640]{1,0:T(8,128)(2,1)S(1)}, bf16[1,256,960]{2,1,0:T(8,12...) custom-call(bf16[1,256,960]{2,1,0:T(8,128)(2,1)} %get-tuple-element.17, ...), custom_call_target="tpu_custom_call" | custom-call | flops 377487360 | bytes 1258291 | tf_op jit(solution)/shard_map/pallas_call | solution.py:48
  144.6 7.1 %shard_map.222 = (bf16[512,640]{1,0:T(8,128)(2,1)S(1)}, bf16[512,640]{1,0:T(8,128)(2,1)S(1)}, bf16[512,640]{1,0:T(8,128)(2,1)S(1)}, bf16[1,256,960]{2,1,0:T(8,12...) custom-call(bf16[1,256,960]{2,1,0:T(8,128)(2,1)} %collective-permute, ...), custom_call_target="tpu_custom_call" | custom-call | flops 377487360 | bytes 1258291 | tf_op jit(solution)/shard_map/pallas_call | solution.py:48
  154.6 7.5 %shard_map.223 = (bf16[512,640]{1,0:T(8,128)(2,1)S(1)}, bf16[512,640]{1,0:T(8,128)(2,1)S(1)}, bf16[512,640]{1,0:T(8,128)(2,1)S(1)}, bf16[1,256,960]{2,1,0:T(8,12...) custom-call(bf16[1,256,960]{2,1,0:T(8,128)(2,1)} %get-tuple-element.18, ...), custom_call_target="tpu_custom_call" | custom-call | flops 377487360 | bytes 1258291 | tf_op jit(solution)/shard_map/pallas_call | solution.py:48
  162.9 7.2 %shard_map.224 = (bf16[512,640]{1,0:T(8,128)(2,1)S(1)}, bf16[512,640]{1,0:T(8,128)(2,1)S(1)}, bf16[512,640]{1,0:T(8,128)(2,1)S(1)}, bf16[1,256,960]{2,1,0:T(8,12...) custom-call(bf16[1,256,960]{2,1,0:T(8,128)(2,1)} %collective-permute, ...), custom_call_target="tpu_custom_call" | custom-call | flops 377487360 | bytes 1258291 | tf_op jit(solution)/shard_map/pallas_call | solution.py:48
  170.6 4.3 %shard_map.225 = (f32[480,640]{1,0:T(8,128)S(1)}, bf16[480,640]{1,0:T(8,128)(2,1)}) custom-call(s32[1]{0:T(128)} %bitcast.place_ref, bf16[2,256,960]{2,1,0:T(8,128)(2,1)S(1)} %get-tuple-element.165.cot_a.refs_0_.refs_4_.cot_ref, bf16[2,256,960]{2,1,0:T(8,128)(2,1)S(1)} %copy.55.cot_b.refs_1_.refs_5_, bf16[2,256,960]{2,1,0:T(8,128)(2,1)S(1)} %copy-done.2, ...), custom_call_target="tpu_custom_call" | custom-call | flops 251658240 | bytes 838860 | tf_op jit(solution)/shard_map/pallas_call | solution.py:48
  176.9 5.4 %shard_map.226 = (f32[480,640]{1,0:T(8,128)S(1)}, bf16[480,640]{1,0:T(8,128)(2,1)S(1)}) custom-call(s32[1]{0:T(128)} %bitcast.place_ref, bf16[1,256,960]{2,1,0:T(8,128)(2,1)} %get-tuple-element.176.nrm_a.refs_0_, bf16[1,256,960]{2,1,0:T(8,128)(2,1)} %collective-permute-done.18.nrm_b.refs_1_, bf16[1,256,960]{2,1,0:T(8,128)(2,1)} %collective-permute-done.19.nrm_a.refs_2_, ...), custom_call_target="tpu_custom_call" | custom-call | flops 251658240 | bytes 838860 | tf_op jit(solution)/shard_map/pallas_call | solution.py:48
  186.7 11.7 %shard_map.228 = (f32[1,256,960]{2,1,0:T(8,128)S(1)}, bf16[1,256,640]{2,1,0:T(8,128)(2,1)}, bf16[1,256,640]{2,1,0:T(8,128)(2,1)S(1)}, f32[1,256,640]{2,1,0:T(8,128)S(1)}, bf16[1,128,640]{2,1,0:T(8,128)(2,1)S(1)}) custom-call(s32[1,5]{1,0:T(1,128)S(1)} %get-tuple-element.296.scal_ref, bf16[1,256,960]{2,1,0:T(8,128)(2,1)S(1)} %copy-done.40, ...), custom_call_target="tpu_custom_call" | custom-call | flops 754974720 | bytes 2516582 | tf_op jit(solution)/shard_map/pallas_call | solution.py:48
  201.6 5.3 %shard_map.229 = (f32[480,640]{1,0:T(8,128)S(1)}, bf16[480,640]{1,0:T(8,128)(2,1)S(1)}) custom-call(s32[1]{0:T(128)} %bitcast.place_ref, bf16[1,256,960]{2,1,0:T(8,128)(2,1)} %get-tuple-element.176.nrm_a.refs_0_, bf16[1,256,960]{2,1,0:T(8,128)(2,1)} %collective-permute-done.18.nrm_b.refs_1_, bf16[1,256,960]{2,1,0:T(8,128)(2,1)} %collective-permute-done.19.nrm_a.refs_2_, ...), custom_call_target="tpu_custom_call" | custom-call | flops 251658240 | bytes 838860 | tf_op jit(solution)/shard_map/pallas_call | solution.py:48
  206.9 1.6 collective-permute-start.34
  212.8 2.4 shard_map.231
  219.5 1.8 add_convert_fusion.8
  223.6 11.7 %shard_map.232 = (f32[1,256,960]{2,1,0:T(8,128)S(1)}, bf16[1,256,640]{2,1,0:T(8,128)(2,1)}, bf16[1,256,640]{2,1,0:T(8,128)(2,1)S(1)}, f32[1,256,640]{2,1,0:T(8,128)S(1)}, bf16[1,128,640]{2,1,0:T(8,128)(2,1)}) custom-call(s32[1,5]{1,0:T(1,128)S(1)} %get-tuple-element.297.scal_ref, bf16[1,256,960]{2,1,0:T(8,128)(2,1)S(1)} %copy-done.27, ...), custom_call_target="tpu_custom_call" | custom-call | flops 754974720 | bytes 2516582 | tf_op jit(solution)/shard_map/pallas_call | solution.py:48
  237.9 4.3 %collective-permute-start.35 = (bf16[1,128,640]{2,1,0:T(8,128)(2,1)}, bf16[1,128,640]{2,1,0:T(8,128)(2,1)S(1)}, u32[]{:S(2)}, u32[]{:S(2)}) collective-permute-start(bf16[1,128,640]{2,1,0:T(8,128)(2,1)} %copy-done.100), channel_id=1, source_target_pairs={{0,4},{4,8},{8,12},{1,5},{5,9},{9,13},{2,6},{6,10},{10,14},{3,7},{... | collective-permute-start | bytes 491528 | tf_op jit(solution)/shard_map/ppermute | solution.py:654
  242.2 2.4 add_convert_fusion
  253.3 2.5 collective-permute-start.41
  255.8 2.1 add_convert_fusion.1
  257.8 5.4 %collective-permute-start.45 = (bf16[1,128,640]{2,1,0:T(8,128)(2,1)}, bf16[1,128,640]{2,1,0:T(8,128)(2,1)}, u32[]{:S(2)}, u32[]{:S(2)}) collective-permute-start(bf16[1,128,640]{2,1,0:T(8,128)(2,1)} %get-tuple-element.256), channel_id=1, source_target_pairs={{0,4},{4,8},{8,12},{1,5},{5,9},{9,13},{2,6},{6,10},{10,14},{3,7},{... | collective-permute-start | bytes 491528 | tf_op jit(solution)/shard_map/ppermute | solution.py:654
  266.5 1.5 collective-permute-start.46
  269.4 5.4 %collective-permute-done.40 = bf16[240,1024]{1,0:T(8,128)(2,1)S(1)} collective-permute-done((bf16[240,1024]{1,0:T(8,128)(2,1)S(1)}, bf16[240,1024]{1,0:T(8,128)(2,1)S(1)}, u32[]{:S(2)}, u32[]{:S(2)}) %collective-permute-start.40) | collective-permute-done | bytes 491552 | tf_op jit(solution)/shard_map/ppermute | solution.py:650
  278.5 1.6 collective-permute-start.43
  280.1 2.0 add_convert_fusion.2
  282.2 7.9 %all-reduce.4.cloned.1.call-done = bf16[480,640]{1,0:T(8,128)(2,1)} async-done(((bf16[480,640]{1,0:T(8,128)(2,1)}), bf16[480,640]{1,0:T(8,128)(2,1)}) %all-reduce.4.cloned.1.call-update) | async-done | bytes 614416 | tf_op jit(solution)/shard_map/psum | solution.py:878
  290.1 2.3 convert_element_type.327
  292.4 1.5 copy-done.5
  295.7 1.7 shard_map.236
  299.3 2.9 shard_map.237
  302.3 1.6 bitcast_add_fusion
  305.9 1.9 shard_map.238
  315.6 1.6 shard_map.240
  323.5 1.9 collective-permute-start.62
  325.4 17.9 %collective-permute-done.50 = bf16[120,960]{1,0:T(8,128)(2,1)S(1)} collective-permute-done((bf16[120,960]{1,0:T(8,128)(2,1)S(1)}, bf16[120,960]{1,0:T(8,128)(2,1)S(1)}, u32[]{:S(2)}, u32[]{:S(2)}) %collective-permute-start.50) | collective-permute-done | bytes 230432 | tf_op jit(solution)/shard_map/ppermute | solution.py:650
  343.9 1.5 collective-permute-start.63
  345.6 3.6 collective-permute-done.56
  350.2 10.3 %collective-permute-done.51 = bf16[120,960]{1,0:T(8,128)(2,1)S(1)} collective-permute-done((bf16[120,960]{1,0:T(8,128)(2,1)S(1)}, bf16[120,960]{1,0:T(8,128)(2,1)S(1)}, u32[]{:S(2)}, u32[]{:S(2)}) %collective-permute-start.51) | collective-permute-done | bytes 230432 | tf_op jit(solution)/shard_map/ppermute | solution.py:650
  363.7 4.0 collective-permute-done.52
  369.2 23.2 %all-reduce.6.cloned.1.call-done = (bf16[480,640]{1,0:T(8,128)(2,1)}, bf16[480,640]{1,0:T(8,128)(2,1)}) async-done(((bf16[480,640]{1,0:T(8,128)(2,1)}, bf16[480,640]{1,0:T(8,128)(2,1)}), (bf16[480,640]{1,0:T(8,128)(2,1)}, bf16[480,640]{1,0:T(8,128)(2,1)})) %all-reduce.6.cloned.1.call-update) | async-done | bytes 1228816 | tf_op jit(solution)/shard_map/psum | solution.py:906
  392.4 2.2 convert_element_type.325
  397.6 3.6 collective-permute-done.59
  403.7 1.7 multiply_reduce_fusion
  (428 shorter events, 123.4 us)
Async XLA Ops:
  7.2 127.4 %all-gather.2.cloned.1.call-start = ((), (), s32[]{:S(2)}) async-start(), calls=%async_computation | async-start | bytes 5529600 | tf_op jit(solution)/shard_map/all_gather | solution.py:761
  10.0 9.1 %collective-permute-start.1 = (bf16[240,640]{1,0:T(8,128)(2,1)S(1)}, bf16[240,640]{1,0:T(8,128)(2,1)S(1)}, u32[]{:S(2)}, u32[]{:S(2)}) collective-permute-start(bf16[240,640]{1,0:T(8,128)(2,1)S(1)} %fusion.9), channel_id=1, source_target_pairs={{0,16},{16,0},{1,17},{17,1},{2,18},{18,2},{3,19},{19,3},{4,20},{20... | collective-permute-start | bytes 921608 | tf_op jit(solution)/shard_map/ppermute | solution.py:650
  19.1 6.7 %collective-permute-start.3 = (bf16[128,960]{1,0:T(8,128)(2,1)S(1)}, bf16[128,960]{1,0:T(8,128)(2,1)}, u32[]{:S(2)}, u32[]{:S(2)}) collective-permute-start(bf16[128,960]{1,0:T(8,128)(2,1)S(1)} %constant_dynamic-slice_fusion.3), channel_id=1, source_target_pairs={{0,16},{16,0},{1,17},{17,1},{2,18},{18,2},{3,19},{19,3},{4,20},{20... | collective-permute-start | bytes 737288 | tf_op jit(solution)/shard_map/ppermute | solution.py:650
  25.8 6.0 %collective-permute-start.7 = (bf16[128,960]{1,0:T(8,128)(2,1)}, bf16[128,960]{1,0:T(8,128)(2,1)}, u32[]{:S(2)}, u32[]{:S(2)}) collective-permute-start(bf16[128,960]{1,0:T(8,128)(2,1)} %constant_dynamic-slice_fusion.2), channel_id=1, source_target_pairs={{0,16},{16,0},{1,17},{17,1},{2,18},{18,2},{3,19},{19,3},{4,20},{20... | collective-permute-start | bytes 737288 | tf_op jit(solution)/shard_map/ppermute | solution.py:650
  31.8 258.3 %all-reduce.4.cloned.1.call-start = ((), (), s32[]{:S(2)}) async-start(), calls=%async_computation.1 | async-start | bytes 1228800 | tf_op jit(solution)/shard_map/psum | solution.py:878
  31.9 9.0 %collective-permute-start = (bf16[2,480]{1,0:T(2,128)(2,1)S(1)}, bf16[2,480]{1,0:T(2,128)(2,1)S(1)}, u32[]{:S(2)}, u32[]{:S(2)}) collective-permute-start(bf16[2,480]{1,0:T(2,128)(2,1)S(1)} %pad_maximum_fusion.4), channel_id=1, source_target_pairs={{0,16},{16,0},{1,17},{17,1},{2,18},{18,2},{3,19},{19,3},{4,20},{20... | collective-permute-start | bytes 5768 | tf_op jit(solution)/shard_map/ppermute | solution.py:650
  41.0 9.2 %collective-permute-start.4 = (bf16[128,960]{1,0:T(8,128)(2,1)}, bf16[128,960]{1,0:T(8,128)(2,1)}, u32[]{:S(2)}, u32[]{:S(2)}) collective-permute-start(bf16[128,960]{1,0:T(8,128)(2,1)} %collective-permute-done.3.refs_4_), channel_id=1, source_target_pairs={{0,2},{1,3},{2,0},{3,1},{4,6},{5,7},{6,4},{7,5},{8,10},{9,11},{10,... | collective-permute-start | bytes 737288 | tf_op jit(solution)/shard_map/ppermute | solution.py:650
  46.2 14.6 %collective-permute-start.11 = (bf16[1,256,640]{2,1,0:T(8,128)(2,1)}, bf16[1,256,640]{2,1,0:T(8,128)(2,1)}, u32[]{:S(2)}, u32[]{:S(2)}) collective-permute-start(bf16[1,256,640]{2,1,0:T(8,128)(2,1)} %get-tuple-element.148.own_ref), channel_id=1, source_target_pairs={{0,4},{4,8},{8,12},{1,5},{5,9},{9,13},{2,6},{6,10},{10,14},{3,7},{... | collective-permute-start | bytes 983048 | tf_op jit(solution)/shard_map/ppermute | solution.py:654
  51.5 54.3 %collective-permute-start.17 = (bf16[2,256,960]{1,2,0:T(8,128)(2,1)}, bf16[2,256,960]{1,2,0:T(8,128)(2,1)}, u32[]{:S(2)}, u32[]{:S(2)}) collective-permute-start(bf16[2,256,960]{1,2,0:T(8,128)(2,1)} %copy.53), channel_id=1, source_target_pairs={{0,2},{1,3},{2,0},{3,1},{4,6},{5,7},{6,4},{7,5},{8,10},{9,11},{10,... | collective-permute-start | bytes 2949128 | tf_op jit(solution)/shard_map/ppermute | solution.py:650
  53.4 6.8 %collective-permute-start.13 = (bf16[1,128,640]{2,1,0:T(8,128)(2,1)S(1)}, bf16[1,128,640]{2,1,0:T(8,128)(2,1)S(1)}, u32[]{:S(2)}, u32[]{:S(2)}) collective-permute-start(bf16[1,128,640]{2,1,0:T(8,128)(2,1)S(1)} %slice.36), channel_id=1, source_target_pairs={{4,0},{8,4},{12,8},{5,1},{9,5},{13,9},{6,2},{10,6},{14,10},{7,3},{... | collective-permute-start | bytes 491528 | tf_op jit(solution)/shard_map/ppermute | solution.py:654
  60.9 20.6 %collective-permute-start.14 = (bf16[1,256,640]{2,1,0:T(8,128)(2,1)}, bf16[1,256,640]{2,1,0:T(8,128)(2,1)}, u32[]{:S(2)}, u32[]{:S(2)}) collective-permute-start(bf16[1,256,640]{2,1,0:T(8,128)(2,1)} %get-tuple-element.162.own_ref), channel_id=1, source_target_pairs={{0,4},{4,8},{8,12},{1,5},{5,9},{9,13},{2,6},{6,10},{10,14},{3,7},{... | collective-permute-start | bytes 983048 | tf_op jit(solution)/shard_map/ppermute | solution.py:654
  66.1 14.0 %collective-permute-start.8 = (bf16[128,960]{1,0:T(8,128)(2,1)}, bf16[128,960]{1,0:T(8,128)(2,1)S(1)}, u32[]{:S(2)}, u32[]{:S(2)}) collective-permute-start(bf16[128,960]{1,0:T(8,128)(2,1)} %collective-permute-done.7.refs_4_), channel_id=1, source_target_pairs={{0,2},{1,3},{2,0},{3,1},{4,6},{5,7},{6,4},{7,5},{8,10},{9,11},{10,... | collective-permute-start | bytes 737288 | tf_op jit(solution)/shard_map/ppermute | solution.py:650
  68.2 18.9 %collective-permute-start.9 = (bf16[128,960]{1,0:T(8,128)(2,1)}, bf16[128,960]{1,0:T(8,128)(2,1)S(1)}, u32[]{:S(2)}, u32[]{:S(2)}) collective-permute-start(bf16[128,960]{1,0:T(8,128)(2,1)} %collective-permute-done.7.refs_4_), channel_id=1, source_target_pairs={{0,1},{1,0},{2,3},{3,2},{4,5},{5,4},{6,7},{7,6},{8,9},{9,8},{10,11... | collective-permute-start | bytes 737288 | tf_op jit(solution)/shard_map/ppermute | solution.py:650
  69.5 28.4 %collective-permute-start.12 = (bf16[1,256,640]{2,1,0:T(8,128)(2,1)}, bf16[1,256,640]{2,1,0:T(8,128)(2,1)}, u32[]{:S(2)}, u32[]{:S(2)}) collective-permute-start(bf16[1,256,640]{2,1,0:T(8,128)(2,1)} %collective-permute-done.11.near_ref), channel_id=1, source_target_pairs={{0,4},{4,8},{8,12},{1,5},{5,9},{9,13},{2,6},{6,10},{10,14},{3,7},{... | collective-permute-start | bytes 983048 | tf_op jit(solution)/shard_map/ppermute | solution.py:654
  80.1 16.6 %collective-permute-start.10 = (bf16[128,960]{1,0:T(8,128)(2,1)S(1)}, bf16[128,960]{1,0:T(8,128)(2,1)}, u32[]{:S(2)}, u32[]{:S(2)}) collective-permute-start(bf16[128,960]{1,0:T(8,128)(2,1)S(1)} %collective-permute-done.8.refs_5_), channel_id=1, source_target_pairs={{0,1},{1,0},{2,3},{3,2},{4,5},{5,4},{6,7},{7,6},{8,9},{9,8},{10,11... | collective-permute-start | bytes 737288 | tf_op jit(solution)/shard_map/ppermute | solution.py:650
  81.5 24.3 %collective-permute-start.15 = (bf16[1,256,640]{2,1,0:T(8,128)(2,1)}, bf16[1,256,640]{2,1,0:T(8,128)(2,1)}, u32[]{:S(2)}, u32[]{:S(2)}) collective-permute-start(bf16[1,256,640]{2,1,0:T(8,128)(2,1)} %collective-permute-done.14.near_ref), channel_id=1, source_target_pairs={{0,4},{4,8},{8,12},{1,5},{5,9},{9,13},{2,6},{6,10},{10,14},{3,7},{... | collective-permute-start | bytes 983048 | tf_op jit(solution)/shard_map/ppermute | solution.py:654
  87.1 18.7 %collective-permute-start.16 = (bf16[1,128,640]{2,1,0:T(8,128)(2,1)S(1)}, bf16[1,128,640]{2,1,0:T(8,128)(2,1)S(1)}, u32[]{:S(2)}, u32[]{:S(2)}) collective-permute-start(bf16[1,128,640]{2,1,0:T(8,128)(2,1)S(1)} %slice.37), channel_id=1, source_target_pairs={{4,0},{8,4},{12,8},{5,1},{9,5},{13,9},{6,2},{10,6},{14,10},{7,3},{... | collective-permute-start | bytes 491528 | tf_op jit(solution)/shard_map/ppermute | solution.py:654
  97.6 31.0 %collective-permute-start.23 = (bf16[2,256,960]{1,2,0:T(8,128)(2,1)S(1)}, bf16[2,256,960]{1,2,0:T(8,128)(2,1)}, u32[]{:S(2)}, u32[]{:S(2)}) collective-permute-start(bf16[2,256,960]{1,2,0:T(8,128)(2,1)S(1)} %copy-done.110), channel_id=1, source_target_pairs={{0,1},{1,0},{2,3},{3,2},{4,5},{5,4},{6,7},{7,6},{8,9},{9,8},{10,11... | collective-permute-start | bytes 2949128 | tf_op jit(solution)/shard_map/ppermute | solution.py:650
  109.8 22.6 %collective-permute-start.24 = (bf16[2,256,960]{1,2,0:T(8,128)(2,1)}, bf16[2,256,960]{1,2,0:T(8,128)(2,1)}, u32[]{:S(2)}, u32[]{:S(2)}) collective-permute-start(bf16[2,256,960]{1,2,0:T(8,128)(2,1)} %collective-permute-done.17), channel_id=1, source_target_pairs={{0,1},{1,0},{2,3},{3,2},{4,5},{5,4},{6,7},{7,6},{8,9},{9,8},{10,11... | collective-permute-start | bytes 2949128 | tf_op jit(solution)/shard_map/ppermute | solution.py:650
  110.0 13.6 %collective-permute-start.19 = (bf16[1,256,960]{2,1,0:T(8,128)(2,1)}, bf16[1,256,960]{2,1,0:T(8,128)(2,1)}, u32[]{:S(2)}, u32[]{:S(2)}) collective-permute-start(bf16[1,256,960]{2,1,0:T(8,128)(2,1)} %get-tuple-element.176.nrm_a.refs_0_), channel_id=1, source_target_pairs={{0,2},{1,3},{2,0},{3,1},{4,6},{5,7},{6,4},{7,5},{8,10},{9,11},{10,... | collective-permute-start | bytes 1474568 | tf_op jit(solution)/shard_map/ppermute | solution.py:650
  111.0 23.6 %collective-permute-start.18 = (bf16[1,256,960]{2,1,0:T(8,128)(2,1)}, bf16[1,256,960]{2,1,0:T(8,128)(2,1)}, u32[]{:S(2)}, u32[]{:S(2)}) collective-permute-start(bf16[1,256,960]{2,1,0:T(8,128)(2,1)} %get-tuple-element.176.nrm_a.refs_0_), channel_id=1, source_target_pairs={{0,1},{1,0},{2,3},{3,2},{4,5},{5,4},{6,7},{7,6},{8,9},{9,8},{10,11... | collective-permute-start | bytes 1474568 | tf_op jit(solution)/shard_map/ppermute | solution.py:650
  126.2 18.3 %collective-permute-start.22 = (bf16[1,256,960]{2,1,0:T(8,128)(2,1)}, bf16[1,256,960]{2,1,0:T(8,128)(2,1)}, u32[]{:S(2)}, u32[]{:S(2)}) collective-permute-start(bf16[1,256,960]{2,1,0:T(8,128)(2,1)} %get-tuple-element.184.nrm_a.refs_4_), channel_id=1, source_target_pairs={{0,2},{1,3},{2,0},{3,1},{4,6},{5,7},{6,4},{7,5},{8,10},{9,11},{10,... | collective-permute-start | bytes 1474568 | tf_op jit(solution)/shard_map/ppermute | solution.py:650
  127.2 17.3 %collective-permute-start.20 = (bf16[1,256,960]{2,1,0:T(8,128)(2,1)}, bf16[1,256,960]{2,1,0:T(8,128)(2,1)}, u32[]{:S(2)}, u32[]{:S(2)}) collective-permute-start(bf16[1,256,960]{2,1,0:T(8,128)(2,1)} %collective-permute-done.19.nrm_a.refs_2_), channel_id=1, source_target_pairs={{0,1},{1,0},{2,3},{3,2},{4,5},{5,4},{6,7},{7,6},{8,9},{9,8},{10,11... | collective-permute-start | bytes 1474568 | tf_op jit(solution)/shard_map/ppermute | solution.py:650
  152.3 10.6 %collective-permute-start.25 = (bf16[1,256,960]{2,1,0:T(8,128)(2,1)}, bf16[1,256,960]{2,1,0:T(8,128)(2,1)S(1)}, u32[]{:S(2)}, u32[]{:S(2)}) collective-permute-start(bf16[1,256,960]{2,1,0:T(8,128)(2,1)} %collective-permute-done.22.nrm_a.refs_6_), channel_id=1, source_target_pairs={{0,1},{1,0},{2,3},{3,2},{4,5},{5,4},{6,7},{7,6},{8,9},{9,8},{10,11... | collective-permute-start | bytes 1474568 | tf_op jit(solution)/shard_map/ppermute | solution.py:650
  153.9 16.8 %collective-permute-start.27 = (bf16[1,256,960]{2,1,0:T(8,128)(2,1)S(1)}, bf16[1,256,960]{2,1,0:T(8,128)(2,1)S(1)}, u32[]{:S(2)}, u32[]{:S(2)}) collective-permute-start(bf16[1,256,960]{2,1,0:T(8,128)(2,1)S(1)} %add_convert_fusion.6), channel_id=1, source_target_pairs={{0,2},{1,3},{2,0},{3,1},{4,6},{5,7},{6,4},{7,5},{8,10},{9,11},{10,... | collective-permute-start | bytes 1474568 | tf_op jit(solution)/shard_map/ppermute | solution.py:650
  170.1 5.5 %collective-permute-start.28 = (bf16[1,256,960]{2,1,0:T(8,128)(2,1)S(1)}, bf16[1,256,960]{2,1,0:T(8,128)(2,1)S(1)}, u32[]{:S(2)}, u32[]{:S(2)}) collective-permute-start(bf16[1,256,960]{2,1,0:T(8,128)(2,1)S(1)} %get-tuple-element.193), channel_id=1, source_target_pairs={{0,1},{1,0},{2,3},{3,2},{4,5},{5,4},{6,7},{7,6},{8,9},{9,8},{10,11... | collective-permute-start | bytes 1474568 | tf_op jit(solution)/shard_map/ppermute | solution.py:650
  170.3 13.1 %collective-permute-start.29 = (bf16[1,256,960]{2,1,0:T(8,128)(2,1)S(1)}, bf16[1,256,960]{2,1,0:T(8,128)(2,1)S(1)}, u32[]{:S(2)}, u32[]{:S(2)}) collective-permute-start(bf16[1,256,960]{2,1,0:T(8,128)(2,1)S(1)} %get-tuple-element.201), channel_id=1, source_target_pairs={{0,1},{1,0},{2,3},{3,2},{4,5},{5,4},{6,7},{7,6},{8,9},{9,8},{10,11... | collective-permute-start | bytes 1474568 | tf_op jit(solution)/shard_map/ppermute | solution.py:650
  174.9 32.0 %collective-permute-start.31 = (bf16[1,256,960]{2,1,0:T(8,128)(2,1)S(1)}, bf16[1,256,960]{2,1,0:T(8,128)(2,1)S(1)}, u32[]{:S(2)}, u32[]{:S(2)}) collective-permute-start(bf16[1,256,960]{2,1,0:T(8,128)(2,1)S(1)} %get-tuple-element.224), channel_id=1, source_target_pairs={{0,1},{1,0},{2,3},{3,2},{4,5},{5,4},{6,7},{7,6},{8,9},{9,8},{10,11... | collective-permute-start | bytes 1474568 | tf_op jit(solution)/shard_map/ppermute | solution.py:650
  175.1 35.4 %collective-permute-start.32 = (bf16[1,256,960]{2,1,0:T(8,128)(2,1)S(1)}, bf16[1,256,960]{2,1,0:T(8,128)(2,1)S(1)}, u32[]{:S(2)}, u32[]{:S(2)}) collective-permute-start(bf16[1,256,960]{2,1,0:T(8,128)(2,1)S(1)} %get-tuple-element.227), channel_id=1, source_target_pairs={{0,1},{1,0},{2,3},{3,2},{4,5},{5,4},{6,7},{7,6},{8,9},{9,8},{10,11... | collective-permute-start | bytes 1474568 | tf_op jit(solution)/shard_map/ppermute | solution.py:650
  175.4 34.0 %collective-permute-start.30 = (bf16[1,256,960]{2,1,0:T(8,128)(2,1)S(1)}, bf16[1,256,960]{2,1,0:T(8,128)(2,1)S(1)}, u32[]{:S(2)}, u32[]{:S(2)}) collective-permute-start(bf16[1,256,960]{2,1,0:T(8,128)(2,1)S(1)} %get-tuple-element.218), channel_id=1, source_target_pairs={{0,1},{1,0},{2,3},{3,2},{4,5},{5,4},{6,7},{7,6},{8,9},{9,8},{10,11... | collective-permute-start | bytes 1474568 | tf_op jit(solution)/shard_map/ppermute | solution.py:650
  175.8 34.7 %collective-permute-start.33 = (bf16[1,256,960]{2,1,0:T(8,128)(2,1)S(1)}, bf16[1,256,960]{2,1,0:T(8,128)(2,1)S(1)}, u32[]{:S(2)}, u32[]{:S(2)}) collective-permute-start(bf16[1,256,960]{2,1,0:T(8,128)(2,1)S(1)} %add_convert_fusion.5), channel_id=1, source_target_pairs={{0,2},{1,3},{2,0},{3,1},{4,6},{5,7},{6,4},{7,5},{8,10},{9,11},{10,... | collective-permute-start | bytes 1474568 | tf_op jit(solution)/shard_map/ppermute | solution.py:650
  183.4 54.5 %collective-permute-start.67 = (bf16[480,640]{1,0:T(8,128)(2,1)}, bf16[480,640]{1,0:T(8,128)(2,1)}, u32[]{:S(2)}, u32[]{:S(2)}) collective-permute-start(bf16[480,640]{1,0:T(8,128)(2,1)} %get-tuple-element.276), channel_id=1, source_target_pairs={{0,16},{16,0},{1,17},{17,1},{2,18},{18,2},{3,19},{19,3},{4,20},{20... | collective-permute-start | bytes 1843208 | tf_op jit(solution)/shard_map/ppermute | solution.py:650
  206.9 12.6 %collective-permute-start.34 = (bf16[1,256,640]{2,1,0:T(8,128)(2,1)}, bf16[1,256,640]{2,1,0:T(8,128)(2,1)}, u32[]{:S(2)}, u32[]{:S(2)}) collective-permute-start(bf16[1,256,640]{2,1,0:T(8,128)(2,1)} %get-tuple-element.235), channel_id=1, source_target_pairs={{4,0},{8,4},{12,8},{5,1},{9,5},{13,9},{6,2},{10,6},{14,10},{7,3},{... | collective-permute-start | bytes 983048 | tf_op jit(solution)/shard_map/ppermute | solution.py:654
  216.4 41.4 %collective-permute-start.39 = (bf16[2,240,1024]{2,1,0:T(8,128)(2,1)}, bf16[2,240,1024]{2,1,0:T(8,128)(2,1)}, u32[]{:S(2)}, u32[]{:S(2)}) collective-permute-start(bf16[2,240,1024]{2,1,0:T(8,128)(2,1)} %get-tuple-element.245), channel_id=1, source_target_pairs={{0,1},{1,0},{2,3},{3,2},{4,5},{5,4},{6,7},{7,6},{8,9},{9,8},{10,11... | collective-permute-start | bytes 2949128 | tf_op jit(solution)/shard_map/ppermute | solution.py:650
  216.8 35.9 %collective-permute-start.66 = (bf16[480,640]{1,0:T(8,128)(2,1)}, bf16[480,640]{1,0:T(8,128)(2,1)}, u32[]{:S(2)}, u32[]{:S(2)}) collective-permute-start(bf16[480,640]{1,0:T(8,128)(2,1)} %copy-done.99), channel_id=1, source_target_pairs={{0,16},{16,0},{1,17},{17,1},{2,18},{18,2},{3,19},{19,3},{4,20},{20... | collective-permute-start | bytes 1843208 | tf_op jit(solution)/shard_map/ppermute | solution.py:650
  217.6 35.6 %collective-permute-start.65 = (bf16[480,640]{1,0:T(8,128)(2,1)}, bf16[480,640]{1,0:T(8,128)(2,1)}, u32[]{:S(2)}, u32[]{:S(2)}) collective-permute-start(bf16[480,640]{1,0:T(8,128)(2,1)} %copy-done.98), channel_id=1, source_target_pairs={{0,16},{16,0},{1,17},{17,1},{2,18},{18,2},{3,19},{19,3},{4,20},{20... | collective-permute-start | bytes 1843208 | tf_op jit(solution)/shard_map/ppermute | solution.py:650
  221.2 24.9 %collective-permute-start.36 = (bf16[1,256,640]{2,1,0:T(8,128)(2,1)}, bf16[1,256,640]{2,1,0:T(8,128)(2,1)S(1)}, u32[]{:S(2)}, u32[]{:S(2)}) collective-permute-start(bf16[1,256,640]{2,1,0:T(8,128)(2,1)} %add_convert_fusion.8), channel_id=1, source_target_pairs={{4,0},{8,4},{12,8},{5,1},{9,5},{13,9},{6,2},{10,6},{14,10},{7,3},{... | collective-permute-start | bytes 983048 | tf_op jit(solution)/shard_map/ppermute | solution.py:654
  237.9 7.2 %collective-permute-start.35 = (bf16[1,128,640]{2,1,0:T(8,128)(2,1)}, bf16[1,128,640]{2,1,0:T(8,128)(2,1)S(1)}, u32[]{:S(2)}, u32[]{:S(2)}) collective-permute-start(bf16[1,128,640]{2,1,0:T(8,128)(2,1)} %copy-done.100), channel_id=1, source_target_pairs={{0,4},{4,8},{8,12},{1,5},{5,9},{9,13},{2,6},{6,10},{10,14},{3,7},{... | collective-permute-start | bytes 491528 | tf_op jit(solution)/shard_map/ppermute | solution.py:654
  244.7 147.7 %all-reduce.6.cloned.1.call-start = ((), (), s32[]{:S(2)}) async-start(), calls=%async_computation.2 | async-start | bytes 2457600 | tf_op jit(solution)/shard_map/psum | solution.py:906
  245.1 53.2 %collective-permute-start.42 = (bf16[1,256,960]{2,1,0:T(8,128)(2,1)}, bf16[1,256,960]{2,1,0:T(8,128)(2,1)}, u32[]{:S(2)}, u32[]{:S(2)}) collective-permute-start(bf16[1,256,960]{2,1,0:T(8,128)(2,1)} %add_convert_fusion.3), channel_id=1, source_target_pairs={{0,2},{1,3},{2,0},{3,1},{4,6},{5,7},{6,4},{7,5},{8,10},{9,11},{10,... | collective-permute-start | bytes 1474568 | tf_op jit(solution)/shard_map/ppermute | solution.py:650
  246.1 18.6 %collective-permute-start.38 = (bf16[1,256,640]{2,1,0:T(8,128)(2,1)}, bf16[1,256,640]{2,1,0:T(8,128)(2,1)S(1)}, u32[]{:S(2)}, u32[]{:S(2)}) collective-permute-start(bf16[1,256,640]{2,1,0:T(8,128)(2,1)} %get-tuple-element.244), channel_id=1, source_target_pairs={{4,0},{8,4},{12,8},{5,1},{9,5},{13,9},{6,2},{10,6},{14,10},{7,3},{... | collective-permute-start | bytes 983048 | tf_op jit(solution)/shard_map/ppermute | solution.py:654
  252.7 25.0 %collective-permute-start.37 = (bf16[1,256,960]{2,1,0:T(8,128)(2,1)S(1)}, bf16[1,256,960]{2,1,0:T(8,128)(2,1)S(1)}, u32[]{:S(2)}, u32[]{:S(2)}) collective-permute-start(bf16[1,256,960]{2,1,0:T(8,128)(2,1)S(1)} %copy-done.115), channel_id=1, source_target_pairs={{0,2},{1,3},{2,0},{3,1},{4,6},{5,7},{6,4},{7,5},{8,10},{9,11},{10,... | collective-permute-start | bytes 1474568 | tf_op jit(solution)/shard_map/ppermute | solution.py:650
  253.3 13.2 %collective-permute-start.41 = (bf16[2,240,960]{2,1,0:T(8,128)(2,1)S(1)}, bf16[2,240,960]{2,1,0:T(8,128)(2,1)S(1)}, u32[]{:S(2)}, u32[]{:S(2)}) collective-permute-start(bf16[2,240,960]{2,1,0:T(8,128)(2,1)S(1)} %get-tuple-element.247), channel_id=1, source_target_pairs={{0,1},{1,0},{2,3},{3,2},{4,5},{5,4},{6,7},{7,6},{8,9},{9,8},{10,11... | collective-permute-start | bytes 2764808 | tf_op jit(solution)/shard_map/ppermute | solution.py:650
  257.8 41.4 %collective-permute-start.45 = (bf16[1,128,640]{2,1,0:T(8,128)(2,1)}, bf16[1,128,640]{2,1,0:T(8,128)(2,1)}, u32[]{:S(2)}, u32[]{:S(2)}) collective-permute-start(bf16[1,128,640]{2,1,0:T(8,128)(2,1)} %get-tuple-element.256), channel_id=1, source_target_pairs={{0,4},{4,8},{8,12},{1,5},{5,9},{9,13},{2,6},{6,10},{10,14},{3,7},{... | collective-permute-start | bytes 491528 | tf_op jit(solution)/shard_map/ppermute | solution.py:654
  264.8 9.9 %collective-permute-start.40 = (bf16[240,1024]{1,0:T(8,128)(2,1)S(1)}, bf16[240,1024]{1,0:T(8,128)(2,1)S(1)}, u32[]{:S(2)}, u32[]{:S(2)}) collective-permute-start(bf16[240,1024]{1,0:T(8,128)(2,1)S(1)} %fusion.3), channel_id=1, source_target_pairs={{0,16},{16,0},{1,17},{17,1},{2,18},{18,2},{3,19},{19,3},{4,20},{20... | collective-permute-start | bytes 1474568 | tf_op jit(solution)/shard_map/ppermute | solution.py:650
  266.5 32.8 %collective-permute-start.46 = (bf16[1,256,640]{2,1,0:T(8,128)(2,1)}, bf16[1,256,640]{2,1,0:T(8,128)(2,1)}, u32[]{:S(2)}, u32[]{:S(2)}) collective-permute-start(bf16[1,256,640]{2,1,0:T(8,128)(2,1)} %add_convert_fusion.7), channel_id=1, source_target_pairs={{4,0},{8,4},{12,8},{5,1},{9,5},{13,9},{6,2},{10,6},{14,10},{7,3},{... | collective-permute-start | bytes 983048 | tf_op jit(solution)/shard_map/ppermute | solution.py:654
  274.7 24.5 %collective-permute-start.44 = (bf16[240,960]{1,0:T(8,128)(2,1)}, bf16[240,960]{1,0:T(8,128)(2,1)}, u32[]{:S(2)}, u32[]{:S(2)}) collective-permute-start(bf16[240,960]{1,0:T(8,128)(2,1)} %fusion.4), channel_id=1, source_target_pairs={{0,16},{16,0},{1,17},{17,1},{2,18},{18,2},{3,19},{19,3},{4,20},{20... | collective-permute-start | bytes 1382408 | tf_op jit(solution)/shard_map/ppermute | solution.py:650
  278.5 20.7 %collective-permute-start.43 = (bf16[120,1024]{1,0:T(8,128)(2,1)}, bf16[120,1024]{1,0:T(8,128)(2,1)}, u32[]{:S(2)}, u32[]{:S(2)}) collective-permute-start(bf16[120,1024]{1,0:T(8,128)(2,1)} %fusion.10), channel_id=1, source_target_pairs={{0,2},{1,3},{2,0},{3,1},{4,6},{5,7},{6,4},{7,5},{8,10},{9,11},{10,... | collective-permute-start | bytes 737288 | tf_op jit(solution)/shard_map/ppermute | solution.py:650
  298.3 13.6 %collective-permute-start.47 = (bf16[1,256,960]{2,1,0:T(8,128)(2,1)}, bf16[1,256,960]{2,1,0:T(8,128)(2,1)}, u32[]{:S(2)}, u32[]{:S(2)}) collective-permute-start(bf16[1,256,960]{2,1,0:T(8,128)(2,1)} %get-tuple-element.261), channel_id=1, source_target_pairs={{0,1},{1,0},{2,3},{3,2},{4,5},{5,4},{6,7},{7,6},{8,9},{9,8},{10,11... | collective-permute-start | bytes 1474568 | tf_op jit(solution)/shard_map/ppermute | solution.py:650
  299.2 15.2 %collective-permute-start.48 = (bf16[1,256,960]{2,1,0:T(8,128)(2,1)}, bf16[1,256,960]{2,1,0:T(8,128)(2,1)}, u32[]{:S(2)}, u32[]{:S(2)}) collective-permute-start(bf16[1,256,960]{2,1,0:T(8,128)(2,1)} %get-tuple-element.264), channel_id=1, source_target_pairs={{0,1},{1,0},{2,3},{3,2},{4,5},{5,4},{6,7},{7,6},{8,9},{9,8},{10,11... | collective-permute-start | bytes 1474568 | tf_op jit(solution)/shard_map/ppermute | solution.py:650
  304.7 14.0 %collective-permute-start.49 = (bf16[120,960]{1,0:T(8,128)(2,1)}, bf16[120,960]{1,0:T(8,128)(2,1)}, u32[]{:S(2)}, u32[]{:S(2)}) collective-permute-start(bf16[120,960]{1,0:T(8,128)(2,1)} %fusion.11), channel_id=1, source_target_pairs={{0,2},{1,3},{2,0},{3,1},{4,6},{5,7},{6,4},{7,5},{8,10},{9,11},{10,... | collective-permute-start | bytes 691208 | tf_op jit(solution)/shard_map/ppermute | solution.py:650
  308.8 11.1 %collective-permute-start.54 = (bf16[2,240,640]{2,1,0:T(8,128)(2,1)}, bf16[2,240,640]{2,1,0:T(8,128)(2,1)}, u32[]{:S(2)}, u32[]{:S(2)}) collective-permute-start(bf16[2,240,640]{2,1,0:T(8,128)(2,1)} %get-tuple-element.268), channel_id=1, source_target_pairs={{0,1},{1,0},{2,3},{3,2},{4,5},{5,4},{6,7},{7,6},{8,9},{9,8},{10,11... | collective-permute-start | bytes 1843208 | tf_op jit(solution)/shard_map/ppermute | solution.py:650
  310.6 11.9 %collective-permute-start.61 = (bf16[120,1024]{1,0:T(8,128)(2,1)S(1)}, bf16[120,1024]{1,0:T(8,128)(2,1)}, u32[]{:S(2)}, u32[]{:S(2)}) collective-permute-start(bf16[120,1024]{1,0:T(8,128)(2,1)S(1)} %fusion.5), channel_id=1, source_target_pairs={{0,4},{4,0},{8,12},{12,8},{1,5},{5,1},{9,13},{13,9},{2,6},{6,2},{1... | collective-permute-start | bytes 737288 | tf_op jit(solution)/shard_map/ppermute | solution.py:650
  319.7 23.6 %collective-permute-start.50 = (bf16[120,960]{1,0:T(8,128)(2,1)S(1)}, bf16[120,960]{1,0:T(8,128)(2,1)S(1)}, u32[]{:S(2)}, u32[]{:S(2)}) collective-permute-start(bf16[120,960]{1,0:T(8,128)(2,1)S(1)} %fusion.6), channel_id=1, source_target_pairs={{0,4},{4,0},{8,12},{12,8},{1,5},{5,1},{9,13},{13,9},{2,6},{6,2},{1... | collective-permute-start | bytes 691208 | tf_op jit(solution)/shard_map/ppermute | solution.py:650
  321.2 22.3 %collective-permute-start.55 = (bf16[240,640]{1,0:T(8,128)(2,1)S(1)}, bf16[240,640]{1,0:T(8,128)(2,1)S(1)}, u32[]{:S(2)}, u32[]{:S(2)}) collective-permute-start(bf16[240,640]{1,0:T(8,128)(2,1)S(1)} %fusion.8), channel_id=1, source_target_pairs={{0,16},{16,0},{1,17},{17,1},{2,18},{18,2},{3,19},{19,3},{4,20},{20... | collective-permute-start | bytes 921608 | tf_op jit(solution)/shard_map/ppermute | solution.py:650
  323.5 20.4 %collective-permute-start.62 = (bf16[120,1024]{1,0:T(8,128)(2,1)S(1)}, bf16[120,1024]{1,0:T(8,128)(2,1)S(1)}, u32[]{:S(2)}, u32[]{:S(2)}) collective-permute-start(bf16[120,1024]{1,0:T(8,128)(2,1)S(1)} %add_convert_fusion.10), channel_id=1, source_target_pairs={{0,8},{4,12},{8,0},{12,4},{1,9},{5,13},{9,1},{13,5},{2,10},{6,14},... | collective-permute-start | bytes 737288 | tf_op jit(solution)/shard_map/ppermute | solution.py:650
  343.4 17.1 %collective-permute-start.51 = (bf16[120,960]{1,0:T(8,128)(2,1)S(1)}, bf16[120,960]{1,0:T(8,128)(2,1)S(1)}, u32[]{:S(2)}, u32[]{:S(2)}) collective-permute-start(bf16[120,960]{1,0:T(8,128)(2,1)S(1)} %add_convert_fusion.12), channel_id=1, source_target_pairs={{0,8},{4,12},{8,0},{12,4},{1,9},{5,13},{9,1},{13,5},{2,10},{6,14},... | collective-permute-start | bytes 691208 | tf_op jit(solution)/shard_map/ppermute | solution.py:650
  343.8 5.4 %collective-permute-start.56 = (bf16[120,640]{0,1:T(8,128)(2,1)S(1)}, bf16[120,640]{0,1:T(8,128)(2,1)S(1)}, u32[]{:S(2)}, u32[]{:S(2)}) collective-permute-start(bf16[120,640]{0,1:T(8,128)(2,1)S(1)} %bitcast.60), channel_id=1, source_target_pairs={{0,2},{1,3},{2,0},{3,1},{4,6},{5,7},{6,4},{7,5},{8,10},{9,11},{10,... | collective-permute-start | bytes 460808 | tf_op jit(solution)/shard_map/ppermute | solution.py:650
  343.9 17.6 %collective-permute-start.63 = (bf16[120,1024]{1,0:T(8,128)(2,1)S(1)}, bf16[120,1024]{1,0:T(8,128)(2,1)S(1)}, u32[]{:S(2)}, u32[]{:S(2)}) collective-permute-start(bf16[120,1024]{1,0:T(8,128)(2,1)S(1)} %add_convert_fusion.9), channel_id=1, source_target_pairs={{0,2},{1,3},{2,0},{3,1},{4,6},{5,7},{6,4},{7,5},{8,10},{9,11},{10,... | collective-permute-start | bytes 737288 | tf_op jit(solution)/shard_map/ppermute | solution.py:650
  349.2 13.3 %collective-permute-start.57 = (bf16[120,640]{0,1:T(8,128)(2,1)S(1)}, bf16[120,640]{0,1:T(8,128)(2,1)S(1)}, u32[]{:S(2)}, u32[]{:S(2)}) collective-permute-start(bf16[120,640]{0,1:T(8,128)(2,1)S(1)} %fusion.7), channel_id=1, source_target_pairs={{0,4},{4,0},{8,12},{12,8},{1,5},{5,1},{9,13},{13,9},{2,6},{6,2},{1... | collective-permute-start | bytes 460808 | tf_op jit(solution)/shard_map/ppermute | solution.py:650
  360.6 7.2 %collective-permute-start.52 = (bf16[120,960]{1,0:T(8,128)(2,1)S(1)}, bf16[120,960]{1,0:T(8,128)(2,1)S(1)}, u32[]{:S(2)}, u32[]{:S(2)}) collective-permute-start(bf16[120,960]{1,0:T(8,128)(2,1)S(1)} %add_convert_fusion.11), channel_id=1, source_target_pairs={{0,2},{1,3},{2,0},{3,1},{4,6},{5,7},{6,4},{7,5},{8,10},{9,11},{10,... | collective-permute-start | bytes 691208 | tf_op jit(solution)/shard_map/ppermute | solution.py:650
  361.7 35.6 %collective-permute-start.64 = (bf16[240,1024]{1,0:T(8,128)(2,1)S(1)}, bf16[240,1024]{1,0:T(8,128)(2,1)S(1)}, u32[]{:S(2)}, u32[]{:S(2)}) collective-permute-start(bf16[240,1024]{1,0:T(8,128)(2,1)S(1)} %maximum_select_fusion.4), channel_id=1, source_target_pairs={{0,1},{1,0},{2,3},{3,2},{4,5},{5,4},{6,7},{7,6},{8,9},{9,8},{10,11... | collective-permute-start | bytes 1474568 | tf_op jit(solution)/shard_map/ppermute | solution.py:650
  362.6 33.1 %collective-permute-start.58 = (bf16[120,640]{0,1:T(8,128)(2,1)S(1)}, bf16[120,640]{0,1:T(8,128)(2,1)S(1)}, u32[]{:S(2)}, u32[]{:S(2)}) collective-permute-start(bf16[120,640]{0,1:T(8,128)(2,1)S(1)} %add_convert_fusion.14), channel_id=1, source_target_pairs={{0,8},{4,12},{8,0},{12,4},{1,9},{5,13},{9,1},{13,5},{2,10},{6,14},... | collective-permute-start | bytes 460808 | tf_op jit(solution)/shard_map/ppermute | solution.py:650
  367.8 35.9 %collective-permute-start.53 = (bf16[240,960]{1,0:T(8,128)(2,1)S(1)}, bf16[240,960]{1,0:T(8,128)(2,1)S(1)}, u32[]{:S(2)}, u32[]{:S(2)}) collective-permute-start(bf16[240,960]{1,0:T(8,128)(2,1)S(1)} %maximum_select_fusion.3), channel_id=1, source_target_pairs={{0,1},{1,0},{2,3},{3,2},{4,5},{5,4},{6,7},{7,6},{8,9},{9,8},{10,11... | collective-permute-start | bytes 1382408 | tf_op jit(solution)/shard_map/ppermute | solution.py:650
  (128 other events, 674.1 us)
Sparse Core Ops, SparseCore 0:
  31.9 54.4 all-gather.1
  244.8 45.2 all-reduce.3
  312.0 80.3 all-reduce.5

commit v4 on v3

v4 whole, which is shorter than its diff:
```python
import functools
import math

import jax
import jax.numpy as jnp
from jax import lax
from jax.experimental import pallas as pl
from jax.experimental.pallas import tpu as pltpu
from jax.sharding import PartitionSpec as P

H = 15
KVH = 5
HD = 64
LEN = 1024
PIECE = 256
GRAIN = 128
MAXDOC = 512
GROUP = H // KVH
KW = KVH * HD
QW = H * HD
SPAN = MAXDOC + 2 * GRAIN

EPS = 1e-05
NEG = -1e30
F32 = jnp.float32
BF16 = jnp.bfloat16
VMEM_LIMIT = 20 * 1024 * 1024
SCALE = 10.0
FLOPS_PER_US = 1.15e9


def dot(left, right, dims):
    return lax.dot_general(left, right, (dims, ((), ())), preferred_element_type=F32)


def nn(left, right):
    return dot(left, right, ((1,), (0,)))


def nt(left, right):
    return dot(left, right, ((1,), (1,)))


def tn(left, right):
    return dot(left, right, ((0,), (0,)))


def wide(width):
    return -(-width // 128) * 128


class Order:
    last = None
    awaited = ()


def arrive(*values):
    Order.awaited += values


def after(value, *deps):
    return lax.optimization_barrier((value, deps))[0] if deps else value


def in_turn(value):
    return value if Order.last is None else after(value, *Order.last)


def struct(shape, dtype):
    return jax.ShapeDtypeStruct(shape, dtype)


def rows_at(array, index, count):
    return array, pl.BlockSpec((count, array.shape[1]), lambda *_: (index, 0))


def rows_each(array, count):
    return array, pl.BlockSpec((count, array.shape[1]), lambda i: (i, 0))


def call(kernel, outs, args, *, us, grid=(1,), scratch=(), limit=VMEM_LIMIT):
    def split(operands):
        arrays, specs = [], []
        for operand in operands:
            if isinstance(operand, tuple):
                array, spec = operand
            elif operand.dtype == jnp.int32:
                array, spec = operand, pl.BlockSpec(memory_space=pltpu.SMEM)
            else:
                array = operand
                spec = pl.BlockSpec(array.shape, lambda *_, n=len(array.shape): (0,) * n)
            arrays.append(array)
            specs.append(spec)
        return arrays, specs

    arrays, in_specs = split(args)
    shapes, out_specs = split(outs)
    first = next(i for i, a in enumerate(arrays) if a.dtype != jnp.int32)
    arrays[first] = after(arrays[first], *(Order.last or ()), *Order.awaited)
    Order.awaited = ()
    result = pl.pallas_call(
        kernel,
        out_shape=shapes,
        grid=grid,
        in_specs=in_specs,
        out_specs=out_specs,
        scratch_shapes=list(scratch),
        compiler_params=pltpu.CompilerParams(vmem_limit_bytes=limit),
        cost_estimate=pl.CostEstimate(
            flops=int(us * SCALE * FLOPS_PER_US), bytes_accessed=0, transcendentals=0
        ),
    )(*arrays)
    Order.last = (result[0],)
    return result


class Chain:
    def __init__(self, steps):
        self.steps, self.result = steps, None
        self.step()

    def step(self):
        if self.result is None:
            try:
                self.got = next(self.steps)
            except StopIteration as stop:
                self.result = stop.value

    def finish(self):
        while self.result is None:
            self.step()
        return self.result


def rotary_tables(offset, length):
    half = HD // 2
    place = (offset + jnp.arange(length, dtype=jnp.int32)).astype(F32)
    freq = jnp.exp(jnp.arange(half).astype(F32) * (-2.0 * math.log(10000.0) / HD))
    angle = place[:, None] * freq[None, :]
    cosine, sine = jnp.cos(angle), jnp.sin(angle)
    return (
        jnp.concatenate([cosine] * 4, axis=1),
        jnp.concatenate([-sine, sine, -sine, sine], axis=1),
    )


def rotate(tile, cosine, sine):
    lane = lax.broadcasted_iota(jnp.int32, tile.shape, 1)
    partner = jnp.where(lane % HD < HD // 2, pltpu.roll(tile, 96, 1), pltpu.roll(tile, 32, 1))
    return tile * cosine + partner * sine


def rotate_into(out_ref, value_ref, width, cosine, sine, factor):
    for start in range(0, width, 128):
        stop = min(start + 128, width)
        turned = rotate(value_ref[:, start : start + 128], cosine, sine) * factor
        out_ref[:, start:stop] = turned[:, : stop - start].astype(out_ref.dtype)


def inverse_mean(value):
    return lax.rsqrt(jnp.mean(value * value, axis=-1, keepdims=True) + EPS)


def prepare_kernel(*refs):
    count = len(refs) // 2
    for source, out in zip(refs[:count], refs[count:]):
        seqs, _, rows = source.shape
        for s in range(seqs):
            out[s * rows : (s + 1) * rows, : source.shape[1]] = source[s].T


def prepare(*arrays):
    outs = [struct((a.shape[0] * a.shape[2], wide(a.shape[1])), a.dtype) for a in arrays]
    return call(prepare_kernel, outs, arrays, us=0.8)


def weight_kernel(kernel, ins, outs, pieces, place_ref, *refs):
    args, parts, rest = refs[:ins], refs[ins : ins + len(pieces)], refs[ins + len(pieces) :]
    if len(pieces) == 1:
        kernel(*args, parts[0], *rest)
        return
    w_ref = rest[outs]

    @pl.when(pl.program_id(0) == 0)
    def _():
        for i, ((start, count), part) in enumerate(zip(pieces, parts)):
            rows = pl.ds(pl.multiple_of(place_ref[i], 16), count)
            w_ref[rows, :] = part[start : start + count, :]

    kernel(*args, w_ref, *rest[:outs], *rest[outs + 1 :])


def with_weight(kernel, outs, args, pieces, places, **kw):
    counts = [(start, count) for _, start, count in pieces]
    arrays = [a for a, _, _ in pieces]
    made = list(outs)
    if len(pieces) > 1:
        made.append(struct((2 * pieces[0][2], arrays[0].shape[1]), arrays[0].dtype))
    body = functools.partial(weight_kernel, kernel, len(args), len(outs), counts)
    result = call(body, made, (places, *args, *arrays), **kw)
    weight = result[-1] if len(pieces) > 1 else arrays[0]
    return result[: len(outs)], [(weight, 0, weight.shape[0])]


def kv_kernel(tok_ref, gain_ref, cos_ref, sin_ref, w_ref, normed_ref, kv_ref, first_ref, ks):
    source = tok_ref[:, : normed_ref.shape[1]].astype(F32)
    normed = (source * inverse_mean(source) * gain_ref[...]).astype(BF16)
    normed_ref[...] = normed
    raw = nn(normed, w_ref[...])
    ks[:, :KW] = raw[:, :KW]
    kv_ref[:, KW:] = raw[:, KW:].astype(BF16)
    rotate_into(kv_ref, ks, KW, cos_ref[...], sin_ref[...], 1.0)
    first_ref[...] = kv_ref[:GRAIN, :]


def project_kv(tokens, seqs, gain, cosine, sine, pieces, places):
    total, width = tokens.shape[0], gain.shape[1]
    rows = total // seqs
    outs = [
        rows_each(struct((total, width), BF16), rows),
        rows_each(struct((total, 2 * KW), BF16), rows),
        rows_each(struct((seqs * GRAIN, 2 * KW), BF16), GRAIN),
    ]
    return with_weight(
        kv_kernel,
        outs,
        (rows_each(tokens, rows), gain, cosine, sine),
        pieces,
        places,
        grid=(seqs,),
        scratch=[pltpu.VMEM((rows, wide(KW)), F32)],
        us=2.2,
    )


def q_kernel(normed_ref, cos_ref, sin_ref, w_ref, q_ref, qs):
    qs[:, :QW] = nn(normed_ref[...], w_ref[...])
    rotate_into(q_ref, qs, QW, cos_ref[...], sin_ref[...], HD**-0.5)


def project_q(normed, seqs, cosine, sine, pieces, places):
    total = normed.shape[0]
    rows = total // seqs
    return with_weight(
        q_kernel,
        [rows_each(struct((total, QW), BF16), rows)],
        (rows_each(normed, rows), cosine, sine),
        pieces,
        places,
        grid=(seqs,),
        scratch=[pltpu.VMEM((rows, wide(QW)), F32)],
        us=2.2,
    )


def residual_kernel(tok_ref, mixed_ref, gain_ref, w_ref, hidden_ref, normed_ref):
    hidden = tok_ref[:, : hidden_ref.shape[1]].astype(F32) + nn(mixed_ref[...], w_ref[...])
    hidden_ref[...] = hidden
    normed_ref[...] = (hidden * inverse_mean(hidden) * gain_ref[...]).astype(BF16)


def residual(tokens, seq, mixed, gain, pieces, places):
    rows, width = mixed.shape[0], gain.shape[1]
    return with_weight(
        residual_kernel,
        [struct((rows, width), F32), struct((rows, width), BF16)],
        (rows_at(tokens, seq, rows), mixed, gain),
        pieces,
        places,
        us=1.8,
    )


def marks(scal_ref, pos, valid):
    segment = jnp.zeros(pos.shape, jnp.int32)
    for d in range(2):
        segment += (pos >= scal_ref[0, d]).astype(jnp.int32)
    number = jnp.zeros(pos.shape, jnp.int32)
    for j in range(2):
        start = scal_ref[0, 2 + j]
        number += jnp.where((pos >= start) & (pos < start + PIECE), j + 1, 0)
    return jnp.where(valid, segment, -1), number


def bias_of(scal_ref, start, across):
    q_shape, k_shape, q_dim, k_dim = (
        ((GRAIN, 1), (1, SPAN), 0, 1) if across else ((1, GRAIN), (SPAN, 1), 1, 0)
    )
    q_pos = start + lax.broadcasted_iota(jnp.int32, q_shape, q_dim)
    k_pos = start - MAXDOC + lax.broadcasted_iota(jnp.int32, k_shape, k_dim)
    q_seg, q_num = marks(scal_ref, q_pos, q_pos >= 0)
    k_seg, k_num = marks(scal_ref, k_pos, (k_pos >= 0) & (k_pos < LEN))
    q_num = jnp.where(q_num > 0, q_num, -1)
    permit = (q_seg == k_seg) & ((k_pos <= q_pos) | (q_num == k_num))
    return jnp.where(permit, 0.0, NEG).astype(F32)


def load_window(window, parts):
    row = 0
    for part in parts:
        window[row : row + part.shape[0], :] = part[...]
        row += part.shape[0]


def head_columns(j):
    return [slice(h * HD, (h + 1) * HD) for h in range(j * GROUP, (j + 1) * GROUP)]


def attend_kernel(scal_ref, q_ref, far_ref, near_ref, own_ref, next_ref, mixed_ref, lse_ref, window):
    sub = pl.program_id(0)

    @pl.when(sub == 0)
    def _():
        load_window(window, (far_ref, near_ref, own_ref, next_ref))

    bias = bias_of(scal_ref, scal_ref[0, 4] + sub * GRAIN, True)
    bias = jnp.concatenate([bias] * GROUP, axis=0)
    rows = pl.ds(pl.multiple_of(sub * GRAIN, GRAIN), SPAN)
    lse = jnp.zeros((GRAIN, 128), F32)
    lane = lax.broadcasted_iota(jnp.int32, (GRAIN, 128), 1)
    for j in range(KVH):
        key = window[rows, j * HD : (j + 1) * HD]
        value = window[rows, KW + j * HD : KW + (j + 1) * HD]
        query = jnp.concatenate([q_ref[:, c] for c in head_columns(j)], axis=0)
        scores = nt(query, key) + bias
        top = jnp.max(scores, axis=-1, keepdims=True)
        raised = jnp.exp(scores - top)
        total = jnp.sum(raised, axis=-1, keepdims=True)
        out = nn(raised.astype(BF16), value) / total
        logsum = top + jnp.log(total)
        for g, c in enumerate(head_columns(j)):
            at = slice(g * GRAIN, (g + 1) * GRAIN)
            mixed_ref[:, c] = out[at].astype(BF16)
            lse = jnp.where(lane == j * GROUP + g, logsum[at], lse)
    lse_ref[...] = lse


def window_parts(windows, seq, rows):
    far, near, own, ahead = windows
    parts = [rows_at(a, seq, rows) for a in (far, near, own)]
    return (*parts, rows_at(ahead, seq, GRAIN))


def sub_rows(array, seq, rows):
    first = seq * (rows // GRAIN)
    return array, pl.BlockSpec((GRAIN, array.shape[1]), lambda i: (first + i, 0))


def attend(scal, q, seq, rows, windows):
    return call(
        attend_kernel,
        [rows_each(struct((rows, w), t), GRAIN) for w, t in ((QW, BF16), (128, F32))],
        (scal, sub_rows(q, seq, rows), *window_parts(windows, seq, rows)),
        grid=(rows // GRAIN,),
        scratch=[pltpu.VMEM((MAXDOC + rows + GRAIN, 2 * KW), BF16)],
        us=6.8,
    )


def attend_back_kernel(
    earlier,
    scal_ref,
    q_ref,
    far_ref,
    near_ref,
    own_ref,
    next_ref,
    mixed_ref,
    lse_ref,
    grad_ref,
    cos_ref,
    sin_ref,
    *refs,
):
    dq_ref, dfar_ref, dnear_ref, down_ref, dnext_ref, window, sums, qs = refs[earlier:]
    sub = pl.program_id(0)

    @pl.when(sub == 0)
    def _():
        load_window(window, (far_ref, near_ref, own_ref, next_ref))
        sums[...] = jnp.zeros_like(sums)

    bias = bias_of(scal_ref, scal_ref[0, 4] + sub * GRAIN, False)
    bias = jnp.concatenate([bias] * GROUP, axis=1)
    rows = pl.ds(pl.multiple_of(sub * GRAIN, GRAIN), SPAN)
    lane = lax.broadcasted_iota(jnp.int32, (GRAIN, 128), 1)
    product = mixed_ref[...].astype(F32) * grad_ref[...].astype(F32)
    delta = jnp.zeros((GRAIN, 128), F32)
    for h in range(H):
        share = jnp.sum(product[:, h * HD : (h + 1) * HD], axis=-1, keepdims=True)
        delta = jnp.where(lane == h, share, delta)
    delta = delta.T
    lse = lse_ref[...].T

    def heads(array, j):
        return jnp.concatenate([array[h : h + 1] for h in range(j * GROUP, (j + 1) * GROUP)], axis=1)

    for j in range(KVH):
        k_cols = slice(j * HD, (j + 1) * HD)
        v_cols = slice(KW + j * HD, KW + (j + 1) * HD)
        key, value = window[rows, k_cols], window[rows, v_cols]
        query = jnp.concatenate([q_ref[:, c] for c in head_columns(j)], axis=0)
        grad = jnp.concatenate([grad_ref[:, c] for c in head_columns(j)], axis=0)
        probs = jnp.exp(nt(key, query) + bias - heads(lse, j))
        grad_scores = (probs * (nt(value, grad) - heads(delta, j))).astype(BF16)
        sums[rows, v_cols] += nn(probs.astype(BF16), grad)
        sums[rows, k_cols] += nn(grad_scores, query)
        dq = tn(key, grad_scores).T
        for g, c in enumerate(head_columns(j)):
            qs[:, c] = dq[g * GRAIN : (g + 1) * GRAIN, :]
    rotate_into(dq_ref, qs, QW, cos_ref[...], -sin_ref[...], HD**-0.5)

    @pl.when(sub == pl.num_programs(0) - 1)
    def _():
        row = 0
        for part in (dfar_ref, dnear_ref, down_ref):
            part[...] = sums[row : row + part.shape[0], :].astype(part.dtype)
            row += part.shape[0]
        done = dnext_ref.shape[0] - GRAIN
        if earlier:
            dnext_ref[:done, :] = refs[0][...]
        dnext_ref[done:, :] = sums[row:, :].astype(BF16)


def attend_back(scal, q, seq, rows, windows, mixed, lse, grad, cosine, sine, earlier):
    window = MAXDOC + rows + GRAIN
    each = lambda a: rows_each(a, GRAIN)
    shapes = ((rows, BF16), (rows, BF16), (rows, F32), ((seq + 1) * GRAIN, BF16))
    return call(
        functools.partial(attend_back_kernel, len(earlier)),
        [each(struct((rows, QW), BF16)), *(struct((r, 2 * KW), t) for r, t in shapes)],
        (
            scal,
            sub_rows(q, seq, rows),
            *window_parts(windows, seq, rows),
            *map(each, (mixed, lse, grad, cosine, sine)),
            *earlier,
        ),
        grid=(rows // GRAIN,),
        scratch=[
            pltpu.VMEM((window, 2 * KW), BF16),
            pltpu.VMEM((window, 2 * KW), F32),
            pltpu.VMEM((GRAIN, wide(QW)), F32),
        ],
        us=11.7,
    )


def ff_kernel(nrm_a, nrm_b, cot_a, cot_b, w_ref, inner_ref, gg_ref, gu_ref, sum_a, sum_b):
    first = pl.program_id(0) == 0
    (rows, units), width = inner_ref.shape, w_ref.shape[0]
    wg, wu, wd = (w_ref[:, k * units : (k + 1) * units] for k in range(3))
    normed = jnp.where(first, nrm_a[...], nrm_b[...])
    gate = nn(normed, wg)
    up = nn(normed, wu)
    grad = nn(jnp.where(first, cot_a[:, :width], cot_b[:, :width]), wd)
    sigma = jax.nn.sigmoid(gate)
    raised = gate * sigma
    inner = (raised * up).astype(BF16)
    grad_gate = (grad * up * (sigma + raised * (1.0 - sigma))).astype(BF16)
    grad_up = (grad * raised).astype(BF16)
    inner_ref[...] = inner
    gg_ref[...] = grad_gate
    gu_ref[...] = grad_up
    grad_normed = (nt(grad_gate, wg) + nt(grad_up, wu)).astype(BF16)
    out = nt(inner, wd).astype(BF16)

    @pl.when(first)
    def _():
        sum_a[:rows, :width] = grad_normed
        sum_a[rows:, :width] = out

    @pl.when(jnp.logical_not(first))
    def _():
        sum_b[:rows, :width] = grad_normed
        sum_b[rows:, :width] = out


def ff(normed_pair, cot_pair, weights, seq):
    rows, width = normed_pair[0].shape
    units = weights.shape[1] // 3
    unit = lambda: rows_each(struct((2 * rows, units), BF16), rows)
    result = call(
        ff_kernel,
        [unit(), unit(), unit()] + [struct((2 * rows, wide(width)), BF16)] * 2,
        (*normed_pair, *(rows_at(c, seq, rows) for c in cot_pair), weights),
        grid=(2,),
        us=7.2,
    )
    return result[:3], result[3:]


def outer_kernel(counts, split, place_ref, *refs):
    acc = refs[-1]
    column = 0
    for lefts, rights, gains in counts:
        left_refs, refs = refs[:lefts], refs[lefts:]
        right_refs, refs = refs[:rights], refs[rights:]
        gain_refs, refs = refs[:gains], refs[gains:]
        width = right_refs[0].shape[-1]
        at = slice(column, column + width)
        join = lambda some, w: jnp.concatenate([r[:, :w] for r in some], axis=0)
        if lefts % rights:
            groups = [(left_refs, right_refs)]
        else:
            per = lefts // rights
            groups = [(left_refs[i * per : (i + 1) * per], [r]) for i, r in enumerate(right_refs)]
        for i, (some_left, some_right) in enumerate(groups):
            product = tn(join(some_left, acc.shape[0]), join(some_right, width))
            if i == 0:
                acc[:, at] = product
            else:
                acc[:, at] += product
        column += width
        if gains:
            total = functools.reduce(jnp.add, [g[...] for g in gain_refs])
            across = jnp.broadcast_to(total, (128, total.shape[1])).T
            stop = wide(column)
            acc[:, column:stop] = across[:, : stop - column]
            column = stop
    outs = refs[:-1]
    if split is None:
        outs[0][...] = acc[...]
        return
    keep_ref, send_ref = outs
    half = keep_ref.shape[0] if split == "shard" else keep_ref.shape[0] // 2
    for s in range(acc.shape[0] // (2 * half)):
        rows = slice(s * half, (s + 1) * half)
        keep_ref[rows, :] = acc[pl.ds(pl.multiple_of(2 * s * half + place_ref[0], 16), half), :]
        other = pl.ds(pl.multiple_of((2 * s + 1) * half - place_ref[0], 16), half)
        send_ref[rows, :] = acc[other, :].astype(BF16)


def outer(products, width, place, split, us, limit=VMEM_LIMIT):
    array = lambda operand: operand[0] if isinstance(operand, tuple) else operand
    full = 0
    for _, rights, gains in products:
        full += array(rights[0]).shape[1]
        full = wide(full) if gains else full
    if split is None:
        outs = [struct((width, full), F32)]
    else:
        outs = [struct((width // 2, full), F32), struct((width // 2, full), BF16)]
    args = [a for product in products for group in product for a in group]
    return call(
        functools.partial(outer_kernel, [tuple(map(len, p)) for p in products], split),
        outs,
        (place, *args),
        scratch=[pltpu.VMEM((width, full), F32)],
        us=us,
        limit=limit,
    )


def output_kernel(hidden_ref, *refs):
    total = hidden_ref[...]
    for term in refs[:-1]:
        total += term[:, : total.shape[1]].astype(F32)
    refs[-1][...] = total.T.astype(BF16)


def output_of(hidden, terms):
    rows, width = hidden.shape
    return call(output_kernel, [struct((width, rows), BF16)], (hidden, *terms), us=1.4)[0]


def ff_back_kernel(
    hidden_ref, cot_ref, a_ref, b_ref, c_ref, gain_ref, wo_ref, gh_ref, gb_ref, gm_ref, gg_ref
):
    hidden, gain = hidden_ref[...], gain_ref[...]
    factor = inverse_mean(hidden)
    width = hidden.shape[1]
    grad = sum(ref[:, :width].astype(F32) for ref in (a_ref, b_ref, c_ref))
    weighted = grad * gain
    back = factor * weighted - hidden * factor**3 * jnp.mean(
        hidden * weighted, axis=-1, keepdims=True
    )
    grad_hidden = cot_ref[:, :width].astype(F32) + back
    branch = grad_hidden.astype(BF16)
    gh_ref[...] = grad_hidden
    gb_ref[...] = branch
    gm_ref[...] = nt(branch, wo_ref[...]).astype(BF16)
    gg_ref[...] = jnp.sum(grad * hidden * factor, axis=0, keepdims=True)


def ff_back(hidden, cotangent, seq, terms, gain, wo):
    rows, width = hidden.shape
    outs = [
        struct((rows, width), F32),
        struct((rows, width), BF16),
        struct((rows, QW), BF16),
        struct((1, width), F32),
    ]
    return call(
        ff_back_kernel,
        outs,
        (hidden, rows_at(cotangent, seq, rows), *terms, gain, wo),
        us=1.8,
    )


def input_kernel(
    tok_ref,
    gh_ref,
    gq_ref,
    own_ref,
    left_ref,
    right_ref,
    gain_ref,
    wq_ref,
    wkv_ref,
    cos_ref,
    sin_ref,
    ig_ref,
    gkv_ref,
    ks,
):
    ks[...] = own_ref[...] + right_ref[...].astype(F32)
    ks[:GRAIN, :] += left_ref[...].astype(F32)
    gkv_ref[:, KW:] = ks[:, KW:].astype(BF16)
    rotate_into(gkv_ref, ks, KW, cos_ref[...], -sin_ref[...], 1.0)
    grad = nt(gq_ref[...], wq_ref[...]) + nt(gkv_ref[...], wkv_ref[...])
    source, gain = tok_ref[:, : gh_ref.shape[1]].astype(F32), gain_ref[...]
    factor = inverse_mean(source)
    weighted = grad * gain
    back = factor * weighted - source * factor**3 * jnp.mean(
        source * weighted, axis=-1, keepdims=True
    )
    ig_ref[...] = (gh_ref[...] + back).T


def input_back(tokens, seq, args):
    rows, width = args[0].shape
    return call(
        input_kernel,
        [struct((width, rows), F32), struct((rows, 2 * KW), BF16)],
        (rows_at(tokens, seq, rows), *args),
        scratch=[pltpu.VMEM((rows, 2 * KW), F32)],
        us=1.8,
    )


def add_kernel(*refs):
    total = refs[0][...].astype(F32)
    for ref in refs[1:-1]:
        total += ref[...].astype(F32)
    refs[-1][...] = total.astype(refs[-1].dtype)


def add_up(terms, shape, dtype):
    return call(add_kernel, [struct(shape, dtype)], terms, us=0.7)[0]


def side_kernel(*refs):
    width = refs[0].shape[1]
    for i, ref in enumerate(refs[:-1]):
        refs[-1][:, i * width : (i + 1) * width] = ref[...]


def side_by_side(*arrays):
    rows, width = arrays[0].shape
    return call(side_kernel, [struct((rows, len(arrays) * width), BF16)], arrays, us=0.8)[0]


def widen_kernel(all_ref, *outs):
    units = outs[0].shape[1]
    for i, out in enumerate(outs):
        out[...] = all_ref[:, i * units : (i + 1) * units].astype(F32)


def widen(value):
    rows, columns = value.shape
    return call(widen_kernel, [struct((rows, columns // 3), F32)] * 3, (value,), us=2.0)


def beside_kernel(left_ref, keep_ref, got_ref, out_ref):
    columns = left_ref.shape[1]
    out_ref[:, :columns] = left_ref[...]
    out_ref[:, columns:] = (keep_ref[...] + got_ref[...].astype(F32)).astype(BF16)


def set_beside(left, keep, got):
    shape = (left.shape[0], left.shape[1] + keep.shape[1])
    return call(beside_kernel, [struct(shape, BF16)], (left, keep, got), us=1.5)[0]


def pair_kernel(*refs):
    out = refs[-1]
    rows = refs[0].shape[0]
    for s in range(len(refs) // 2):
        total = refs[2 * s][...].astype(F32) + refs[2 * s + 1][...].astype(F32)
        out[s * rows : (s + 1) * rows, :] = total.astype(BF16)


def split_kernel(at_ref, keep_ref, got_ref, kept_ref, sent_ref, total):
    total[...] = keep_ref[...].astype(F32) + got_ref[...].astype(F32)
    half = kept_ref.shape[0]
    kept_ref[...] = total[pl.ds(pl.multiple_of(at_ref[0] * half, 8), half), :]
    sent_ref[...] = total[pl.ds(pl.multiple_of((1 - at_ref[0]) * half, 8), half), :].astype(BF16)


def split_sum(at, keep, got):
    shape = (keep.shape[0] // 2, keep.shape[1])
    return call(
        split_kernel,
        [struct(shape, F32), struct(shape, BF16)],
        (at, keep, got),
        scratch=[pltpu.VMEM(keep.shape, F32)],
        us=0.9,
    )


def put_halves(both, at_ref, own_ref, got_ref):
    half = own_ref.shape[0]
    if half == both.shape[0]:
        both[...] = own_ref[...].astype(F32)
        return
    for place, ref in ((at_ref[0], own_ref), (1 - at_ref[0], got_ref)):
        both[pl.ds(pl.multiple_of(place * half, 8), half), :] = ref[...].astype(F32)


def join_kernel(at_ref, own_ref, got_ref, out_ref, both):
    put_halves(both, at_ref, own_ref, got_ref)
    out_ref[...] = both[...].astype(out_ref.dtype)


def join_rows(at, own, got):
    shape = (2 * own.shape[0], own.shape[1])
    return call(
        join_kernel,
        [struct(shape, BF16)],
        (at, own, got),
        scratch=[pltpu.VMEM(shape, F32)],
        us=0.9,
    )[0]


def as_row(column):
    return jnp.broadcast_to(column, (column.shape[0], 128)).T[:1]


def finish_pair_kernel(at_ref, own_ref, got_ref, w_ref, out_ref, gain_ref, query_ref, sum_ref, both):
    put_halves(both, at_ref, own_ref, got_ref)
    width = out_ref.shape[1]
    out_ref[...] = both[:, :width]
    gain_ref[...] = as_row(both[:, width : width + 1])
    query = both[:, both.shape[1] - QW :]
    query_ref[...] = query
    sum_ref[...] = as_row(jnp.sum(query * w_ref[...].astype(F32), axis=-1, keepdims=True))


def finish_pair(at, own, got, weight, width):
    rows = weight.shape[0]
    return call(
        finish_pair_kernel,
        [struct(s, F32) for s in ((rows, width), (1, rows), (rows, QW), (1, rows))],
        (at, own, got, weight),
        scratch=[pltpu.VMEM((rows, own.shape[1]), F32)],
        us=1.5,
    )


def finish_kv_kernel(at_ref, own_ref, got_ref, w_ref, sum_ref, gain_ref, k_ref, v_ref, grad_ref, both):
    put_halves(both, at_ref, own_ref, got_ref)
    k_ref[...] = both[:, :KW].T
    v_ref[...] = both[:, KW:].T
    rest = as_row(jnp.sum(both[...] * w_ref[...].astype(F32), axis=-1, keepdims=True))
    grad_ref[...] = (sum_ref[...] + rest) / gain_ref[...]


def finish_kv(at, own, got, weight, sums, gain):
    rows = weight.shape[0]
    return call(
        finish_kv_kernel,
        [struct(s, F32) for s in ((KW, rows), (KW, rows), (1, rows))],
        (at, own, got, weight, sums, gain),
        scratch=[pltpu.VMEM((rows, own.shape[1]), F32)],
        us=1.5,
    )


def program(mesh):
    shards, ctxs = mesh.shape["shard"], mesh.shape["ctx"]

    def swap(value, axis, bit):
        count = mesh.shape[axis]
        return lax.ppermute(value, axis, [(i, i ^ bit) for i in range(count)])

    def shift(value, by):
        pairs = [(i, i + by) for i in range(ctxs) if 0 <= i + by < ctxs]
        return lax.ppermute(value, "ctx", pairs)

    def place_of(index):
        return index.astype(jnp.int32)[None]

    def over_shard(terms):
        return lax.psum_scatter(terms[0], "shard", scatter_dimension=0, tiled=True)

    def reduce_units(terms, finish):
        if shards != 2:
            return finish(over_shard(terms), None)
        keep, send = terms
        got = swap(send, "shard", 1)
        yield got
        return finish(keep, got)

    def all_over_ctx(value):
        part = lax.psum_scatter(value, "ctx", scatter_dimension=0, tiled=True)
        return lax.all_gather(part, "ctx", axis=0, tiled=True)

    def reduce_attention(terms, finish):
        zero = jnp.zeros((1,), jnp.int32)
        if shards != 2:
            total = lax.psum(over_shard(terms), ("ctx", "tp"))
            return finish(zero, total, total)
        tp = lax.axis_index("tp")
        mine, core, row = map(place_of, (lax.axis_index("shard"), tp % 2, tp // 2))
        held, low = terms
        got = swap(low, "tp", 1)
        yield got
        held, low = split_sum(mine, held, got)
        got = swap(low, "shard", 1)
        yield got
        held, low = split_sum(row, held, got)
        got = swap(low, "tp", 2)
        yield got
        low = add_up((held, got), held.shape, BF16)
        bit = 1
        while bit < ctxs:
            got = swap(low, "ctx", bit)
            yield got
            low = add_up((low, got), low.shape, BF16)
            bit *= 2
        got = swap(low, "tp", 2)
        yield got
        low = join_rows(row, low, got)
        got = swap(low, "tp", 1)
        yield got
        return finish(core, low, got)

    def per_device(
        tokens,
        cotangent,
        piece_starts,
        doc_lengths,
        attn_gain,
        w_query,
        w_key,
        w_value,
        w_out,
        ff_gain,
        w_gate,
        w_up,
        w_down,
    ):
        Order.last, Order.awaited = None, ()
        seqs, rows, width = tokens.shape
        offset = (lax.axis_index("ctx") * rows).astype(jnp.int32)
        mine, tp = lax.axis_index("shard"), lax.axis_index("tp")
        core, row = tp % 2, tp // 2
        every = range(seqs)
        last = seqs - 1

        (tokens,) = prepare(tokens.transpose(0, 2, 1))
        cosine, sine = rotary_tables(offset, rows)
        ends = jnp.cumsum(doc_lengths, axis=1)[:, :-1]
        scal = jnp.concatenate(
            [ends, piece_starts, jnp.broadcast_to(offset, (seqs, 1))], axis=1
        ).astype(jnp.int32)
        scals = [scal[s : s + 1] for s in every]

        w_kv = jnp.concatenate([w_key, w_value], axis=1)
        gains = jnp.stack([attn_gain, ff_gain])
        if shards == 2:
            full = w_query.shape[0]
            half = full // 2
            span = -(-half // 32) * 16
            other = (1 - mine) * full
            near_rows, far_rows = other + core * half, other + (1 - core) * half
            step, back = row * (half - span), (1 - row) * (half - span)
            kv_places = jnp.stack([mine * full, near_rows, far_rows]).astype(jnp.int32)
            places = [near_rows + step, near_rows + back, far_rows + step, far_rows + back]
            places = jnp.stack([mine * full, *places]).astype(jnp.int32)
            quarter = lambda w: lax.dynamic_slice_in_dim(w, core * half + step, span)

            got = swap(gains, "shard", 1)
            all_gains = jnp.where(
                mine == 0,
                jnp.concatenate([gains, got], axis=1),
                jnp.concatenate([got, gains], axis=1),
            )
            kv_part = swap(lax.dynamic_slice_in_dim(w_kv, core * half, half), "shard", 1)
            kv_beside = swap(in_turn(kv_part), "tp", 1)
            kv_pieces = [(w_kv, 0, full), (kv_part, 0, half), (kv_beside, 0, half)]
            two = jnp.concatenate([quarter(w_query), quarter(w_out)], axis=0)
            two_x = swap(after(two, kv_part), "shard", 1)
        else:
            gather = lambda w: lax.all_gather(w, "shard", axis=0, tiled=True)
            kv_places = places = jnp.zeros((1,), jnp.int32)
            all_gains = lax.all_gather(gains, "shard", axis=1, tiled=True)
            kv_pieces = [(gather(w_kv), 0, width)]
        gain_one, gain_two = all_gains[:1].astype(F32), all_gains[1:].astype(F32)

        (normed_one, kv, first), kv_pieces = project_kv(
            tokens, seqs, gain_one, cosine, sine, kv_pieces, kv_places
        )
        wkv = kv_pieces[0][0]
        near, ahead = shift(kv, 1), shift(first, -1)
        (cotangent,) = prepare(cotangent.transpose(0, 2, 1))
        if shards == 2:
            two_x = in_turn(two_x)
            two_y, two_beside = swap(two_x, "tp", 2), swap(two_x, "tp", 1)
        ff_weights = lax.all_gather(side_by_side(w_gate, w_up, w_down), "shard", axis=0, tiled=True)
        if shards == 2:
            two_y = in_turn(two_y)
            parts = (two_x, two_y, two_beside, swap(two_y, "tp", 1))
            q_pieces = [(w_query, 0, full), *((p, 0, span) for p in parts)]
            out_pieces = [(w_out, 0, full), *((p, span, span) for p in parts)]
        else:
            q_pieces, out_pieces = ([(gather(w), 0, width)] for w in (w_query, w_out))
            two_y = w_query
        windows = (shift(in_turn(near), 1), near, kv, ahead)
        cot_y = swap(after(cotangent, two_y, near), "tp", 2)
        arrive(ahead)
        (query,), q_pieces = project_q(normed_one, seqs, cosine, sine, q_pieces, places)
        wq = q_pieces[0][0]
        cot_core = swap(in_turn(cotangent), "tp", 1)

        mixed, lse, hidden, normed_rows = [], [], [], []
        for s in every:
            if s == 1:
                cot_y = in_turn(cot_y)
                cot_diagonal = swap(cot_y, "tp", 1)
            m, l = attend(scals[s], query, s, rows, windows)
            if s == 0:
                arrive(cot_core)
            else:
                arrive(normed_rows[-1][1])
            if s == 1:
                arrive(cot_diagonal)
            (h, own), out_pieces = residual(tokens, s, m, gain_two, out_pieces, places)
            normed_rows.append((own, swap(own, "tp", 1), swap(own, "tp", 2)))
            mixed.append(m)
            lse.append(l)
            hidden.append(h)
        wo = out_pieces[0][0]
        if seqs == 1:
            cot_diagonal = swap(cot_y, "tp", 1)
        cots = (cotangent, cot_core, cot_y, cot_diagonal)

        row_blocks, units, near_sums, far_sums = [], [], [], []
        grad_at = lambda a: rows_at(a, 0, rows)
        out_at = lambda a: rows_at(a, 1, rows)

        def cross_grad(s):
            partial = add_up([grad_at(a) for a in far_sums[s]], (rows, wide(width)), BF16)
            return (*map(grad_at, near_sums[s]), swap(partial, "tp", 2))

        grad_terms = []
        for s in every:
            own, beside, facing = normed_rows[s]
            diagonal = swap(in_turn(facing), "tp", 1)
            if s > 0:
                arrive(near_sums[s - 1][1])
            unit, (a, b) = ff((own, beside), cots[:2], ff_weights, s)
            near_sums.append((a, swap(b, "tp", 1)))
            units.append(unit)
            if s > 0:
                grad_terms.append(cross_grad(s - 1))
            arrive(*(n[1] for n in normed_rows[s + 1 : s + 2]))
            unit, (a, b) = ff((facing, diagonal), cots[2:], ff_weights, s)
            far_sums.append((a, swap(b, "tp", 1)))
            units.append(unit)
            row_blocks += [own, beside, facing, diagonal]

        by_shard, by_core = ("shard", "core") if shards == 2 else (None, None)
        shard_place, core_place = place_of(mine * (width // 2)), place_of(core * (width // 4))
        cot_lefts = [rows_at(c, s, rows) for s in every for c in cots]

        def unit_product(lefts, k):
            return lefts, [u[k] for u in units], ()

        arrive(near_sums[last][1])
        def down_sum(keep, got):
            if got is None:
                return keep.astype(BF16)
            return add_up((keep, got), keep.shape, BF16)

        def units_sum(keep, got):
            left = down.finish()
            if got is None:
                return jnp.concatenate([left, keep.astype(BF16)], axis=1)
            return set_beside(left, keep, got)

        down_grad = outer([unit_product(cot_lefts, 0)], width, shard_place, by_shard, 5.0)
        down = Chain(reduce_units(down_grad, down_sum))
        grad_terms.append(cross_grad(last))
        both = [unit_product(row_blocks, 1), unit_product(row_blocks, 2)]
        arrive(*(t[2] for t in grad_terms[:-1]))
        gate_up_grad = outer(both, width, shard_place, by_shard, 10.0, 2 * VMEM_LIMIT)
        gate_up = Chain(reduce_units(gate_up_grad, units_sum))
        out_terms = [out_at(a) for s in every for a in far_sums[s]]
        out_partial = call(
            pair_kernel, [struct((seqs * rows, wide(width)), BF16)], out_terms, us=0.9
        )[0]
        outs_got = swap(after(out_partial, grad_terms[last][2]), "tp", 2)

        branch, gain_two_grad, grad_hidden = [], [], []
        backs, input_grads, gkv = [], [], []
        ahead_grads = ()

        def mixed_back(s, ahead_grads):
            gh, gb, gm, gg = ff_back(hidden[s], cotangent, s, grad_terms[s], gain_two, wo)
            grad_hidden.append(gh)
            branch.append(gb)
            gain_two_grad.append(gg)
            dq, dfar, dnear, own, dnext = attend_back(
                scals[s], query, s, rows, windows, mixed[s], lse[s], gm, cosine, sine, ahead_grads
            )
            backs.append((dq, dnear, own, shift(dfar, -1)))
            return (dnext,)

        def pass_on(s):
            dq, dnear, own, passed = backs[s]
            backs[s] = dq, own, shift(add_up((dnear, passed), dnear.shape, BF16), -1)

        def rows_back(s):
            dq, own, right = backs[s]
            args = (grad_hidden[s], dq, own, rows_at(left, s, GRAIN), right)
            args += (gain_one, wq, wkv, cosine, sine)
            input_grad, g = input_back(tokens, s, args)
            input_grads.append(input_grad)
            gkv.append(g)

        for s in every:
            ahead_grads = mixed_back(s, ahead_grads)
            if s == 0:
                down.step()
                down.finish()
        left = shift(ahead_grads[0], 1)
        for s in every[:-1]:
            pass_on(s)
        arrive(outs_got)
        gate_up.step()
        unit_sums = all_over_ctx(gate_up.finish())
        pass_on(last)
        grads = [b[0] for b in backs]
        pair = Chain(
            reduce_attention(
                outer(
                    [(mixed, branch, gain_two_grad), ([normed_one], grads, ())],
                    width,
                    core_place,
                    by_core,
                    2.7,
                    2 * VMEM_LIMIT,
                ),
                lambda at, own, got: finish_pair(at, own, got, w_query, width),
            )
        )
        outputs = []
        for s in every:
            near_terms = [out_at(a) for a in near_sums[s]]
            outputs.append(output_of(hidden[s], (*near_terms, rows_at(outs_got, s, rows))))
        pair.step()
        for s in every:
            rows_back(s)
        pair.step()
        finish_last = lambda at, own, got: (at, own, got)
        keys = Chain(
            reduce_attention(
                outer([([normed_one], gkv, ())], width, core_place, by_core, 1.1), finish_last
            )
        )
        for chain in (keys, pair, keys, pair, keys):
            chain.step()
        for chain in (pair, keys):
            chain.step()
        sum_down, sum_gate, sum_up = widen(unit_sums)
        for chain in (pair, keys, pair, keys):
            chain.step()
        sum_out, sum_gain_two, sum_query, products = pair.finish()
        keys_done = keys.finish()
        sum_key, sum_value, sum_gain_one = finish_kv(
            *keys_done, w_kv, products, gains[:1].astype(F32)
        )
        join = lambda blocks: jnp.stack(blocks).transpose(0, 2, 1)
        return (
            join(outputs),
            join(input_grads),
            sum_gain_one[0],
            sum_query,
            sum_key.T,
            sum_value.T,
            sum_out,
            sum_gain_two[0],
            sum_gate,
            sum_up,
            sum_down,
        )

    return per_device


def solution(mesh):
    rows = P(("shard", "tp"), "ctx", None)
    seq = P(("shard", "tp"), None)
    gain, weight, ff_weight = P("shard"), P("shard", None), P("shard", "tp")
    weights = (gain, weight, weight, weight, weight, gain, ff_weight, ff_weight, ff_weight)
    return jax.shard_map(
        program(mesh),
        mesh=mesh,
        in_specs=(rows, rows, seq, seq, *weights),
        out_specs=(rows, rows, *weights),
        check_vma=False,
    )
```

time: 423 us -> 386 us (0.913)
  other arithmetic: 37 us -> 4.86 us
  local copies, waits for them, and re-layouts: 62.2 us -> 39.5 us
  Pallas kernels: 111 us -> 130 us
  waiting for transfers between devices: 108 us -> 124 us
  starting transfers between devices: 80.8 us -> 68.1 us
    ppermute x56 -> x39, waiting for transfers between devices: 73.3 us -> 108 us  [swap(): return lax.ppermute(value, axis, [(i, i ^ bit) for i in range(count)])]
    psum x2 -> x0, waiting for transfers between devices: 31.1 us -> none  [the longest x1 23.2 us: per_device(): sum_gate, sum_up = lax.psum(after(sums, sum_down, kv_grad[0]), 'ctx')]
    convert_element_type x24 -> x2, other arithmetic: 21.2 us -> 0.01 us  [the longest x1 0.01 us: per_device(): gain_one, gain_two = (all_gains[:1].astype(F32), all_gains[1:].astype(F32))]
    pallas_call x29 -> x47, Pallas kernels: 111 us -> 130 us  [call(): pl.pallas_call(kernel, out_shape=shapes, grid=grid, in_specs=in_specs, ou...]
    ppermute x12 -> x8, starting transfers between devices: 31.5 us -> 20.1 us  [shift(): return lax.ppermute(value, 'ctx', pairs)]
    ppermute x12 -> x8, waiting for transfers between devices: 3.9 us -> 15 us  [shift(): return lax.ppermute(value, 'ctx', pairs)]
    unnamed x245 -> x204, local copies, waits for them, and re-layouts: 45.5 us -> 38.3 us
    ppermute x3 -> x0, local copies, waits for them, and re-layouts: 5.98 us -> none  [swap(): return lax.ppermute(value, axis, [(i, i ^ bit) for i in range(count)])]
  transfers between devices with their start and end apart: 71 -> 50, of which waited for: 19 -> 15; matrix products, arithmetic and copies ran while one was open for 12% -> 2% of each run, Pallas kernels for 25% -> 33%
where the time goes in v4:
time: 386 us; the launch traced here: 381 us
  Pallas kernels  130 us (34%)
  waiting for transfers between devices  124 us (32%)
  starting transfers between devices  68.1 us (18%)
  local copies, waits for them, and re-layouts  39.5 us (10%)
  between operations  15.1 us (4%)
  other arithmetic  4.86 us (1%)
    pallas_call x47, Pallas kernels, call(): pl.pallas_call(kernel, out_shape=shapes, grid=grid, in_specs=in_specs, ou...  130 us
    ppermute x39, waiting for transfers between devices, swap(): return lax.ppermute(value, axis, [(i, i ^ bit) for i in range(count)])  108 us
    ppermute x39, starting transfers between devices, swap(): return lax.ppermute(value, axis, [(i, i ^ bit) for i in range(count)])  47.7 us
    unnamed x204, local copies, waits for them, and re-layouts  38.3 us
    ppermute x8, starting transfers between devices, shift(): return lax.ppermute(value, 'ctx', pairs)  20.1 us
    ppermute x8, waiting for transfers between devices, shift(): return lax.ppermute(value, 'ctx', pairs)  15 us
  transfers between devices with their start and end apart: 50, of which 15 were waited for; matrix products, arithmetic and copies ran while one was open for 2% of the time, Pallas kernels for 33%

profile of v4, /device:TPU:1, one launch (start us, length us, event | category | flops | bytes accessed | tf_op | source)
XLA Modules:
  0.0 380.8 jit_solution(8951479952194829935)
XLA Ops:
  7.3 1.3 copy.29
  9.9 2.1 collective-permute-start.1
  16.5 2.5 collective-permute-done.1.refs_5_
  20.4 1.5 collective-permute-start.4
  23.2 3.0 shard_map.213
  28.9 4.2 %collective-permute-start.8 = (bf16[512,640]{1,0:T(8,128)(2,1)}, bf16[512,640]{1,0:T(8,128)(2,1)}, u32[]{:S(2)}, u32[]{:S(2)}) collective-permute-start(bf16[512,640]{1,0:T(8,128)(2,1)} %get-tuple-element.162.own_ref), channel_id=1, source_target_pairs={{0,4},{4,8},{8,12},{1,5},{5,9},{9,13},{2,6},{6,10},{10,14},{3,7},{... | collective-permute-start | bytes 1966088 | tf_op jit(solution)/shard_map/ppermute | solution.py:791
  34.2 1.5 collective-permute-start.5
  35.7 1.4 shard_map.215
  38.2 8.7 %collective-permute-done.5.refs_5_ = bf16[256,960]{1,0:T(8,128)(2,1)S(1)} collective-permute-done((bf16[256,960]{1,0:T(8,128)(2,1)S(1)}, bf16[256,960]{1,0:T(8,128)(2,1)S(1)}, u32[]{:S(2)}, u32[]{:S(2)}) %collective-permute-start.5) | collective-permute-done | bytes 491552 | tf_op jit(solution)/shard_map/ppermute | solution.py:787
  46.9 1.7 collective-permute-start.7
  48.8 1.3 collective-permute-start.3
  50.4 10.1 %collective-permute-done.3.next_ref = bf16[256,640]{1,0:T(8,128)(2,1)} collective-permute-done((bf16[256,640]{1,0:T(8,128)(2,1)}, bf16[256,640]{1,0:T(8,128)(2,1)}, u32[]{:S(2)}, u32[]{:S(2)}) %collective-permute-start.3) | collective-permute-done | bytes 327712 | tf_op jit(solution)/shard_map/ppermute | solution.py:791
  60.5 3.5 collective-permute-start.9
  64.0 1.3 collective-permute-start.12
  66.6 3.4 shard_map.216
  71.3 1.3 collective-permute-start.10
  72.6 4.8 %collective-permute-done.9.far_ref = bf16[512,640]{1,0:T(8,128)(2,1)S(1)} collective-permute-done((bf16[512,640]{1,0:T(8,128)(2,1)}, bf16[512,640]{1,0:T(8,128)(2,1)S(1)}, u32[]{:S(2)}, u32[]{:S(2)}) %collective-permute-start.9) | collective-permute-done | bytes 655392 | tf_op jit(solution)/shard_map/ppermute | solution.py:791
  77.4 7.2 %shard_map.217 = (bf16[256,960]{1,0:T(8,128)(2,1)S(1)}, f32[256,128]{1,0:T(8,128)S(1)}) custom-call(s32[1,5]{1,0:T(1,128)S(1)} %get-tuple-element.294.scal_ref, bf16[512,960]{1,0:T(8,128)(2,1)S(1)} %get-tuple-element.220.q_ref, bf16[512,640]{1,0:T(8,128)(2,1)S(1)} %collective-permute-done.9.far_ref, bf16[512,640]{1,0:T(8,128)(2,1)} %collective-permute-done.8.near_ref, ...), custom_call_target="tpu_custom_call" | custom-call | flops 78199996416 | tf_op jit(solution)/shard_map/pallas_call | solution.py:101
  85.5 2.2 shard_map.218
  89.6 1.7 collective-permute-start.11
  92.8 7.0 %shard_map.219 = (bf16[256,960]{1,0:T(8,128)(2,1)S(1)}, f32[256,128]{1,0:T(8,128)S(1)}) custom-call(s32[1,5]{1,0:T(1,128)S(1)} %get-tuple-element.295.scal_ref, bf16[512,960]{1,0:T(8,128)(2,1)S(1)} %get-tuple-element.220.q_ref, bf16[512,640]{1,0:T(8,128)(2,1)S(1)} %collective-permute-done.9.far_ref, bf16[512,640]{1,0:T(8,128)(2,1)} %collective-permute-done.8.near_ref, ...), custom_call_target="tpu_custom_call" | custom-call | flops 78199996416 | tf_op jit(solution)/shard_map/pallas_call | solution.py:101
  100.9 2.2 shard_map.220
  105.9 2.0 copy-done.11
  109.2 5.7 %shard_map.221 = (bf16[512,640]{1,0:T(8,128)(2,1)S(1)}, bf16[512,640]{1,0:T(8,128)(2,1)S(1)}, bf16[512,640]{1,0:T(8,128)(2,1)S(1)}, bf16[512,1024]{1,0:T(8,128)(2,1)S(1)}, bf16[512,1024]{1,0:T(8,128)(2,1)S(1)}) custom-call(bf16[256,960]{1,0:T(8,128)(2,1)S(1)} %get-tuple-element.197.nrm_a.refs_0_.refs_12_, ...), custom_call_target="tpu_custom_call" | custom-call | flops 82800001024 | tf_op jit(solution)/shard_map/pallas_call | solution.py:101
  115.2 7.1 %shard_map.222 = (bf16[512,640]{1,0:T(8,128)(2,1)S(1)}, bf16[512,640]{1,0:T(8,128)(2,1)S(1)}, bf16[512,640]{1,0:T(8,128)(2,1)S(1)}, bf16[512,1024]{1,0:T(8,128)(2,1)S(1)}, bf16[512,1024]{1,0:T(8,128)(2,1)S(1)}) custom-call(bf16[256,960]{1,0:T(8,128)(2,1)S(1)} %collective-permute-done.15.nrm_a.refs_2_.refs_14_, ...), custom_call_target="tpu_custom_call" | custom-call | flops 82800001024 | tf_op jit(solution)/shard_map/pallas_call | solution.py:101
  123.8 6.9 %shard_map.223 = (bf16[512,640]{1,0:T(8,128)(2,1)S(1)}, bf16[512,640]{1,0:T(8,128)(2,1)S(1)}, bf16[512,640]{1,0:T(8,128)(2,1)S(1)}, bf16[512,1024]{1,0:T(8,128)(2,1)S(1)}, bf16[512,1024]{1,0:T(8,128)(2,1)S(1)}) custom-call(bf16[256,960]{1,0:T(8,128)(2,1)} %get-tuple-element.184.nrm_a.refs_4_.refs_16_, ...), custom_call_target="tpu_custom_call" | custom-call | flops 82800001024 | tf_op jit(solution)/shard_map/pallas_call | solution.py:101
  134.5 7.1 %shard_map.225 = (bf16[512,640]{1,0:T(8,128)(2,1)S(1)}, bf16[512,640]{1,0:T(8,128)(2,1)S(1)}, bf16[512,640]{1,0:T(8,128)(2,1)S(1)}, bf16[512,1024]{1,0:T(8,128)(2,1)S(1)}, bf16[512,1024]{1,0:T(8,128)(2,1)S(1)}) custom-call(bf16[256,960]{1,0:T(8,128)(2,1)} %collective-permute-done.14.nrm_a.refs_6_.refs_18_, ...), custom_call_target="tpu_custom_call" | custom-call | flops 82800001024 | tf_op jit(solution)/shard_map/pallas_call | solution.py:101
  143.2 4.3 %shard_map.226 = (f32[480,640]{1,0:T(8,128)S(1)}, bf16[480,640]{1,0:T(8,128)(2,1)}) custom-call(s32[1]{0:T(128)} %bitcast.place_ref, bf16[512,1024]{1,0:T(8,128)(2,1)S(1)} %shard_map.214.cot_a.refs_0_.refs_4_.cot_ref, bf16[512,1024]{1,0:T(8,128)(2,1)S(1)} %copy-done.24, bf16[512,1024]{1,0:T(8,128)(2,1)S(1)} %copy-done.21, bf16[512,1024]{1,0:T(8,128)(2,1)S(1)} %copy-done.26, ...), custom_call_target="tpu_custom_call" | custom-call | flops 57500000256 | tf_op jit(solution)/shard_map/pallas_call | solution.py:101
  149.8 10.1 %shard_map.228 = (f32[480,1280]{1,0:T(8,128)S(1)}, bf16[480,1280]{1,0:T(8,128)(2,1)}) custom-call(s32[1]{0:T(128)} %bitcast.place_ref, bf16[256,960]{1,0:T(8,128)(2,1)S(1)} %get-tuple-element.197.nrm_a.refs_0_.refs_12_, bf16[256,960]{1,0:T(8,128)(2,1)S(1)} %collective-permute-done.11.nrm_b.refs_1_.refs_13_, ...), custom_call_target="tpu_custom_call" | custom-call | flops 115000000512 | tf_op jit(solution)/shard_map/pallas_call | solution.py:101
  162.5 2.5 shard_map.230
  165.0 12.6 %shard_map.231 = (bf16[256,960]{1,0:T(8,128)(2,1)S(1)}, bf16[256,640]{1,0:T(8,128)(2,1)}, bf16[256,640]{1,0:T(8,128)(2,1)S(1)}, f32[256,640]{1,0:T(8,128)S(1)}, bf16[128,640]{1,0:T(8,128)(2,1)S(1)}) custom-call(s32[1,5]{1,0:T(1,128)S(1)} %get-tuple-element.294.scal_ref, bf16[512,960]{1,0:T(8,128)(2,1)S(1)} %copy-done.80, bf16[512,640]{1,0:T(8,128)(2,1)S(1)} %copy-done.32, ...), custom_call_target="tpu_custom_call" | custom-call | flops 134550003712 | tf_op jit(solution)/shard_map/pallas_call | solution.py:101
  178.5 1.3 collective-permute-start.26
  182.6 2.4 shard_map.233
  185.1 11.9 %shard_map.234 = (bf16[256,960]{1,0:T(8,128)(2,1)S(1)}, bf16[256,640]{1,0:T(8,128)(2,1)S(1)}, bf16[256,640]{1,0:T(8,128)(2,1)S(1)}, f32[256,640]{1,0:T(8,128)S(1)}, bf16[256,640]{1,0:T(8,128)(2,1)S(1)}) custom-call(s32[1,5]{1,0:T(1,128)S(1)} %get-tuple-element.295.scal_ref, bf16[512,960]{1,0:T(8,128)(2,1)S(1)} %copy-done.80, ...), custom_call_target="tpu_custom_call" | custom-call | flops 134550003712 | tf_op jit(solution)/shard_map/pallas_call | solution.py:101
  197.0 1.3 collective-permute-start.29
  199.4 1.3 collective-permute-start.32
  200.8 6.0 %collective-permute-start.31 = (bf16[256,640]{1,0:T(8,128)(2,1)S(1)}, bf16[256,640]{1,0:T(8,128)(2,1)S(1)}, u32[]{:S(2)}, u32[]{:S(2)}) collective-permute-start(bf16[256,640]{1,0:T(8,128)(2,1)S(1)} %get-tuple-element.247), channel_id=1, source_target_pairs={{0,4},{4,8},{8,12},{1,5},{5,9},{9,13},{2,6},{6,10},{10,14},{3,7},{... | collective-permute-start | bytes 983048 | tf_op jit(solution)/shard_map/ppermute | solution.py:791
  206.8 1.4 collective-permute-done.28.got_ref
  208.1 2.8 shard_map.236
  220.8 2.7 shard_map.238
  223.5 1.5 collective-permute-start.30
  225.0 1.5 shard_map.239
  227.0 1.4 shard_map.240
  231.6 1.7 shard_map.242
  233.9 2.7 shard_map.243
  236.6 19.8 %collective-permute-done.34.got_ref = bf16[240,1984]{1,0:T(8,128)(2,1)S(1)} collective-permute-done((bf16[240,1984]{1,0:T(8,128)(2,1)S(1)}, bf16[240,1984]{1,0:T(8,128)(2,1)S(1)}, u32[]{:S(2)}, u32[]{:S(2)}) %collective-permute-start.34) | collective-permute-done | bytes 952352 | tf_op jit(solution)/shard_map/ppermute | solution.py:787
  263.2 9.7 %collective-permute-done.36.refs_1_ = bf16[120,1984]{1,0:T(8,128)(2,1)S(1)} collective-permute-done((bf16[120,1984]{1,0:T(8,128)(2,1)S(1)}, bf16[120,1984]{1,0:T(8,128)(2,1)S(1)}, u32[]{:S(2)}, u32[]{:S(2)}) %collective-permute-start.36) | collective-permute-done | bytes 476192 | tf_op jit(solution)/shard_map/ppermute | solution.py:787
  272.9 3.4 collective-permute-start.38
  278.5 1.3 collective-permute-start.39
  279.8 7.3 %collective-permute-done.38.refs_1_ = bf16[120,1984]{1,0:T(8,128)(2,1)} collective-permute-done((bf16[120,1984]{1,0:T(8,128)(2,1)S(1)}, bf16[120,1984]{1,0:T(8,128)(2,1)}, u32[]{:S(2)}, u32[]{:S(2)}) %collective-permute-start.38) | collective-permute-done | bytes 476192 | tf_op jit(solution)/shard_map/ppermute | solution.py:787
  288.3 5.5 %collective-permute-start.40 = (bf16[120,1984]{1,0:T(8,128)(2,1)S(1)}, bf16[120,1984]{1,0:T(8,128)(2,1)S(1)}, u32[]{:S(2)}, u32[]{:S(2)}) collective-permute-start(bf16[120,1984]{1,0:T(8,128)(2,1)S(1)} %shard_map.249.refs_0_), channel_id=1, source_target_pairs={{0,8},{4,12},{8,0},{12,4},{1,9},{5,13},{9,1},{13,5},{2,10},{6,14},... | collective-permute-start | bytes 1428488 | tf_op jit(solution)/shard_map/ppermute | solution.py:787
  293.8 2.9 collective-permute-start.41
  296.7 41.4 %collective-permute-done.40.refs_1_ = bf16[120,1984]{1,0:T(8,128)(2,1)S(1)} collective-permute-done((bf16[120,1984]{1,0:T(8,128)(2,1)S(1)}, bf16[120,1984]{1,0:T(8,128)(2,1)S(1)}, u32[]{:S(2)}, u32[]{:S(2)}) %collective-permute-start.40) | collective-permute-done | bytes 476192 | tf_op jit(solution)/shard_map/ppermute | solution.py:787
  338.3 1.3 collective-permute-start.42
  340.3 1.5 copy-done.13
  341.8 2.0 shard_map.253
  343.8 4.9 %collective-permute-done.42.got_ref = bf16[120,1984]{1,0:T(8,128)(2,1)} collective-permute-done((bf16[120,1984]{1,0:T(8,128)(2,1)S(1)}, bf16[120,1984]{1,0:T(8,128)(2,1)}, u32[]{:S(2)}, u32[]{:S(2)}) %collective-permute-start.42) | collective-permute-done | bytes 476192 | tf_op jit(solution)/shard_map/ppermute | solution.py:787
  350.0 3.4 collective-permute-start.44
  353.4 9.8 %collective-permute-done.43.refs_1_ = bf16[120,640]{1,0:T(8,128)(2,1)S(1)} collective-permute-done((bf16[120,640]{1,0:T(8,128)(2,1)S(1)}, bf16[120,640]{1,0:T(8,128)(2,1)S(1)}, u32[]{:S(2)}, u32[]{:S(2)}) %collective-permute-start.43) | collective-permute-done | bytes 153632 | tf_op jit(solution)/shard_map/ppermute | solution.py:787
  363.2 1.5 collective-permute-start.45
  364.7 2.6 shard_map.256
  368.5 1.3 collective-permute-start.46
  370.9 1.4 maximum_bitcast_fusion
  372.3 1.7 shard_map.258
  (312 shorter events, 71.1 us)
Async XLA Ops:
  7.2 98.7 %all-gather.3.cloned.1.call-start = ((), (), s32[]{:S(2)}) async-start(), calls=%async_computation.1 | async-start | bytes 5529600 | tf_op jit(solution)/shard_map/all_gather | solution.py:913
  9.9 9.1 %collective-permute-start.1 = (bf16[240,640]{1,0:T(8,128)(2,1)S(1)}, bf16[240,640]{1,0:T(8,128)(2,1)S(1)}, u32[]{:S(2)}, u32[]{:S(2)}) collective-permute-start(bf16[240,640]{1,0:T(8,128)(2,1)S(1)} %fusion), channel_id=1, source_target_pairs={{0,16},{16,0},{1,17},{17,1},{2,18},{18,2},{3,19},{19,3},{4,20},{20... | collective-permute-start | bytes 921608 | tf_op jit(solution)/shard_map/ppermute | solution.py:787
  12.1 8.2 %collective-permute-start = (bf16[2,480]{1,0:T(2,128)(2,1)S(1)}, bf16[2,480]{1,0:T(2,128)(2,1)S(1)}, u32[]{:S(2)}, u32[]{:S(2)}) collective-permute-start(bf16[2,480]{1,0:T(2,128)(2,1)S(1)} %pad_maximum_fusion.4), channel_id=1, source_target_pairs={{0,16},{16,0},{1,17},{17,1},{2,18},{18,2},{3,19},{19,3},{4,20},{20... | collective-permute-start | bytes 5768 | tf_op jit(solution)/shard_map/ppermute | solution.py:787
  16.2 168.8 %copy-start.2 = (f32[256,128]{1,0:T(8,128)}, f32[256,128]{1,0:T(8,128)S(1)}, u32[]{:S(2)}) copy-start(f32[256,128]{1,0:T(8,128)S(1)} %get-tuple-element.296.refs_2_.refs_1_.cos_ref) | copy-start | bytes 393220
  16.2 168.8 %copy-start.4 = (f32[256,128]{1,0:T(8,128)}, f32[256,128]{1,0:T(8,128)S(1)}, u32[]{:S(2)}) copy-start(f32[256,128]{1,0:T(8,128)S(1)} %get-tuple-element.297.refs_3_.refs_2_.sin_ref) | copy-start | bytes 393220
  19.0 2.9 collective-permute-start.2
  20.4 13.8 %collective-permute-start.4 = (bf16[256,960]{1,0:T(8,128)(2,1)}, bf16[256,960]{1,0:T(8,128)(2,1)S(1)}, u32[]{:S(2)}, u32[]{:S(2)}) collective-permute-start(bf16[256,960]{1,0:T(8,128)(2,1)} %pad_maximum_fusion.1), channel_id=1, source_target_pairs={{0,16},{16,0},{1,17},{17,1},{2,18},{18,2},{3,19},{19,3},{4,20},{20... | collective-permute-start | bytes 1474568 | tf_op jit(solution)/shard_map/ppermute | solution.py:787
  28.9 19.8 %copy-start.100 = (s32[2,3]{1,0:T(2,128)S(1)}, s32[2,3]{1,0:T(2,128)}, u32[]{:S(2)}) copy-start(s32[2,3]{1,0:T(2,128)} %param.16) | copy-start | bytes 76
  28.9 21.2 %copy-start.99 = (s32[2,2]{1,0:T(2,128)S(1)}, s32[2,2]{1,0:T(2,128)}, u32[]{:S(2)}) copy-start(s32[2,2]{1,0:T(2,128)} %param.15) | copy-start | bytes 52
  28.9 31.6 %collective-permute-start.8 = (bf16[512,640]{1,0:T(8,128)(2,1)}, bf16[512,640]{1,0:T(8,128)(2,1)}, u32[]{:S(2)}, u32[]{:S(2)}) collective-permute-start(bf16[512,640]{1,0:T(8,128)(2,1)} %get-tuple-element.162.own_ref), channel_id=1, source_target_pairs={{0,4},{4,8},{8,12},{1,5},{5,9},{9,13},{2,6},{6,10},{10,14},{3,7},{... | collective-permute-start | bytes 1966088 | tf_op jit(solution)/shard_map/ppermute | solution.py:791
  34.2 12.7 %collective-permute-start.5 = (bf16[256,960]{1,0:T(8,128)(2,1)S(1)}, bf16[256,960]{1,0:T(8,128)(2,1)S(1)}, u32[]{:S(2)}, u32[]{:S(2)}) collective-permute-start(bf16[256,960]{1,0:T(8,128)(2,1)S(1)} %collective-permute-done.4.refs_4_), channel_id=1, source_target_pairs={{0,2},{1,3},{2,0},{3,1},{4,6},{5,7},{6,4},{7,5},{8,10},{9,11},{10,... | collective-permute-start | bytes 1474568 | tf_op jit(solution)/shard_map/ppermute | solution.py:787
  37.1 28.2 %collective-permute-start.6 = (bf16[256,960]{1,0:T(8,128)(2,1)S(1)}, bf16[256,960]{1,0:T(8,128)(2,1)}, u32[]{:S(2)}, u32[]{:S(2)}) collective-permute-start(bf16[256,960]{1,0:T(8,128)(2,1)S(1)} %collective-permute-done.4.refs_4_), channel_id=1, source_target_pairs={{0,1},{1,0},{2,3},{3,2},{4,5},{5,4},{6,7},{7,6},{8,9},{9,8},{10,11... | collective-permute-start | bytes 1474568 | tf_op jit(solution)/shard_map/ppermute | solution.py:787
  46.9 23.1 %copy-start.36 = (bf16[256,960]{1,0:T(8,128)(2,1)}, bf16[256,960]{1,0:T(8,128)(2,1)S(1)}, u32[]{:S(2)}) copy-start(bf16[256,960]{1,0:T(8,128)(2,1)S(1)} %collective-permute-done.5.refs_5_) | copy-start | bytes 1474564
  46.9 18.4 %collective-permute-start.7 = (bf16[256,960]{1,0:T(8,128)(2,1)S(1)}, bf16[256,960]{1,0:T(8,128)(2,1)}, u32[]{:S(2)}, u32[]{:S(2)}) collective-permute-start(bf16[256,960]{1,0:T(8,128)(2,1)S(1)} %collective-permute-done.5.refs_5_), channel_id=1, source_target_pairs={{0,1},{1,0},{2,3},{3,2},{4,5},{5,4},{6,7},{7,6},{8,9},{9,8},{10,11... | collective-permute-start | bytes 1474568 | tf_op jit(solution)/shard_map/ppermute | solution.py:787
  48.8 11.7 %collective-permute-start.3 = (bf16[256,640]{1,0:T(8,128)(2,1)}, bf16[256,640]{1,0:T(8,128)(2,1)}, u32[]{:S(2)}, u32[]{:S(2)}) collective-permute-start(bf16[256,640]{1,0:T(8,128)(2,1)} %copy-done.38), channel_id=1, source_target_pairs={{4,0},{8,4},{12,8},{5,1},{9,5},{13,9},{6,2},{10,6},{14,10},{7,3},{... | collective-permute-start | bytes 983048 | tf_op jit(solution)/shard_map/ppermute | solution.py:791
  50.3 225.9 %reduce-scatter.4.cloned.1.call-start = ((), (), s32[]{:S(2)}) async-start(), calls=%async_computation.3 | async-start | bytes 2304000
  60.5 16.9 %collective-permute-start.9 = (bf16[512,640]{1,0:T(8,128)(2,1)}, bf16[512,640]{1,0:T(8,128)(2,1)S(1)}, u32[]{:S(2)}, u32[]{:S(2)}) collective-permute-start(bf16[512,640]{1,0:T(8,128)(2,1)} %collective-permute-done.8.near_ref), channel_id=1, source_target_pairs={{0,4},{4,8},{8,12},{1,5},{5,9},{9,13},{2,6},{6,10},{10,14},{3,7},{... | collective-permute-start | bytes 1966088 | tf_op jit(solution)/shard_map/ppermute | solution.py:791
  64.0 28.5 %collective-permute-start.12 = (bf16[512,1024]{1,0:T(8,128)(2,1)S(1)}, bf16[512,1024]{1,0:T(8,128)(2,1)S(1)}, u32[]{:S(2)}, u32[]{:S(2)}) collective-permute-start(bf16[512,1024]{1,0:T(8,128)(2,1)S(1)} %shard_map.214.cot_a.refs_0_.refs_4_.cot_ref), channel_id=1, source_target_pairs={{0,2},{1,3},{2,0},{3,1},{4,6},{5,7},{6,4},{7,5},{8,10},{9,11},{10,... | collective-permute-start | bytes 3145736 | tf_op jit(solution)/shard_map/ppermute | solution.py:787
  71.3 21.6 %copy-start.79 = (bf16[512,960]{1,0:T(8,128)(2,1)}, bf16[512,960]{1,0:T(8,128)(2,1)S(1)}, u32[]{:S(2)}) copy-start(bf16[512,960]{1,0:T(8,128)(2,1)S(1)} %get-tuple-element.220.q_ref) | copy-start | bytes 2949124
  71.3 13.3 %collective-permute-start.10 = (bf16[512,1024]{1,0:T(8,128)(2,1)S(1)}, bf16[512,1024]{1,0:T(8,128)(2,1)S(1)}, u32[]{:S(2)}, u32[]{:S(2)}) collective-permute-start(bf16[512,1024]{1,0:T(8,128)(2,1)S(1)} %shard_map.214.cot_a.refs_0_.refs_4_.cot_ref), channel_id=1, source_target_pairs={{0,1},{1,0},{2,3},{3,2},{4,5},{5,4},{6,7},{7,6},{8,9},{9,8},{10,11... | collective-permute-start | bytes 3145736 | tf_op jit(solution)/shard_map/ppermute | solution.py:787
  77.4 15.5 %copy-start.31 = (bf16[512,640]{1,0:T(8,128)(2,1)}, bf16[512,640]{1,0:T(8,128)(2,1)S(1)}, u32[]{:S(2)}) copy-start(bf16[512,640]{1,0:T(8,128)(2,1)S(1)} %collective-permute-done.9.far_ref) | copy-start | bytes 1966084
  89.6 10.2 %collective-permute-start.11 = (bf16[256,960]{1,0:T(8,128)(2,1)S(1)}, bf16[256,960]{1,0:T(8,128)(2,1)S(1)}, u32[]{:S(2)}, u32[]{:S(2)}) collective-permute-start(bf16[256,960]{1,0:T(8,128)(2,1)S(1)} %get-tuple-element.197.nrm_a.refs_0_.refs_12_), channel_id=1, source_target_pairs={{0,1},{1,0},{2,3},{3,2},{4,5},{5,4},{6,7},{7,6},{8,9},{9,8},{10,11... | collective-permute-start | bytes 1474568 | tf_op jit(solution)/shard_map/ppermute | solution.py:787
  91.3 14.3 %collective-permute-start.15 = (bf16[256,960]{1,0:T(8,128)(2,1)S(1)}, bf16[256,960]{1,0:T(8,128)(2,1)S(1)}, u32[]{:S(2)}, u32[]{:S(2)}) collective-permute-start(bf16[256,960]{1,0:T(8,128)(2,1)S(1)} %get-tuple-element.197.nrm_a.refs_0_.refs_12_), channel_id=1, source_target_pairs={{0,2},{1,3},{2,0},{3,1},{4,6},{5,7},{6,4},{7,5},{8,10},{9,11},{10,... | collective-permute-start | bytes 1474568 | tf_op jit(solution)/shard_map/ppermute | solution.py:787
  92.6 7.3 %collective-permute-start.13 = (bf16[512,1024]{1,0:T(8,128)(2,1)S(1)}, bf16[512,1024]{1,0:T(8,128)(2,1)S(1)}, u32[]{:S(2)}, u32[]{:S(2)}) collective-permute-start(bf16[512,1024]{1,0:T(8,128)(2,1)S(1)} %collective-permute-done.12.cot_a.refs_2_.refs_6_), channel_id=1, source_target_pairs={{0,1},{1,0},{2,3},{3,2},{4,5},{5,4},{6,7},{7,6},{8,9},{9,8},{10,11... | collective-permute-start | bytes 3145736 | tf_op jit(solution)/shard_map/ppermute | solution.py:787
  104.9 10.2 %collective-permute-start.16 = (bf16[256,960]{1,0:T(8,128)(2,1)}, bf16[256,960]{1,0:T(8,128)(2,1)}, u32[]{:S(2)}, u32[]{:S(2)}) collective-permute-start(bf16[256,960]{1,0:T(8,128)(2,1)} %get-tuple-element.184.nrm_a.refs_4_.refs_16_), channel_id=1, source_target_pairs={{0,1},{1,0},{2,3},{3,2},{4,5},{5,4},{6,7},{7,6},{8,9},{9,8},{10,11... | collective-permute-start | bytes 1474568 | tf_op jit(solution)/shard_map/ppermute | solution.py:787
  105.2 17.1 %collective-permute-start.14 = (bf16[256,960]{1,0:T(8,128)(2,1)}, bf16[256,960]{1,0:T(8,128)(2,1)}, u32[]{:S(2)}, u32[]{:S(2)}) collective-permute-start(bf16[256,960]{1,0:T(8,128)(2,1)} %get-tuple-element.184.nrm_a.refs_4_.refs_16_), channel_id=1, source_target_pairs={{0,2},{1,3},{2,0},{3,1},{4,6},{5,7},{6,4},{7,5},{8,10},{9,11},{10,... | collective-permute-start | bytes 1474568 | tf_op jit(solution)/shard_map/ppermute | solution.py:787
  105.6 9.5 %collective-permute-start.17 = (bf16[256,960]{1,0:T(8,128)(2,1)S(1)}, bf16[256,960]{1,0:T(8,128)(2,1)}, u32[]{:S(2)}, u32[]{:S(2)}) collective-permute-start(bf16[256,960]{1,0:T(8,128)(2,1)S(1)} %collective-permute-done.15.nrm_a.refs_2_.refs_14_), channel_id=1, source_target_pairs={{0,1},{1,0},{2,3},{3,2},{4,5},{5,4},{6,7},{7,6},{8,9},{9,8},{10,11... | collective-permute-start | bytes 1474568 | tf_op jit(solution)/shard_map/ppermute | solution.py:787
  114.9 46.3 %copy-start.65 = (bf16[512,1024]{1,0:T(8,128)(2,1)}, bf16[512,1024]{1,0:T(8,128)(2,1)S(1)}, u32[]{:S(2)}) copy-start(bf16[512,1024]{1,0:T(8,128)(2,1)S(1)} %get-tuple-element.209.a_ref.refs_0_) | copy-start | bytes 3145732
  114.9 8.0 %collective-permute-start.18 = (bf16[512,1024]{1,0:T(8,128)(2,1)S(1)}, bf16[512,1024]{1,0:T(8,128)(2,1)S(1)}, u32[]{:S(2)}, u32[]{:S(2)}) collective-permute-start(bf16[512,1024]{1,0:T(8,128)(2,1)S(1)} %get-tuple-element.183), channel_id=1, source_target_pairs={{0,1},{1,0},{2,3},{3,2},{4,5},{5,4},{6,7},{7,6},{8,9},{9,8},{10,11... | collective-permute-start | bytes 3145736 | tf_op jit(solution)/shard_map/ppermute | solution.py:787
  122.3 12.2 %collective-permute-start.20 = (bf16[256,960]{1,0:T(8,128)(2,1)}, bf16[256,960]{1,0:T(8,128)(2,1)S(1)}, u32[]{:S(2)}, u32[]{:S(2)}) collective-permute-start(bf16[256,960]{1,0:T(8,128)(2,1)} %collective-permute-done.14.nrm_a.refs_6_.refs_18_), channel_id=1, source_target_pairs={{0,1},{1,0},{2,3},{3,2},{4,5},{5,4},{6,7},{7,6},{8,9},{9,8},{10,11... | collective-permute-start | bytes 1474568 | tf_op jit(solution)/shard_map/ppermute | solution.py:787
  122.6 8.4 %collective-permute-start.19 = (bf16[512,1024]{1,0:T(8,128)(2,1)S(1)}, bf16[512,1024]{1,0:T(8,128)(2,1)S(1)}, u32[]{:S(2)}, u32[]{:S(2)}) collective-permute-start(bf16[512,1024]{1,0:T(8,128)(2,1)S(1)} %get-tuple-element.187), channel_id=1, source_target_pairs={{0,1},{1,0},{2,3},{3,2},{4,5},{5,4},{6,7},{7,6},{8,9},{9,8},{10,11... | collective-permute-start | bytes 3145736 | tf_op jit(solution)/shard_map/ppermute | solution.py:787
  130.7 51.8 %copy-start.67 = (bf16[512,1024]{1,0:T(8,128)(2,1)}, bf16[512,1024]{1,0:T(8,128)(2,1)S(1)}, u32[]{:S(2)}) copy-start(bf16[512,1024]{1,0:T(8,128)(2,1)S(1)} %get-tuple-element.218.a_ref.refs_0_) | copy-start | bytes 3145732
  130.7 11.4 %collective-permute-start.21 = (bf16[512,1024]{1,0:T(8,128)(2,1)S(1)}, bf16[512,1024]{1,0:T(8,128)(2,1)S(1)}, u32[]{:S(2)}, u32[]{:S(2)}) collective-permute-start(bf16[512,1024]{1,0:T(8,128)(2,1)S(1)} %get-tuple-element.191), channel_id=1, source_target_pairs={{0,1},{1,0},{2,3},{3,2},{4,5},{5,4},{6,7},{7,6},{8,9},{9,8},{10,11... | collective-permute-start | bytes 3145736 | tf_op jit(solution)/shard_map/ppermute | solution.py:787
  133.2 16.6 %collective-permute-start.23 = (bf16[256,1024]{1,0:T(8,128)(2,1)}, bf16[256,1024]{1,0:T(8,128)(2,1)}, u32[]{:S(2)}, u32[]{:S(2)}) collective-permute-start(bf16[256,1024]{1,0:T(8,128)(2,1)} %shard_map.224), channel_id=1, source_target_pairs={{0,2},{1,3},{2,0},{3,1},{4,6},{5,7},{6,4},{7,5},{8,10},{9,11},{10,... | collective-permute-start | bytes 1572872 | tf_op jit(solution)/shard_map/ppermute | solution.py:787
  141.6 7.1 %collective-permute-start.22 = (bf16[512,1024]{1,0:T(8,128)(2,1)S(1)}, bf16[512,1024]{1,0:T(8,128)(2,1)S(1)}, u32[]{:S(2)}, u32[]{:S(2)}) collective-permute-start(bf16[512,1024]{1,0:T(8,128)(2,1)S(1)} %get-tuple-element.196), channel_id=1, source_target_pairs={{0,1},{1,0},{2,3},{3,2},{4,5},{5,4},{6,7},{7,6},{8,9},{9,8},{10,11... | collective-permute-start | bytes 3145736 | tf_op jit(solution)/shard_map/ppermute | solution.py:787
  147.4 33.9 %collective-permute-start.24 = (bf16[480,640]{1,0:T(8,128)(2,1)}, bf16[480,640]{1,0:T(8,128)(2,1)}, u32[]{:S(2)}, u32[]{:S(2)}) collective-permute-start(bf16[480,640]{1,0:T(8,128)(2,1)} %get-tuple-element.216), channel_id=1, source_target_pairs={{0,16},{16,0},{1,17},{17,1},{2,18},{18,2},{3,19},{19,3},{4,20},{20... | collective-permute-start | bytes 1843208 | tf_op jit(solution)/shard_map/ppermute | solution.py:787
  149.6 30.5 %collective-permute-start.25 = (bf16[256,1024]{1,0:T(8,128)(2,1)}, bf16[256,1024]{1,0:T(8,128)(2,1)}, u32[]{:S(2)}, u32[]{:S(2)}) collective-permute-start(bf16[256,1024]{1,0:T(8,128)(2,1)} %shard_map.227), channel_id=1, source_target_pairs={{0,2},{1,3},{2,0},{3,1},{4,6},{5,7},{6,4},{7,5},{8,10},{9,11},{10,... | collective-permute-start | bytes 1572872 | tf_op jit(solution)/shard_map/ppermute | solution.py:787
  165.0 12.6 %copy-start.71 = (f32[256,960]{1,0:T(8,128)}, f32[256,960]{1,0:T(8,128)S(1)}, u32[]{:S(2)}) copy-start(f32[256,960]{1,0:T(8,128)S(1)} %get-tuple-element.210.gh_ref) | copy-start | bytes 2949124
  165.0 12.6 %copy-start.86 = (bf16[256,960]{1,0:T(8,128)(2,1)}, bf16[256,960]{1,0:T(8,128)(2,1)S(1)}, u32[]{:S(2)}) copy-start(bf16[256,960]{1,0:T(8,128)(2,1)S(1)} %get-tuple-element.235.refs_2_) | copy-start | bytes 1474564
  178.5 19.9 %collective-permute-start.26 = (bf16[256,640]{1,0:T(8,128)(2,1)}, bf16[256,640]{1,0:T(8,128)(2,1)}, u32[]{:S(2)}, u32[]{:S(2)}) collective-permute-start(bf16[256,640]{1,0:T(8,128)(2,1)} %get-tuple-element.228), channel_id=1, source_target_pairs={{4,0},{8,4},{12,8},{5,1},{9,5},{13,9},{6,2},{10,6},{14,10},{7,3},{... | collective-permute-start | bytes 983048 | tf_op jit(solution)/shard_map/ppermute | solution.py:791
  179.8 28.4 %collective-permute-start.28 = (bf16[480,1280]{1,0:T(8,128)(2,1)}, bf16[480,1280]{1,0:T(8,128)(2,1)}, u32[]{:S(2)}, u32[]{:S(2)}) collective-permute-start(bf16[480,1280]{1,0:T(8,128)(2,1)} %get-tuple-element.231), channel_id=1, source_target_pairs={{0,16},{16,0},{1,17},{17,1},{2,18},{18,2},{3,19},{19,3},{4,20},{20... | collective-permute-start | bytes 3686408 | tf_op jit(solution)/shard_map/ppermute | solution.py:787
  180.1 26.7 %collective-permute-start.27 = (bf16[512,1024]{1,0:T(8,128)(2,1)}, bf16[512,1024]{1,0:T(8,128)(2,1)}, u32[]{:S(2)}, u32[]{:S(2)}) collective-permute-start(bf16[512,1024]{1,0:T(8,128)(2,1)} %shard_map.229), channel_id=1, source_target_pairs={{0,2},{1,3},{2,0},{3,1},{4,6},{5,7},{6,4},{7,5},{8,10},{9,11},{10,... | collective-permute-start | bytes 3145736 | tf_op jit(solution)/shard_map/ppermute | solution.py:787
  185.0 12.0 %copy-start.73 = (f32[256,960]{1,0:T(8,128)}, f32[256,960]{1,0:T(8,128)S(1)}, u32[]{:S(2)}) copy-start(f32[256,960]{1,0:T(8,128)S(1)} %get-tuple-element.219.gh_ref) | copy-start | bytes 2949124
  185.0 12.0 %copy-start.88 = (bf16[256,960]{1,0:T(8,128)(2,1)}, bf16[256,960]{1,0:T(8,128)(2,1)S(1)}, u32[]{:S(2)}) copy-start(bf16[256,960]{1,0:T(8,128)(2,1)S(1)} %get-tuple-element.236.refs_3_) | copy-start | bytes 1474564
  197.0 13.9 %collective-permute-start.29 = (bf16[256,640]{1,0:T(8,128)(2,1)S(1)}, bf16[256,640]{1,0:T(8,128)(2,1)S(1)}, u32[]{:S(2)}, u32[]{:S(2)}) collective-permute-start(bf16[256,640]{1,0:T(8,128)(2,1)S(1)} %get-tuple-element.233), channel_id=1, source_target_pairs={{4,0},{8,4},{12,8},{5,1},{9,5},{13,9},{6,2},{10,6},{14,10},{7,3},{... | collective-permute-start | bytes 983048 | tf_op jit(solution)/shard_map/ppermute | solution.py:791
  199.4 29.9 %collective-permute-start.32 = (bf16[256,640]{1,0:T(8,128)(2,1)S(1)}, bf16[256,640]{1,0:T(8,128)(2,1)S(1)}, u32[]{:S(2)}, u32[]{:S(2)}) collective-permute-start(bf16[256,640]{1,0:T(8,128)(2,1)S(1)} %shard_map.235), channel_id=1, source_target_pairs={{4,0},{8,4},{12,8},{5,1},{9,5},{13,9},{6,2},{10,6},{14,10},{7,3},{... | collective-permute-start | bytes 983048 | tf_op jit(solution)/shard_map/ppermute | solution.py:791
  200.8 28.6 %collective-permute-start.31 = (bf16[256,640]{1,0:T(8,128)(2,1)S(1)}, bf16[256,640]{1,0:T(8,128)(2,1)S(1)}, u32[]{:S(2)}, u32[]{:S(2)}) collective-permute-start(bf16[256,640]{1,0:T(8,128)(2,1)S(1)} %get-tuple-element.247), channel_id=1, source_target_pairs={{0,4},{4,8},{8,12},{1,5},{5,9},{9,13},{2,6},{6,10},{10,14},{3,7},{... | collective-permute-start | bytes 983048 | tf_op jit(solution)/shard_map/ppermute | solution.py:791
  211.7 22.2 %collective-permute-start.33 = (bf16[256,640]{1,0:T(8,128)(2,1)}, bf16[256,640]{1,0:T(8,128)(2,1)}, u32[]{:S(2)}, u32[]{:S(2)}) collective-permute-start(bf16[256,640]{1,0:T(8,128)(2,1)} %shard_map.237), channel_id=1, source_target_pairs={{4,0},{8,4},{12,8},{5,1},{9,5},{13,9},{6,2},{10,6},{14,10},{7,3},{... | collective-permute-start | bytes 983048 | tf_op jit(solution)/shard_map/ppermute | solution.py:791
  213.0 127.3 %all-gather.5.cloned.1.call-start = ((), (), s32[]{:S(2)}) async-start(), calls=%async_computation.2 | async-start | bytes 2304000 | tf_op jit(solution)/shard_map/all_gather | solution.py:809
  223.5 5.1 %collective-permute-start.30 = (bf16[480,1984]{1,0:T(8,128)(2,1)S(1)}, bf16[480,1984]{1,0:T(8,128)(2,1)S(1)}, u32[]{:S(2)}, u32[]{:S(2)}) collective-permute-start(bf16[480,1984]{1,0:T(8,128)(2,1)S(1)} %get-tuple-element.243), channel_id=1, source_target_pairs={{0,1},{1,0},{2,3},{3,2},{4,5},{5,4},{6,7},{7,6},{8,9},{9,8},{10,11... | collective-permute-start | bytes 5713928 | tf_op jit(solution)/shard_map/ppermute | solution.py:787
  233.3 23.1 %collective-permute-start.34 = (bf16[240,1984]{1,0:T(8,128)(2,1)S(1)}, bf16[240,1984]{1,0:T(8,128)(2,1)S(1)}, u32[]{:S(2)}, u32[]{:S(2)}) collective-permute-start(bf16[240,1984]{1,0:T(8,128)(2,1)S(1)} %get-tuple-element.255), channel_id=1, source_target_pairs={{0,16},{16,0},{1,17},{17,1},{2,18},{18,2},{3,19},{19,3},{4,20},{20... | collective-permute-start | bytes 2856968 | tf_op jit(solution)/shard_map/ppermute | solution.py:787
  258.9 2.8 collective-permute-start.35
  260.0 12.8 %collective-permute-start.36 = (bf16[120,1984]{1,0:T(8,128)(2,1)S(1)}, bf16[120,1984]{1,0:T(8,128)(2,1)S(1)}, u32[]{:S(2)}, u32[]{:S(2)}) collective-permute-start(bf16[120,1984]{1,0:T(8,128)(2,1)S(1)} %get-tuple-element.264), channel_id=1, source_target_pairs={{0,2},{1,3},{2,0},{3,1},{4,6},{5,7},{6,4},{7,5},{8,10},{9,11},{10,... | collective-permute-start | bytes 1428488 | tf_op jit(solution)/shard_map/ppermute | solution.py:787
  262.6 13.7 %collective-permute-start.37 = (bf16[240,640]{1,0:T(8,128)(2,1)}, bf16[240,640]{1,0:T(8,128)(2,1)}, u32[]{:S(2)}, u32[]{:S(2)}) collective-permute-start(bf16[240,640]{1,0:T(8,128)(2,1)} %get-tuple-element.266), channel_id=1, source_target_pairs={{0,16},{16,0},{1,17},{17,1},{2,18},{18,2},{3,19},{19,3},{4,20},{20... | collective-permute-start | bytes 921608 | tf_op jit(solution)/shard_map/ppermute | solution.py:787
  272.9 14.2 %collective-permute-start.38 = (bf16[120,1984]{1,0:T(8,128)(2,1)S(1)}, bf16[120,1984]{1,0:T(8,128)(2,1)}, u32[]{:S(2)}, u32[]{:S(2)}) collective-permute-start(bf16[120,1984]{1,0:T(8,128)(2,1)S(1)} %shard_map.247.refs_0_), channel_id=1, source_target_pairs={{0,4},{4,0},{8,12},{12,8},{1,5},{5,1},{9,13},{13,9},{2,6},{6,2},{1... | collective-permute-start | bytes 1428488 | tf_op jit(solution)/shard_map/ppermute | solution.py:787
  278.5 15.3 %collective-permute-start.39 = (bf16[120,640]{1,0:T(8,128)(2,1)S(1)}, bf16[120,640]{1,0:T(8,128)(2,1)S(1)}, u32[]{:S(2)}, u32[]{:S(2)}) collective-permute-start(bf16[120,640]{1,0:T(8,128)(2,1)S(1)} %get-tuple-element.270), channel_id=1, source_target_pairs={{0,2},{1,3},{2,0},{3,1},{4,6},{5,7},{6,4},{7,5},{8,10},{9,11},{10,... | collective-permute-start | bytes 460808 | tf_op jit(solution)/shard_map/ppermute | solution.py:787
  288.3 49.9 %collective-permute-start.40 = (bf16[120,1984]{1,0:T(8,128)(2,1)S(1)}, bf16[120,1984]{1,0:T(8,128)(2,1)S(1)}, u32[]{:S(2)}, u32[]{:S(2)}) collective-permute-start(bf16[120,1984]{1,0:T(8,128)(2,1)S(1)} %shard_map.249.refs_0_), channel_id=1, source_target_pairs={{0,8},{4,12},{8,0},{12,4},{1,9},{5,13},{9,1},{13,5},{2,10},{6,14},... | collective-permute-start | bytes 1428488 | tf_op jit(solution)/shard_map/ppermute | solution.py:787
  293.8 45.8 %collective-permute-start.41 = (bf16[120,640]{1,0:T(8,128)(2,1)S(1)}, bf16[120,640]{1,0:T(8,128)(2,1)S(1)}, u32[]{:S(2)}, u32[]{:S(2)}) collective-permute-start(bf16[120,640]{1,0:T(8,128)(2,1)S(1)} %shard_map.250.refs_0_), channel_id=1, source_target_pairs={{0,4},{4,0},{8,12},{12,8},{1,5},{5,1},{9,13},{13,9},{2,6},{6,2},{1... | collective-permute-start | bytes 460808 | tf_op jit(solution)/shard_map/ppermute | solution.py:787
  338.3 10.4 %collective-permute-start.42 = (bf16[120,1984]{1,0:T(8,128)(2,1)S(1)}, bf16[120,1984]{1,0:T(8,128)(2,1)}, u32[]{:S(2)}, u32[]{:S(2)}) collective-permute-start(bf16[120,1984]{1,0:T(8,128)(2,1)S(1)} %shard_map.251.own_ref), channel_id=1, source_target_pairs={{0,2},{1,3},{2,0},{3,1},{4,6},{5,7},{6,4},{7,5},{8,10},{9,11},{10,... | collective-permute-start | bytes 1428488 | tf_op jit(solution)/shard_map/ppermute | solution.py:787
  350.0 14.8 %copy-start.8 = (bf16[480,960]{1,0:T(8,128)(2,1)S(1)}, bf16[480,960]{1,0:T(8,128)(2,1)}, u32[]{:S(2)}) copy-start(bf16[480,960]{1,0:T(8,128)(2,1)} %w_ref.1) | copy-start | bytes 2764804
  350.0 14.8 %collective-permute-start.44 = (bf16[240,1984]{1,0:T(8,128)(2,1)S(1)}, bf16[240,1984]{1,0:T(8,128)(2,1)S(1)}, u32[]{:S(2)}, u32[]{:S(2)}) collective-permute-start(bf16[240,1984]{1,0:T(8,128)(2,1)S(1)} %shard_map.254.own_ref), channel_id=1, source_target_pairs={{0,1},{1,0},{2,3},{3,2},{4,5},{5,4},{6,7},{7,6},{8,9},{9,8},{10,11... | collective-permute-start | bytes 2856968 | tf_op jit(solution)/shard_map/ppermute | solution.py:787
  353.4 9.8 %collective-permute-start.43 = (bf16[120,640]{1,0:T(8,128)(2,1)S(1)}, bf16[120,640]{1,0:T(8,128)(2,1)S(1)}, u32[]{:S(2)}, u32[]{:S(2)}) collective-permute-start(bf16[120,640]{1,0:T(8,128)(2,1)S(1)} %copy-done.40), channel_id=1, source_target_pairs={{0,8},{4,12},{8,0},{12,4},{1,9},{5,13},{9,1},{13,5},{2,10},{6,14},... | collective-permute-start | bytes 460808 | tf_op jit(solution)/shard_map/ppermute | solution.py:787
  363.2 5.2 %collective-permute-start.45 = (bf16[120,640]{1,0:T(8,128)(2,1)S(1)}, bf16[120,640]{1,0:T(8,128)(2,1)S(1)}, u32[]{:S(2)}, u32[]{:S(2)}) collective-permute-start(bf16[120,640]{1,0:T(8,128)(2,1)S(1)} %shard_map.255.own_ref), channel_id=1, source_target_pairs={{0,2},{1,3},{2,0},{3,1},{4,6},{5,7},{6,4},{7,5},{8,10},{9,11},{10,... | collective-permute-start | bytes 460808 | tf_op jit(solution)/shard_map/ppermute | solution.py:787
  368.5 3.8 collective-permute-start.46
  (87 other events, 290.1 us)
Sparse Core Ops, SparseCore 0:
  50.5 53.6 all-gather.2
  213.2 43.8 reduce-scatter.3
  276.4 62.9 all-gather.4

commit v5 on v4

--- a/solution.py
+++ b/solution.py
@@ -442,7 +442,7 @@
             pltpu.VMEM((window, 2 * KW), F32),
             pltpu.VMEM((GRAIN, wide(QW)), F32),
         ],
-        us=11.7,
+        us=0.05 if earlier else 11.7,
     )
 
 
@@ -595,7 +595,7 @@
         ff_back_kernel,
         outs,
         (hidden, rows_at(cotangent, seq, rows), *terms, gain, wo),
-        us=1.8,
+        us=0.05,
     )
 
 
@@ -636,7 +636,7 @@
         [struct((width, rows), F32), struct((rows, 2 * KW), BF16)],
         (rows_at(tokens, seq, rows), *args),
         scratch=[pltpu.VMEM((rows, 2 * KW), F32)],
-        us=1.8,
+        us=0.05,
     )
 
 
@@ -647,8 +647,8 @@
     refs[-1][...] = total.astype(refs[-1].dtype)
 
 
-def add_up(terms, shape, dtype):
-    return call(add_kernel, [struct(shape, dtype)], terms, us=0.7)[0]
+def add_up(terms, shape, dtype, us=0.7):
+    return call(add_kernel, [struct(shape, dtype)], terms, us=us)[0]
 
 
 def side_kernel(*refs):
@@ -706,7 +706,7 @@
         [struct(shape, F32), struct(shape, BF16)],
         (at, keep, got),
         scratch=[pltpu.VMEM(keep.shape, F32)],
-        us=0.9,
+        us=0.05,
     )
 
 
@@ -906,11 +906,15 @@
         )
         wkv = kv_pieces[0][0]
         near, ahead = shift(kv, 1), shift(first, -1)
+        if shards == 2:
+            arrive(two_x)
+        ff_weights = lax.all_gather(side_by_side(w_gate, w_up, w_down), "shard", axis=0, tiled=True)
+        if shards == 2:
+            two_y, two_beside = swap(two_x, "tp", 2), swap(two_x, "tp", 1)
+            arrive(two_beside)
+        arrive(near, ahead)
         (cotangent,) = prepare(cotangent.transpose(0, 2, 1))
-        if shards == 2:
-            two_x = in_turn(two_x)
-            two_y, two_beside = swap(two_x, "tp", 2), swap(two_x, "tp", 1)
-        ff_weights = lax.all_gather(side_by_side(w_gate, w_up, w_down), "shard", axis=0, tiled=True)
+        windows = (shift(in_turn(near), 1), near, kv, ahead)
         if shards == 2:
             two_y = in_turn(two_y)
             parts = (two_x, two_y, two_beside, swap(two_y, "tp", 1))
@@ -919,9 +923,7 @@
         else:
             q_pieces, out_pieces = ([(gather(w), 0, width)] for w in (w_query, w_out))
             two_y = w_query
-        windows = (shift(in_turn(near), 1), near, kv, ahead)
-        cot_y = swap(after(cotangent, two_y, near), "tp", 2)
-        arrive(ahead)
+        cot_y = swap(after(cotangent, two_y), "tp", 2)
         (query,), q_pieces = project_q(normed_one, seqs, cosine, sine, q_pieces, places)
         wq = q_pieces[0][0]
         cot_core = swap(in_turn(cotangent), "tp", 1)
@@ -984,7 +986,7 @@
         def down_sum(keep, got):
             if got is None:
                 return keep.astype(BF16)
-            return add_up((keep, got), keep.shape, BF16)
+            return add_up((keep, got), keep.shape, BF16, 0.05)
 
         def units_sum(keep, got):
             left = down.finish()
@@ -1001,7 +1003,7 @@
         gate_up = Chain(reduce_units(gate_up_grad, units_sum))
         out_terms = [out_at(a) for s in every for a in far_sums[s]]
         out_partial = call(
-            pair_kernel, [struct((seqs * rows, wide(width)), BF16)], out_terms, us=0.9
+            pair_kernel, [struct((seqs * rows, wide(width)), BF16)], out_terms, us=0.05
         )[0]
         outs_got = swap(after(out_partial, grad_terms[last][2]), "tp", 2)
 
@@ -1014,6 +1016,8 @@
             grad_hidden.append(gh)
             branch.append(gb)
             gain_two_grad.append(gg)
+            if s == 0:
+                down.step()
             dq, dfar, dnear, own, dnext = attend_back(
                 scals[s], query, s, rows, windows, mixed[s], lse[s], gm, cosine, sine, ahead_grads
             )
@@ -1022,7 +1026,7 @@
 
         def pass_on(s):
             dq, dnear, own, passed = backs[s]
-            backs[s] = dq, own, shift(add_up((dnear, passed), dnear.shape, BF16), -1)
+            backs[s] = dq, own, shift(add_up((dnear, passed), dnear.shape, BF16, 0.05), -1)
 
         def rows_back(s):
             dq, own, right = backs[s]
@@ -1034,9 +1038,6 @@
 
         for s in every:
             ahead_grads = mixed_back(s, ahead_grads)
-            if s == 0:
-                down.step()
-                down.finish()
         left = shift(ahead_grads[0], 1)
         for s in every[:-1]:
             pass_on(s)
@@ -1065,19 +1066,16 @@
         pair.step()
         for s in every:
             rows_back(s)
-        pair.step()
         finish_last = lambda at, own, got: (at, own, got)
         keys = Chain(
             reduce_attention(
-                outer([([normed_one], gkv, ())], width, core_place, by_core, 1.1), finish_last
+                outer([([normed_one], gkv, ())], width, core_place, by_core, 0.05), finish_last
             )
         )
-        for chain in (keys, pair, keys, pair, keys):
-            chain.step()
-        for chain in (pair, keys):
+        for chain in (keys, pair, keys, pair, keys, pair, keys, pair, keys):
             chain.step()
         sum_down, sum_gate, sum_up = widen(unit_sums)
-        for chain in (pair, keys, pair, keys):
+        for chain in (pair, keys):
             chain.step()
         sum_out, sum_gain_two, sum_query, products = pair.finish()
         keys_done = keys.finish()

time: 386 us -> 365 us (0.946)
  waiting for transfers between devices: 124 us -> 105 us
  Pallas kernels: 130 us -> 123 us
  local copies, waits for them, and re-layouts: 39.5 us -> 45.6 us
  starting transfers between devices: 68.1 us -> 64.2 us
    ppermute x39, waiting for transfers between devices: 108 us -> 74.2 us  [swap(): return lax.ppermute(value, axis, [(i, i ^ bit) for i in range(count)])]
    all_gather x1, waiting for transfers between devices: 0.01 us -> 13.6 us  [all_over_ctx(): return lax.all_gather(part, 'ctx', axis=0, tiled=True)]
    pallas_call x47, Pallas kernels: 130 us -> 123 us  [call(): pl.pallas_call(kernel, out_shape=shapes, grid=grid, in_specs=in_specs, ou...]
    unnamed x204 -> x234, local copies, waits for them, and re-layouts: 38.3 us -> 44.4 us
    all_gather x1, waiting for transfers between devices: 0.01 us -> 5.9 us  [per_device(): lax.all_gather(side_by_side(w_gate, w_up, w_down), 'shard', axis=0, tiled...]
  transfers between devices with their start and end apart: 50 -> 50, of which waited for: 15 -> 19; matrix products, arithmetic and copies ran while one was open for 2% -> 2% of each run, Pallas kernels for 33% -> 34%
where the time goes in v5:
time: 365 us; the launch traced here: 359 us
  Pallas kernels  123 us (34%)
  waiting for transfers between devices  105 us (29%)
  starting transfers between devices  64.2 us (18%)
  local copies, waits for them, and re-layouts  45.6 us (12%)
  between operations  15.2 us (4%)
  other arithmetic  6.4 us (2%)
    pallas_call x47, Pallas kernels, call(): pl.pallas_call(kernel, out_shape=shapes, grid=grid, in_specs=in_specs, ou...  123 us
    ppermute x39, waiting for transfers between devices, swap(): return lax.ppermute(value, axis, [(i, i ^ bit) for i in range(count)])  74.2 us
    ppermute x39, starting transfers between devices, swap(): return lax.ppermute(value, axis, [(i, i ^ bit) for i in range(count)])  44.7 us
    unnamed x234, local copies, waits for them, and re-layouts  44.4 us
    ppermute x8, starting transfers between devices, shift(): return lax.ppermute(value, 'ctx', pairs)  19.2 us
    all_gather x1, waiting for transfers between devices, all_over_ctx(): return lax.all_gather(part, 'ctx', axis=0, tiled=True)  13.6 us
    ppermute x8, waiting for transfers between devices, shift(): return lax.ppermute(value, 'ctx', pairs)  11.2 us
  transfers between devices with their start and end apart: 50, of which 19 were waited for; matrix products, arithmetic and copies ran while one was open for 2% of the time, Pallas kernels for 34%

profile of v5, /device:TPU:1, one launch (start us, length us, event | category | flops | bytes accessed | tf_op | source)
XLA Modules:
  0.0 359.4 jit_solution(18059420401434325034)
XLA Ops:
  7.3 1.3 copy.29
  10.6 2.0 collective-permute-start.1
  17.1 2.8 collective-permute-done.1.refs_5_
  22.0 1.5 collective-permute-start.3
  25.6 2.9 shard_map.213
  29.4 4.0 %collective-permute-start.5 = (bf16[512,640]{1,0:T(8,128)(2,1)S(1)}, bf16[512,640]{1,0:T(8,128)(2,1)}, u32[]{:S(2)}, u32[]{:S(2)}) collective-permute-start(bf16[512,640]{1,0:T(8,128)(2,1)S(1)} %get-tuple-element.154.own_ref), channel_id=1, source_target_pairs={{0,4},{4,8},{8,12},{1,5},{5,9},{9,13},{2,6},{6,10},{10,14},{3,7},{... | collective-permute-start | bytes 1966088 | tf_op jit(solution)/shard_map/ppermute | solution.py:791
  33.5 1.3 collective-permute-start.6
  36.7 1.4 shard_map.214
  38.1 1.5 collective-permute-start.7
  39.6 4.8 %collective-permute-done.6.next_ref = bf16[256,640]{1,0:T(8,128)(2,1)S(1)} collective-permute-done((bf16[256,640]{1,0:T(8,128)(2,1)}, bf16[256,640]{1,0:T(8,128)(2,1)S(1)}, u32[]{:S(2)}, u32[]{:S(2)}) %collective-permute-start.6) | collective-permute-done | bytes 327712 | tf_op jit(solution)/shard_map/ppermute | solution.py:791
  44.4 2.1 collective-permute-done.5.near_ref
  48.5 1.3 shard_map.215.cot_a.refs_0_.refs_4_.cot_ref
  49.8 2.2 collective-permute-done.7.refs_5_
  53.3 1.5 collective-permute-start.12
  54.8 3.4 collective-permute-start.9
  62.5 1.4 copy-done.103
  63.9 3.4 shard_map.216
  67.9 4.3 %collective-permute-done.9.far_ref = bf16[512,640]{1,0:T(8,128)(2,1)S(1)} collective-permute-done((bf16[512,640]{1,0:T(8,128)(2,1)}, bf16[512,640]{1,0:T(8,128)(2,1)S(1)}, u32[]{:S(2)}, u32[]{:S(2)}) %collective-permute-start.9) | collective-permute-done | bytes 655392 | tf_op jit(solution)/shard_map/ppermute | solution.py:791
  72.2 7.0 %shard_map.217 = (bf16[256,960]{1,0:T(8,128)(2,1)S(1)}, f32[256,128]{1,0:T(8,128)S(1)}) custom-call(s32[1,5]{1,0:T(1,128)S(1)} %get-tuple-element.292.scal_ref, bf16[512,960]{1,0:T(8,128)(2,1)S(1)} %get-tuple-element.218.q_ref, bf16[512,640]{1,0:T(8,128)(2,1)S(1)} %collective-permute-done.9.far_ref, bf16[512,640]{1,0:T(8,128)(2,1)} %collective-permute-done.5.near_ref, ...), custom_call_target="tpu_custom_call" | custom-call | flops 78199996416 | tf_op jit(solution)/shard_map/pallas_call | solution.py:101
  80.9 2.2 shard_map.218
  85.6 6.8 %shard_map.219 = (bf16[256,960]{1,0:T(8,128)(2,1)S(1)}, f32[256,128]{1,0:T(8,128)S(1)}) custom-call(s32[1,5]{1,0:T(1,128)S(1)} %get-tuple-element.293.scal_ref, bf16[512,960]{1,0:T(8,128)(2,1)S(1)} %get-tuple-element.218.q_ref, bf16[512,640]{1,0:T(8,128)(2,1)S(1)} %collective-permute-done.9.far_ref, bf16[512,640]{1,0:T(8,128)(2,1)} %collective-permute-done.5.near_ref, ...), custom_call_target="tpu_custom_call" | custom-call | flops 78199996416 | tf_op jit(solution)/shard_map/pallas_call | solution.py:101
  93.1 2.2 shard_map.220
  99.5 5.9 %all-gather.3.cloned.1.call-done.w_ref = bf16[960,1920]{1,0:T(8,128)(2,1)} async-done(((bf16[480,1920]{1,0:T(8,128)(2,1)}), bf16[960,1920]{1,0:T(8,128)(2,1)}) %all-gather.3.cloned.1.call-update) | async-done | bytes 3686416 | tf_op jit(solution)/shard_map/all_gather | solution.py:911
  105.4 2.0 copy-done.63
  110.7 6.8 %shard_map.221 = (bf16[512,640]{1,0:T(8,128)(2,1)S(1)}, bf16[512,640]{1,0:T(8,128)(2,1)S(1)}, bf16[512,640]{1,0:T(8,128)(2,1)S(1)}, bf16[512,1024]{1,0:T(8,128)(2,1)S(1)}, bf16[512,1024]{1,0:T(8,128)(2,1)S(1)}) custom-call(bf16[256,960]{1,0:T(8,128)(2,1)S(1)} %copy-done.81, bf16[256,960]{1,0:T(8,128)(2,1)S(1)} %copy-done.84, ...), custom_call_target="tpu_custom_call" | custom-call | flops 82800001024 | tf_op jit(solution)/shard_map/pallas_call | solution.py:101
  118.3 7.1 %shard_map.222 = (bf16[512,640]{1,0:T(8,128)(2,1)S(1)}, bf16[512,640]{1,0:T(8,128)(2,1)S(1)}, bf16[512,640]{1,0:T(8,128)(2,1)S(1)}, bf16[512,1024]{1,0:T(8,128)(2,1)S(1)}, bf16[512,1024]{1,0:T(8,128)(2,1)S(1)}) custom-call(bf16[256,960]{1,0:T(8,128)(2,1)} %collective-permute-done.15.nrm_a.refs_2_.refs_14_, ...), custom_call_target="tpu_custom_call" | custom-call | flops 82800001024 | tf_op jit(solution)/shard_map/pallas_call | solution.py:101
  127.0 7.0 %shard_map.223 = (bf16[512,640]{1,0:T(8,128)(2,1)S(1)}, bf16[512,640]{1,0:T(8,128)(2,1)S(1)}, bf16[512,640]{1,0:T(8,128)(2,1)S(1)}, bf16[512,1024]{1,0:T(8,128)(2,1)S(1)}, bf16[512,1024]{1,0:T(8,128)(2,1)S(1)}) custom-call(bf16[256,960]{1,0:T(8,128)(2,1)} %get-tuple-element.182.nrm_a.refs_4_.refs_16_, ...), custom_call_target="tpu_custom_call" | custom-call | flops 82800001024 | tf_op jit(solution)/shard_map/pallas_call | solution.py:101
  137.1 7.3 %shard_map.225 = (bf16[512,640]{1,0:T(8,128)(2,1)S(1)}, bf16[512,640]{1,0:T(8,128)(2,1)S(1)}, bf16[512,640]{1,0:T(8,128)(2,1)S(1)}, bf16[512,1024]{1,0:T(8,128)(2,1)S(1)}, bf16[512,1024]{1,0:T(8,128)(2,1)S(1)}) custom-call(bf16[256,960]{1,0:T(8,128)(2,1)} %collective-permute-done.14.nrm_a.refs_6_.refs_18_, ...), custom_call_target="tpu_custom_call" | custom-call | flops 82800001024 | tf_op jit(solution)/shard_map/pallas_call | solution.py:101
  145.8 5.5 %shard_map.226 = (f32[480,640]{1,0:T(8,128)S(1)}, bf16[480,640]{1,0:T(8,128)(2,1)}) custom-call(s32[1]{0:T(128)} %bitcast.place_ref, bf16[512,1024]{1,0:T(8,128)(2,1)} %shard_map.215.cot_a.refs_0_.refs_4_.cot_ref, bf16[512,1024]{1,0:T(8,128)(2,1)S(1)} %copy-done.70, bf16[512,1024]{1,0:T(8,128)(2,1)S(1)} %copy-done.67, bf16[512,1024]{1,0:T(8,128)(2,1)S(1)} %copy-done.74, ...), custom_call_target="tpu_custom_call" | custom-call | flops 57500000256 | tf_op jit(solution)/shard_map/pallas_call | solution.py:101
  153.5 9.3 %shard_map.228 = (f32[480,1280]{1,0:T(8,128)S(1)}, bf16[480,1280]{1,0:T(8,128)(2,1)S(1)}) custom-call(s32[1]{0:T(128)} %bitcast.place_ref, bf16[256,960]{1,0:T(8,128)(2,1)S(1)} %copy-done.82, bf16[256,960]{1,0:T(8,128)(2,1)S(1)} %copy-done.85, bf16[256,960]{1,0:T(8,128)(2,1)} %collective-permute-done.15.nrm_a.refs_2_.refs_14_, ...), custom_call_target="tpu_custom_call" | custom-call | flops 115000000512 | tf_op jit(solution)/shard_map/pallas_call | solution.py:101
  165.0 2.5 shard_map.230
  169.7 11.5 %shard_map.232 = (bf16[256,960]{1,0:T(8,128)(2,1)S(1)}, bf16[256,640]{1,0:T(8,128)(2,1)S(1)}, bf16[256,640]{1,0:T(8,128)(2,1)S(1)}, f32[256,640]{1,0:T(8,128)S(1)}, bf16[128,640]{1,0:T(8,128)(2,1)S(1)}) custom-call(s32[1,5]{1,0:T(1,128)S(1)} %get-tuple-element.292.scal_ref, bf16[512,960]{1,0:T(8,128)(2,1)S(1)} %copy-done.7, bf16[512,640]{1,0:T(8,128)(2,1)S(1)} %copy-done.37, ...), custom_call_target="tpu_custom_call" | custom-call | flops 134550003712 | tf_op jit(solution)/shard_map/pallas_call | solution.py:101
  182.9 1.3 collective-permute-start.26
  184.2 2.5 shard_map.233
  187.8 12.3 %shard_map.234 = (bf16[256,960]{1,0:T(8,128)(2,1)S(1)}, bf16[256,640]{1,0:T(8,128)(2,1)}, bf16[256,640]{1,0:T(8,128)(2,1)S(1)}, f32[256,640]{1,0:T(8,128)S(1)}, bf16[256,640]{1,0:T(8,128)(2,1)}) custom-call(s32[1,5]{1,0:T(1,128)S(1)} %get-tuple-element.293.scal_ref, bf16[512,960]{1,0:T(8,128)(2,1)S(1)} %copy-done.7, bf16[512,640]{1,0:T(8,128)(2,1)S(1)} %copy-done.37, ...), custom_call_target="tpu_custom_call" | custom-call | flops 575000000 | tf_op jit(solution)/shard_map/pallas_call | solution.py:101
  200.1 1.3 collective-permute-start.29
  201.4 5.3 %collective-permute-start.31 = (bf16[256,640]{1,0:T(8,128)(2,1)}, bf16[256,640]{1,0:T(8,128)(2,1)}, u32[]{:S(2)}, u32[]{:S(2)}) collective-permute-start(bf16[256,640]{1,0:T(8,128)(2,1)} %get-tuple-element.245), channel_id=1, source_target_pairs={{0,4},{4,8},{8,12},{1,5},{5,9},{9,13},{2,6},{6,10},{10,14},{3,7},{... | collective-permute-start | bytes 983048 | tf_op jit(solution)/shard_map/ppermute | solution.py:791
  207.5 1.3 collective-permute-start.32
  212.3 1.8 shard_map.237
  223.1 2.7 shard_map.238
  225.9 1.9 collective-permute-start.30
  229.9 1.4 collective-permute-done.30.got_ref
  233.4 2.8 shard_map.242
  236.4 2.8 shard_map.243
  241.1 1.7 collective-permute-done.34.got_ref
  243.0 12.2 %collective-permute-done.35.got_ref = bf16[240,1984]{1,0:T(8,128)(2,1)S(1)} collective-permute-done((bf16[240,1984]{1,0:T(8,128)(2,1)S(1)}, bf16[240,1984]{1,0:T(8,128)(2,1)S(1)}, u32[]{:S(2)}, u32[]{:S(2)}) %collective-permute-start.35) | collective-permute-done | bytes 952352 | tf_op jit(solution)/shard_map/ppermute | solution.py:787
  258.4 1.4 maximum_bitcast_fusion
  259.8 4.4 %collective-permute-done.36.got_ref = bf16[240,640]{1,0:T(8,128)(2,1)S(1)} collective-permute-done((bf16[240,640]{1,0:T(8,128)(2,1)S(1)}, bf16[240,640]{1,0:T(8,128)(2,1)S(1)}, u32[]{:S(2)}, u32[]{:S(2)}) %collective-permute-start.36) | collective-permute-done | bytes 307232 | tf_op jit(solution)/shard_map/ppermute | solution.py:787
  264.6 2.6 collective-permute-done.37.refs_1_
  267.3 3.1 collective-permute-start.39
  270.6 3.1 collective-permute-start.40
  273.7 4.6 %collective-permute-done.39.refs_1_ = bf16[120,1984]{1,0:T(8,128)(2,1)S(1)} collective-permute-done((bf16[120,1984]{1,0:T(8,128)(2,1)S(1)}, bf16[120,1984]{1,0:T(8,128)(2,1)S(1)}, u32[]{:S(2)}, u32[]{:S(2)}) %collective-permute-start.39) | collective-permute-done | bytes 476192 | tf_op jit(solution)/shard_map/ppermute | solution.py:787
  278.4 3.3 collective-permute-start.41
  281.8 3.2 collective-permute-start.42
  284.9 25.5 %collective-permute-done.41.refs_1_ = bf16[120,1984]{1,0:T(8,128)(2,1)S(1)} collective-permute-done((bf16[120,1984]{1,0:T(8,128)(2,1)S(1)}, bf16[120,1984]{1,0:T(8,128)(2,1)S(1)}, u32[]{:S(2)}, u32[]{:S(2)}) %collective-permute-start.41) | collective-permute-done | bytes 476192 | tf_op jit(solution)/shard_map/ppermute | solution.py:787
  310.5 1.3 collective-permute-start.43
  311.8 13.9 %collective-permute-done.42.refs_1_ = bf16[120,640]{1,0:T(8,128)(2,1)S(1)} collective-permute-done((bf16[120,640]{1,0:T(8,128)(2,1)S(1)}, bf16[120,640]{1,0:T(8,128)(2,1)S(1)}, u32[]{:S(2)}, u32[]{:S(2)}) %collective-permute-start.42) | collective-permute-done | bytes 153632 | tf_op jit(solution)/shard_map/ppermute | solution.py:787
  326.6 13.6 %all-gather.5.cloned.1.call-done.all_ref = bf16[480,1920]{1,0:T(8,128)(2,1)} async-done(((bf16[120,1920]{1,0:T(8,128)(2,1)}), bf16[480,1920]{1,0:T(8,128)(2,1)}) %all-gather.5.cloned.1.call-update) | async-done | bytes 1843216 | tf_op jit(solution)/shard_map/all_gather | solution.py:809
  340.2 1.5 copy-done.65
  341.7 2.0 shard_map.254
  343.9 2.1 collective-permute-start.45
  346.1 1.4 collective-permute-start.46
  348.3 2.6 shard_map.257
  350.9 1.7 shard_map.258
  (342 shorter events, 75.2 us)
Async XLA Ops:
  7.2 98.1 %all-gather.3.cloned.1.call-start = ((), (), s32[]{:S(2)}) async-start(), calls=%async_computation.1 | async-start | bytes 5529600 | tf_op jit(solution)/shard_map/all_gather | solution.py:911
  10.6 9.2 %collective-permute-start.1 = (bf16[240,640]{1,0:T(8,128)(2,1)}, bf16[240,640]{1,0:T(8,128)(2,1)S(1)}, u32[]{:S(2)}, u32[]{:S(2)}) collective-permute-start(bf16[240,640]{1,0:T(8,128)(2,1)} %fusion), channel_id=1, source_target_pairs={{0,16},{16,0},{1,17},{17,1},{2,18},{18,2},{3,19},{19,3},{4,20},{20... | collective-permute-start | bytes 921608 | tf_op jit(solution)/shard_map/ppermute | solution.py:787
  12.7 9.1 %collective-permute-start = (bf16[2,480]{1,0:T(2,128)(2,1)S(1)}, bf16[2,480]{1,0:T(2,128)(2,1)S(1)}, u32[]{:S(2)}, u32[]{:S(2)}) collective-permute-start(bf16[2,480]{1,0:T(2,128)(2,1)S(1)} %pad_maximum_fusion.4), channel_id=1, source_target_pairs={{0,16},{16,0},{1,17},{17,1},{2,18},{18,2},{3,19},{19,3},{4,20},{20... | collective-permute-start | bytes 5768 | tf_op jit(solution)/shard_map/ppermute | solution.py:787
  13.2 10.3 %copy-start.2 = (bf16[512,1024]{1,0:T(8,128)(2,1)}, bf16[512,1024]{1,0:T(8,128)(2,1)S(1)}, u32[]{:S(2)}) copy-start(bf16[512,1024]{1,0:T(8,128)(2,1)S(1)} %shard_map.212.refs_0_.tok_ref) | copy-start | bytes 3145732
  19.9 3.6 %collective-permute-start.2 = (bf16[240,640]{1,0:T(8,128)(2,1)S(1)}, bf16[240,640]{1,0:T(8,128)(2,1)S(1)}, u32[]{:S(2)}, u32[]{:S(2)}) collective-permute-start(bf16[240,640]{1,0:T(8,128)(2,1)S(1)} %collective-permute-done.1.refs_5_), channel_id=1, source_target_pairs={{0,1},{1,0},{2,3},{3,2},{4,5},{5,4},{6,7},{7,6},{8,9},{9,8},{10,11... | collective-permute-start | bytes 921608 | tf_op jit(solution)/shard_map/ppermute | solution.py:787
  22.0 13.9 %collective-permute-start.3 = (bf16[256,960]{1,0:T(8,128)(2,1)}, bf16[256,960]{1,0:T(8,128)(2,1)}, u32[]{:S(2)}, u32[]{:S(2)}) collective-permute-start(bf16[256,960]{1,0:T(8,128)(2,1)} %pad_maximum_fusion.1), channel_id=1, source_target_pairs={{0,16},{16,0},{1,17},{17,1},{2,18},{18,2},{3,19},{19,3},{4,20},{20... | collective-permute-start | bytes 1474568 | tf_op jit(solution)/shard_map/ppermute | solution.py:787
  25.6 11.2 %copy-start.77 = (bf16[480,640]{1,0:T(8,128)(2,1)S(1)}, bf16[480,640]{1,0:T(8,128)(2,1)}, u32[]{:S(2)}) copy-start(bf16[480,640]{1,0:T(8,128)(2,1)} %refs_0_) | copy-start | bytes 1843204
  25.6 11.2 %copy-start.78 = (bf16[480,640]{1,0:T(8,128)(2,1)S(1)}, bf16[480,640]{1,0:T(8,128)(2,1)}, u32[]{:S(2)}) copy-start(bf16[480,640]{1,0:T(8,128)(2,1)} %refs_1_.1) | copy-start | bytes 1843204
  25.6 11.2 %copy-start.79 = (bf16[480,640]{1,0:T(8,128)(2,1)S(1)}, bf16[480,640]{1,0:T(8,128)(2,1)}, u32[]{:S(2)}) copy-start(bf16[480,640]{1,0:T(8,128)(2,1)} %refs_2_.1) | copy-start | bytes 1843204
  29.4 17.0 %collective-permute-start.5 = (bf16[512,640]{1,0:T(8,128)(2,1)S(1)}, bf16[512,640]{1,0:T(8,128)(2,1)}, u32[]{:S(2)}, u32[]{:S(2)}) collective-permute-start(bf16[512,640]{1,0:T(8,128)(2,1)S(1)} %get-tuple-element.154.own_ref), channel_id=1, source_target_pairs={{0,4},{4,8},{8,12},{1,5},{5,9},{9,13},{2,6},{6,10},{10,14},{3,7},{... | collective-permute-start | bytes 1966088 | tf_op jit(solution)/shard_map/ppermute | solution.py:791
  33.5 10.9 %collective-permute-start.6 = (bf16[256,640]{1,0:T(8,128)(2,1)}, bf16[256,640]{1,0:T(8,128)(2,1)S(1)}, u32[]{:S(2)}, u32[]{:S(2)}) collective-permute-start(bf16[256,640]{1,0:T(8,128)(2,1)} %get-tuple-element.155), channel_id=1, source_target_pairs={{4,0},{8,4},{12,8},{5,1},{9,5},{13,9},{6,2},{10,6},{14,10},{7,3},{... | collective-permute-start | bytes 983048 | tf_op jit(solution)/shard_map/ppermute | solution.py:791
  35.9 10.5 %collective-permute-start.4 = (bf16[256,960]{1,0:T(8,128)(2,1)}, bf16[256,960]{1,0:T(8,128)(2,1)S(1)}, u32[]{:S(2)}, u32[]{:S(2)}) collective-permute-start(bf16[256,960]{1,0:T(8,128)(2,1)} %collective-permute-done.3.refs_4_), channel_id=1, source_target_pairs={{0,1},{1,0},{2,3},{3,2},{4,5},{5,4},{6,7},{7,6},{8,9},{9,8},{10,11... | collective-permute-start | bytes 1474568 | tf_op jit(solution)/shard_map/ppermute | solution.py:787
  38.1 13.9 %collective-permute-start.7 = (bf16[256,960]{1,0:T(8,128)(2,1)}, bf16[256,960]{1,0:T(8,128)(2,1)}, u32[]{:S(2)}, u32[]{:S(2)}) collective-permute-start(bf16[256,960]{1,0:T(8,128)(2,1)} %collective-permute-done.3.refs_4_), channel_id=1, source_target_pairs={{0,2},{1,3},{2,0},{3,1},{4,6},{5,7},{6,4},{7,5},{8,10},{9,11},{10,... | collective-permute-start | bytes 1474568 | tf_op jit(solution)/shard_map/ppermute | solution.py:787
  52.0 6.2 %collective-permute-start.8 = (bf16[256,960]{1,0:T(8,128)(2,1)}, bf16[256,960]{1,0:T(8,128)(2,1)S(1)}, u32[]{:S(2)}, u32[]{:S(2)}) collective-permute-start(bf16[256,960]{1,0:T(8,128)(2,1)} %collective-permute-done.7.refs_5_), channel_id=1, source_target_pairs={{0,1},{1,0},{2,3},{3,2},{4,5},{5,4},{6,7},{7,6},{8,9},{9,8},{10,11... | collective-permute-start | bytes 1474568 | tf_op jit(solution)/shard_map/ppermute | solution.py:787
  53.2 220.4 %reduce-scatter.4.cloned.1.call-start = ((), (), s32[]{:S(2)}) async-start(), calls=%async_computation.3 | async-start | bytes 2304000
  53.3 18.9 %copy-start.34 = (bf16[512,640]{1,0:T(8,128)(2,1)S(1)}, bf16[512,640]{1,0:T(8,128)(2,1)}, u32[]{:S(2)}) copy-start(bf16[512,640]{1,0:T(8,128)(2,1)} %copy-done.33) | copy-start | bytes 1966084
  53.3 18.9 %copy-start.54 = (bf16[256,640]{1,0:T(8,128)(2,1)S(1)}, bf16[256,640]{1,0:T(8,128)(2,1)}, u32[]{:S(2)}) copy-start(bf16[256,640]{1,0:T(8,128)(2,1)} %copy-done.53) | copy-start | bytes 983044
  53.3 31.9 %collective-permute-start.12 = (bf16[512,1024]{1,0:T(8,128)(2,1)}, bf16[512,1024]{1,0:T(8,128)(2,1)S(1)}, u32[]{:S(2)}, u32[]{:S(2)}) collective-permute-start(bf16[512,1024]{1,0:T(8,128)(2,1)} %shard_map.215.cot_a.refs_0_.refs_4_.cot_ref), channel_id=1, source_target_pairs={{0,2},{1,3},{2,0},{3,1},{4,6},{5,7},{6,4},{7,5},{8,10},{9,11},{10,... | collective-permute-start | bytes 3145736 | tf_op jit(solution)/shard_map/ppermute | solution.py:787
  54.8 17.3 %collective-permute-start.9 = (bf16[512,640]{1,0:T(8,128)(2,1)}, bf16[512,640]{1,0:T(8,128)(2,1)S(1)}, u32[]{:S(2)}, u32[]{:S(2)}) collective-permute-start(bf16[512,640]{1,0:T(8,128)(2,1)} %collective-permute-done.5.near_ref), channel_id=1, source_target_pairs={{0,4},{4,8},{8,12},{1,5},{5,9},{9,13},{2,6},{6,10},{10,14},{3,7},{... | collective-permute-start | bytes 1966088 | tf_op jit(solution)/shard_map/ppermute | solution.py:791
  67.3 18.3 %copy-start.6 = (bf16[512,960]{1,0:T(8,128)(2,1)}, bf16[512,960]{1,0:T(8,128)(2,1)S(1)}, u32[]{:S(2)}) copy-start(bf16[512,960]{1,0:T(8,128)(2,1)S(1)} %get-tuple-element.218.q_ref) | copy-start | bytes 2949124
  67.3 12.6 %collective-permute-start.10 = (bf16[512,1024]{1,0:T(8,128)(2,1)}, bf16[512,1024]{1,0:T(8,128)(2,1)S(1)}, u32[]{:S(2)}, u32[]{:S(2)}) collective-permute-start(bf16[512,1024]{1,0:T(8,128)(2,1)} %shard_map.215.cot_a.refs_0_.refs_4_.cot_ref), channel_id=1, source_target_pairs={{0,1},{1,0},{2,3},{3,2},{4,5},{5,4},{6,7},{7,6},{8,9},{9,8},{10,11... | collective-permute-start | bytes 3145736 | tf_op jit(solution)/shard_map/ppermute | solution.py:787
  72.2 13.4 %copy-start.36 = (bf16[512,640]{1,0:T(8,128)(2,1)}, bf16[512,640]{1,0:T(8,128)(2,1)S(1)}, u32[]{:S(2)}) copy-start(bf16[512,640]{1,0:T(8,128)(2,1)S(1)} %collective-permute-done.9.far_ref) | copy-start | bytes 1966084
  83.9 9.1 %collective-permute-start.11 = (bf16[256,960]{1,0:T(8,128)(2,1)S(1)}, bf16[256,960]{1,0:T(8,128)(2,1)S(1)}, u32[]{:S(2)}, u32[]{:S(2)}) collective-permute-start(bf16[256,960]{1,0:T(8,128)(2,1)S(1)} %get-tuple-element.195.nrm_a.refs_0_.refs_12_), channel_id=1, source_target_pairs={{0,1},{1,0},{2,3},{3,2},{4,5},{5,4},{6,7},{7,6},{8,9},{9,8},{10,11... | collective-permute-start | bytes 1474568 | tf_op jit(solution)/shard_map/ppermute | solution.py:787
  85.0 13.6 %collective-permute-start.15 = (bf16[256,960]{1,0:T(8,128)(2,1)S(1)}, bf16[256,960]{1,0:T(8,128)(2,1)}, u32[]{:S(2)}, u32[]{:S(2)}) collective-permute-start(bf16[256,960]{1,0:T(8,128)(2,1)S(1)} %get-tuple-element.195.nrm_a.refs_0_.refs_12_), channel_id=1, source_target_pairs={{0,2},{1,3},{2,0},{3,1},{4,6},{5,7},{6,4},{7,5},{8,10},{9,11},{10,... | collective-permute-start | bytes 1474568 | tf_op jit(solution)/shard_map/ppermute | solution.py:787
  85.2 7.8 %collective-permute-start.13 = (bf16[512,1024]{1,0:T(8,128)(2,1)S(1)}, bf16[512,1024]{1,0:T(8,128)(2,1)S(1)}, u32[]{:S(2)}, u32[]{:S(2)}) collective-permute-start(bf16[512,1024]{1,0:T(8,128)(2,1)S(1)} %collective-permute-done.12.cot_a.refs_2_.refs_6_), channel_id=1, source_target_pairs={{0,1},{1,0},{2,3},{3,2},{4,5},{5,4},{6,7},{7,6},{8,9},{9,8},{10,11... | collective-permute-start | bytes 3145736 | tf_op jit(solution)/shard_map/ppermute | solution.py:787
  96.2 21.4 %collective-permute-start.16 = (bf16[256,960]{1,0:T(8,128)(2,1)}, bf16[256,960]{1,0:T(8,128)(2,1)}, u32[]{:S(2)}, u32[]{:S(2)}) collective-permute-start(bf16[256,960]{1,0:T(8,128)(2,1)} %get-tuple-element.182.nrm_a.refs_4_.refs_16_), channel_id=1, source_target_pairs={{0,1},{1,0},{2,3},{3,2},{4,5},{5,4},{6,7},{7,6},{8,9},{9,8},{10,11... | collective-permute-start | bytes 1474568 | tf_op jit(solution)/shard_map/ppermute | solution.py:787
  96.6 28.8 %collective-permute-start.14 = (bf16[256,960]{1,0:T(8,128)(2,1)}, bf16[256,960]{1,0:T(8,128)(2,1)}, u32[]{:S(2)}, u32[]{:S(2)}) collective-permute-start(bf16[256,960]{1,0:T(8,128)(2,1)} %get-tuple-element.182.nrm_a.refs_4_.refs_16_), channel_id=1, source_target_pairs={{0,2},{1,3},{2,0},{3,1},{4,6},{5,7},{6,4},{7,5},{8,10},{9,11},{10,... | collective-permute-start | bytes 1474568 | tf_op jit(solution)/shard_map/ppermute | solution.py:787
  98.6 19.7 %collective-permute-start.17 = (bf16[256,960]{1,0:T(8,128)(2,1)}, bf16[256,960]{1,0:T(8,128)(2,1)}, u32[]{:S(2)}, u32[]{:S(2)}) collective-permute-start(bf16[256,960]{1,0:T(8,128)(2,1)} %collective-permute-done.15.nrm_a.refs_2_.refs_14_), channel_id=1, source_target_pairs={{0,1},{1,0},{2,3},{3,2},{4,5},{5,4},{6,7},{7,6},{8,9},{9,8},{10,11... | collective-permute-start | bytes 1474568 | tf_op jit(solution)/shard_map/ppermute | solution.py:787
  117.6 45.5 %copy-start.22 = (bf16[512,1024]{1,0:T(8,128)(2,1)}, bf16[512,1024]{1,0:T(8,128)(2,1)S(1)}, u32[]{:S(2)}) copy-start(bf16[512,1024]{1,0:T(8,128)(2,1)S(1)} %get-tuple-element.207.a_ref.refs_0_) | copy-start | bytes 3145732
  117.6 8.5 %collective-permute-start.18 = (bf16[512,1024]{1,0:T(8,128)(2,1)S(1)}, bf16[512,1024]{1,0:T(8,128)(2,1)S(1)}, u32[]{:S(2)}, u32[]{:S(2)}) collective-permute-start(bf16[512,1024]{1,0:T(8,128)(2,1)S(1)} %get-tuple-element.181), channel_id=1, source_target_pairs={{0,1},{1,0},{2,3},{3,2},{4,5},{5,4},{6,7},{7,6},{8,9},{9,8},{10,11... | collective-permute-start | bytes 3145736 | tf_op jit(solution)/shard_map/ppermute | solution.py:787
  125.5 11.6 %collective-permute-start.20 = (bf16[256,960]{1,0:T(8,128)(2,1)}, bf16[256,960]{1,0:T(8,128)(2,1)S(1)}, u32[]{:S(2)}, u32[]{:S(2)}) collective-permute-start(bf16[256,960]{1,0:T(8,128)(2,1)} %collective-permute-done.14.nrm_a.refs_6_.refs_18_), channel_id=1, source_target_pairs={{0,1},{1,0},{2,3},{3,2},{4,5},{5,4},{6,7},{7,6},{8,9},{9,8},{10,11... | collective-permute-start | bytes 1474568 | tf_op jit(solution)/shard_map/ppermute | solution.py:787
  125.6 8.5 %collective-permute-start.19 = (bf16[512,1024]{1,0:T(8,128)(2,1)S(1)}, bf16[512,1024]{1,0:T(8,128)(2,1)S(1)}, u32[]{:S(2)}, u32[]{:S(2)}) collective-permute-start(bf16[512,1024]{1,0:T(8,128)(2,1)S(1)} %get-tuple-element.185), channel_id=1, source_target_pairs={{0,1},{1,0},{2,3},{3,2},{4,5},{5,4},{6,7},{7,6},{8,9},{9,8},{10,11... | collective-permute-start | bytes 3145736 | tf_op jit(solution)/shard_map/ppermute | solution.py:787
  135.5 17.6 %collective-permute-start.23 = (bf16[256,1024]{1,0:T(8,128)(2,1)}, bf16[256,1024]{1,0:T(8,128)(2,1)}, u32[]{:S(2)}, u32[]{:S(2)}) collective-permute-start(bf16[256,1024]{1,0:T(8,128)(2,1)} %shard_map.224), channel_id=1, source_target_pairs={{0,2},{1,3},{2,0},{3,1},{4,6},{5,7},{6,4},{7,5},{8,10},{9,11},{10,... | collective-permute-start | bytes 1572872 | tf_op jit(solution)/shard_map/ppermute | solution.py:787
  136.8 8.0 %collective-permute-start.21 = (bf16[512,1024]{1,0:T(8,128)(2,1)S(1)}, bf16[512,1024]{1,0:T(8,128)(2,1)S(1)}, u32[]{:S(2)}, u32[]{:S(2)}) collective-permute-start(bf16[512,1024]{1,0:T(8,128)(2,1)S(1)} %get-tuple-element.189), channel_id=1, source_target_pairs={{0,1},{1,0},{2,3},{3,2},{4,5},{5,4},{6,7},{7,6},{8,9},{9,8},{10,11... | collective-permute-start | bytes 3145736 | tf_op jit(solution)/shard_map/ppermute | solution.py:787
  144.5 6.8 %collective-permute-start.22 = (bf16[512,1024]{1,0:T(8,128)(2,1)S(1)}, bf16[512,1024]{1,0:T(8,128)(2,1)S(1)}, u32[]{:S(2)}, u32[]{:S(2)}) collective-permute-start(bf16[512,1024]{1,0:T(8,128)(2,1)S(1)} %get-tuple-element.194), channel_id=1, source_target_pairs={{0,1},{1,0},{2,3},{3,2},{4,5},{5,4},{6,7},{7,6},{8,9},{9,8},{10,11... | collective-permute-start | bytes 3145736 | tf_op jit(solution)/shard_map/ppermute | solution.py:787
  152.2 16.6 %collective-permute-start.25 = (bf16[256,1024]{1,0:T(8,128)(2,1)}, bf16[256,1024]{1,0:T(8,128)(2,1)}, u32[]{:S(2)}, u32[]{:S(2)}) collective-permute-start(bf16[256,1024]{1,0:T(8,128)(2,1)} %shard_map.227), channel_id=1, source_target_pairs={{0,2},{1,3},{2,0},{3,1},{4,6},{5,7},{6,4},{7,5},{8,10},{9,11},{10,... | collective-permute-start | bytes 1572872 | tf_op jit(solution)/shard_map/ppermute | solution.py:787
  153.2 16.2 %collective-permute-start.24 = (bf16[480,640]{1,0:T(8,128)(2,1)}, bf16[480,640]{1,0:T(8,128)(2,1)S(1)}, u32[]{:S(2)}, u32[]{:S(2)}) collective-permute-start(bf16[480,640]{1,0:T(8,128)(2,1)} %get-tuple-element.210), channel_id=1, source_target_pairs={{0,16},{16,0},{1,17},{17,1},{2,18},{18,2},{3,19},{19,3},{4,20},{20... | collective-permute-start | bytes 1843208 | tf_op jit(solution)/shard_map/ppermute | solution.py:787
  167.6 42.2 %collective-permute-start.28 = (bf16[480,1280]{1,0:T(8,128)(2,1)S(1)}, bf16[480,1280]{1,0:T(8,128)(2,1)S(1)}, u32[]{:S(2)}, u32[]{:S(2)}) collective-permute-start(bf16[480,1280]{1,0:T(8,128)(2,1)S(1)} %get-tuple-element.229), channel_id=1, source_target_pairs={{0,16},{16,0},{1,17},{17,1},{2,18},{18,2},{3,19},{19,3},{4,20},{20... | collective-permute-start | bytes 3686408 | tf_op jit(solution)/shard_map/ppermute | solution.py:787
  168.8 40.0 %collective-permute-start.27 = (bf16[512,1024]{1,0:T(8,128)(2,1)S(1)}, bf16[512,1024]{1,0:T(8,128)(2,1)S(1)}, u32[]{:S(2)}, u32[]{:S(2)}) collective-permute-start(bf16[512,1024]{1,0:T(8,128)(2,1)S(1)} %shard_map.229), channel_id=1, source_target_pairs={{0,2},{1,3},{2,0},{3,1},{4,6},{5,7},{6,4},{7,5},{8,10},{9,11},{10,... | collective-permute-start | bytes 3145736 | tf_op jit(solution)/shard_map/ppermute | solution.py:787
  169.7 14.5 %copy-start.20 = (f32[256,960]{1,0:T(8,128)S(1)}, f32[256,960]{1,0:T(8,128)}, u32[]{:S(2)}) copy-start(f32[256,960]{1,0:T(8,128)} %copy-done.19) | copy-start | bytes 2949124
  169.7 14.5 %copy-start.28 = (bf16[512,1024]{1,0:T(8,128)(2,1)S(1)}, bf16[512,1024]{1,0:T(8,128)(2,1)}, u32[]{:S(2)}) copy-start(bf16[512,1024]{1,0:T(8,128)(2,1)} %copy-done.27) | copy-start | bytes 3145732
  169.7 14.5 %copy-start.31 = (bf16[512,1024]{1,0:T(8,128)(2,1)S(1)}, bf16[512,1024]{1,0:T(8,128)(2,1)}, u32[]{:S(2)}) copy-start(bf16[512,1024]{1,0:T(8,128)(2,1)} %copy-done.30) | copy-start | bytes 3145732
  182.9 23.8 %collective-permute-start.26 = (bf16[256,640]{1,0:T(8,128)(2,1)S(1)}, bf16[256,640]{1,0:T(8,128)(2,1)S(1)}, u32[]{:S(2)}, u32[]{:S(2)}) collective-permute-start(bf16[256,640]{1,0:T(8,128)(2,1)S(1)} %get-tuple-element.226), channel_id=1, source_target_pairs={{4,0},{8,4},{12,8},{5,1},{9,5},{13,9},{6,2},{10,6},{14,10},{7,3},{... | collective-permute-start | bytes 983048 | tf_op jit(solution)/shard_map/ppermute | solution.py:791
  187.8 12.3 %copy-start.93 = (bf16[256,960]{1,0:T(8,128)(2,1)}, bf16[256,960]{1,0:T(8,128)(2,1)S(1)}, u32[]{:S(2)}) copy-start(bf16[256,960]{1,0:T(8,128)(2,1)S(1)} %get-tuple-element.234.refs_3_) | copy-start | bytes 1474564
  200.1 11.3 %collective-permute-start.29 = (bf16[256,640]{1,0:T(8,128)(2,1)}, bf16[256,640]{1,0:T(8,128)(2,1)}, u32[]{:S(2)}, u32[]{:S(2)}) collective-permute-start(bf16[256,640]{1,0:T(8,128)(2,1)} %get-tuple-element.231), channel_id=1, source_target_pairs={{4,0},{8,4},{12,8},{5,1},{9,5},{13,9},{6,2},{10,6},{14,10},{7,3},{... | collective-permute-start | bytes 983048 | tf_op jit(solution)/shard_map/ppermute | solution.py:791
  201.4 32.0 %collective-permute-start.31 = (bf16[256,640]{1,0:T(8,128)(2,1)}, bf16[256,640]{1,0:T(8,128)(2,1)}, u32[]{:S(2)}, u32[]{:S(2)}) collective-permute-start(bf16[256,640]{1,0:T(8,128)(2,1)} %get-tuple-element.245), channel_id=1, source_target_pairs={{0,4},{4,8},{8,12},{1,5},{5,9},{9,13},{2,6},{6,10},{10,14},{3,7},{... | collective-permute-start | bytes 983048 | tf_op jit(solution)/shard_map/ppermute | solution.py:791
  207.5 25.8 %collective-permute-start.32 = (bf16[256,640]{1,0:T(8,128)(2,1)}, bf16[256,640]{1,0:T(8,128)(2,1)}, u32[]{:S(2)}, u32[]{:S(2)}) collective-permute-start(bf16[256,640]{1,0:T(8,128)(2,1)} %shard_map.235), channel_id=1, source_target_pairs={{4,0},{8,4},{12,8},{5,1},{9,5},{13,9},{6,2},{10,6},{14,10},{7,3},{... | collective-permute-start | bytes 983048 | tf_op jit(solution)/shard_map/ppermute | solution.py:791
  214.1 22.2 %collective-permute-start.33 = (bf16[256,640]{1,0:T(8,128)(2,1)}, bf16[256,640]{1,0:T(8,128)(2,1)}, u32[]{:S(2)}, u32[]{:S(2)}) collective-permute-start(bf16[256,640]{1,0:T(8,128)(2,1)} %shard_map.237), channel_id=1, source_target_pairs={{4,0},{8,4},{12,8},{5,1},{9,5},{13,9},{6,2},{10,6},{14,10},{7,3},{... | collective-permute-start | bytes 983048 | tf_op jit(solution)/shard_map/ppermute | solution.py:791
  215.4 124.8 %all-gather.5.cloned.1.call-start = ((), (), s32[]{:S(2)}) async-start(), calls=%async_computation.2 | async-start | bytes 2304000 | tf_op jit(solution)/shard_map/all_gather | solution.py:809
  225.9 5.5 %collective-permute-start.30 = (bf16[480,1984]{1,0:T(8,128)(2,1)S(1)}, bf16[480,1984]{1,0:T(8,128)(2,1)S(1)}, u32[]{:S(2)}, u32[]{:S(2)}) collective-permute-start(bf16[480,1984]{1,0:T(8,128)(2,1)S(1)} %get-tuple-element.241), channel_id=1, source_target_pairs={{0,1},{1,0},{2,3},{3,2},{4,5},{5,4},{6,7},{7,6},{8,9},{9,8},{10,11... | collective-permute-start | bytes 5713928 | tf_op jit(solution)/shard_map/ppermute | solution.py:787
  232.1 23.1 %collective-permute-start.35 = (bf16[240,1984]{1,0:T(8,128)(2,1)S(1)}, bf16[240,1984]{1,0:T(8,128)(2,1)S(1)}, u32[]{:S(2)}, u32[]{:S(2)}) collective-permute-start(bf16[240,1984]{1,0:T(8,128)(2,1)S(1)} %get-tuple-element.259), channel_id=1, source_target_pairs={{0,16},{16,0},{1,17},{17,1},{2,18},{18,2},{3,19},{19,3},{4,20},{20... | collective-permute-start | bytes 2856968 | tf_op jit(solution)/shard_map/ppermute | solution.py:787
  240.4 2.4 collective-permute-start.34
  243.0 14.4 %copy-start.112 = (bf16[480]{0:T(512)(128)(2,1)S(1)}, bf16[480]{0:T(512)(128)(2,1)}, u32[]{:S(2)}) copy-start(bf16[480]{0:T(512)(128)(2,1)} %param.17) | copy-start | bytes 2884
  255.6 11.7 %collective-permute-start.37 = (bf16[120,1984]{1,0:T(8,128)(2,1)S(1)}, bf16[120,1984]{1,0:T(8,128)(2,1)S(1)}, u32[]{:S(2)}, u32[]{:S(2)}) collective-permute-start(bf16[120,1984]{1,0:T(8,128)(2,1)S(1)} %get-tuple-element.265), channel_id=1, source_target_pairs={{0,2},{1,3},{2,0},{3,1},{4,6},{5,7},{6,4},{7,5},{8,10},{9,11},{10,... | collective-permute-start | bytes 1428488 | tf_op jit(solution)/shard_map/ppermute | solution.py:787
  256.8 7.4 %collective-permute-start.36 = (bf16[240,640]{1,0:T(8,128)(2,1)S(1)}, bf16[240,640]{1,0:T(8,128)(2,1)S(1)}, u32[]{:S(2)}, u32[]{:S(2)}) collective-permute-start(bf16[240,640]{1,0:T(8,128)(2,1)S(1)} %get-tuple-element.262), channel_id=1, source_target_pairs={{0,16},{16,0},{1,17},{17,1},{2,18},{18,2},{3,19},{19,3},{4,20},{20... | collective-permute-start | bytes 921608 | tf_op jit(solution)/shard_map/ppermute | solution.py:787
  264.3 6.3 %collective-permute-start.38 = (bf16[120,640]{1,0:T(8,128)(2,1)S(1)}, bf16[120,640]{1,0:T(8,128)(2,1)S(1)}, u32[]{:S(2)}, u32[]{:S(2)}) collective-permute-start(bf16[120,640]{1,0:T(8,128)(2,1)S(1)} %get-tuple-element.267), channel_id=1, source_target_pairs={{0,2},{1,3},{2,0},{3,1},{4,6},{5,7},{6,4},{7,5},{8,10},{9,11},{10,... | collective-permute-start | bytes 460808 | tf_op jit(solution)/shard_map/ppermute | solution.py:787
  267.3 10.9 %collective-permute-start.39 = (bf16[120,1984]{1,0:T(8,128)(2,1)S(1)}, bf16[120,1984]{1,0:T(8,128)(2,1)S(1)}, u32[]{:S(2)}, u32[]{:S(2)}) collective-permute-start(bf16[120,1984]{1,0:T(8,128)(2,1)S(1)} %shard_map.248.refs_0_), channel_id=1, source_target_pairs={{0,4},{4,0},{8,12},{12,8},{1,5},{5,1},{9,13},{13,9},{2,6},{6,2},{1... | collective-permute-start | bytes 1428488 | tf_op jit(solution)/shard_map/ppermute | solution.py:787
  270.6 11.2 %collective-permute-start.40 = (bf16[120,640]{1,0:T(8,128)(2,1)S(1)}, bf16[120,640]{1,0:T(8,128)(2,1)S(1)}, u32[]{:S(2)}, u32[]{:S(2)}) collective-permute-start(bf16[120,640]{1,0:T(8,128)(2,1)S(1)} %shard_map.249.refs_0_), channel_id=1, source_target_pairs={{0,4},{4,0},{8,12},{12,8},{1,5},{5,1},{9,13},{13,9},{2,6},{6,2},{1... | collective-permute-start | bytes 460808 | tf_op jit(solution)/shard_map/ppermute | solution.py:787
  278.4 32.0 %collective-permute-start.41 = (bf16[120,1984]{1,0:T(8,128)(2,1)S(1)}, bf16[120,1984]{1,0:T(8,128)(2,1)S(1)}, u32[]{:S(2)}, u32[]{:S(2)}) collective-permute-start(bf16[120,1984]{1,0:T(8,128)(2,1)S(1)} %shard_map.250.refs_0_), channel_id=1, source_target_pairs={{0,8},{4,12},{8,0},{12,4},{1,9},{5,13},{9,1},{13,5},{2,10},{6,14},... | collective-permute-start | bytes 1428488 | tf_op jit(solution)/shard_map/ppermute | solution.py:787
  281.8 44.0 %collective-permute-start.42 = (bf16[120,640]{1,0:T(8,128)(2,1)S(1)}, bf16[120,640]{1,0:T(8,128)(2,1)S(1)}, u32[]{:S(2)}, u32[]{:S(2)}) collective-permute-start(bf16[120,640]{1,0:T(8,128)(2,1)S(1)} %shard_map.251.refs_0_), channel_id=1, source_target_pairs={{0,8},{4,12},{8,0},{12,4},{1,9},{5,13},{9,1},{13,5},{2,10},{6,14},... | collective-permute-start | bytes 460808 | tf_op jit(solution)/shard_map/ppermute | solution.py:787
  310.5 33.2 %collective-permute-start.43 = (bf16[120,1984]{1,0:T(8,128)(2,1)S(1)}, bf16[120,1984]{1,0:T(8,128)(2,1)S(1)}, u32[]{:S(2)}, u32[]{:S(2)}) collective-permute-start(bf16[120,1984]{1,0:T(8,128)(2,1)S(1)} %shard_map.252.own_ref), channel_id=1, source_target_pairs={{0,2},{1,3},{2,0},{3,1},{4,6},{5,7},{6,4},{7,5},{8,10},{9,11},{10,... | collective-permute-start | bytes 1428488 | tf_op jit(solution)/shard_map/ppermute | solution.py:787
  325.8 20.3 %collective-permute-start.44 = (bf16[120,640]{1,0:T(8,128)(2,1)S(1)}, bf16[120,640]{1,0:T(8,128)(2,1)S(1)}, u32[]{:S(2)}, u32[]{:S(2)}) collective-permute-start(bf16[120,640]{1,0:T(8,128)(2,1)S(1)} %shard_map.253.own_ref), channel_id=1, source_target_pairs={{0,2},{1,3},{2,0},{3,1},{4,6},{5,7},{6,4},{7,5},{8,10},{9,11},{10,... | collective-permute-start | bytes 460808 | tf_op jit(solution)/shard_map/ppermute | solution.py:787
  343.9 4.3 %collective-permute-start.45 = (bf16[240,1984]{1,0:T(8,128)(2,1)S(1)}, bf16[240,1984]{1,0:T(8,128)(2,1)S(1)}, u32[]{:S(2)}, u32[]{:S(2)}) collective-permute-start(bf16[240,1984]{1,0:T(8,128)(2,1)S(1)} %shard_map.255.own_ref), channel_id=1, source_target_pairs={{0,1},{1,0},{2,3},{3,2},{4,5},{5,4},{6,7},{7,6},{8,9},{9,8},{10,11... | collective-permute-start | bytes 2856968 | tf_op jit(solution)/shard_map/ppermute | solution.py:787
  346.1 4.8 %collective-permute-start.46 = (bf16[240,640]{1,0:T(8,128)(2,1)S(1)}, bf16[240,640]{1,0:T(8,128)(2,1)S(1)}, u32[]{:S(2)}, u32[]{:S(2)}) collective-permute-start(bf16[240,640]{1,0:T(8,128)(2,1)S(1)} %shard_map.256.own_ref), channel_id=1, source_target_pairs={{0,1},{1,0},{2,3},{3,2},{4,5},{5,4},{6,7},{7,6},{8,9},{9,8},{10,11... | collective-permute-start | bytes 921608 | tf_op jit(solution)/shard_map/ppermute | solution.py:787
  (102 other events, 344.9 us)
Sparse Core Ops, SparseCore 0:
  53.3 51.9 all-gather.2
  215.5 43.6 reduce-scatter.3
  273.8 66.3 all-gather.4

commit v6 on v5

--- a/solution.py
+++ b/solution.py
@@ -861,7 +861,7 @@
         every = range(seqs)
         last = seqs - 1
 
-        (tokens,) = prepare(tokens.transpose(0, 2, 1))
+        tokens, cotangent = prepare(tokens.transpose(0, 2, 1), cotangent.transpose(0, 2, 1))
         cosine, sine = rotary_tables(offset, rows)
         ends = jnp.cumsum(doc_lengths, axis=1)[:, :-1]
         scal = jnp.concatenate(
@@ -912,8 +912,7 @@
         if shards == 2:
             two_y, two_beside = swap(two_x, "tp", 2), swap(two_x, "tp", 1)
             arrive(two_beside)
-        arrive(near, ahead)
-        (cotangent,) = prepare(cotangent.transpose(0, 2, 1))
+        arrive(ahead)
         windows = (shift(in_turn(near), 1), near, kv, ahead)
         if shards == 2:
             two_y = in_turn(two_y)

time: 365 us -> 365 us (level)
    ppermute x39, waiting for transfers between devices: 74.2 us -> 81.8 us  [swap(): return lax.ppermute(value, axis, [(i, i ^ bit) for i in range(count)])]
    ppermute x8, waiting for transfers between devices: 11.2 us -> 5.77 us  [shift(): return lax.ppermute(value, 'ctx', pairs)]
    unnamed x234 -> x238, local copies, waits for them, and re-layouts: 44.4 us -> 42.5 us
    pallas_call x47 -> x46, Pallas kernels: 123 us -> 123 us  [call(): pl.pallas_call(kernel, out_shape=shapes, grid=grid, in_specs=in_specs, ou...]
  transfers between devices with their start and end apart: 50 -> 50, of which waited for: 19 -> 17; matrix products, arithmetic and copies ran while one was open for 2% -> 2% of each run, Pallas kernels for 34% -> 34%
where the time goes in v6:
time: 365 us; the launch traced here: 359 us
  Pallas kernels  123 us (34%)
  waiting for transfers between devices  104 us (28%)
  starting transfers between devices  67.7 us (19%)
  local copies, waits for them, and re-layouts  43.7 us (12%)
  between operations  15.2 us (4%)
  other arithmetic  6.4 us (2%)
    pallas_call x46, Pallas kernels, call(): pl.pallas_call(kernel, out_shape=shapes, grid=grid, in_specs=in_specs, ou...  123 us
    ppermute x39, waiting for transfers between devices, swap(): return lax.ppermute(value, axis, [(i, i ^ bit) for i in range(count)])  81.8 us
    ppermute x39, starting transfers between devices, swap(): return lax.ppermute(value, axis, [(i, i ^ bit) for i in range(count)])  47.3 us
    unnamed x238, local copies, waits for them, and re-layouts  42.5 us
    ppermute x8, starting transfers between devices, shift(): return lax.ppermute(value, 'ctx', pairs)  20.1 us
    all_gather x1, waiting for transfers between devices, all_over_ctx(): return lax.all_gather(part, 'ctx', axis=0, tiled=True)  13.6 us
  transfers between devices with their start and end apart: 50, of which 17 were waited for; matrix products, arithmetic and copies ran while one was open for 2% of the time, Pallas kernels for 34%

profile of v6, /device:TPU:1, one launch (start us, length us, event | category | flops | bytes accessed | tf_op | source)
XLA Modules:
  0.0 359.5 jit_solution(7472792226852430416)
XLA Ops:
  7.3 1.3 copy.29
  8.6 1.4 copy.30
  10.8 2.0 collective-permute-start.1
  14.3 1.6 shard_map.212
  22.1 1.5 collective-permute-start.3
  25.7 2.3 shard_map.213
  29.0 4.0 %collective-permute-start.8 = (bf16[512,640]{1,0:T(8,128)(2,1)S(1)}, bf16[512,640]{1,0:T(8,128)(2,1)}, u32[]{:S(2)}, u32[]{:S(2)}) collective-permute-start(bf16[512,640]{1,0:T(8,128)(2,1)S(1)} %get-tuple-element.161.own_ref), channel_id=1, source_target_pairs={{0,4},{4,8},{8,12},{1,5},{5,9},{9,13},{2,6},{6,10},{10,14},{3,7},{... | collective-permute-start | bytes 1966088 | tf_op jit(solution)/shard_map/ppermute | solution.py:791
  33.0 3.0 collective-permute-done.3.refs_4_
  36.1 1.5 collective-permute-start.6
  38.6 1.4 shard_map.214
  40.0 9.0 %collective-permute-done.6.refs_5_ = bf16[256,960]{1,0:T(8,128)(2,1)S(1)} collective-permute-done((bf16[256,960]{1,0:T(8,128)(2,1)}, bf16[256,960]{1,0:T(8,128)(2,1)S(1)}, u32[]{:S(2)}, u32[]{:S(2)}) %collective-permute-start.6) | collective-permute-done | bytes 491552 | tf_op jit(solution)/shard_map/ppermute | solution.py:787
  49.0 1.6 collective-permute-start.7
  52.5 4.3 %collective-permute-start.9 = (bf16[512,640]{1,0:T(8,128)(2,1)}, bf16[512,640]{1,0:T(8,128)(2,1)S(1)}, u32[]{:S(2)}, u32[]{:S(2)}) collective-permute-start(bf16[512,640]{1,0:T(8,128)(2,1)} %collective-permute-done.8.near_ref), channel_id=1, source_target_pairs={{0,4},{4,8},{8,12},{1,5},{5,9},{9,13},{2,6},{6,10},{10,14},{3,7},{... | collective-permute-start | bytes 1966088 | tf_op jit(solution)/shard_map/ppermute | solution.py:791
  56.7 5.8 %collective-permute-done.5.next_ref = bf16[256,640]{1,0:T(8,128)(2,1)S(1)} collective-permute-done((bf16[256,640]{1,0:T(8,128)(2,1)}, bf16[256,640]{1,0:T(8,128)(2,1)S(1)}, u32[]{:S(2)}, u32[]{:S(2)}) %collective-permute-start.5) | collective-permute-done | bytes 327712 | tf_op jit(solution)/shard_map/ppermute | solution.py:791
  63.2 1.3 collective-permute-start.12
  64.6 1.3 copy-done.59
  68.2 3.5 shard_map.215
  72.9 7.0 %shard_map.216 = (bf16[256,960]{1,0:T(8,128)(2,1)S(1)}, f32[256,128]{1,0:T(8,128)S(1)}) custom-call(s32[1,5]{1,0:T(1,128)S(1)} %get-tuple-element.294.scal_ref, bf16[512,960]{1,0:T(8,128)(2,1)S(1)} %get-tuple-element.220.q_ref, bf16[512,640]{1,0:T(8,128)(2,1)S(1)} %collective-permute-done.9.far_ref, bf16[512,640]{1,0:T(8,128)(2,1)} %collective-permute-done.8.near_ref, ...), custom_call_target="tpu_custom_call" | custom-call | flops 78199996416 | tf_op jit(solution)/shard_map/pallas_call | solution.py:101
  81.6 2.4 shard_map.217
  85.2 2.3 collective-permute-done.12.cot_a.refs_2_.refs_6_
  87.5 2.3 collective-permute-start.13
  89.9 6.7 %shard_map.218 = (bf16[256,960]{1,0:T(8,128)(2,1)S(1)}, f32[256,128]{1,0:T(8,128)S(1)}) custom-call(s32[1,5]{1,0:T(1,128)S(1)} %get-tuple-element.295.scal_ref, bf16[512,960]{1,0:T(8,128)(2,1)S(1)} %get-tuple-element.220.q_ref, bf16[512,640]{1,0:T(8,128)(2,1)S(1)} %collective-permute-done.9.far_ref, bf16[512,640]{1,0:T(8,128)(2,1)} %collective-permute-done.8.near_ref, ...), custom_call_target="tpu_custom_call" | custom-call | flops 78199996416 | tf_op jit(solution)/shard_map/pallas_call | solution.py:101
  97.3 2.2 shard_map.219
  100.8 1.8 collective-permute-start.14
  103.1 2.4 all-gather.3.cloned.1.call-done.w_ref
  105.5 2.0 copy-done.63
  110.8 6.8 %shard_map.220 = (bf16[512,640]{1,0:T(8,128)(2,1)S(1)}, bf16[512,640]{1,0:T(8,128)(2,1)S(1)}, bf16[512,640]{1,0:T(8,128)(2,1)S(1)}, bf16[512,1024]{1,0:T(8,128)(2,1)S(1)}, bf16[512,1024]{1,0:T(8,128)(2,1)S(1)}) custom-call(bf16[256,960]{1,0:T(8,128)(2,1)S(1)} %copy-done.81, bf16[256,960]{1,0:T(8,128)(2,1)S(1)} %copy-done.84, ...), custom_call_target="tpu_custom_call" | custom-call | flops 82800001024 | tf_op jit(solution)/shard_map/pallas_call | solution.py:101
  118.5 7.1 %shard_map.221 = (bf16[512,640]{1,0:T(8,128)(2,1)S(1)}, bf16[512,640]{1,0:T(8,128)(2,1)S(1)}, bf16[512,640]{1,0:T(8,128)(2,1)S(1)}, bf16[512,1024]{1,0:T(8,128)(2,1)S(1)}, bf16[512,1024]{1,0:T(8,128)(2,1)S(1)}) custom-call(bf16[256,960]{1,0:T(8,128)(2,1)} %collective-permute-done.15.nrm_a.refs_2_.refs_14_, ...), custom_call_target="tpu_custom_call" | custom-call | flops 82800001024 | tf_op jit(solution)/shard_map/pallas_call | solution.py:101
  127.1 7.0 %shard_map.222 = (bf16[512,640]{1,0:T(8,128)(2,1)S(1)}, bf16[512,640]{1,0:T(8,128)(2,1)S(1)}, bf16[512,640]{1,0:T(8,128)(2,1)S(1)}, bf16[512,1024]{1,0:T(8,128)(2,1)S(1)}, bf16[512,1024]{1,0:T(8,128)(2,1)S(1)}) custom-call(bf16[256,960]{1,0:T(8,128)(2,1)} %get-tuple-element.184.nrm_a.refs_4_.refs_16_, ...), custom_call_target="tpu_custom_call" | custom-call | flops 82800001024 | tf_op jit(solution)/shard_map/pallas_call | solution.py:101
  137.2 7.3 %shard_map.224 = (bf16[512,640]{1,0:T(8,128)(2,1)S(1)}, bf16[512,640]{1,0:T(8,128)(2,1)S(1)}, bf16[512,640]{1,0:T(8,128)(2,1)S(1)}, bf16[512,1024]{1,0:T(8,128)(2,1)S(1)}, bf16[512,1024]{1,0:T(8,128)(2,1)S(1)}) custom-call(bf16[256,960]{1,0:T(8,128)(2,1)} %collective-permute-done.14.nrm_a.refs_6_.refs_18_, ...), custom_call_target="tpu_custom_call" | custom-call | flops 82800001024 | tf_op jit(solution)/shard_map/pallas_call | solution.py:101
  145.9 5.5 %shard_map.225 = (f32[480,640]{1,0:T(8,128)S(1)}, bf16[480,640]{1,0:T(8,128)(2,1)}) custom-call(s32[1]{0:T(128)} %bitcast.place_ref, bf16[512,1024]{1,0:T(8,128)(2,1)} %get-tuple-element.192.cot_a.refs_0_.refs_4_.cot_ref, bf16[512,1024]{1,0:T(8,128)(2,1)S(1)} %copy-done.70, bf16[512,1024]{1,0:T(8,128)(2,1)S(1)} %copy-done.67, ...), custom_call_target="tpu_custom_call" | custom-call | flops 57500000256 | tf_op jit(solution)/shard_map/pallas_call | solution.py:101
  153.6 9.3 %shard_map.227 = (f32[480,1280]{1,0:T(8,128)S(1)}, bf16[480,1280]{1,0:T(8,128)(2,1)S(1)}) custom-call(s32[1]{0:T(128)} %bitcast.place_ref, bf16[256,960]{1,0:T(8,128)(2,1)S(1)} %copy-done.82, bf16[256,960]{1,0:T(8,128)(2,1)S(1)} %copy-done.85, bf16[256,960]{1,0:T(8,128)(2,1)} %collective-permute-done.15.nrm_a.refs_2_.refs_14_, ...), custom_call_target="tpu_custom_call" | custom-call | flops 115000000512 | tf_op jit(solution)/shard_map/pallas_call | solution.py:101
  165.1 2.5 shard_map.229
  169.8 11.5 %shard_map.231 = (bf16[256,960]{1,0:T(8,128)(2,1)S(1)}, bf16[256,640]{1,0:T(8,128)(2,1)S(1)}, bf16[256,640]{1,0:T(8,128)(2,1)S(1)}, f32[256,640]{1,0:T(8,128)S(1)}, bf16[128,640]{1,0:T(8,128)(2,1)S(1)}) custom-call(s32[1,5]{1,0:T(1,128)S(1)} %get-tuple-element.294.scal_ref, bf16[512,960]{1,0:T(8,128)(2,1)S(1)} %copy-done.7, bf16[512,640]{1,0:T(8,128)(2,1)S(1)} %copy-done.37, ...), custom_call_target="tpu_custom_call" | custom-call | flops 134550003712 | tf_op jit(solution)/shard_map/pallas_call | solution.py:101
  184.4 2.5 shard_map.232
  187.9 12.3 %shard_map.233 = (bf16[256,960]{1,0:T(8,128)(2,1)S(1)}, bf16[256,640]{1,0:T(8,128)(2,1)}, bf16[256,640]{1,0:T(8,128)(2,1)S(1)}, f32[256,640]{1,0:T(8,128)S(1)}, bf16[256,640]{1,0:T(8,128)(2,1)}) custom-call(s32[1,5]{1,0:T(1,128)S(1)} %get-tuple-element.295.scal_ref, bf16[512,960]{1,0:T(8,128)(2,1)S(1)} %copy-done.7, bf16[512,640]{1,0:T(8,128)(2,1)S(1)} %copy-done.37, ...), custom_call_target="tpu_custom_call" | custom-call | flops 575000000 | tf_op jit(solution)/shard_map/pallas_call | solution.py:101
  200.2 1.3 collective-permute-start.29
  201.5 5.3 %collective-permute-start.31 = (bf16[256,640]{1,0:T(8,128)(2,1)}, bf16[256,640]{1,0:T(8,128)(2,1)}, u32[]{:S(2)}, u32[]{:S(2)}) collective-permute-start(bf16[256,640]{1,0:T(8,128)(2,1)} %get-tuple-element.247), channel_id=1, source_target_pairs={{0,4},{4,8},{8,12},{1,5},{5,9},{9,13},{2,6},{6,10},{10,14},{3,7},{... | collective-permute-start | bytes 983048 | tf_op jit(solution)/shard_map/ppermute | solution.py:791
  212.4 1.8 shard_map.236
  223.3 2.7 shard_map.237
  226.0 1.9 collective-permute-start.30
  230.1 1.4 collective-permute-done.30.got_ref
  233.6 2.8 shard_map.241
  236.5 2.8 shard_map.242
  241.2 1.7 collective-permute-done.34.got_ref
  243.1 12.3 %collective-permute-done.35.got_ref = bf16[240,1984]{1,0:T(8,128)(2,1)S(1)} collective-permute-done((bf16[240,1984]{1,0:T(8,128)(2,1)S(1)}, bf16[240,1984]{1,0:T(8,128)(2,1)S(1)}, u32[]{:S(2)}, u32[]{:S(2)}) %collective-permute-start.35) | collective-permute-done | bytes 952352 | tf_op jit(solution)/shard_map/ppermute | solution.py:787
  258.5 1.4 maximum_bitcast_fusion
  260.0 4.3 %collective-permute-done.36.got_ref = bf16[240,640]{1,0:T(8,128)(2,1)S(1)} collective-permute-done((bf16[240,640]{1,0:T(8,128)(2,1)S(1)}, bf16[240,640]{1,0:T(8,128)(2,1)S(1)}, u32[]{:S(2)}, u32[]{:S(2)}) %collective-permute-start.36) | collective-permute-done | bytes 307232 | tf_op jit(solution)/shard_map/ppermute | solution.py:787
  264.8 2.6 collective-permute-done.37.refs_1_
  267.5 3.1 collective-permute-start.39
  270.7 3.1 collective-permute-start.40
  273.8 4.6 %collective-permute-done.39.refs_1_ = bf16[120,1984]{1,0:T(8,128)(2,1)S(1)} collective-permute-done((bf16[120,1984]{1,0:T(8,128)(2,1)S(1)}, bf16[120,1984]{1,0:T(8,128)(2,1)S(1)}, u32[]{:S(2)}, u32[]{:S(2)}) %collective-permute-start.39) | collective-permute-done | bytes 476192 | tf_op jit(solution)/shard_map/ppermute | solution.py:787
  278.5 3.3 collective-permute-start.41
  281.9 3.2 collective-permute-start.42
  285.1 25.5 %collective-permute-done.41.refs_1_ = bf16[120,1984]{1,0:T(8,128)(2,1)S(1)} collective-permute-done((bf16[120,1984]{1,0:T(8,128)(2,1)S(1)}, bf16[120,1984]{1,0:T(8,128)(2,1)S(1)}, u32[]{:S(2)}, u32[]{:S(2)}) %collective-permute-start.41) | collective-permute-done | bytes 476192 | tf_op jit(solution)/shard_map/ppermute | solution.py:787
  310.6 1.3 collective-permute-start.43
  311.9 13.9 %collective-permute-done.42.refs_1_ = bf16[120,640]{1,0:T(8,128)(2,1)S(1)} collective-permute-done((bf16[120,640]{1,0:T(8,128)(2,1)S(1)}, bf16[120,640]{1,0:T(8,128)(2,1)S(1)}, u32[]{:S(2)}, u32[]{:S(2)}) %collective-permute-start.42) | collective-permute-done | bytes 153632 | tf_op jit(solution)/shard_map/ppermute | solution.py:787
  326.7 13.6 %all-gather.5.cloned.1.call-done.all_ref = bf16[480,1920]{1,0:T(8,128)(2,1)} async-done(((bf16[120,1920]{1,0:T(8,128)(2,1)}), bf16[480,1920]{1,0:T(8,128)(2,1)}) %all-gather.5.cloned.1.call-update) | async-done | bytes 1843216 | tf_op jit(solution)/shard_map/all_gather | solution.py:809
  340.3 1.5 copy-done.65
  341.8 2.0 shard_map.253
  344.1 2.1 collective-permute-start.45
  346.3 1.4 collective-permute-start.46
  348.4 2.6 shard_map.256
  351.0 1.7 shard_map.257
  (345 shorter events, 71.1 us)
Async XLA Ops:
  7.2 98.3 %all-gather.3.cloned.1.call-start = ((), (), s32[]{:S(2)}) async-start(), calls=%async_computation.1 | async-start | bytes 5529600 | tf_op jit(solution)/shard_map/all_gather | solution.py:911
  10.8 9.2 %collective-permute-start.1 = (bf16[240,640]{1,0:T(8,128)(2,1)}, bf16[240,640]{1,0:T(8,128)(2,1)S(1)}, u32[]{:S(2)}, u32[]{:S(2)}) collective-permute-start(bf16[240,640]{1,0:T(8,128)(2,1)} %fusion), channel_id=1, source_target_pairs={{0,16},{16,0},{1,17},{17,1},{2,18},{18,2},{3,19},{19,3},{4,20},{20... | collective-permute-start | bytes 921608 | tf_op jit(solution)/shard_map/ppermute | solution.py:787
  12.9 9.1 %collective-permute-start = (bf16[2,480]{1,0:T(2,128)(2,1)S(1)}, bf16[2,480]{1,0:T(2,128)(2,1)S(1)}, u32[]{:S(2)}, u32[]{:S(2)}) collective-permute-start(bf16[2,480]{1,0:T(2,128)(2,1)S(1)} %pad_maximum_fusion.4), channel_id=1, source_target_pairs={{0,16},{16,0},{1,17},{17,1},{2,18},{18,2},{3,19},{19,3},{4,20},{20... | collective-permute-start | bytes 5768 | tf_op jit(solution)/shard_map/ppermute | solution.py:787
  20.1 3.6 %collective-permute-start.2 = (bf16[240,640]{1,0:T(8,128)(2,1)S(1)}, bf16[240,640]{1,0:T(8,128)(2,1)S(1)}, u32[]{:S(2)}, u32[]{:S(2)}) collective-permute-start(bf16[240,640]{1,0:T(8,128)(2,1)S(1)} %collective-permute-done.1.refs_5_), channel_id=1, source_target_pairs={{0,1},{1,0},{2,3},{3,2},{4,5},{5,4},{6,7},{7,6},{8,9},{9,8},{10,11... | collective-permute-start | bytes 921608 | tf_op jit(solution)/shard_map/ppermute | solution.py:787
  22.1 13.9 %collective-permute-start.3 = (bf16[256,960]{1,0:T(8,128)(2,1)}, bf16[256,960]{1,0:T(8,128)(2,1)}, u32[]{:S(2)}, u32[]{:S(2)}) collective-permute-start(bf16[256,960]{1,0:T(8,128)(2,1)} %pad_maximum_fusion.1), channel_id=1, source_target_pairs={{0,16},{16,0},{1,17},{17,1},{2,18},{18,2},{3,19},{19,3},{4,20},{20... | collective-permute-start | bytes 1474568 | tf_op jit(solution)/shard_map/ppermute | solution.py:787
  25.7 12.9 %copy-start.77 = (bf16[480,640]{1,0:T(8,128)(2,1)S(1)}, bf16[480,640]{1,0:T(8,128)(2,1)}, u32[]{:S(2)}) copy-start(bf16[480,640]{1,0:T(8,128)(2,1)} %refs_0_) | copy-start | bytes 1843204
  25.7 12.9 %copy-start.78 = (bf16[480,640]{1,0:T(8,128)(2,1)S(1)}, bf16[480,640]{1,0:T(8,128)(2,1)}, u32[]{:S(2)}) copy-start(bf16[480,640]{1,0:T(8,128)(2,1)} %refs_1_.1) | copy-start | bytes 1843204
  25.7 12.9 %copy-start.79 = (bf16[480,640]{1,0:T(8,128)(2,1)S(1)}, bf16[480,640]{1,0:T(8,128)(2,1)}, u32[]{:S(2)}) copy-start(bf16[480,640]{1,0:T(8,128)(2,1)} %refs_2_.1) | copy-start | bytes 1843204
  29.0 23.5 %collective-permute-start.8 = (bf16[512,640]{1,0:T(8,128)(2,1)S(1)}, bf16[512,640]{1,0:T(8,128)(2,1)}, u32[]{:S(2)}, u32[]{:S(2)}) collective-permute-start(bf16[512,640]{1,0:T(8,128)(2,1)S(1)} %get-tuple-element.161.own_ref), channel_id=1, source_target_pairs={{0,4},{4,8},{8,12},{1,5},{5,9},{9,13},{2,6},{6,10},{10,14},{3,7},{... | collective-permute-start | bytes 1966088 | tf_op jit(solution)/shard_map/ppermute | solution.py:791
  36.1 14.7 %copy-start.117 = (s32[2,3]{1,0:T(2,128)S(1)}, s32[2,3]{1,0:T(2,128)}, u32[]{:S(2)}) copy-start(s32[2,3]{1,0:T(2,128)} %param.16) | copy-start | bytes 76
  36.1 16.1 %copy-start.116 = (s32[2,2]{1,0:T(2,128)S(1)}, s32[2,2]{1,0:T(2,128)}, u32[]{:S(2)}) copy-start(s32[2,2]{1,0:T(2,128)} %param.15) | copy-start | bytes 52
  36.1 12.9 %collective-permute-start.6 = (bf16[256,960]{1,0:T(8,128)(2,1)}, bf16[256,960]{1,0:T(8,128)(2,1)S(1)}, u32[]{:S(2)}, u32[]{:S(2)}) collective-permute-start(bf16[256,960]{1,0:T(8,128)(2,1)} %collective-permute-done.3.refs_4_), channel_id=1, source_target_pairs={{0,2},{1,3},{2,0},{3,1},{4,6},{5,7},{6,4},{7,5},{8,10},{9,11},{10,... | collective-permute-start | bytes 1474568 | tf_op jit(solution)/shard_map/ppermute | solution.py:787
  37.6 25.6 %collective-permute-start.4 = (bf16[256,960]{1,0:T(8,128)(2,1)}, bf16[256,960]{1,0:T(8,128)(2,1)}, u32[]{:S(2)}, u32[]{:S(2)}) collective-permute-start(bf16[256,960]{1,0:T(8,128)(2,1)} %collective-permute-done.3.refs_4_), channel_id=1, source_target_pairs={{0,1},{1,0},{2,3},{3,2},{4,5},{5,4},{6,7},{7,6},{8,9},{9,8},{10,11... | collective-permute-start | bytes 1474568 | tf_op jit(solution)/shard_map/ppermute | solution.py:787
  49.0 15.5 %copy-start.88 = (bf16[256,960]{1,0:T(8,128)(2,1)}, bf16[256,960]{1,0:T(8,128)(2,1)S(1)}, u32[]{:S(2)}) copy-start(bf16[256,960]{1,0:T(8,128)(2,1)S(1)} %collective-permute-done.6.refs_5_) | copy-start | bytes 1474564
  49.0 15.5 %collective-permute-start.7 = (bf16[256,960]{1,0:T(8,128)(2,1)S(1)}, bf16[256,960]{1,0:T(8,128)(2,1)}, u32[]{:S(2)}, u32[]{:S(2)}) collective-permute-start(bf16[256,960]{1,0:T(8,128)(2,1)S(1)} %collective-permute-done.6.refs_5_), channel_id=1, source_target_pairs={{0,1},{1,0},{2,3},{3,2},{4,5},{5,4},{6,7},{7,6},{8,9},{9,8},{10,11... | collective-permute-start | bytes 1474568 | tf_op jit(solution)/shard_map/ppermute | solution.py:787
  50.9 11.6 %collective-permute-start.5 = (bf16[256,640]{1,0:T(8,128)(2,1)}, bf16[256,640]{1,0:T(8,128)(2,1)S(1)}, u32[]{:S(2)}, u32[]{:S(2)}) collective-permute-start(bf16[256,640]{1,0:T(8,128)(2,1)} %copy-done.95), channel_id=1, source_target_pairs={{4,0},{8,4},{12,8},{5,1},{9,5},{13,9},{6,2},{10,6},{14,10},{7,3},{... | collective-permute-start | bytes 983048 | tf_op jit(solution)/shard_map/ppermute | solution.py:791
  52.4 221.4 %reduce-scatter.4.cloned.1.call-start = ((), (), s32[]{:S(2)}) async-start(), calls=%async_computation.3 | async-start | bytes 2304000
  52.5 20.4 %collective-permute-start.9 = (bf16[512,640]{1,0:T(8,128)(2,1)}, bf16[512,640]{1,0:T(8,128)(2,1)S(1)}, u32[]{:S(2)}, u32[]{:S(2)}) collective-permute-start(bf16[512,640]{1,0:T(8,128)(2,1)} %collective-permute-done.8.near_ref), channel_id=1, source_target_pairs={{0,4},{4,8},{8,12},{1,5},{5,9},{9,13},{2,6},{6,10},{10,14},{3,7},{... | collective-permute-start | bytes 1966088 | tf_op jit(solution)/shard_map/ppermute | solution.py:791
  63.2 24.3 %collective-permute-start.12 = (bf16[512,1024]{1,0:T(8,128)(2,1)}, bf16[512,1024]{1,0:T(8,128)(2,1)S(1)}, u32[]{:S(2)}, u32[]{:S(2)}) collective-permute-start(bf16[512,1024]{1,0:T(8,128)(2,1)} %get-tuple-element.192.cot_a.refs_0_.refs_4_.cot_ref), channel_id=1, source_target_pairs={{0,2},{1,3},{2,0},{3,1},{4,6},{5,7},{6,4},{7,5},{8,10},{9,11},{10,... | collective-permute-start | bytes 3145736 | tf_op jit(solution)/shard_map/ppermute | solution.py:787
  71.7 18.1 %copy-start.6 = (bf16[512,960]{1,0:T(8,128)(2,1)}, bf16[512,960]{1,0:T(8,128)(2,1)S(1)}, u32[]{:S(2)}) copy-start(bf16[512,960]{1,0:T(8,128)(2,1)S(1)} %get-tuple-element.220.q_ref) | copy-start | bytes 2949124
  71.7 8.9 %collective-permute-start.10 = (bf16[512,1024]{1,0:T(8,128)(2,1)}, bf16[512,1024]{1,0:T(8,128)(2,1)S(1)}, u32[]{:S(2)}, u32[]{:S(2)}) collective-permute-start(bf16[512,1024]{1,0:T(8,128)(2,1)} %get-tuple-element.192.cot_a.refs_0_.refs_4_.cot_ref), channel_id=1, source_target_pairs={{0,1},{1,0},{2,3},{3,2},{4,5},{5,4},{6,7},{7,6},{8,9},{9,8},{10,11... | collective-permute-start | bytes 3145736 | tf_op jit(solution)/shard_map/ppermute | solution.py:787
  72.8 17.0 %copy-start.36 = (bf16[512,640]{1,0:T(8,128)(2,1)}, bf16[512,640]{1,0:T(8,128)(2,1)S(1)}, u32[]{:S(2)}) copy-start(bf16[512,640]{1,0:T(8,128)(2,1)S(1)} %collective-permute-done.9.far_ref) | copy-start | bytes 1966084
  84.8 12.6 %copy-start = (bf16[960,960]{1,0:T(8,128)(2,1)}, bf16[960,960]{1,0:T(8,128)(2,1)S(1)}, u32[]{:S(2)}) copy-start(bf16[960,960]{1,0:T(8,128)(2,1)S(1)} %get-tuple-element.174.refs_3_.wo_ref) | copy-start | bytes 5529604
  84.8 12.5 %collective-permute-start.11 = (bf16[256,960]{1,0:T(8,128)(2,1)S(1)}, bf16[256,960]{1,0:T(8,128)(2,1)S(1)}, u32[]{:S(2)}, u32[]{:S(2)}) collective-permute-start(bf16[256,960]{1,0:T(8,128)(2,1)S(1)} %get-tuple-element.197.nrm_a.refs_0_.refs_12_), channel_id=1, source_target_pairs={{0,1},{1,0},{2,3},{3,2},{4,5},{5,4},{6,7},{7,6},{8,9},{9,8},{10,11... | collective-permute-start | bytes 1474568 | tf_op jit(solution)/shard_map/ppermute | solution.py:787
  85.0 17.5 %collective-permute-start.15 = (bf16[256,960]{1,0:T(8,128)(2,1)S(1)}, bf16[256,960]{1,0:T(8,128)(2,1)}, u32[]{:S(2)}, u32[]{:S(2)}) collective-permute-start(bf16[256,960]{1,0:T(8,128)(2,1)S(1)} %get-tuple-element.197.nrm_a.refs_0_.refs_12_), channel_id=1, source_target_pairs={{0,2},{1,3},{2,0},{3,1},{4,6},{5,7},{6,4},{7,5},{8,10},{9,11},{10,... | collective-permute-start | bytes 1474568 | tf_op jit(solution)/shard_map/ppermute | solution.py:787
  87.5 9.8 %collective-permute-start.13 = (bf16[512,1024]{1,0:T(8,128)(2,1)S(1)}, bf16[512,1024]{1,0:T(8,128)(2,1)S(1)}, u32[]{:S(2)}, u32[]{:S(2)}) collective-permute-start(bf16[512,1024]{1,0:T(8,128)(2,1)S(1)} %collective-permute-done.12.cot_a.refs_2_.refs_6_), channel_id=1, source_target_pairs={{0,1},{1,0},{2,3},{3,2},{4,5},{5,4},{6,7},{7,6},{8,9},{9,8},{10,11... | collective-permute-start | bytes 3145736 | tf_op jit(solution)/shard_map/ppermute | solution.py:787
  100.5 17.2 %collective-permute-start.16 = (bf16[256,960]{1,0:T(8,128)(2,1)}, bf16[256,960]{1,0:T(8,128)(2,1)}, u32[]{:S(2)}, u32[]{:S(2)}) collective-permute-start(bf16[256,960]{1,0:T(8,128)(2,1)} %get-tuple-element.184.nrm_a.refs_4_.refs_16_), channel_id=1, source_target_pairs={{0,1},{1,0},{2,3},{3,2},{4,5},{5,4},{6,7},{7,6},{8,9},{9,8},{10,11... | collective-permute-start | bytes 1474568 | tf_op jit(solution)/shard_map/ppermute | solution.py:787
  100.8 24.8 %collective-permute-start.14 = (bf16[256,960]{1,0:T(8,128)(2,1)}, bf16[256,960]{1,0:T(8,128)(2,1)}, u32[]{:S(2)}, u32[]{:S(2)}) collective-permute-start(bf16[256,960]{1,0:T(8,128)(2,1)} %get-tuple-element.184.nrm_a.refs_4_.refs_16_), channel_id=1, source_target_pairs={{0,2},{1,3},{2,0},{3,1},{4,6},{5,7},{6,4},{7,5},{8,10},{9,11},{10,... | collective-permute-start | bytes 1474568 | tf_op jit(solution)/shard_map/ppermute | solution.py:787
  102.5 15.9 %collective-permute-start.17 = (bf16[256,960]{1,0:T(8,128)(2,1)}, bf16[256,960]{1,0:T(8,128)(2,1)}, u32[]{:S(2)}, u32[]{:S(2)}) collective-permute-start(bf16[256,960]{1,0:T(8,128)(2,1)} %collective-permute-done.15.nrm_a.refs_2_.refs_14_), channel_id=1, source_target_pairs={{0,1},{1,0},{2,3},{3,2},{4,5},{5,4},{6,7},{7,6},{8,9},{9,8},{10,11... | collective-permute-start | bytes 1474568 | tf_op jit(solution)/shard_map/ppermute | solution.py:787
  117.7 45.5 %copy-start.22 = (bf16[512,1024]{1,0:T(8,128)(2,1)}, bf16[512,1024]{1,0:T(8,128)(2,1)S(1)}, u32[]{:S(2)}) copy-start(bf16[512,1024]{1,0:T(8,128)(2,1)S(1)} %get-tuple-element.209.a_ref.refs_0_) | copy-start | bytes 3145732
  117.7 8.5 %collective-permute-start.18 = (bf16[512,1024]{1,0:T(8,128)(2,1)S(1)}, bf16[512,1024]{1,0:T(8,128)(2,1)S(1)}, u32[]{:S(2)}, u32[]{:S(2)}) collective-permute-start(bf16[512,1024]{1,0:T(8,128)(2,1)S(1)} %get-tuple-element.183), channel_id=1, source_target_pairs={{0,1},{1,0},{2,3},{3,2},{4,5},{5,4},{6,7},{7,6},{8,9},{9,8},{10,11... | collective-permute-start | bytes 3145736 | tf_op jit(solution)/shard_map/ppermute | solution.py:787
  125.6 11.6 %collective-permute-start.20 = (bf16[256,960]{1,0:T(8,128)(2,1)}, bf16[256,960]{1,0:T(8,128)(2,1)S(1)}, u32[]{:S(2)}, u32[]{:S(2)}) collective-permute-start(bf16[256,960]{1,0:T(8,128)(2,1)} %collective-permute-done.14.nrm_a.refs_6_.refs_18_), channel_id=1, source_target_pairs={{0,1},{1,0},{2,3},{3,2},{4,5},{5,4},{6,7},{7,6},{8,9},{9,8},{10,11... | collective-permute-start | bytes 1474568 | tf_op jit(solution)/shard_map/ppermute | solution.py:787
  125.7 8.5 %collective-permute-start.19 = (bf16[512,1024]{1,0:T(8,128)(2,1)S(1)}, bf16[512,1024]{1,0:T(8,128)(2,1)S(1)}, u32[]{:S(2)}, u32[]{:S(2)}) collective-permute-start(bf16[512,1024]{1,0:T(8,128)(2,1)S(1)} %get-tuple-element.187), channel_id=1, source_target_pairs={{0,1},{1,0},{2,3},{3,2},{4,5},{5,4},{6,7},{7,6},{8,9},{9,8},{10,11... | collective-permute-start | bytes 3145736 | tf_op jit(solution)/shard_map/ppermute | solution.py:787
  135.7 17.6 %collective-permute-start.23 = (bf16[256,1024]{1,0:T(8,128)(2,1)}, bf16[256,1024]{1,0:T(8,128)(2,1)}, u32[]{:S(2)}, u32[]{:S(2)}) collective-permute-start(bf16[256,1024]{1,0:T(8,128)(2,1)} %shard_map.223), channel_id=1, source_target_pairs={{0,2},{1,3},{2,0},{3,1},{4,6},{5,7},{6,4},{7,5},{8,10},{9,11},{10,... | collective-permute-start | bytes 1572872 | tf_op jit(solution)/shard_map/ppermute | solution.py:787
  136.9 8.0 %collective-permute-start.21 = (bf16[512,1024]{1,0:T(8,128)(2,1)S(1)}, bf16[512,1024]{1,0:T(8,128)(2,1)S(1)}, u32[]{:S(2)}, u32[]{:S(2)}) collective-permute-start(bf16[512,1024]{1,0:T(8,128)(2,1)S(1)} %get-tuple-element.191), channel_id=1, source_target_pairs={{0,1},{1,0},{2,3},{3,2},{4,5},{5,4},{6,7},{7,6},{8,9},{9,8},{10,11... | collective-permute-start | bytes 3145736 | tf_op jit(solution)/shard_map/ppermute | solution.py:787
  144.6 6.8 %collective-permute-start.22 = (bf16[512,1024]{1,0:T(8,128)(2,1)S(1)}, bf16[512,1024]{1,0:T(8,128)(2,1)S(1)}, u32[]{:S(2)}, u32[]{:S(2)}) collective-permute-start(bf16[512,1024]{1,0:T(8,128)(2,1)S(1)} %get-tuple-element.196), channel_id=1, source_target_pairs={{0,1},{1,0},{2,3},{3,2},{4,5},{5,4},{6,7},{7,6},{8,9},{9,8},{10,11... | collective-permute-start | bytes 3145736 | tf_op jit(solution)/shard_map/ppermute | solution.py:787
  152.3 16.6 %collective-permute-start.25 = (bf16[256,1024]{1,0:T(8,128)(2,1)}, bf16[256,1024]{1,0:T(8,128)(2,1)}, u32[]{:S(2)}, u32[]{:S(2)}) collective-permute-start(bf16[256,1024]{1,0:T(8,128)(2,1)} %shard_map.226), channel_id=1, source_target_pairs={{0,2},{1,3},{2,0},{3,1},{4,6},{5,7},{6,4},{7,5},{8,10},{9,11},{10,... | collective-permute-start | bytes 1572872 | tf_op jit(solution)/shard_map/ppermute | solution.py:787
  153.3 16.2 %collective-permute-start.24 = (bf16[480,640]{1,0:T(8,128)(2,1)}, bf16[480,640]{1,0:T(8,128)(2,1)S(1)}, u32[]{:S(2)}, u32[]{:S(2)}) collective-permute-start(bf16[480,640]{1,0:T(8,128)(2,1)} %get-tuple-element.212), channel_id=1, source_target_pairs={{0,16},{16,0},{1,17},{17,1},{2,18},{18,2},{3,19},{19,3},{4,20},{20... | collective-permute-start | bytes 1843208 | tf_op jit(solution)/shard_map/ppermute | solution.py:787
  167.7 42.3 %collective-permute-start.28 = (bf16[480,1280]{1,0:T(8,128)(2,1)S(1)}, bf16[480,1280]{1,0:T(8,128)(2,1)S(1)}, u32[]{:S(2)}, u32[]{:S(2)}) collective-permute-start(bf16[480,1280]{1,0:T(8,128)(2,1)S(1)} %get-tuple-element.231), channel_id=1, source_target_pairs={{0,16},{16,0},{1,17},{17,1},{2,18},{18,2},{3,19},{19,3},{4,20},{20... | collective-permute-start | bytes 3686408 | tf_op jit(solution)/shard_map/ppermute | solution.py:787
  168.9 40.0 %collective-permute-start.27 = (bf16[512,1024]{1,0:T(8,128)(2,1)S(1)}, bf16[512,1024]{1,0:T(8,128)(2,1)S(1)}, u32[]{:S(2)}, u32[]{:S(2)}) collective-permute-start(bf16[512,1024]{1,0:T(8,128)(2,1)S(1)} %shard_map.228), channel_id=1, source_target_pairs={{0,2},{1,3},{2,0},{3,1},{4,6},{5,7},{6,4},{7,5},{8,10},{9,11},{10,... | collective-permute-start | bytes 3145736 | tf_op jit(solution)/shard_map/ppermute | solution.py:787
  169.8 14.5 %copy-start.20 = (f32[256,960]{1,0:T(8,128)S(1)}, f32[256,960]{1,0:T(8,128)}, u32[]{:S(2)}) copy-start(f32[256,960]{1,0:T(8,128)} %copy-done.19) | copy-start | bytes 2949124
  169.8 14.5 %copy-start.28 = (bf16[512,1024]{1,0:T(8,128)(2,1)S(1)}, bf16[512,1024]{1,0:T(8,128)(2,1)}, u32[]{:S(2)}) copy-start(bf16[512,1024]{1,0:T(8,128)(2,1)} %copy-done.27) | copy-start | bytes 3145732
  169.8 14.5 %copy-start.31 = (bf16[512,1024]{1,0:T(8,128)(2,1)S(1)}, bf16[512,1024]{1,0:T(8,128)(2,1)}, u32[]{:S(2)}) copy-start(bf16[512,1024]{1,0:T(8,128)(2,1)} %copy-done.30) | copy-start | bytes 3145732
  183.0 23.8 %collective-permute-start.26 = (bf16[256,640]{1,0:T(8,128)(2,1)S(1)}, bf16[256,640]{1,0:T(8,128)(2,1)S(1)}, u32[]{:S(2)}, u32[]{:S(2)}) collective-permute-start(bf16[256,640]{1,0:T(8,128)(2,1)S(1)} %get-tuple-element.228), channel_id=1, source_target_pairs={{4,0},{8,4},{12,8},{5,1},{9,5},{13,9},{6,2},{10,6},{14,10},{7,3},{... | collective-permute-start | bytes 983048 | tf_op jit(solution)/shard_map/ppermute | solution.py:791
  200.2 11.3 %collective-permute-start.29 = (bf16[256,640]{1,0:T(8,128)(2,1)}, bf16[256,640]{1,0:T(8,128)(2,1)}, u32[]{:S(2)}, u32[]{:S(2)}) collective-permute-start(bf16[256,640]{1,0:T(8,128)(2,1)} %get-tuple-element.233), channel_id=1, source_target_pairs={{4,0},{8,4},{12,8},{5,1},{9,5},{13,9},{6,2},{10,6},{14,10},{7,3},{... | collective-permute-start | bytes 983048 | tf_op jit(solution)/shard_map/ppermute | solution.py:791
  201.5 32.0 %collective-permute-start.31 = (bf16[256,640]{1,0:T(8,128)(2,1)}, bf16[256,640]{1,0:T(8,128)(2,1)}, u32[]{:S(2)}, u32[]{:S(2)}) collective-permute-start(bf16[256,640]{1,0:T(8,128)(2,1)} %get-tuple-element.247), channel_id=1, source_target_pairs={{0,4},{4,8},{8,12},{1,5},{5,9},{9,13},{2,6},{6,10},{10,14},{3,7},{... | collective-permute-start | bytes 983048 | tf_op jit(solution)/shard_map/ppermute | solution.py:791
  207.7 25.8 %collective-permute-start.32 = (bf16[256,640]{1,0:T(8,128)(2,1)}, bf16[256,640]{1,0:T(8,128)(2,1)}, u32[]{:S(2)}, u32[]{:S(2)}) collective-permute-start(bf16[256,640]{1,0:T(8,128)(2,1)} %shard_map.234), channel_id=1, source_target_pairs={{4,0},{8,4},{12,8},{5,1},{9,5},{13,9},{6,2},{10,6},{14,10},{7,3},{... | collective-permute-start | bytes 983048 | tf_op jit(solution)/shard_map/ppermute | solution.py:791
  214.2 22.2 %collective-permute-start.33 = (bf16[256,640]{1,0:T(8,128)(2,1)}, bf16[256,640]{1,0:T(8,128)(2,1)}, u32[]{:S(2)}, u32[]{:S(2)}) collective-permute-start(bf16[256,640]{1,0:T(8,128)(2,1)} %shard_map.236), channel_id=1, source_target_pairs={{4,0},{8,4},{12,8},{5,1},{9,5},{13,9},{6,2},{10,6},{14,10},{7,3},{... | collective-permute-start | bytes 983048 | tf_op jit(solution)/shard_map/ppermute | solution.py:791
  215.5 124.8 %all-gather.5.cloned.1.call-start = ((), (), s32[]{:S(2)}) async-start(), calls=%async_computation.2 | async-start | bytes 2304000 | tf_op jit(solution)/shard_map/all_gather | solution.py:809
  226.0 5.5 %collective-permute-start.30 = (bf16[480,1984]{1,0:T(8,128)(2,1)S(1)}, bf16[480,1984]{1,0:T(8,128)(2,1)S(1)}, u32[]{:S(2)}, u32[]{:S(2)}) collective-permute-start(bf16[480,1984]{1,0:T(8,128)(2,1)S(1)} %get-tuple-element.243), channel_id=1, source_target_pairs={{0,1},{1,0},{2,3},{3,2},{4,5},{5,4},{6,7},{7,6},{8,9},{9,8},{10,11... | collective-permute-start | bytes 5713928 | tf_op jit(solution)/shard_map/ppermute | solution.py:787
  232.3 23.1 %collective-permute-start.35 = (bf16[240,1984]{1,0:T(8,128)(2,1)S(1)}, bf16[240,1984]{1,0:T(8,128)(2,1)S(1)}, u32[]{:S(2)}, u32[]{:S(2)}) collective-permute-start(bf16[240,1984]{1,0:T(8,128)(2,1)S(1)} %get-tuple-element.261), channel_id=1, source_target_pairs={{0,16},{16,0},{1,17},{17,1},{2,18},{18,2},{3,19},{19,3},{4,20},{20... | collective-permute-start | bytes 2856968 | tf_op jit(solution)/shard_map/ppermute | solution.py:787
  240.5 2.4 collective-permute-start.34
  243.1 14.4 %copy-start.114 = (bf16[480]{0:T(512)(128)(2,1)S(1)}, bf16[480]{0:T(512)(128)(2,1)}, u32[]{:S(2)}) copy-start(bf16[480]{0:T(512)(128)(2,1)} %param.17) | copy-start | bytes 2884
  255.7 11.7 %collective-permute-start.37 = (bf16[120,1984]{1,0:T(8,128)(2,1)S(1)}, bf16[120,1984]{1,0:T(8,128)(2,1)S(1)}, u32[]{:S(2)}, u32[]{:S(2)}) collective-permute-start(bf16[120,1984]{1,0:T(8,128)(2,1)S(1)} %get-tuple-element.267), channel_id=1, source_target_pairs={{0,2},{1,3},{2,0},{3,1},{4,6},{5,7},{6,4},{7,5},{8,10},{9,11},{10,... | collective-permute-start | bytes 1428488 | tf_op jit(solution)/shard_map/ppermute | solution.py:787
  256.9 7.4 %collective-permute-start.36 = (bf16[240,640]{1,0:T(8,128)(2,1)S(1)}, bf16[240,640]{1,0:T(8,128)(2,1)S(1)}, u32[]{:S(2)}, u32[]{:S(2)}) collective-permute-start(bf16[240,640]{1,0:T(8,128)(2,1)S(1)} %get-tuple-element.264), channel_id=1, source_target_pairs={{0,16},{16,0},{1,17},{17,1},{2,18},{18,2},{3,19},{19,3},{4,20},{20... | collective-permute-start | bytes 921608 | tf_op jit(solution)/shard_map/ppermute | solution.py:787
  264.4 6.3 %collective-permute-start.38 = (bf16[120,640]{1,0:T(8,128)(2,1)S(1)}, bf16[120,640]{1,0:T(8,128)(2,1)S(1)}, u32[]{:S(2)}, u32[]{:S(2)}) collective-permute-start(bf16[120,640]{1,0:T(8,128)(2,1)S(1)} %get-tuple-element.269), channel_id=1, source_target_pairs={{0,2},{1,3},{2,0},{3,1},{4,6},{5,7},{6,4},{7,5},{8,10},{9,11},{10,... | collective-permute-start | bytes 460808 | tf_op jit(solution)/shard_map/ppermute | solution.py:787
  267.5 10.9 %collective-permute-start.39 = (bf16[120,1984]{1,0:T(8,128)(2,1)S(1)}, bf16[120,1984]{1,0:T(8,128)(2,1)S(1)}, u32[]{:S(2)}, u32[]{:S(2)}) collective-permute-start(bf16[120,1984]{1,0:T(8,128)(2,1)S(1)} %shard_map.247.refs_0_), channel_id=1, source_target_pairs={{0,4},{4,0},{8,12},{12,8},{1,5},{5,1},{9,13},{13,9},{2,6},{6,2},{1... | collective-permute-start | bytes 1428488 | tf_op jit(solution)/shard_map/ppermute | solution.py:787
  270.7 11.1 %collective-permute-start.40 = (bf16[120,640]{1,0:T(8,128)(2,1)S(1)}, bf16[120,640]{1,0:T(8,128)(2,1)S(1)}, u32[]{:S(2)}, u32[]{:S(2)}) collective-permute-start(bf16[120,640]{1,0:T(8,128)(2,1)S(1)} %shard_map.248.refs_0_), channel_id=1, source_target_pairs={{0,4},{4,0},{8,12},{12,8},{1,5},{5,1},{9,13},{13,9},{2,6},{6,2},{1... | collective-permute-start | bytes 460808 | tf_op jit(solution)/shard_map/ppermute | solution.py:787
  278.5 32.0 %collective-permute-start.41 = (bf16[120,1984]{1,0:T(8,128)(2,1)S(1)}, bf16[120,1984]{1,0:T(8,128)(2,1)S(1)}, u32[]{:S(2)}, u32[]{:S(2)}) collective-permute-start(bf16[120,1984]{1,0:T(8,128)(2,1)S(1)} %shard_map.249.refs_0_), channel_id=1, source_target_pairs={{0,8},{4,12},{8,0},{12,4},{1,9},{5,13},{9,1},{13,5},{2,10},{6,14},... | collective-permute-start | bytes 1428488 | tf_op jit(solution)/shard_map/ppermute | solution.py:787
  281.9 44.0 %collective-permute-start.42 = (bf16[120,640]{1,0:T(8,128)(2,1)S(1)}, bf16[120,640]{1,0:T(8,128)(2,1)S(1)}, u32[]{:S(2)}, u32[]{:S(2)}) collective-permute-start(bf16[120,640]{1,0:T(8,128)(2,1)S(1)} %shard_map.250.refs_0_), channel_id=1, source_target_pairs={{0,8},{4,12},{8,0},{12,4},{1,9},{5,13},{9,1},{13,5},{2,10},{6,14},... | collective-permute-start | bytes 460808 | tf_op jit(solution)/shard_map/ppermute | solution.py:787
  310.6 33.2 %collective-permute-start.43 = (bf16[120,1984]{1,0:T(8,128)(2,1)S(1)}, bf16[120,1984]{1,0:T(8,128)(2,1)S(1)}, u32[]{:S(2)}, u32[]{:S(2)}) collective-permute-start(bf16[120,1984]{1,0:T(8,128)(2,1)S(1)} %shard_map.251.own_ref), channel_id=1, source_target_pairs={{0,2},{1,3},{2,0},{3,1},{4,6},{5,7},{6,4},{7,5},{8,10},{9,11},{10,... | collective-permute-start | bytes 1428488 | tf_op jit(solution)/shard_map/ppermute | solution.py:787
  325.9 20.3 %collective-permute-start.44 = (bf16[120,640]{1,0:T(8,128)(2,1)S(1)}, bf16[120,640]{1,0:T(8,128)(2,1)S(1)}, u32[]{:S(2)}, u32[]{:S(2)}) collective-permute-start(bf16[120,640]{1,0:T(8,128)(2,1)S(1)} %shard_map.252.own_ref), channel_id=1, source_target_pairs={{0,2},{1,3},{2,0},{3,1},{4,6},{5,7},{6,4},{7,5},{8,10},{9,11},{10,... | collective-permute-start | bytes 460808 | tf_op jit(solution)/shard_map/ppermute | solution.py:787
  344.1 4.3 %collective-permute-start.45 = (bf16[240,1984]{1,0:T(8,128)(2,1)S(1)}, bf16[240,1984]{1,0:T(8,128)(2,1)S(1)}, u32[]{:S(2)}, u32[]{:S(2)}) collective-permute-start(bf16[240,1984]{1,0:T(8,128)(2,1)S(1)} %shard_map.254.own_ref), channel_id=1, source_target_pairs={{0,1},{1,0},{2,3},{3,2},{4,5},{5,4},{6,7},{7,6},{8,9},{9,8},{10,11... | collective-permute-start | bytes 2856968 | tf_op jit(solution)/shard_map/ppermute | solution.py:787
  346.3 4.8 %collective-permute-start.46 = (bf16[240,640]{1,0:T(8,128)(2,1)S(1)}, bf16[240,640]{1,0:T(8,128)(2,1)S(1)}, u32[]{:S(2)}, u32[]{:S(2)}) collective-permute-start(bf16[240,640]{1,0:T(8,128)(2,1)S(1)} %shard_map.255.own_ref), channel_id=1, source_target_pairs={{0,1},{1,0},{2,3},{3,2},{4,5},{5,4},{6,7},{7,6},{8,9},{9,8},{10,11... | collective-permute-start | bytes 921608 | tf_op jit(solution)/shard_map/ppermute | solution.py:787
  (104 other events, 381.2 us)
Sparse Core Ops, SparseCore 0:
  52.5 52.8 all-gather.2
  215.7 43.5 reduce-scatter.3
  273.9 66.3 all-gather.4
